TPU v7x, 128 devices: a whole 4x4x4 slice. The times are simulated.
128 devices in a mesh: dp: 8 (over z, core), mp: 16 (over x, y).
Axes of the slice: x: 4, y: 4, z: 4, core: 2. Of those that a mesh axis runs over, the one named last changes fastest.
Arguments:
- hidden_in: bfloat16 [32768, 2048], P(('dp', 'mp')), may hold values from -6 to 6
- mlp_gain: bfloat16 [2048], replicated, may hold values from 0.25 to 1.75
- w_gate: bfloat16 [2048, 5504], P(None, 'mp'), may hold values from -0.125 to 0.125
- w_up: bfloat16 [2048, 5504], P(None, 'mp'), may hold values from -0.125 to 0.125
- w_down: bfloat16 [5504, 2048], P('mp'), may hold values from -0.078125 to 0.078125
- lengths: int32 [1024], P(('dp', 'mp')), may hold values from 1 to 32
- file_cluster: int32 [1024], P(('dp', 'mp')), may hold values from 0 to 127, as said below
- file_order: int32 [1024], P(('dp', 'mp')), may hold values from 0 to 1048575
- cluster_slot: int32 [128], replicated, may hold values from 0 to 127, as said below
- bank: bfloat16 [262144, 2048], P(('dp', 'mp')), may hold values from -0.125 to 0.125
- bank_slot: int32 [262144], P(('dp', 'mp')), may hold values from 0 to 15
- bank_order: int32 [262144], P(('dp', 'mp')), may hold values from 0 to 1048575
- centroid_old: float32 [128, 2048], P(('dp', 'mp')), may hold values from -0.125 to 0.125
- count_old: float32 [128], P(('dp', 'mp')), may hold values from 1 to 8
Outputs:
- max_sim: float32 [1024], P(('dp', 'mp'))
- centroid_new: float32 [128, 2048], P(('dp', 'mp'))
Inputs may be any that keep to these rules, and one draw needn't show every extreme that they name: `file_cluster`: the files of one device have at most 2 slots in any one owner's range of 16 slots; the first device has exactly 2 files in one range. `cluster_slot`: A permutation of the 128 slots.
All inputs are finite; a program needn't handle non-finite values.
Results may differ from a plain program's by a relative error of at most 0.0023.
Values may be sent and summed in bfloat16 or wider, within the bound.
No kernel may reach another device: no remote copies, remote signals or barrier semaphores. Data moves between devices by JAX's collectives and lax.ppermute only.
A program may use at most 192 MiB of HBM per device.

v0:
```python
import jax
import jax.numpy as jnp
from jax import lax
from jax.sharding import PartitionSpec as P


def bank_match(flat, local_plus, orders, bank, bank_slot, bank_order):
    sims = lax.dot_general(flat, bank, (((1,), (1,)), ((), ())), preferred_element_type=jnp.float32)
    valid = (bank_slot[None, :] + 1 == local_plus[:, None]) & (
        bank_order[None, :] < orders[:, None]
    )
    return jnp.max(jnp.where(valid, sims, jnp.float32(-1.0)), axis=1)


def on_device(
    hidden_in,
    mlp_gain,
    w_gate,
    w_up,
    w_down,
    lengths,
    file_cluster,
    file_order,
    cluster_slot,
    bank,
    bank_slot,
    bank_order,
    centroid_old,
    count_old,
):
    n_model = lax.axis_size("mp")
    n_data = lax.axis_size("dp")
    tok_dev, width = hidden_in.shape
    files_dev = lengths.shape[0]
    file_len = tok_dev // files_dev
    resid = hidden_in.astype(jnp.float32)
    scale = lax.rsqrt(jnp.mean(resid * resid, axis=-1, keepdims=True) + 1e-05)
    normed = (resid * scale * mlp_gain.astype(jnp.float32)).astype(jnp.bfloat16)
    piece = lax.all_gather(normed, "mp", axis=0, tiled=True)
    gate = jnp.dot(piece, w_gate, preferred_element_type=jnp.float32)
    upper = jnp.dot(piece, w_up, preferred_element_type=jnp.float32)
    units = (jax.nn.silu(gate) * upper).astype(jnp.bfloat16)
    valid_own = (jnp.arange(file_len)[None, :] < lengths[:, None]).astype(jnp.float32)
    block_out = lax.psum_scatter(
        jnp.dot(units, w_down, preferred_element_type=jnp.float32),
        "mp",
        scatter_dimension=0,
        tiled=True,
    )
    mixed = resid + block_out
    pooled = jnp.sum(mixed.reshape(files_dev, file_len, width) * valid_own[:, :, None], axis=1)
    pooled = pooled / lengths.astype(jnp.float32)[:, None]
    emb = (pooled * lax.rsqrt(jnp.sum(pooled * pooled, axis=-1, keepdims=True) + 1e-06)).astype(
        jnp.bfloat16
    )
    k_total = cluster_slot.shape[0]
    owned = k_total // n_data
    rows_mine = centroid_old.shape[0]
    my_data = lax.axis_index("dp")
    my_model = lax.axis_index("mp")
    lookup = file_cluster[:, None] == jnp.arange(k_total, dtype=jnp.int32)[None, :]
    slot = jnp.sum(jnp.where(lookup, cluster_slot[None, :], 0), axis=1)
    slot_ids = jnp.arange(owned, dtype=jnp.int32)[:, None] + 1
    meta = jnp.stack([slot, file_order], axis=1)
    rows_piece = lax.all_gather(emb, ("dp", "mp"), axis=0, tiled=True)
    meta_piece = lax.all_gather(meta, ("dp", "mp"), axis=0, tiled=True)
    slot_piece = meta_piece[:, 0]
    local_plus = jnp.where(slot_piece // owned == my_data, slot_piece % owned + 1, 0)
    best = bank_match(rows_piece, local_plus, meta_piece[:, 1], bank, bank_slot, bank_order)
    maxima = best
    member = local_plus[None, :] == slot_ids
    sums = jnp.dot(member.astype(jnp.bfloat16), rows_piece, preferred_element_type=jnp.float32)
    counts = jnp.sum(member.astype(jnp.float32), axis=1)
    maxima, sums, counts = (maxima, sums, counts)
    every_top = lax.pmax(maxima, ("dp", "mp"))
    first = (my_data * n_model + my_model) * files_dev
    max_sim = lax.dynamic_slice_in_dim(every_top, first, files_dev, 0)
    my_sums = lax.dynamic_slice_in_dim(sums, my_model * rows_mine, rows_mine, 0)
    my_counts = lax.dynamic_slice_in_dim(counts, my_model * rows_mine, rows_mine, 0)
    centroid_new = (count_old[:, None] * centroid_old + my_sums) / (count_old + my_counts)[:, None]
    return (max_sim, centroid_new)


def solution(mesh):
    return jax.shard_map(
        on_device,
        mesh=mesh,
        in_specs=(
            P(("dp", "mp"), None),
            P(),
            P(None, "mp"),
            P(None, "mp"),
            P("mp", None),
            P(("dp", "mp")),
            P(("dp", "mp")),
            P(("dp", "mp")),
            P(),
            P(("dp", "mp"), None),
            P(("dp", "mp")),
            P(("dp", "mp")),
            P(("dp", "mp"), None),
            P(("dp", "mp")),
        ),
        out_specs=(P(("dp", "mp")), P(("dp", "mp"), None)),
        check_vma=False,
    )
```

profile of v0, /device:TPU:1, one launch (start us, length us, event | category | flops | bytes accessed | tf_op | source)
XLA Modules:
  0.0 516.4 jit_solution(6005557115383443319)
XLA Ops:
  7.2 0.8 convert_element_type.30
  8.1 1.5 fusion.3
  9.6 2.5 fusion.5
  12.1 0.0 reduce-scatter.2.cloned.1.call-start
  12.2 114.5 %all-gather.4.cloned.1.call-done = bf16[4096,2048]{1,0:T(8,128)(2,1)} async-done(((bf16[256,2048]{1,0:T(8,128)(2,1)}), bf16[4096,2048]{1,0:T(8,128)(2,1)}) %all-gather.4.cloned.1.call-update) | async-done | bytes 16777232 | tf_op jit(solution)/shard_map/all_gather | solution.py:39
  126.7 12.1 %fusion.20 = f32[4096,344]{0,1:T(8,128)} fusion(bf16[4096,2048]{1,0:T(8,128)(2,1)} %all-gather.4.cloned.1.call-done, bf16[2048,344]{0,1:T(8,128)(2,1)S(1)} %copy-done.7), kind=kOutput, calls=%fused_computation.51 | convolution fusion | flops 5771362304 | bytes 23822336 | tf_op jit(solution)/shard_map/dot_general | solution.py:40
  138.8 26.6 %fusion.1 = f32[4096,2048]{1,0:T(8,128)} fusion(bf16[344,2048]{1,0:T(8,128)(2,1)S(1)} %copy-done, bf16[4096,2048]{1,0:T(8,128)(2,1)} %all-gather.4.cloned.1.call-done, bf16[2048,344]{0,1:T(8,128)(2,1)} %param.17, f32[4096,344]{0,1:T(8,128)} %fusion.20), kind=kOutput, calls=%fused_computation.3 | convolution fusion | flops 11551178752 | bytes 58785792 | tf_op jit(solution)/shard_map/dot_general | solution.py:45
  165.5 0.5 copy-done.5
  166.1 0.1 fusion.15
  166.1 194.1 %reduce-scatter.2.cloned.1.call-done = f32[256,2048]{1,0:T(8,128)} async-done(((f32[4096,2048]{1,0:T(8,128)}), f32[256,2048]{1,0:T(8,128)}) %reduce-scatter.2.cloned.1.call-update) | async-done | bytes 2097168 | tf_op jit(solution)/shard_map/reduce_scatter | solution.py:44
  360.2 2.1 multiply_reduce_fusion
  362.3 0.2 multiply_reduce_fusion.1
  362.5 0.7 multiply_convert_fusion
  363.3 0.2 select_reduce_fusion.1
  363.5 55.4 %all-gather = s32[128,8,2]{1,2,0:T(2,128)S(1)} all-gather(s32[1,8,2]{1,2,0:T(2,128)S(1)} %add_bitcast_fusion), channel_id=1, replica_groups=mesh['dp'=8,'mp'=16] {'dp','mp'}, dimensions={0}, use_global_device_ids=true | all-gather | bytes 8256 | tf_op jit(solution)/shard_map/all_gather | solution.py:66
  418.9 0.1 reshape.114
  419.7 0.2 fusion.8
  419.9 0.6 dynamic_slice.11
  421.2 9.1 %all-gather.6.cloned.1.call-done = bf16[1024,2048]{1,0:T(8,128)(2,1)} async-done(((bf16[8,2048]{1,0:T(8,128)(2,1)}), bf16[1024,2048]{1,0:T(8,128)(2,1)}) %all-gather.6.cloned.1.call-update) | async-done | bytes 4194320 | tf_op jit(solution)/shard_map/all_gather | solution.py:65
  430.3 13.1 %select_reduce_fusion = f32[1024]{0:T(1024)S(1)} fusion(s32[2048]{0:T(1024)S(1)} %copy-done.8, s32[2048]{0:T(1024)S(1)} %broadcast_add_fusion, s32[1024]{0:T(1024)S(1)} %bitcast.24, s32[1024]{0:T(1024)S(1)} %bitcast.23, bf16[1024,2048]{1,0:T(8,128)(2,1)} %all-gather.6.cloned.1.call-done, bf16[2048,2048]{1,0:T(8,128)(2,1)} %param.23), kind=kOutput, calls=%fused_computation | convolution fusion | flops 8600419328 | bytes 12611584 | tf_op jit(solution)/shard_map/dot_general | solution.py:8
  443.4 62.4 %pmax.7 = f32[1024]{0:T(1024)S(1)} all-reduce(f32[1024]{0:T(1024)S(1)} %select_reduce_fusion), channel_id=1, replica_groups=mesh['dp'=8,'mp'=16] {'dp','mp'}, use_global_device_ids=true, to_apply=%region_6.7 | all-reduce | flops 1024 | bytes 8192 | tf_op jit(solution)/shard_map/pmax | solution.py:75
  505.8 0.6 dynamic_slice.9
  506.4 2.9 fusion.6
  509.2 0.6 add_divide_fusion
  (35 shorter events, 0.3 us)
Async XLA Ops:
  7.2 131.6 %copy-start = (bf16[344,2048]{1,0:T(8,128)(2,1)S(1)}, bf16[344,2048]{1,0:T(8,128)(2,1)}, u32[]{:S(2)}) copy-start(bf16[344,2048]{1,0:T(8,128)(2,1)} %param.18) | copy-start | bytes 4227076
  7.2 119.5 %copy-start.7 = (bf16[2048,344]{0,1:T(8,128)(2,1)S(1)}, bf16[2048,344]{0,1:T(8,128)(2,1)}, u32[]{:S(2)}) copy-start(bf16[2048,344]{0,1:T(8,128)(2,1)} %param.16) | copy-start | bytes 4227076
  7.2 119.5 %all-gather.4.cloned.1.call-start = ((), (), s32[]{:S(2)}) async-start(), calls=%async_computation.1 | async-start | bytes 17825792 | tf_op jit(solution)/shard_map/all_gather | solution.py:39
  12.1 348.1 %reduce-scatter.2.cloned.1.call-start = ((), (), s32[]{:S(2)}) async-start(), calls=%async_computation.2 | async-start | bytes 35651584 | tf_op jit(solution)/shard_map/reduce_scatter | solution.py:44
  165.4 0.7 copy-start.5
  165.4 194.8 %copy-start.2 = (bf16[256,2048]{1,0:T(8,128)(2,1)S(1)}, bf16[256,2048]{1,0:T(8,128)(2,1)}, u32[]{:S(2)}) copy-start(bf16[256,2048]{1,0:T(8,128)(2,1)} %param.14) | copy-start | bytes 3145732
  165.4 197.8 %copy-start.9 = (s32[128]{0:T(128)S(1)}, s32[128]{0:T(128)}, u32[]{:S(2)}) copy-start(s32[128]{0:T(128)} %param.22) | copy-start | bytes 1540
  165.4 197.8 %copy-start.10 = (s32[8]{0:T(128)S(1)}, s32[8]{0:T(128)}, u32[]{:S(2)}) copy-start(s32[8]{0:T(128)} %param.20) | copy-start | bytes 100
  165.4 198.0 %copy-start.6 = (s32[8]{0:T(128)S(1)}, s32[8]{0:T(128)}, u32[]{:S(2)}) copy-start(s32[8]{0:T(128)} %param.21) | copy-start | bytes 100
  165.4 255.7 %copy-start.4 = (s32[2048]{0:T(1024)S(1)}, s32[2048]{0:T(1024)}, u32[]{:S(2)}) copy-start(s32[2048]{0:T(1024)} %param.24) | copy-start | bytes 24580
  165.4 264.8 %copy-start.8 = (s32[2048]{0:T(1024)S(1)}, s32[2048]{0:T(1024)}, u32[]{:S(2)}) copy-start(s32[2048]{0:T(1024)} %param.25) | copy-start | bytes 24580
  165.5 264.8 %all-gather.6.cloned.1.call-start = ((), (), s32[]{:S(2)}) async-start(), calls=%async_computation.3 | async-start | bytes 4227072 | tf_op jit(solution)/shard_map/all_gather | solution.py:65
  430.3 79.6 %copy-start.1 = (bf16[344,2048]{1,0:T(8,128)(2,1)S(1)}, bf16[344,2048]{1,0:T(8,128)(2,1)}, u32[]{:S(2)}) copy-start(bf16[344,2048]{1,0:T(8,128)(2,1)} %param.18) | copy-start | bytes 4227076
  443.4 65.9 %copy-start.3 = (f32[1,2048]{1,0:T(1,128)S(1)}, f32[1,2048]{1,0:T(1,128)}, u32[]{:S(2)}) copy-start(f32[1,2048]{1,0:T(1,128)} %param.26) | copy-start | bytes 24580
Sparse Core Ops, SparseCore 0:
  12.3 114.3 all-gather.3
  165.6 194.5 reduce-scatter.1
  363.3 66.8 all-gather.5
where the time goes:
time: 517 us; the launch traced here: 516 us
  waiting for transfers between devices  318 us (62%)
  blocking collectives  118 us (23%)
  matrix products  54.7 us (11%)
  between operations  15.2 us (3%)
  other arithmetic  9.01 us (2%)
    reduce_scatter x1, waiting for transfers between devices, on_device(): lax.psum_scatter(jnp.dot(units, w_down, preferred_element_type=jnp.float3...  194 us
    all_gather x1, waiting for transfers between devices, on_device(): piece = lax.all_gather(normed, 'mp', axis=0, tiled=True)  114 us
    pmax x1, blocking collectives, on_device(): every_top = lax.pmax(maxima, ('dp', 'mp'))  62.4 us
    all_gather x1, blocking collectives, on_device(): meta_piece = lax.all_gather(meta, ('dp', 'mp'), axis=0, tiled=True)  55.4 us
    dot_general x1, matrix products, on_device(): jnp.dot(units, w_down, preferred_element_type=jnp.float32)  26.6 us
    dot_general x1, matrix products, bank_match(): lax.dot_general(flat, bank, (((1,), (1,)), ((), ())), preferred_element_t...  13.1 us
    dot_general x1, matrix products, on_device(): gate = jnp.dot(piece, w_gate, preferred_element_type=jnp.float32)  12.1 us
  transfers between devices with their start and end apart: 3, of which 3 were waited for; matrix products, arithmetic and copies ran while one was open for 0% of the time, Pallas kernels for 0%

commit v1 on v0

v1 whole, which is shorter than its diff:
```python
import functools

import jax
import jax.numpy as jnp
from jax import lax
from jax.experimental import pallas as pl
from jax.experimental.pallas import tpu as pltpu
from jax.sharding import PartitionSpec as P

ALL = ("dp", "mp")
NX, NY, NZ, NC = 4, 4, 4, 2
BF, F32, I32 = jnp.bfloat16, jnp.float32, jnp.int32
VMEM = pltpu.CompilerParams(vmem_limit_bytes=56 * 1024 * 1024)
NT = (((1,), (1,)), ((), ()))


def from_x(v, j):
    perm = [(((x + j) % NX) * NY + y, x * NY + y) for x in range(NX) for y in range(NY)]
    return lax.ppermute(v, "mp", perm)


def from_y(v, k):
    perm = [(x * NY + (y + k) % NY, x * NY + y) for x in range(NX) for y in range(NY)]
    return lax.ppermute(v, "mp", perm)


def from_z(v, k):
    perm = [(((z + k) % NZ) * NC + c, z * NC + c) for z in range(NZ) for c in range(NC)]
    return lax.ppermute(v, "dp", perm)


def from_core(v):
    return lax.ppermute(v, "dp", [(d ^ 1, d) for d in range(NZ * NC)])


def block_ones(files, file_len, dtype):
    row = lax.broadcasted_iota(I32, (files, files * file_len), 0)
    col = lax.broadcasted_iota(I32, (files, files * file_len), 1)
    return jnp.where(col // file_len == row, 1.0, 0.0).astype(dtype)


def prep_kernel(file_len, h_ref, gain_ref, mask_ref, n_ref, p_ref):
    resid = h_ref[...].astype(F32)
    scale = lax.rsqrt(jnp.mean(resid * resid, axis=-1, keepdims=True) + 1e-05)
    normed = resid * scale * gain_ref[...].astype(F32)
    keep = mask_ref[...] > 0.5
    n_ref[...] = jnp.where(keep, normed, 0.0).astype(BF)
    files = p_ref.shape[0]
    valid = jnp.where(keep, resid, 0.0).astype(BF)
    p_ref[...] = jnp.dot(block_ones(files, file_len, BF), valid, preferred_element_type=F32)


def prep(hidden, gain, mask, files):
    tok, width = hidden.shape
    return pl.pallas_call(
        functools.partial(prep_kernel, tok // files),
        out_shape=(jax.ShapeDtypeStruct((tok, width), BF), jax.ShapeDtypeStruct((files, width), F32)),
        compiler_params=VMEM,
        name="prep",
    )(hidden, gain[None, :], mask)


def ffn_kernel(n_tok, n_slices, n_parts, files, off_ref, *refs):
    toks = refs[:n_tok]
    parts = refs[n_tok:n_tok + n_slices * n_parts]
    outs = refs[n_tok + n_slices * n_parts:n_tok + n_slices * n_parts + n_slices]
    t_buf, w_buf, t_sem, w_sem = refs[n_tok + n_slices * n_parts + n_slices:]
    tok = toks[0].shape[0]
    half = w_buf.shape[2] // 2
    w_copies = []
    t_copies = []
    for s in range(n_slices):
        row = []
        for p in range(n_parts):
            src = parts[s * n_parts + p]
            rows = src.shape[0]
            start = pl.multiple_of(off_ref[s * n_parts + p], 256)
            cp = pltpu.make_async_copy(src, w_buf.at[s, pl.ds(start, rows)], w_sem.at[s, p])
            cp.start()
            row.append(cp)
        w_copies.append(row)
        if s == 0:
            for t in range(n_tok):
                cp = pltpu.make_async_copy(toks[t], t_buf.at[pl.ds(t * tok, tok)], t_sem.at[t])
                cp.start()
                t_copies.append(cp)
    ones = block_ones(files, tok // files, BF)
    for s in range(n_slices):
        for cp in w_copies[s]:
            cp.wait()
        for t in range(n_tok):
            if s == 0:
                t_copies[t].wait()
            x = t_buf[t * tok:(t + 1) * tok, :]
            both = jnp.dot(x, w_buf[s], preferred_element_type=F32)
            gate = both[:, :half]
            units = (gate / (1.0 + jnp.exp(-gate)) * both[:, half:]).astype(BF)
            outs[s][t * files:(t + 1) * files, :] = jnp.dot(ones, units, preferred_element_type=F32)


def ffn(toks, slices, offs, files, name):
    n_tok, n_slices, n_parts = len(toks), len(slices), len(slices[0])
    tok, width = toks[0].shape
    cols = slices[0][0].shape[1]
    flat = [p for s in slices for p in s]
    anyspec = pl.BlockSpec(memory_space=pl.ANY)
    out = jax.ShapeDtypeStruct((n_tok * files, cols // 2), F32)
    return pl.pallas_call(
        functools.partial(ffn_kernel, n_tok, n_slices, n_parts, files),
        in_specs=[pl.BlockSpec(memory_space=pltpu.SMEM)] + [anyspec] * (n_tok + len(flat)),
        out_specs=tuple(pl.BlockSpec(memory_space=pltpu.VMEM) for _ in slices),
        out_shape=tuple(out for _ in slices),
        scratch_shapes=[
            pltpu.VMEM((n_tok * tok, width), BF),
            pltpu.VMEM((n_slices, width, cols), BF),
            pltpu.SemaphoreType.DMA((n_tok,)),
            pltpu.SemaphoreType.DMA((n_slices, n_parts)),
        ],
        compiler_params=VMEM,
        name=name,
    )(offs, *toks, *flat)


def down_kernel(files, pos_ref, u0, u1, u2, u3, w_ref, o_ref, buf):
    for k, u in enumerate((u0, u1, u2, u3)):
        for j in range(NX):
            dst = pl.multiple_of(pos_ref[k * NX + j], files)
            buf[pl.ds(dst, files), :] = u[j * files:(j + 1) * files, :]
    hid = w_ref.shape[0]
    rows = buf[:, :hid]
    hi = rows.astype(BF)
    lo = (rows - hi.astype(F32)).astype(BF)
    w = w_ref[...]
    o_ref[...] = jnp.dot(hi, w, preferred_element_type=F32) + jnp.dot(lo, w, preferred_element_type=F32)


def down(us, w_down, pos, files):
    rows = NX * NY * files
    vm = pl.BlockSpec(memory_space=pltpu.VMEM)
    return pl.pallas_call(
        functools.partial(down_kernel, files),
        in_specs=[pl.BlockSpec(memory_space=pltpu.SMEM)] + [vm] * 5,
        out_specs=vm,
        out_shape=jax.ShapeDtypeStruct((rows, w_down.shape[1]), F32),
        scratch_shapes=[pltpu.VMEM((rows, us[0].shape[1]), F32)],
        compiler_params=VMEM,
        name="down",
    )(pos, *us, w_down)


def emb_kernel(files, t_ref, p_ref, len_ref, o_ref):
    total = p_ref[...]
    for m in range(t_ref.shape[0] // files):
        total = total + t_ref[m * files:(m + 1) * files, :]
    pooled = total / len_ref[...]
    norm = lax.rsqrt(jnp.sum(pooled * pooled, axis=-1, keepdims=True) + 1e-06)
    o_ref[...] = (pooled * norm).astype(BF)


def emb_of(terms, pooled, lens, files):
    return pl.pallas_call(
        functools.partial(emb_kernel, files),
        out_shape=jax.ShapeDtypeStruct(pooled.shape, BF),
        compiler_params=VMEM,
        name="emb",
    )(terms, pooled, lens)


def spread_kernel(emb_ref, sel_ref, o_ref):
    o_ref[...] = jnp.dot(sel_ref[...], emb_ref[...], preferred_element_type=F32).astype(BF)


def spread(emb, sel):
    return pl.pallas_call(
        spread_kernel,
        out_shape=jax.ShapeDtypeStruct((sel.shape[0], emb.shape[1]), BF),
        compiler_params=VMEM,
        name="spread",
    )(emb, sel)


def match_kernel(rows_ref, lp_ref, ord_ref, mem_ref, bank_ref, slot_ref, border_ref, best_ref, sums_ref, acc):
    step = pl.program_id(0)

    @pl.when(step == 0)
    def _():
        acc[...] = jnp.full(acc.shape, -1.0, F32)
        sums_ref[...] = jnp.dot(mem_ref[...], rows_ref[...], preferred_element_type=F32)

    sims = lax.dot_general(rows_ref[...], bank_ref[...], NT, preferred_element_type=F32)
    valid = (slot_ref[...] + 1 == lp_ref[...]) & (border_ref[...] < ord_ref[...])
    acc[...] = jnp.maximum(acc[...], jnp.where(valid, sims, -1.0))

    @pl.when(step == pl.num_programs(0) - 1)
    def _():
        best_ref[...] = jnp.max(acc[...], axis=1, keepdims=True)


def match(rows, lp, order, member, bank, bank_slot, bank_order):
    n, width = rows.shape
    block = 512
    whole = lambda shape: pl.BlockSpec(shape, lambda i: (0, 0))
    return pl.pallas_call(
        match_kernel,
        grid=(bank.shape[0] // block,),
        in_specs=[
            whole((n, width)),
            whole((n, 1)),
            whole((n, 1)),
            whole(member.shape),
            pl.BlockSpec((block, width), lambda i: (i, 0)),
            pl.BlockSpec((1, block), lambda i: (0, i)),
            pl.BlockSpec((1, block), lambda i: (0, i)),
        ],
        out_specs=(whole((n, 1)), whole((member.shape[0], width))),
        out_shape=(jax.ShapeDtypeStruct((n, 1), F32), jax.ShapeDtypeStruct((member.shape[0], width), F32)),
        scratch_shapes=[pltpu.VMEM((n, block), F32)],
        compiler_params=VMEM,
        name="match",
    )(rows, lp, order, member, bank, bank_slot[None, :], bank_order[None, :])


def on_device(
    hidden_in,
    mlp_gain,
    w_gate,
    w_up,
    w_down,
    lengths,
    file_cluster,
    file_order,
    cluster_slot,
    bank,
    bank_slot,
    bank_order,
    centroid_old,
    count_old,
):
    tok, width = hidden_in.shape
    files = lengths.shape[0]
    file_len = tok // files
    n_dp, n_mp = NZ * NC, NX * NY
    hid = w_gate.shape[1]
    lanes = -(-hid // 128) * 128
    dp, mp = lax.axis_index("dp"), lax.axis_index("mp")
    z, c, x, y = dp // NC, dp % NC, mp // NY, mp % NY

    def packed(start, rows):
        pad = ((0, 0), (0, lanes - hid))
        g = jnp.pad(lax.dynamic_slice_in_dim(w_gate, start, rows, 0), pad)
        u = jnp.pad(lax.dynamic_slice_in_dim(w_up, start, rows, 0), pad)
        return jnp.concatenate([g, u], axis=1)

    eighth, half = width // 8, width // 2
    w_e = packed(dp * eighth, eighth)
    w_h = packed(c * half, half)
    e0 = from_y(w_e, 2)
    h1, h3 = from_y(w_h, 1), from_y(w_h, 3)

    mask = (jnp.arange(file_len, dtype=I32)[None, :] < lengths[:, None]).astype(F32).reshape(tok, 1)
    normed, pooled_in = prep(hidden_in, mlp_gain, mask, files)
    toks = [normed] + [from_x(normed, j) for j in (1, 2, 3)]

    es = [e0] + [from_z(e0, k) for k in (1, 2, 3)]
    es = es + [from_core(e) for e in es]
    e_off = jnp.stack(
        [(((z + k) % NZ) * NC + c) * eighth for k in range(NZ)]
        + [(((z + k) % NZ) * NC + (1 - c)) * eighth for k in range(NZ)]
    ).astype(I32)
    h_off = jnp.stack([c * half, (1 - c) * half] * 2).astype(I32)
    g1, g3 = from_core(h1), from_core(h3)

    w_own = packed(0, width)
    (u0,) = ffn(toks, [[w_own]], jnp.zeros((1,), I32), files, "ffn_own")
    (u2,) = ffn(toks, [es], e_off, files, "ffn_far")
    r2 = from_y(u2, NY - 2)
    u1, u3 = ffn(toks, [[h1, g1], [h3, g3]], h_off, files, "ffn_near")
    r1, r3 = from_y(u1, NY - 1), from_y(u3, NY - 3)
    pos = jnp.stack(
        [(((x + j) % NX) * NY + (y - k) % NY) * files for k in range(NY) for j in range(NX)]
    ).astype(I32)
    terms = down([u0, r1, r2, r3], w_down, pos, files)
    terms = lax.all_to_all(terms, "mp", 0, 0, tiled=True)
    emb = emb_of(terms, pooled_in, lengths.astype(F32)[:, None], files)

    k_total = cluster_slot.shape[0]
    owned = k_total // n_dp
    lookup = file_cluster[:, None] == jnp.arange(k_total, dtype=I32)[None, :]
    slot = jnp.sum(jnp.where(lookup, cluster_slot[None, :], 0), axis=1)
    owner, local = slot // owned, slot % owned + 1
    same = owner[:, None] == owner[None, :]
    earlier = jnp.arange(files, dtype=I32)[None, :] < jnp.arange(files, dtype=I32)[:, None]
    rank = jnp.sum((same & earlier).astype(I32), axis=1)
    place = (owner[None, None, :] == jnp.arange(n_dp, dtype=I32)[:, None, None]) & (
        rank[None, None, :] == jnp.arange(files, dtype=I32)[None, :, None]
    )
    send_lp = jnp.sum(jnp.where(place, local[None, None, :], 0), axis=2)
    send_ord = jnp.sum(jnp.where(place, file_order[None, None, :], 0), axis=2)
    most = jnp.broadcast_to(jnp.max(rank) + 1, (n_dp, 1)).astype(I32)
    meta = jnp.concatenate([send_lp, send_ord, most], axis=1)
    meta = jnp.broadcast_to(meta[:, None, :], (n_dp, n_mp, 2 * files + 1)).reshape(n_dp * n_mp, 2 * files + 1)
    meta, _ = lax.optimization_barrier((meta, e0))
    meta = lax.all_to_all(meta, ALL, 0, 0, tiled=True)
    got_lp, got_ord = meta[:, :files], meta[:, files:2 * files]
    rounds = (jnp.max(meta[:, 2 * files]) + 1) // 2

    def one_round(r, best, sums, counts):
        here = lax.dynamic_slice_in_dim(place, 2 * r, 2, 1)
        sel = jnp.broadcast_to(here[:, None], (n_dp, n_mp, 2, files)).reshape(-1, files).astype(BF)
        rows = lax.all_to_all(spread(emb, sel), ALL, 0, 0, tiled=True)
        lp = lax.dynamic_slice_in_dim(got_lp, 2 * r, 2, 1).reshape(-1)
        order = lax.dynamic_slice_in_dim(got_ord, 2 * r, 2, 1).reshape(-1)
        mine = lp == mp + 1
        member = jnp.broadcast_to(mine[None, :], (8, lp.shape[0])).astype(BF)
        top, new = match(rows, lp[:, None], order[:, None], member, bank, bank_slot, bank_order)
        back = lax.all_to_all(top.reshape(-1, 2), ALL, 0, 0, tiled=True)
        back = jnp.max(back.reshape(n_dp, n_mp, 2), axis=1)
        best = jnp.maximum(best, jnp.max(jnp.where(here, back[:, :, None], -1.0), axis=(0, 1)))
        return best, sums + new[:1], counts + jnp.sum(mine.astype(F32))

    state = one_round(0, jnp.full((files,), -1.0, F32), jnp.zeros((1, width), F32), jnp.float32(0))
    _, best, sums, counts = lax.while_loop(
        lambda s: s[0] < rounds, lambda s: (s[0] + 1,) + one_round(*s), (jnp.int32(1),) + state
    )
    centroid_new = (count_old[:, None] * centroid_old + sums) / (count_old + counts)[:, None]
    return best, centroid_new


def solution(mesh):
    both = P(ALL)
    rows = P(ALL, None)
    return jax.shard_map(
        on_device,
        mesh=mesh,
        in_specs=(
            rows, P(), P(None, "mp"), P(None, "mp"), P("mp", None), both, both, both, P(), rows, both, both, rows, both,
        ),
        out_specs=(both, rows),
        check_vma=False,
    )
```

time: 517 us -> 265 us (0.51)
  waiting for transfers between devices: 318 us -> 132 us
  blocking collectives: 118 us -> 0 us
  matrix products: 54.7 us -> 0 us
  starting transfers between devices: 0.12 us -> 50.5 us
  Pallas kernels: 0 us -> 49.9 us
  local copies, waits for them, and re-layouts: 1.87 us -> 18.4 us
  between operations: 15.2 us -> 3.73 us
    reduce_scatter x1 -> x0, waiting for transfers between devices: 194 us -> none  [on_device(): lax.psum_scatter(jnp.dot(units, w_down, preferred_element_type=jnp.float3...]
    all_gather x2 -> x0, waiting for transfers between devices: 124 us -> none  [the longest x1 114 us: on_device(): piece = lax.all_gather(normed, 'mp', axis=0, tiled=True)]
    ppermute x0 -> x18, waiting for transfers between devices: none -> 92.7 us  [the longest x6 41.8 us: from_y(): return lax.ppermute(v, 'mp', perm)]
    pmax x1 -> x0, blocking collectives: 62.4 us -> none  [on_device(): every_top = lax.pmax(maxima, ('dp', 'mp'))]
    all_gather x1 -> x0, blocking collectives: 55.4 us -> none  [on_device(): meta_piece = lax.all_gather(meta, ('dp', 'mp'), axis=0, tiled=True)]
    dot_general x4 -> x0, matrix products: 54.7 us -> none  [the longest x1 26.6 us: on_device(): jnp.dot(units, w_down, preferred_element_type=jnp.float32)]
    pallas_call x0 -> x8, Pallas kernels: none -> 49.9 us  [the longest x3 33.2 us: ffn(): pl.pallas_call(functools.partial(ffn_kernel, n_tok, n_slices, n_parts, fi...]
    all_to_all x0 -> x4, waiting for transfers between devices: none -> 39.3 us  [the longest x1 15.4 us: one_round(): rows = lax.all_to_all(spread(emb, sel), ALL, 0, 0, tiled=True)]
  transfers between devices with their start and end apart: 3 -> 22, of which waited for: 3 -> 10; matrix products, arithmetic and copies ran while one was open for 0% -> 5% of each run, Pallas kernels for 0% -> 15%
where the time goes in v1:
time: 265 us; the launch traced here: 264 us
  waiting for transfers between devices  132 us (50%)
  starting transfers between devices  50.5 us (19%)
  Pallas kernels  49.9 us (19%)
  local copies, waits for them, and re-layouts  18.4 us (7%)
  other arithmetic  9.24 us (3%)
  between operations  3.73 us (1%)
    ppermute x6, waiting for transfers between devices, from_y(): return lax.ppermute(v, 'mp', perm)  41.8 us
    ppermute x3, waiting for transfers between devices, from_x(): return lax.ppermute(v, 'mp', perm)  41 us
    pallas_call x3, Pallas kernels, ffn(): pl.pallas_call(functools.partial(ffn_kernel, n_tok, n_slices, n_parts, fi...  33.2 us
    all_to_all x1, waiting for transfers between devices, one_round(): rows = lax.all_to_all(spread(emb, sel), ALL, 0, 0, tiled=True)  15.4 us
    all_to_all x1, waiting for transfers between devices, on_device(): terms = lax.all_to_all(terms, 'mp', 0, 0, tiled=True)  14.2 us
    ppermute x3, waiting for transfers between devices, from_z(): return lax.ppermute(v, 'dp', perm)  9.88 us
    ppermute x6, starting transfers between devices, from_y(): return lax.ppermute(v, 'mp', perm)  9.17 us
    all_to_all x1, starting transfers between devices, one_round(): rows = lax.all_to_all(spread(emb, sel), ALL, 0, 0, tiled=True)  7.75 us
  transfers between devices with their start and end apart: 22, of which 10 were waited for; matrix products, arithmetic and copies ran while one was open for 5% of the time, Pallas kernels for 15%

profile of v1, /device:TPU:1, one launch (start us, length us, event | category | flops | bytes accessed | tf_op | source)
XLA Modules:
  0.0 264.1 jit_solution(10067862446958152109)
XLA Ops:
  5.9 2.1 collective-permute-start.5
  11.3 41.8 %collective-permute-done.8.refs_4_ = bf16[256,768]{1,0:T(8,128)(2,1)S(1)} collective-permute-done((bf16[256,768]{1,0:T(8,128)(2,1)S(1)}, bf16[256,768]{1,0:T(8,128)(2,1)S(1)}, u32[]{:S(2)}, u32[]{:S(2)}) %collective-permute-start.8) | collective-permute-done | bytes 393248 | tf_op jit(solution)/shard_map/ppermute | solution.py:24
  56.3 3.3 %collective-permute-start.10 = (bf16[256,768]{1,0:T(8,128)(2,1)S(1)}, bf16[256,768]{1,0:T(8,128)(2,1)}, u32[]{:S(2)}, u32[]{:S(2)}) collective-permute-start(bf16[256,768]{1,0:T(8,128)(2,1)S(1)} %collective-permute-done.8.refs_4_), channel_id=1, source_target_pairs={{64,0},{80,16},{96,32},{112,48},{0,64},{16,80},{32,96},{48,112},{6... | collective-permute-start | bytes 1179656 | tf_op jit(solution)/shard_map/ppermute | solution.py:29
  63.5 2.8 %prep.1 = (bf16[256,2048]{1,0:T(8,128)(2,1)}, f32[8,2048]{1,0:T(8,128)}) custom-call(bf16[256,2048]{1,0:T(8,128)(2,1)} %h_ref.1, bf16[1,2048]{1,0:T(2,128)(2,1)} %broadcast_in_dim.133.gain_ref, f32[256,1]{1,0:T(8,128)} %reshape.235.mask_ref), custom_call_target="tpu_custom_call" | custom-call | tf_op jit(solution)/shard_map/prep/pallas_call | solution.py:55
  69.2 8.2 %collective-permute-done.10.refs_6_ = bf16[256,768]{1,0:T(8,128)(2,1)} collective-permute-done((bf16[256,768]{1,0:T(8,128)(2,1)S(1)}, bf16[256,768]{1,0:T(8,128)(2,1)}, u32[]{:S(2)}, u32[]{:S(2)}) %collective-permute-start.10) | collective-permute-done | bytes 393248 | tf_op jit(solution)/shard_map/ppermute | solution.py:29
  77.4 2.7 %collective-permute-start.1 = (bf16[256,2048]{1,0:T(8,128)(2,1)}, bf16[256,2048]{1,0:T(8,128)(2,1)}, u32[]{:S(2)}, u32[]{:S(2)}) collective-permute-start(bf16[256,2048]{1,0:T(8,128)(2,1)} %get-tuple-element.163.refs_0_), channel_id=1, source_target_pairs={{8,0},{9,1},{10,2},{11,3},{12,4},{13,5},{14,6},{15,7},{0,8},{1,9},... | collective-permute-start | bytes 3145736 | tf_op jit(solution)/shard_map/ppermute | solution.py:19
  81.9 11.8 %collective-permute-done.2.refs_3_ = bf16[256,2048]{1,0:T(8,128)(2,1)} collective-permute-done((bf16[256,2048]{1,0:T(8,128)(2,1)}, bf16[256,2048]{1,0:T(8,128)(2,1)}, u32[]{:S(2)}, u32[]{:S(2)}) %collective-permute-start.2) | collective-permute-done | bytes 1048608 | tf_op jit(solution)/shard_map/ppermute | solution.py:19
  95.2 22.0 %collective-permute-done.1.refs_2_ = bf16[256,2048]{1,0:T(8,128)(2,1)} collective-permute-done((bf16[256,2048]{1,0:T(8,128)(2,1)}, bf16[256,2048]{1,0:T(8,128)(2,1)}, u32[]{:S(2)}, u32[]{:S(2)}) %collective-permute-start.1) | collective-permute-done | bytes 1048608 | tf_op jit(solution)/shard_map/ppermute | solution.py:19
  118.6 7.3 %collective-permute-done.refs_1_ = bf16[256,2048]{1,0:T(8,128)(2,1)} collective-permute-done((bf16[256,2048]{1,0:T(8,128)(2,1)}, bf16[256,2048]{1,0:T(8,128)(2,1)}, u32[]{:S(2)}, u32[]{:S(2)}) %collective-permute-start) | collective-permute-done | bytes 1048608 | tf_op jit(solution)/shard_map/ppermute | solution.py:19
  130.5 10.0 %ffn_far.1 = f32[32,384]{1,0:T(8,128)} custom-call(s32[8]{0:T(128)} %stack.117.off_ref, bf16[256,2048]{1,0:T(8,128)(2,1)} %get-tuple-element.163.refs_0_, bf16[256,2048]{1,0:T(8,128)(2,1)} %collective-permute-done.refs_1_, bf16[256,2048]{1,0:T(8,128)(2,1)} %collective-permute-done.1.refs_2_, bf16[256,2048]{1,0:T(8,128)(2,1)} %collective-permute-done.2.refs_3_, ...), custom_call_target="tpu_custom_call" | custom-call | tf_op jit(solution)/shard_map/ffn_far/pallas_call | solution.py:108
  141.2 14.2 %ffn_near.1 = (f32[32,384]{1,0:T(8,128)}, f32[32,384]{1,0:T(8,128)}) custom-call(s32[4]{0:T(128)} %pad_add_fusion.off_ref, bf16[256,2048]{1,0:T(8,128)(2,1)} %get-tuple-element.163.refs_0_, bf16[256,2048]{1,0:T(8,128)(2,1)} %collective-permute-done.refs_1_, bf16[256,2048]{1,0:T(8,128)(2,1)} %collective-permute-done.1.refs_2_, ...), custom_call_target="tpu_custom_call" | custom-call | tf_op jit(solution)/shard_map/ffn_near/pallas_call | solution.py:108
  161.0 9.0 %ffn_own.1.u0 = f32[32,384]{1,0:T(8,128)} custom-call(s32[1]{0:T(128)} %constant.234.clone.1.off_ref, bf16[256,2048]{1,0:T(8,128)(2,1)} %get-tuple-element.163.refs_0_, bf16[256,2048]{1,0:T(8,128)(2,1)} %collective-permute-done.refs_1_, bf16[256,2048]{1,0:T(8,128)(2,1)} %collective-permute-done.1.refs_2_, bf16[256,2048]{1,0:T(8,128)(2,1)} %collective-permute-done.2.refs_3_, ...), custom_call_target="tpu_custom_call" | custom-call | tf_op jit(solution)/shard_map/ffn_own/pallas_call | solution.py:108
  171.3 3.2 %down.1 = f32[128,2048]{1,0:T(8,128)} custom-call(s32[16]{0:T(128)} %stack.105.pos_ref, f32[32,384]{1,0:T(8,128)} %ffn_own.1.u0, f32[32,384]{1,0:T(8,128)} %copy-done.6, f32[32,384]{1,0:T(8,128)} %copy-done.5, f32[32,384]{1,0:T(8,128)} %copy-done.7, bf16[344,2048]{1,0:T(8,128)(2,1)} %w_ref.1), custom_call_target="tpu_custom_call" | custom-call | tf_op jit(solution)/shard_map/down/pallas_call | solution.py:140
  174.4 4.7 %all-to-all-start.2 = ((f32[16,8,2048]{2,1,0:T(8,128)}), f32[16,8,2048]{2,1,0:T(8,128)S(1)}, u32[]{:S(2)}, u32[]{:S(2)}) async-start(f32[16,8,2048]{2,1,0:T(8,128)} %bitcast.65), calls=%async_computation.2 | async-start | bytes 2097152 | tf_op jit(solution)/shard_map/all_to_all | solution.py:283
  180.3 14.2 %all-to-all-done.2 = f32[16,8,2048]{2,1,0:T(8,128)S(1)} async-done(((f32[16,8,2048]{2,1,0:T(8,128)}), f32[16,8,2048]{2,1,0:T(8,128)S(1)}, u32[]{:S(2)}, u32[]{:S(2)}) %all-to-all-start.2) | async-done | bytes 1048608 | tf_op jit(solution)/shard_map/all_to_all | solution.py:283
  194.5 6.5 %all-to-all-start.4 = ((s32[128,1,17]{2,1,0:T(1,128)}), s32[128,1,17]{2,1,0:T(1,128)S(1)}, u32[]{:S(2)}, u32[]{:S(2)}) async-start(s32[128,1,17]{2,1,0:T(1,128)} %bitcast.36), calls=%async_computation.4 | async-start | bytes 131072 | tf_op jit(solution)/shard_map/all_to_all | solution.py:303
  203.9 2.2 spread.4
  206.1 2.5 all_to_all.46
  208.6 2.1 all-to-all-done.4
  210.8 7.8 %all-to-all-start.3 = ((bf16[128,2,2048]{2,1,0:T(2,128)(2,1)}), bf16[128,2,2048]{2,1,0:T(2,128)(2,1)S(1)}, u32[]{:S(2)}, u32[]{:S(2)}) async-start(bf16[128,2,2048]{2,1,0:T(2,128)(2,1)} %all_to_all.46), calls=%async_computation.3 | async-start | bytes 2097152 | tf_op jit(solution)/shard_map/all_to_all | solution.py:310
  221.7 15.4 %all-to-all-done.3 = bf16[128,2,2048]{2,1,0:T(2,128)(2,1)S(1)} async-done(((bf16[128,2,2048]{2,1,0:T(2,128)(2,1)}), bf16[128,2,2048]{2,1,0:T(2,128)(2,1)S(1)}, u32[]{:S(2)}, u32[]{:S(2)}) %all-to-all-start.3) | async-done | bytes 1048608 | tf_op jit(solution)/shard_map/all_to_all | solution.py:310
  239.0 7.0 %match.4 = (f32[256,1]{1,0:T(8,128)}, f32[8,2048]{1,0:T(8,128)}) custom-call(bf16[256,2048]{1,0:T(8,128)(2,1)} %all_to_all.48.rows_ref, s32[256,1]{1,0:T(8,128)} %broadcast_in_dim_reshape.8.lp_ref, s32[256,1]{1,0:T(8,128)} %broadcast_in_dim_reshape.9.ord_ref, bf16[8,256]{1,0:T(8,128)(2,1)} %broadcast_in_dim.141.mem_ref, bf16[2048,2048]{1,0:T(8,128)(2,1)} %bank_ref.1, ...), custom_call_target="tpu_custom_call" | custom-call | tf_op jit(solution)/shard_map/match/pallas_call | solution.py:203
  247.8 4.9 %all-to-all-start.5 = ((f32[128,1,2]{2,1,0:T(1,128)}), f32[128,1,2]{2,1,0:T(1,128)S(1)}, u32[]{:S(2)}, u32[]{:S(2)}) async-start(f32[128,1,2]{2,1,0:T(1,128)} %bitcast.40), calls=%async_computation.5 | async-start | bytes 131072 | tf_op jit(solution)/shard_map/all_to_all | solution.py:316
  254.9 7.5 %all-to-all-done.5 = f32[128,1,2]{2,1,0:T(1,128)S(1)} async-done(((f32[128,1,2]{2,1,0:T(1,128)}), f32[128,1,2]{2,1,0:T(1,128)S(1)}, u32[]{:S(2)}, u32[]{:S(2)}) %all-to-all-start.5) | async-done | bytes 1056 | tf_op jit(solution)/shard_map/all_to_all | solution.py:316
  (102 shorter events, 46.9 us)
Async XLA Ops:
  5.9 75.1 %copy-start.12 = (s32[128]{0:T(128)S(1)}, s32[128]{0:T(128)}, u32[]{:S(2)}) copy-start(s32[128]{0:T(128)} %param.24) | copy-start | bytes 1540
  5.9 55.2 %collective-permute-start.5 = (bf16[1024,768]{1,0:T(8,128)(2,1)}, bf16[1024,768]{1,0:T(8,128)(2,1)}, u32[]{:S(2)}, u32[]{:S(2)}) collective-permute-start(bf16[1024,768]{1,0:T(8,128)(2,1)} %fusion.5), channel_id=1, source_target_pairs={{3,0},{0,1},{1,2},{2,3},{7,4},{4,5},{5,6},{6,7},{11,8},{8,9},{9,10... | collective-permute-start | bytes 4718600 | tf_op jit(solution)/shard_map/ppermute | solution.py:24
  8.1 53.9 %collective-permute-start.3 = (bf16[1024,768]{1,0:T(8,128)(2,1)}, bf16[1024,768]{1,0:T(8,128)(2,1)}, u32[]{:S(2)}, u32[]{:S(2)}) collective-permute-start(bf16[1024,768]{1,0:T(8,128)(2,1)} %fusion.5), channel_id=1, source_target_pairs={{1,0},{2,1},{3,2},{0,3},{5,4},{6,5},{7,6},{4,7},{9,8},{10,9},{11,1... | collective-permute-start | bytes 4718600 | tf_op jit(solution)/shard_map/ppermute | solution.py:24
  9.7 43.4 %collective-permute-start.8 = (bf16[256,768]{1,0:T(8,128)(2,1)S(1)}, bf16[256,768]{1,0:T(8,128)(2,1)S(1)}, u32[]{:S(2)}, u32[]{:S(2)}) collective-permute-start(bf16[256,768]{1,0:T(8,128)(2,1)S(1)} %fusion.8), channel_id=1, source_target_pairs={{2,0},{3,1},{0,2},{1,3},{6,4},{7,5},{4,6},{5,7},{10,8},{11,9},{8,1... | collective-permute-start | bytes 1179656 | tf_op jit(solution)/shard_map/ppermute | solution.py:24
  53.1 77.4 %copy-start.1 = (bf16[256,768]{1,0:T(8,128)(2,1)}, bf16[256,768]{1,0:T(8,128)(2,1)S(1)}, u32[]{:S(2)}) copy-start(bf16[256,768]{1,0:T(8,128)(2,1)S(1)} %collective-permute-done.8.refs_4_) | copy-start | bytes 1179652
  53.1 6.5 %collective-permute-start.12 = (bf16[256,768]{1,0:T(8,128)(2,1)S(1)}, bf16[256,768]{1,0:T(8,128)(2,1)S(1)}, u32[]{:S(2)}, u32[]{:S(2)}) collective-permute-start(bf16[256,768]{1,0:T(8,128)(2,1)S(1)} %collective-permute-done.8.refs_4_), channel_id=1, source_target_pairs={{16,0},{0,16},{48,32},{32,48},{80,64},{64,80},{112,96},{96,112},{1... | collective-permute-start | bytes 1179656 | tf_op jit(solution)/shard_map/ppermute | solution.py:33
  54.7 13.3 %collective-permute-start.11 = (bf16[256,768]{1,0:T(8,128)(2,1)S(1)}, bf16[256,768]{1,0:T(8,128)(2,1)}, u32[]{:S(2)}, u32[]{:S(2)}) collective-permute-start(bf16[256,768]{1,0:T(8,128)(2,1)S(1)} %collective-permute-done.8.refs_4_), channel_id=1, source_target_pairs={{96,0},{112,16},{0,32},{16,48},{32,64},{48,80},{64,96},{80,112},{9... | collective-permute-start | bytes 1179656 | tf_op jit(solution)/shard_map/ppermute | solution.py:29
  56.3 21.1 %collective-permute-start.10 = (bf16[256,768]{1,0:T(8,128)(2,1)S(1)}, bf16[256,768]{1,0:T(8,128)(2,1)}, u32[]{:S(2)}, u32[]{:S(2)}) collective-permute-start(bf16[256,768]{1,0:T(8,128)(2,1)S(1)} %collective-permute-done.8.refs_4_), channel_id=1, source_target_pairs={{64,0},{80,16},{96,32},{112,48},{0,64},{16,80},{32,96},{48,112},{6... | collective-permute-start | bytes 1179656 | tf_op jit(solution)/shard_map/ppermute | solution.py:29
  60.4 19.8 %collective-permute-start.9 = (bf16[256,768]{1,0:T(8,128)(2,1)S(1)}, bf16[256,768]{1,0:T(8,128)(2,1)}, u32[]{:S(2)}, u32[]{:S(2)}) collective-permute-start(bf16[256,768]{1,0:T(8,128)(2,1)S(1)} %collective-permute-done.8.refs_4_), channel_id=1, source_target_pairs={{32,0},{48,16},{64,32},{80,48},{96,64},{112,80},{0,96},{16,112},{3... | collective-permute-start | bytes 1179656 | tf_op jit(solution)/shard_map/ppermute | solution.py:29
  61.1 80.1 %collective-permute-start.6 = (bf16[1024,768]{1,0:T(8,128)(2,1)}, bf16[1024,768]{1,0:T(8,128)(2,1)}, u32[]{:S(2)}, u32[]{:S(2)}) collective-permute-start(bf16[1024,768]{1,0:T(8,128)(2,1)} %collective-permute-done.5.refs_6_), channel_id=1, source_target_pairs={{16,0},{0,16},{48,32},{32,48},{80,64},{64,80},{112,96},{96,112},{1... | collective-permute-start | bytes 4718600 | tf_op jit(solution)/shard_map/ppermute | solution.py:33
  61.9 79.3 %collective-permute-start.4 = (bf16[1024,768]{1,0:T(8,128)(2,1)}, bf16[1024,768]{1,0:T(8,128)(2,1)}, u32[]{:S(2)}, u32[]{:S(2)}) collective-permute-start(bf16[1024,768]{1,0:T(8,128)(2,1)} %collective-permute-done.3.refs_4_), channel_id=1, source_target_pairs={{16,0},{0,16},{48,32},{32,48},{80,64},{64,80},{112,96},{96,112},{1... | collective-permute-start | bytes 4718600 | tf_op jit(solution)/shard_map/ppermute | solution.py:33
  68.0 25.7 %collective-permute-start.2 = (bf16[256,2048]{1,0:T(8,128)(2,1)}, bf16[256,2048]{1,0:T(8,128)(2,1)}, u32[]{:S(2)}, u32[]{:S(2)}) collective-permute-start(bf16[256,2048]{1,0:T(8,128)(2,1)} %get-tuple-element.163.refs_0_), channel_id=1, source_target_pairs={{12,0},{13,1},{14,2},{15,3},{0,4},{1,5},{2,6},{3,7},{4,8},{5,9},{6... | collective-permute-start | bytes 3145736 | tf_op jit(solution)/shard_map/ppermute | solution.py:19
  77.4 39.7 %collective-permute-start.1 = (bf16[256,2048]{1,0:T(8,128)(2,1)}, bf16[256,2048]{1,0:T(8,128)(2,1)}, u32[]{:S(2)}, u32[]{:S(2)}) collective-permute-start(bf16[256,2048]{1,0:T(8,128)(2,1)} %get-tuple-element.163.refs_0_), channel_id=1, source_target_pairs={{8,0},{9,1},{10,2},{11,3},{12,4},{13,5},{14,6},{15,7},{0,8},{1,9},... | collective-permute-start | bytes 3145736 | tf_op jit(solution)/shard_map/ppermute | solution.py:19
  80.2 45.7 %collective-permute-start = (bf16[256,2048]{1,0:T(8,128)(2,1)}, bf16[256,2048]{1,0:T(8,128)(2,1)}, u32[]{:S(2)}, u32[]{:S(2)}) collective-permute-start(bf16[256,2048]{1,0:T(8,128)(2,1)} %get-tuple-element.163.refs_0_), channel_id=1, source_target_pairs={{4,0},{5,1},{6,2},{7,3},{8,4},{9,5},{10,6},{11,7},{12,8},{13,9},{1... | collective-permute-start | bytes 3145736 | tf_op jit(solution)/shard_map/ppermute | solution.py:19
  93.7 36.8 %collective-permute-start.15 = (bf16[256,768]{1,0:T(8,128)(2,1)}, bf16[256,768]{1,0:T(8,128)(2,1)}, u32[]{:S(2)}, u32[]{:S(2)}) collective-permute-start(bf16[256,768]{1,0:T(8,128)(2,1)} %collective-permute-done.11.refs_7_), channel_id=1, source_target_pairs={{16,0},{0,16},{48,32},{32,48},{80,64},{64,80},{112,96},{96,112},{1... | collective-permute-start | bytes 1179656 | tf_op jit(solution)/shard_map/ppermute | solution.py:33
  117.1 13.4 %collective-permute-start.14 = (bf16[256,768]{1,0:T(8,128)(2,1)}, bf16[256,768]{1,0:T(8,128)(2,1)}, u32[]{:S(2)}, u32[]{:S(2)}) collective-permute-start(bf16[256,768]{1,0:T(8,128)(2,1)} %collective-permute-done.10.refs_6_), channel_id=1, source_target_pairs={{16,0},{0,16},{48,32},{32,48},{80,64},{64,80},{112,96},{96,112},{1... | collective-permute-start | bytes 1179656 | tf_op jit(solution)/shard_map/ppermute | solution.py:33
  125.9 4.6 %collective-permute-start.13 = (bf16[256,768]{1,0:T(8,128)(2,1)}, bf16[256,768]{1,0:T(8,128)(2,1)}, u32[]{:S(2)}, u32[]{:S(2)}) collective-permute-start(bf16[256,768]{1,0:T(8,128)(2,1)} %collective-permute-done.9.refs_5_), channel_id=1, source_target_pairs={{16,0},{0,16},{48,32},{32,48},{80,64},{64,80},{112,96},{96,112},{1... | collective-permute-start | bytes 1179656 | tf_op jit(solution)/shard_map/ppermute | solution.py:33
  140.5 29.5 %collective-permute-start.16 = (f32[32,384]{1,0:T(8,128)}, f32[32,384]{1,0:T(8,128)S(1)}, u32[]{:S(2)}, u32[]{:S(2)}) collective-permute-start(f32[32,384]{1,0:T(8,128)} %ffn_far.1), channel_id=1, source_target_pairs={{2,0},{3,1},{0,2},{1,3},{6,4},{7,5},{4,6},{5,7},{10,8},{11,9},{8,1... | collective-permute-start | bytes 147464 | tf_op jit(solution)/shard_map/ppermute | solution.py:24
  155.4 14.6 %collective-permute-start.7 = (f32[32,384]{1,0:T(8,128)}, f32[32,384]{1,0:T(8,128)S(1)}, u32[]{:S(2)}, u32[]{:S(2)}) collective-permute-start(f32[32,384]{1,0:T(8,128)} %get-tuple-element.164), channel_id=1, source_target_pairs={{3,0},{0,1},{1,2},{2,3},{7,4},{4,5},{5,6},{6,7},{11,8},{8,9},{9,10... | collective-permute-start | bytes 147464 | tf_op jit(solution)/shard_map/ppermute | solution.py:24
  157.0 13.1 %collective-permute-start.17 = (f32[32,384]{1,0:T(8,128)}, f32[32,384]{1,0:T(8,128)S(1)}, u32[]{:S(2)}, u32[]{:S(2)}) collective-permute-start(f32[32,384]{1,0:T(8,128)} %get-tuple-element.165), channel_id=1, source_target_pairs={{1,0},{2,1},{3,2},{0,3},{5,4},{6,5},{7,6},{4,7},{9,8},{10,9},{11,1... | collective-permute-start | bytes 147464 | tf_op jit(solution)/shard_map/ppermute | solution.py:24
  174.4 20.1 %all-to-all-start.2 = ((f32[16,8,2048]{2,1,0:T(8,128)}), f32[16,8,2048]{2,1,0:T(8,128)S(1)}, u32[]{:S(2)}, u32[]{:S(2)}) async-start(f32[16,8,2048]{2,1,0:T(8,128)} %bitcast.65), calls=%async_computation.2 | async-start | bytes 2097152 | tf_op jit(solution)/shard_map/all_to_all | solution.py:283
  194.5 16.3 %all-to-all-start.4 = ((s32[128,1,17]{2,1,0:T(1,128)}), s32[128,1,17]{2,1,0:T(1,128)S(1)}, u32[]{:S(2)}, u32[]{:S(2)}) async-start(s32[128,1,17]{2,1,0:T(1,128)} %bitcast.36), calls=%async_computation.4 | async-start | bytes 131072 | tf_op jit(solution)/shard_map/all_to_all | solution.py:303
  210.8 26.4 %all-to-all-start.3 = ((bf16[128,2,2048]{2,1,0:T(2,128)(2,1)}), bf16[128,2,2048]{2,1,0:T(2,128)(2,1)S(1)}, u32[]{:S(2)}, u32[]{:S(2)}) async-start(bf16[128,2,2048]{2,1,0:T(2,128)(2,1)} %all_to_all.46), calls=%async_computation.3 | async-start | bytes 2097152 | tf_op jit(solution)/shard_map/all_to_all | solution.py:310
  247.8 14.6 %all-to-all-start.5 = ((f32[128,1,2]{2,1,0:T(1,128)}), f32[128,1,2]{2,1,0:T(1,128)S(1)}, u32[]{:S(2)}, u32[]{:S(2)}) async-start(f32[128,1,2]{2,1,0:T(1,128)} %bitcast.40), calls=%async_computation.5 | async-start | bytes 131072 | tf_op jit(solution)/shard_map/all_to_all | solution.py:316
  (12 other events, 167.3 us)

commit v2 on v1

v2 whole, which is shorter than its diff:
```python
import functools

import jax
import jax.numpy as jnp
from jax import lax
from jax.experimental import pallas as pl
from jax.experimental.pallas import tpu as pltpu
from jax.sharding import PartitionSpec as P

ALL = ("dp", "mp")
NX, NY, NZ, NC = 4, 4, 4, 2
ORDERS = 1 << 20
BF, F32, I32 = jnp.bfloat16, jnp.float32, jnp.int32
VMEM = pltpu.CompilerParams(vmem_limit_bytes=56 * 1024 * 1024)
NT = (((1,), (1,)), ((), ()))


def from_x(v, j):
    perm = [(((x + j) % NX) * NY + y, x * NY + y) for x in range(NX) for y in range(NY)]
    return lax.ppermute(v, "mp", perm)


def from_y(v, k):
    perm = [(x * NY + (y + k) % NY, x * NY + y) for x in range(NX) for y in range(NY)]
    return lax.ppermute(v, "mp", perm)


def from_z(v, k):
    perm = [(((z + k) % NZ) * NC + c, z * NC + c) for z in range(NZ) for c in range(NC)]
    return lax.ppermute(v, "dp", perm)


def from_core(v):
    return lax.ppermute(v, "dp", [(d ^ 1, d) for d in range(NZ * NC)])


def block_ones(files, file_len, dtype):
    row = lax.broadcasted_iota(I32, (files, files * file_len), 0)
    col = lax.broadcasted_iota(I32, (files, files * file_len), 1)
    return jnp.where(col // file_len == row, 1.0, 0.0).astype(dtype)


def prep_kernel(file_len, h_ref, gain_ref, mask_ref, n_ref, p_ref):
    resid = h_ref[...].astype(F32)
    scale = lax.rsqrt(jnp.mean(resid * resid, axis=-1, keepdims=True) + 1e-05)
    normed = resid * scale * gain_ref[...].astype(F32)
    keep = mask_ref[...] > 0.5
    n_ref[...] = jnp.where(keep, normed, 0.0).astype(BF)
    files = p_ref.shape[0]
    valid = jnp.where(keep, resid, 0.0).astype(BF)
    p_ref[...] = jnp.dot(block_ones(files, file_len, BF), valid, preferred_element_type=F32)


def prep(hidden, gain, mask, files):
    tok, width = hidden.shape
    return pl.pallas_call(
        functools.partial(prep_kernel, tok // files),
        out_shape=(jax.ShapeDtypeStruct((tok, width), BF), jax.ShapeDtypeStruct((files, width), F32)),
        compiler_params=VMEM,
        name="prep",
    )(hidden, gain[None, :], mask)


def ffn_kernel(n_tok, slice_parts, files, file_len, off_ref, *refs):
    toks, refs = refs[:n_tok], refs[n_tok:]
    n_parts = sum(slice_parts)
    parts, refs = refs[:n_parts], refs[n_parts:]
    outs, refs = refs[:len(slice_parts)], refs[len(slice_parts):]
    t_buf, w_buf, t_sem, w_sem = refs
    copies, at, row = [], 0, 0
    for s, count in enumerate(slice_parts):
        for p in range(at, at + count):
            cols = parts[p].shape[1]
            start = pl.multiple_of(off_ref[p], 128)
            copies.append(pltpu.make_async_copy(parts[p], w_buf.at[s, :, pl.ds(start, cols)], w_sem.at[p]))
            copies[-1].start()
        at += count
        if s == 0:
            t_copies = []
            for t in range(n_tok):
                rows = toks[t].shape[0]
                t_copies.append(pltpu.make_async_copy(toks[t], t_buf.at[pl.ds(row, rows)], t_sem.at[t]))
                t_copies[-1].start()
                row += rows
    n_rows = t_buf.shape[0]
    hid = w_buf.shape[1] // 2
    ones = block_ones(n_rows // file_len, file_len, BF)
    at = 0
    for s, count in enumerate(slice_parts):
        if s == 0:
            for cp in t_copies:
                cp.wait()
        for cp in copies[at:at + count]:
            cp.wait()
        at += count
        both = lax.dot_general(w_buf[s], t_buf[...], NT, preferred_element_type=F32)
        gate = both[:hid]
        units = (0.5 * gate * (1.0 + jnp.tanh(0.5 * gate)) * both[hid:]).astype(BF)
        outs[s][...] = lax.dot_general(ones, units, NT, preferred_element_type=F32)


def ffn(toks, slices, offs, file_len, name):
    n_tok = len(toks)
    width = toks[0].shape[1]
    n_rows = sum(t.shape[0] for t in toks)
    rows = slices[0][0].shape[0]
    flat = [p for s in slices for p in s]
    anyspec = pl.BlockSpec(memory_space=pl.ANY)
    out = jax.ShapeDtypeStruct((n_rows // file_len, rows // 2), F32)
    return pl.pallas_call(
        functools.partial(ffn_kernel, n_tok, tuple(len(s) for s in slices), n_rows // file_len, file_len),
        in_specs=[pl.BlockSpec(memory_space=pltpu.SMEM)] + [anyspec] * (n_tok + len(flat)),
        out_specs=tuple(pl.BlockSpec(memory_space=pltpu.VMEM) for _ in slices),
        out_shape=tuple(out for _ in slices),
        scratch_shapes=[
            pltpu.VMEM((n_rows, width), BF),
            pltpu.VMEM((len(slices), rows, width), BF),
            pltpu.SemaphoreType.DMA((n_tok,)),
            pltpu.SemaphoreType.DMA((len(flat),)),
        ],
        compiler_params=VMEM,
        name=name,
    )(offs, *toks, *flat)


def down_kernel(files, pos_ref, u0, u1, u2, u3, w_ref, o_ref, buf):
    for k, u in enumerate((u0, u1, u2, u3)):
        for j in range(NX):
            dst = pl.multiple_of(pos_ref[k * NX + j], files)
            buf[pl.ds(dst, files), :] = u[j * files:(j + 1) * files, :]
    rows = buf[...]
    hi = rows.astype(BF)
    lo = (rows - hi.astype(F32)).astype(BF)
    w = w_ref[...]
    o_ref[...] = jnp.dot(hi, w, preferred_element_type=F32) + jnp.dot(lo, w, preferred_element_type=F32)


def down(us, w_down, pos, files):
    rows = NX * NY * files
    vm = pl.BlockSpec(memory_space=pltpu.VMEM)
    return pl.pallas_call(
        functools.partial(down_kernel, files),
        in_specs=[pl.BlockSpec(memory_space=pltpu.SMEM)] + [vm] * 5,
        out_specs=vm,
        out_shape=jax.ShapeDtypeStruct((rows, w_down.shape[1]), F32),
        scratch_shapes=[pltpu.VMEM((rows, us[0].shape[1]), F32)],
        compiler_params=VMEM,
        name="down",
    )(pos, *us, w_down)


def emb_kernel(files, copies, t_ref, p_ref, len_ref, sel_ref, o_ref):
    total = p_ref[...]
    for m in range(t_ref.shape[0] // files):
        total = total + t_ref[m * files:(m + 1) * files, :]
    pooled = total / len_ref[...]
    norm = lax.rsqrt(jnp.sum(pooled * pooled, axis=-1, keepdims=True) + 1e-06)
    emb = (pooled * norm).astype(BF)
    rows = jnp.dot(sel_ref[...], emb, preferred_element_type=F32)
    for d in range(sel_ref.shape[0] // 2):
        pair = rows[2 * d:2 * d + 2, :].astype(BF)
        for m in range(copies):
            o_ref[d * copies + m] = pair


def emb_to_owners(terms, pooled, lens, sel, files, copies):
    return pl.pallas_call(
        functools.partial(emb_kernel, files, copies),
        out_shape=jax.ShapeDtypeStruct((sel.shape[0] // 2 * copies, 2, pooled.shape[1]), BF),
        compiler_params=VMEM,
        name="emb",
    )(terms, pooled, lens, sel)


def match_kernel(rows_ref, low_ref, high_ref, mem_ref, bank_ref, key_ref, best_ref, sums_ref):
    step = pl.program_id(0)

    @pl.when(step == 0)
    def _():
        best_ref[...] = jnp.full(best_ref.shape, -1.0, F32)
        sums_ref[...] = jnp.dot(mem_ref[...], rows_ref[...], preferred_element_type=F32)

    sims = lax.dot_general(bank_ref[...], rows_ref[...], NT, preferred_element_type=F32)
    key = key_ref[...]
    valid = (key >= low_ref[...]) & (key < high_ref[...])
    top = jnp.max(jnp.where(valid, sims, -1.0), axis=0, keepdims=True)
    best_ref[...] = jnp.maximum(best_ref[...], top)


def match(rows, low, high, member, bank, key):
    n, width = rows.shape
    block = 512
    whole = lambda shape: pl.BlockSpec(shape, lambda i: (0, 0))
    return pl.pallas_call(
        match_kernel,
        grid=(bank.shape[0] // block,),
        in_specs=[
            whole((n, width)),
            whole((1, n)),
            whole((1, n)),
            whole(member.shape),
            pl.BlockSpec((block, width), lambda i: (i, 0)),
            pl.BlockSpec((block, 1), lambda i: (i, 0)),
        ],
        out_specs=(whole((1, n)), whole((member.shape[0], width))),
        out_shape=(jax.ShapeDtypeStruct((1, n), F32), jax.ShapeDtypeStruct((member.shape[0], width), F32)),
        compiler_params=VMEM,
        name="match",
    )(rows, low, high, member, bank, key)


def on_device(
    hidden_in,
    mlp_gain,
    w_gate,
    w_up,
    w_down,
    lengths,
    file_cluster,
    file_order,
    cluster_slot,
    bank,
    bank_slot,
    bank_order,
    centroid_old,
    count_old,
):
    tok, width = hidden_in.shape
    files = lengths.shape[0]
    file_len = tok // files
    n_dp, n_mp = NZ * NC, NX * NY
    dp, mp = lax.axis_index("dp"), lax.axis_index("mp")
    z, c, x, y = dp // NC, dp % NC, mp // NY, mp % NY
    tie = lax.optimization_barrier

    k_total = cluster_slot.shape[0]
    owned = k_total // n_dp
    lookup = file_cluster[:, None] == jnp.arange(k_total, dtype=I32)[None, :]
    slot = jnp.sum(jnp.where(lookup, cluster_slot[None, :], 0), axis=1)
    owner = slot // owned
    ids = jnp.arange(files, dtype=I32)
    rank = jnp.sum(((owner[:, None] == owner[None, :]) & (ids[None, :] < ids[:, None])).astype(I32), axis=1)
    place = (owner[None, None, :] == jnp.arange(n_dp, dtype=I32)[:, None, None]) & (
        rank[None, None, :] == ids[None, :, None]
    )
    first = slot % owned * ORDERS
    send_low = jnp.sum(jnp.where(place, first[None, None, :] + 1, 0), axis=2) - 1
    send_high = jnp.sum(jnp.where(place, (first + file_order)[None, None, :] + 1, 0), axis=2) - 1
    most = jnp.broadcast_to(jnp.max(rank) + 1, (n_dp, 1)).astype(I32)
    meta = jnp.concatenate([send_low, send_high, most], axis=1)
    meta = jnp.broadcast_to(meta[:, None, :], (n_dp, n_mp, 2 * files + 1)).reshape(n_dp * n_mp, 2 * files + 1)
    bank_key = (bank_slot * ORDERS + bank_order)[:, None]

    eighth, half = width // 8, width // 2
    w_t = [w_gate.T, w_up.T]
    cut = lambda start, n: jnp.concatenate([lax.dynamic_slice_in_dim(w, start, n, 1) for w in w_t], axis=0)
    w_own = jnp.concatenate(w_t, axis=0)
    w_e, w_h = cut(dp * eighth, eighth), cut(c * half, half)
    mask = (jnp.arange(file_len, dtype=I32)[None, :] < lengths[:, None]).astype(F32).reshape(tok, 1)
    normed, pooled_in = prep(hidden_in, mlp_gain, mask, files)
    w_e, w_h, normed = tie((w_e, w_h, normed))

    e0 = from_y(w_e, 2)
    t1, t3 = from_x(normed, 1), from_x(normed, 3)
    h1, h3 = from_y(w_h, 1), from_y(w_h, 3)
    meta, e0 = tie((meta, e0))
    meta = lax.all_to_all(meta, ALL, 0, 0, tiled=True)
    es = [e0] + [from_z(e0, k) for k in (1, 2, 3)]
    es = es + [from_core(e) for e in es]
    t2a, t2b = from_x(t1[:tok // 2], 1), from_x(t3[tok // 2:], 3)
    toks = [normed, t1, t2a, t2b, t3]

    e_off = jnp.stack(
        [(((z + k) % NZ) * NC + c) * eighth for k in range(NZ)]
        + [(((z + k) % NZ) * NC + (1 - c)) * eighth for k in range(NZ)]
    ).astype(I32)
    h_off = jnp.stack([c * half, (1 - c) * half] * 2).astype(I32)
    pos = jnp.stack(
        [(((x + j) % NX) * NY + (y - k) % NY) * files for k in range(NY) for j in range(NX)]
    ).astype(I32)
    lens = lengths.astype(F32)[:, None]
    got_low, got_high = meta[:, :files], meta[:, files:2 * files]
    rounds = (jnp.max(meta[:, 2 * files]) + 1) // 2

    def files_of(r):
        here = lax.dynamic_slice_in_dim(place, 2 * r, 2, 1)
        low = lax.dynamic_slice_in_dim(got_low, 2 * r, 2, 1).reshape(1, -1)
        high = lax.dynamic_slice_in_dim(got_high, 2 * r, 2, 1).reshape(1, -1)
        mine = low // ORDERS == mp
        mine = mine & (low >= 0)
        member = jnp.broadcast_to(mine, (8, low.shape[1])).astype(BF)
        return here.reshape(-1, files).astype(BF), here, low, high, member, jnp.sum(mine.astype(F32))

    ready = files_of(0)
    normed, e_off, h_off, pos, lens, rounds, bank_key, ready = tie(
        (normed, e_off, h_off, pos, lens, rounds, bank_key, ready)
    )
    toks[0] = normed

    (u0,) = ffn(toks, [[w_own]], jnp.zeros((1,), I32), file_len, "ffn_own")
    (u2,) = ffn(toks, [es], e_off, file_len, "ffn_far")
    h1, h3, u0, u2 = tie((h1, h3, u0, u2))
    g1, g3 = from_core(h1), from_core(h3)
    r2 = from_y(u2, NY - 2)
    u1, u3 = ffn(toks, [[h1, g1], [h3, g3]], h_off, file_len, "ffn_near")
    r1, r3 = from_y(u1, NY - 1), from_y(u3, NY - 3)
    terms = down([u0, r1, r2, r3], w_down, pos, files)
    terms = lax.all_to_all(terms, "mp", 0, 0, tiled=True)

    def one_round(ready, best, sums, counts):
        sel, here, low, high, member, count = ready
        rows = emb_to_owners(terms, pooled_in, lens, sel, files, n_mp)
        rows = lax.all_to_all(rows, ALL, 0, 0, tiled=True).reshape(-1, width)
        top, new = match(rows, low, high, member, bank, bank_key)
        back = lax.all_to_all(top.reshape(-1, 2), ALL, 0, 0, tiled=True)
        back = jnp.max(back.reshape(n_dp, n_mp, 2), axis=1)
        best = jnp.maximum(best, jnp.max(jnp.where(here, back[:, :, None], -1.0), axis=(0, 1)))
        return best, sums + new[:1], counts + count

    state = one_round(ready, jnp.full((files,), -1.0, F32), jnp.zeros((1, width), F32), jnp.float32(0))
    _, best, sums, counts = lax.while_loop(
        lambda s: s[0] < rounds,
        lambda s: (s[0] + 1,) + one_round(files_of(s[0]), *s[1:]),
        (jnp.int32(1),) + state,
    )
    centroid_new = (count_old[:, None] * centroid_old + sums) / (count_old + counts)[:, None]
    return best, centroid_new


def solution(mesh):
    both = P(ALL)
    rows = P(ALL, None)
    return jax.shard_map(
        on_device,
        mesh=mesh,
        in_specs=(
            rows, P(), P(None, "mp"), P(None, "mp"), P("mp", None), both, both, both, P(), rows, both, both, rows, both,
        ),
        out_specs=(both, rows),
        check_vma=False,
    )
```

time: 265 us -> 221 us (0.83)
  waiting for transfers between devices: 132 us -> 93.7 us
  Pallas kernels: 49.9 us -> 41.2 us
    ppermute x3 -> x4, waiting for transfers between devices: 41 us -> 0.01 us  [from_x(): return lax.ppermute(v, 'mp', perm)]
    pallas_call x5 -> x4, Pallas kernels: 36.9 us -> 28.4 us  [the longest x3 26.3 us: ffn(): pl.pallas_call(functools.partial(ffn_kernel, n_tok, tuple((len(s) for s i...]
    ppermute x3, waiting for transfers between devices: 9.88 us -> 3.17 us  [from_z(): return lax.ppermute(v, 'dp', perm)]
    all_to_all x1, waiting for transfers between devices: 2.15 us -> 8.74 us  [on_device(): meta = lax.all_to_all(meta, ALL, 0, 0, tiled=True)]
    ppermute x6, waiting for transfers between devices: 41.8 us -> 37 us  [from_y(): return lax.ppermute(v, 'mp', perm)]
    ppermute x6, starting transfers between devices: 6.97 us -> 10.7 us  [from_core(): return lax.ppermute(v, 'dp', [(d ^ 1, d) for d in range(NZ * NC)])]
    all_to_all x2 -> x1, local copies, waits for them, and re-layouts: 3.74 us -> 0.06 us  [on_device(): meta = lax.all_to_all(meta, ALL, 0, 0, tiled=True)]
    ppermute x6, waiting for transfers between devices: 0.02 us -> 3.47 us  [from_core(): return lax.ppermute(v, 'dp', [(d ^ 1, d) for d in range(NZ * NC)])]
  transfers between devices with their start and end apart: 22 -> 23, of which waited for: 10 -> 10; matrix products, arithmetic and copies ran while one was open for 5% -> 6% of each run, Pallas kernels for 15% -> 12%
where the time goes in v2:
time: 221 us; the launch traced here: 220 us
  waiting for transfers between devices  93.7 us (42%)
  starting transfers between devices  53 us (24%)
  Pallas kernels  41.2 us (19%)
  local copies, waits for them, and re-layouts  17.1 us (8%)
  other arithmetic  11.4 us (5%)
  between operations  3.88 us (2%)
    ppermute x6, waiting for transfers between devices, from_y(): return lax.ppermute(v, 'mp', perm)  37 us
    pallas_call x3, Pallas kernels, ffn(): pl.pallas_call(functools.partial(ffn_kernel, n_tok, tuple((len(s) for s i...  26.3 us
    all_to_all x1, waiting for transfers between devices, one_round(): rows = lax.all_to_all(rows, ALL, 0, 0, tiled=True).reshape(-1, width)  17.6 us
    all_to_all x1, waiting for transfers between devices, on_device(): terms = lax.all_to_all(terms, 'mp', 0, 0, tiled=True)  14.9 us
    ppermute x6, starting transfers between devices, from_core(): return lax.ppermute(v, 'dp', [(d ^ 1, d) for d in range(NZ * NC)])  10.7 us
    all_to_all x1, waiting for transfers between devices, one_round(): back = lax.all_to_all(top.reshape(-1, 2), ALL, 0, 0, tiled=True)  8.86 us
    all_to_all x1, waiting for transfers between devices, on_device(): meta = lax.all_to_all(meta, ALL, 0, 0, tiled=True)  8.74 us
    ppermute x6, starting transfers between devices, from_y(): return lax.ppermute(v, 'mp', perm)  8.56 us
  transfers between devices with their start and end apart: 23, of which 10 were waited for; matrix products, arithmetic and copies ran while one was open for 6% of the time, Pallas kernels for 12%

profile of v2, /device:TPU:1, one launch (start us, length us, event | category | flops | bytes accessed | tf_op | source)
XLA Modules:
  0.0 220.3 jit_solution(1604849635734450138)
XLA Ops:
  6.9 2.8 %prep.1 = (bf16[256,2048]{1,0:T(8,128)(2,1)}, f32[8,2048]{1,0:T(8,128)}) custom-call(bf16[256,2048]{1,0:T(8,128)(2,1)} %h_ref.1, bf16[1,2048]{1,0:T(2,128)(2,1)} %broadcast_in_dim.108.gain_ref, f32[256,1]{1,0:T(8,128)} %reshape.405.mask_ref), custom_call_target="tpu_custom_call" | custom-call | tf_op jit(solution)/shard_map/prep/pallas_call | solution.py:56
  9.7 3.3 %collective-permute-start.3 = (bf16[256,2048]{1,0:T(8,128)(2,1)}, bf16[256,2048]{1,0:T(8,128)(2,1)S(1)}, u32[]{:S(2)}, u32[]{:S(2)}) collective-permute-start(bf16[256,2048]{1,0:T(8,128)(2,1)} %get-tuple-element.213.refs_0_), channel_id=1, source_target_pairs={{4,0},{5,1},{6,2},{7,3},{8,4},{9,5},{10,6},{11,7},{12,8},{13,9},{1... | collective-permute-start | bytes 3145736 | tf_op jit(solution)/shard_map/ppermute | solution.py:20
  13.0 2.7 %collective-permute-start.1 = (bf16[688,1024]{1,0:T(8,128)(2,1)}, bf16[688,1024]{1,0:T(8,128)(2,1)}, u32[]{:S(2)}, u32[]{:S(2)}) collective-permute-start(bf16[688,1024]{1,0:T(8,128)(2,1)} %pad_maximum_fusion.1), channel_id=1, source_target_pairs={{1,0},{2,1},{3,2},{0,3},{5,4},{6,5},{7,6},{4,7},{9,8},{10,9},{11,1... | collective-permute-start | bytes 4227080 | tf_op jit(solution)/shard_map/ppermute | solution.py:25
  19.7 35.3 %collective-permute-done.refs_5_ = bf16[688,256]{1,0:T(8,128)(2,1)} collective-permute-done((bf16[688,256]{1,0:T(8,128)(2,1)}, bf16[688,256]{1,0:T(8,128)(2,1)}, u32[]{:S(2)}, u32[]{:S(2)}) %collective-permute-start) | collective-permute-done | bytes 352288 | tf_op jit(solution)/shard_map/ppermute | solution.py:25
  55.6 3.8 %collective-permute-start.7 = (bf16[688,256]{1,0:T(8,128)(2,1)}, bf16[688,256]{1,0:T(8,128)(2,1)S(1)}, u32[]{:S(2)}, u32[]{:S(2)}) collective-permute-start(bf16[688,256]{1,0:T(8,128)(2,1)} %collective-permute-done.refs_5_), channel_id=1, source_target_pairs={{32,0},{48,16},{64,32},{80,48},{96,64},{112,80},{0,96},{16,112},{3... | collective-permute-start | bytes 1056776 | tf_op jit(solution)/shard_map/ppermute | solution.py:30
  60.7 3.2 %pad_maximum_fusion.refs_5_ = bf16[688,2048]{1,0:T(8,128)(2,1)} fusion(bf16[344,2048]{1,0:T(8,128)(2,1)S(1)} %bitcast.69, bf16[344,2048]{1,0:T(8,128)(2,1)} %bitcast.70), kind=kLoop, calls=%fused_computation.17 | loop fusion | flops 5636096 | bytes 5636096 | tf_op jit(solution)/shard_map/concatenate | solution.py:257
  64.0 2.9 %collective-permute-done.7.refs_6_ = bf16[688,256]{1,0:T(8,128)(2,1)S(1)} collective-permute-done((bf16[688,256]{1,0:T(8,128)(2,1)}, bf16[688,256]{1,0:T(8,128)(2,1)S(1)}, u32[]{:S(2)}, u32[]{:S(2)}) %collective-permute-start.7) | collective-permute-done | bytes 352288 | tf_op jit(solution)/shard_map/ppermute | solution.py:30
  66.8 8.9 %collective-permute-start.10 = (bf16[688,256]{1,0:T(8,128)(2,1)}, bf16[688,256]{1,0:T(8,128)(2,1)S(1)}, u32[]{:S(2)}, u32[]{:S(2)}) collective-permute-start(bf16[688,256]{1,0:T(8,128)(2,1)} %collective-permute-done.refs_5_), channel_id=1, source_target_pairs={{16,0},{0,16},{48,32},{32,48},{80,64},{64,80},{112,96},{96,112},{1... | collective-permute-start | bytes 1056776 | tf_op jit(solution)/shard_map/ppermute | solution.py:34
  75.7 2.4 %collective-permute-start.4 = (bf16[128,2048]{1,0:T(8,128)(2,1)S(1)}, bf16[128,2048]{1,0:T(8,128)(2,1)S(1)}, u32[]{:S(2)}, u32[]{:S(2)}) collective-permute-start(bf16[128,2048]{1,0:T(8,128)(2,1)S(1)} %slice.33), channel_id=1, source_target_pairs={{4,0},{5,1},{6,2},{7,3},{8,4},{9,5},{10,6},{11,7},{12,8},{13,9},{1... | collective-permute-start | bytes 1572872 | tf_op jit(solution)/shard_map/ppermute | solution.py:20
  79.8 7.8 %all-to-all-start.2 = ((s32[128,1,17]{2,1,0:T(1,128)}), s32[128,1,17]{2,1,0:T(1,128)S(1)}, u32[]{:S(2)}, u32[]{:S(2)}) async-start(s32[128,1,17]{2,1,0:T(1,128)} %bitcast.35), calls=%async_computation.2 | async-start | bytes 131072 | tf_op jit(solution)/shard_map/all_to_all | solution.py:267
  89.1 8.7 %all-to-all-done.2 = s32[128,1,17]{2,1,0:T(1,128)S(1)} async-done(((s32[128,1,17]{2,1,0:T(1,128)}), s32[128,1,17]{2,1,0:T(1,128)S(1)}, u32[]{:S(2)}, u32[]{:S(2)}) %all-to-all-start.2) | async-done | bytes 8736 | tf_op jit(solution)/shard_map/all_to_all | solution.py:267
  103.5 7.0 %ffn_own.1.u0 = f32[32,344]{1,0:T(8,128)} custom-call(s32[1]{0:T(128)} %constant.295.clone.1.off_ref, bf16[256,2048]{1,0:T(8,128)(2,1)} %get-tuple-element.213.refs_0_, bf16[256,2048]{1,0:T(8,128)(2,1)} %copy-done, bf16[128,2048]{1,0:T(8,128)(2,1)} %copy-done.2, bf16[128,2048]{1,0:T(8,128)(2,1)} %copy-done.3, bf16[256,2048]{1,0:T(8,128)(2,1)} %copy-done.1, ...), custom_call_target="tpu_custom_call" | custom-call | tf_op jit(solution)/shard_map/ffn_own/pallas_call | solution.py:110
  112.2 7.8 %ffn_far.1 = f32[32,344]{1,0:T(8,128)} custom-call(s32[8]{0:T(128)} %stack.97.off_ref, bf16[256,2048]{1,0:T(8,128)(2,1)} %get-tuple-element.213.refs_0_, bf16[256,2048]{1,0:T(8,128)(2,1)} %copy-done, bf16[128,2048]{1,0:T(8,128)(2,1)} %copy-done.2, bf16[128,2048]{1,0:T(8,128)(2,1)} %copy-done.3, bf16[256,2048]{1,0:T(8,128)(2,1)} %copy-done.1, ...), custom_call_target="tpu_custom_call" | custom-call | tf_op jit(solution)/shard_map/ffn_far/pallas_call | solution.py:110
  126.5 11.5 %ffn_near.1 = (f32[32,344]{1,0:T(8,128)}, f32[32,344]{1,0:T(8,128)}) custom-call(s32[4]{0:T(128)} %pad_add_fusion.off_ref, bf16[256,2048]{1,0:T(8,128)(2,1)} %get-tuple-element.213.refs_0_, bf16[256,2048]{1,0:T(8,128)(2,1)} %copy-done, bf16[128,2048]{1,0:T(8,128)(2,1)} %copy-done.2, bf16[128,2048]{1,0:T(8,128)(2,1)} %copy-done.3, ...), custom_call_target="tpu_custom_call" | custom-call | tf_op jit(solution)/shard_map/ffn_near/pallas_call | solution.py:110
  138.2 2.6 %collective-permute-start.18 = (f32[32,344]{1,0:T(8,128)}, f32[32,344]{1,0:T(8,128)S(1)}, u32[]{:S(2)}, u32[]{:S(2)}) collective-permute-start(f32[32,344]{1,0:T(8,128)} %get-tuple-element.222), channel_id=1, source_target_pairs={{1,0},{2,1},{3,2},{0,3},{5,4},{6,5},{7,6},{4,7},{9,8},{10,9},{11,1... | collective-permute-start | bytes 132104 | tf_op jit(solution)/shard_map/ppermute | solution.py:25
  143.7 3.2 %down.1 = f32[128,2048]{1,0:T(8,128)} custom-call(s32[16]{0:T(128)} %stack.117.pos_ref, f32[32,344]{1,0:T(8,128)} %ffn_own.1.u0, f32[32,344]{1,0:T(8,128)} %copy-done.16, f32[32,344]{1,0:T(8,128)} %copy-done.15, f32[32,344]{1,0:T(8,128)} %copy-done.17, bf16[344,2048]{1,0:T(8,128)(2,1)} %w_ref.1), custom_call_target="tpu_custom_call" | custom-call | tf_op jit(solution)/shard_map/down/pallas_call | solution.py:141
  146.9 3.8 %all-to-all-start.3 = ((f32[16,8,2048]{2,1,0:T(8,128)}), f32[16,8,2048]{2,1,0:T(8,128)S(1)}, u32[]{:S(2)}, u32[]{:S(2)}) async-start(f32[16,8,2048]{2,1,0:T(8,128)} %bitcast.68), calls=%async_computation.3 | async-start | bytes 2097152 | tf_op jit(solution)/shard_map/all_to_all | solution.py:308
  150.8 14.9 %all-to-all-done.3 = f32[16,8,2048]{2,1,0:T(8,128)S(1)} async-done(((f32[16,8,2048]{2,1,0:T(8,128)}), f32[16,8,2048]{2,1,0:T(8,128)S(1)}, u32[]{:S(2)}, u32[]{:S(2)}) %all-to-all-start.3) | async-done | bytes 1048608 | tf_op jit(solution)/shard_map/all_to_all | solution.py:308
  165.7 2.1 emb.5
  167.8 7.1 %all-to-all-start.4 = ((bf16[128,2,2048]{2,1,0:T(2,128)(2,1)}), bf16[128,2,2048]{2,1,0:T(2,128)(2,1)S(1)}, u32[]{:S(2)}, u32[]{:S(2)}) async-start(bf16[128,2,2048]{2,1,0:T(2,128)(2,1)} %emb.5), calls=%async_computation.4 | async-start | bytes 2097152 | tf_op jit(solution)/shard_map/all_to_all | solution.py:313
  175.9 17.6 %all-to-all-done.4 = bf16[128,2,2048]{2,1,0:T(2,128)(2,1)S(1)} async-done(((bf16[128,2,2048]{2,1,0:T(2,128)(2,1)}), bf16[128,2,2048]{2,1,0:T(2,128)(2,1)S(1)}, u32[]{:S(2)}, u32[]{:S(2)}) %all-to-all-start.4) | async-done | bytes 1048608 | tf_op jit(solution)/shard_map/all_to_all | solution.py:313
  194.7 6.7 %match.5 = (f32[1,256]{1,0:T(1,128)}, f32[8,2048]{1,0:T(8,128)}) custom-call(bf16[256,2048]{1,0:T(8,128)(2,1)} %reshape.400.rows_ref, s32[1,256]{1,0:T(1,128)} %reshape.397.low_ref, s32[1,256]{1,0:T(1,128)} %reshape.398.high_ref, bf16[8,256]{1,0:T(8,128)(2,1)} %broadcast_in_dim.118.mem_ref, bf16[2048,2048]{1,0:T(8,128)(2,1)} %bank_ref.1, ...), custom_call_target="tpu_custom_call" | custom-call | tf_op jit(solution)/shard_map/match/pallas_call | solution.py:194
  204.2 4.9 %all-to-all-start.5 = ((f32[128,1,2]{2,1,0:T(1,128)}), f32[128,1,2]{2,1,0:T(1,128)S(1)}, u32[]{:S(2)}, u32[]{:S(2)}) async-start(f32[128,1,2]{2,1,0:T(1,128)} %bitcast.43), calls=%async_computation.5 | async-start | bytes 131072 | tf_op jit(solution)/shard_map/all_to_all | solution.py:315
  210.0 8.9 %all-to-all-done.5 = f32[128,1,2]{2,1,0:T(1,128)S(1)} async-done(((f32[128,1,2]{2,1,0:T(1,128)}), f32[128,1,2]{2,1,0:T(1,128)S(1)}, u32[]{:S(2)}, u32[]{:S(2)}) %all-to-all-start.5) | async-done | bytes 1056 | tf_op jit(solution)/shard_map/all_to_all | solution.py:315
  (136 shorter events, 36.6 us)
Async XLA Ops:
  9.7 49.7 %collective-permute-start.3 = (bf16[256,2048]{1,0:T(8,128)(2,1)}, bf16[256,2048]{1,0:T(8,128)(2,1)S(1)}, u32[]{:S(2)}, u32[]{:S(2)}) collective-permute-start(bf16[256,2048]{1,0:T(8,128)(2,1)} %get-tuple-element.213.refs_0_), channel_id=1, source_target_pairs={{4,0},{5,1},{6,2},{7,3},{8,4},{9,5},{10,6},{11,7},{12,8},{13,9},{1... | collective-permute-start | bytes 3145736 | tf_op jit(solution)/shard_map/ppermute | solution.py:20
  13.0 46.4 %collective-permute-start.5 = (bf16[256,2048]{1,0:T(8,128)(2,1)}, bf16[256,2048]{1,0:T(8,128)(2,1)S(1)}, u32[]{:S(2)}, u32[]{:S(2)}) collective-permute-start(bf16[256,2048]{1,0:T(8,128)(2,1)} %get-tuple-element.213.refs_0_), channel_id=1, source_target_pairs={{12,0},{13,1},{14,2},{15,3},{0,4},{1,5},{2,6},{3,7},{4,8},{5,9},{6... | collective-permute-start | bytes 3145736 | tf_op jit(solution)/shard_map/ppermute | solution.py:20
  13.0 106.9 %collective-permute-start.1 = (bf16[688,1024]{1,0:T(8,128)(2,1)}, bf16[688,1024]{1,0:T(8,128)(2,1)}, u32[]{:S(2)}, u32[]{:S(2)}) collective-permute-start(bf16[688,1024]{1,0:T(8,128)(2,1)} %pad_maximum_fusion.1), channel_id=1, source_target_pairs={{1,0},{2,1},{3,2},{0,3},{5,4},{6,5},{7,6},{4,7},{9,8},{10,9},{11,1... | collective-permute-start | bytes 4227080 | tf_op jit(solution)/shard_map/ppermute | solution.py:25
  15.8 104.2 %collective-permute-start.2 = (bf16[688,1024]{1,0:T(8,128)(2,1)}, bf16[688,1024]{1,0:T(8,128)(2,1)}, u32[]{:S(2)}, u32[]{:S(2)}) collective-permute-start(bf16[688,1024]{1,0:T(8,128)(2,1)} %pad_maximum_fusion.1), channel_id=1, source_target_pairs={{3,0},{0,1},{1,2},{2,3},{7,4},{4,5},{5,6},{6,7},{11,8},{8,9},{9,10... | collective-permute-start | bytes 4227080 | tf_op jit(solution)/shard_map/ppermute | solution.py:25
  15.8 39.2 %collective-permute-start = (bf16[688,256]{1,0:T(8,128)(2,1)}, bf16[688,256]{1,0:T(8,128)(2,1)}, u32[]{:S(2)}, u32[]{:S(2)}) collective-permute-start(bf16[688,256]{1,0:T(8,128)(2,1)} %pad_maximum_fusion.2), channel_id=1, source_target_pairs={{2,0},{3,1},{0,2},{1,3},{6,4},{7,5},{4,6},{5,7},{10,8},{11,9},{8,1... | collective-permute-start | bytes 1056776 | tf_op jit(solution)/shard_map/ppermute | solution.py:25
  55.6 11.2 %collective-permute-start.7 = (bf16[688,256]{1,0:T(8,128)(2,1)}, bf16[688,256]{1,0:T(8,128)(2,1)S(1)}, u32[]{:S(2)}, u32[]{:S(2)}) collective-permute-start(bf16[688,256]{1,0:T(8,128)(2,1)} %collective-permute-done.refs_5_), channel_id=1, source_target_pairs={{32,0},{48,16},{64,32},{80,48},{96,64},{112,80},{0,96},{16,112},{3... | collective-permute-start | bytes 1056776 | tf_op jit(solution)/shard_map/ppermute | solution.py:30
  59.4 16.3 %collective-permute-start.8 = (bf16[688,256]{1,0:T(8,128)(2,1)}, bf16[688,256]{1,0:T(8,128)(2,1)S(1)}, u32[]{:S(2)}, u32[]{:S(2)}) collective-permute-start(bf16[688,256]{1,0:T(8,128)(2,1)} %collective-permute-done.refs_5_), channel_id=1, source_target_pairs={{64,0},{80,16},{96,32},{112,48},{0,64},{16,80},{32,96},{48,112},{6... | collective-permute-start | bytes 1056776 | tf_op jit(solution)/shard_map/ppermute | solution.py:30
  59.4 19.0 %collective-permute-start.9 = (bf16[688,256]{1,0:T(8,128)(2,1)}, bf16[688,256]{1,0:T(8,128)(2,1)S(1)}, u32[]{:S(2)}, u32[]{:S(2)}) collective-permute-start(bf16[688,256]{1,0:T(8,128)(2,1)} %collective-permute-done.refs_5_), channel_id=1, source_target_pairs={{96,0},{112,16},{0,32},{16,48},{32,64},{48,80},{64,96},{80,112},{9... | collective-permute-start | bytes 1056776 | tf_op jit(solution)/shard_map/ppermute | solution.py:30
  66.8 31.1 %collective-permute-start.10 = (bf16[688,256]{1,0:T(8,128)(2,1)}, bf16[688,256]{1,0:T(8,128)(2,1)S(1)}, u32[]{:S(2)}, u32[]{:S(2)}) collective-permute-start(bf16[688,256]{1,0:T(8,128)(2,1)} %collective-permute-done.refs_5_), channel_id=1, source_target_pairs={{16,0},{0,16},{48,32},{32,48},{80,64},{64,80},{112,96},{96,112},{1... | collective-permute-start | bytes 1056776 | tf_op jit(solution)/shard_map/ppermute | solution.py:34
  75.7 23.0 %collective-permute-start.4 = (bf16[128,2048]{1,0:T(8,128)(2,1)S(1)}, bf16[128,2048]{1,0:T(8,128)(2,1)S(1)}, u32[]{:S(2)}, u32[]{:S(2)}) collective-permute-start(bf16[128,2048]{1,0:T(8,128)(2,1)S(1)} %slice.33), channel_id=1, source_target_pairs={{4,0},{5,1},{6,2},{7,3},{8,4},{9,5},{10,6},{11,7},{12,8},{13,9},{1... | collective-permute-start | bytes 1572872 | tf_op jit(solution)/shard_map/ppermute | solution.py:20
  78.4 20.4 %collective-permute-start.6 = (bf16[128,2048]{1,0:T(8,128)(2,1)S(1)}, bf16[128,2048]{1,0:T(8,128)(2,1)S(1)}, u32[]{:S(2)}, u32[]{:S(2)}) collective-permute-start(bf16[128,2048]{1,0:T(8,128)(2,1)S(1)} %slice.34), channel_id=1, source_target_pairs={{12,0},{13,1},{14,2},{15,3},{0,4},{1,5},{2,6},{3,7},{4,8},{5,9},{6... | collective-permute-start | bytes 1572872 | tf_op jit(solution)/shard_map/ppermute | solution.py:20
  79.8 18.0 %all-to-all-start.2 = ((s32[128,1,17]{2,1,0:T(1,128)}), s32[128,1,17]{2,1,0:T(1,128)S(1)}, u32[]{:S(2)}, u32[]{:S(2)}) async-start(s32[128,1,17]{2,1,0:T(1,128)} %bitcast.35), calls=%async_computation.2 | async-start | bytes 131072 | tf_op jit(solution)/shard_map/all_to_all | solution.py:267
  98.0 12.6 %collective-permute-start.11 = (bf16[688,256]{1,0:T(8,128)(2,1)}, bf16[688,256]{1,0:T(8,128)(2,1)S(1)}, u32[]{:S(2)}, u32[]{:S(2)}) collective-permute-start(bf16[688,256]{1,0:T(8,128)(2,1)} %copy-done.8), channel_id=1, source_target_pairs={{16,0},{0,16},{48,32},{32,48},{80,64},{64,80},{112,96},{96,112},{1... | collective-permute-start | bytes 1056776 | tf_op jit(solution)/shard_map/ppermute | solution.py:34
  98.7 11.9 %collective-permute-start.12 = (bf16[688,256]{1,0:T(8,128)(2,1)}, bf16[688,256]{1,0:T(8,128)(2,1)S(1)}, u32[]{:S(2)}, u32[]{:S(2)}) collective-permute-start(bf16[688,256]{1,0:T(8,128)(2,1)} %copy-done.9), channel_id=1, source_target_pairs={{16,0},{0,16},{48,32},{32,48},{80,64},{64,80},{112,96},{96,112},{1... | collective-permute-start | bytes 1056776 | tf_op jit(solution)/shard_map/ppermute | solution.py:34
  98.8 11.8 %collective-permute-start.13 = (bf16[688,256]{1,0:T(8,128)(2,1)}, bf16[688,256]{1,0:T(8,128)(2,1)S(1)}, u32[]{:S(2)}, u32[]{:S(2)}) collective-permute-start(bf16[688,256]{1,0:T(8,128)(2,1)} %copy-done.10), channel_id=1, source_target_pairs={{16,0},{0,16},{48,32},{32,48},{80,64},{64,80},{112,96},{96,112},{1... | collective-permute-start | bytes 1056776 | tf_op jit(solution)/shard_map/ppermute | solution.py:34
  119.9 3.5 %collective-permute-start.14 = (bf16[688,1024]{1,0:T(8,128)(2,1)}, bf16[688,1024]{1,0:T(8,128)(2,1)S(1)}, u32[]{:S(2)}, u32[]{:S(2)}) collective-permute-start(bf16[688,1024]{1,0:T(8,128)(2,1)} %collective-permute-done.1.refs_5_), channel_id=1, source_target_pairs={{16,0},{0,16},{48,32},{32,48},{80,64},{64,80},{112,96},{96,112},{1... | collective-permute-start | bytes 4227080 | tf_op jit(solution)/shard_map/ppermute | solution.py:34
  120.3 5.1 %collective-permute-start.15 = (bf16[688,1024]{1,0:T(8,128)(2,1)}, bf16[688,1024]{1,0:T(8,128)(2,1)S(1)}, u32[]{:S(2)}, u32[]{:S(2)}) collective-permute-start(bf16[688,1024]{1,0:T(8,128)(2,1)} %collective-permute-done.2.refs_7_), channel_id=1, source_target_pairs={{16,0},{0,16},{48,32},{32,48},{80,64},{64,80},{112,96},{96,112},{1... | collective-permute-start | bytes 4227080 | tf_op jit(solution)/shard_map/ppermute | solution.py:34
  120.5 20.3 %collective-permute-start.17 = (f32[32,344]{1,0:T(8,128)}, f32[32,344]{1,0:T(8,128)S(1)}, u32[]{:S(2)}, u32[]{:S(2)}) collective-permute-start(f32[32,344]{1,0:T(8,128)} %ffn_far.1), channel_id=1, source_target_pairs={{2,0},{3,1},{0,2},{1,3},{6,4},{7,5},{4,6},{5,7},{10,8},{11,9},{8,1... | collective-permute-start | bytes 132104 | tf_op jit(solution)/shard_map/ppermute | solution.py:25
  138.0 4.4 %collective-permute-start.16 = (f32[32,344]{1,0:T(8,128)}, f32[32,344]{1,0:T(8,128)S(1)}, u32[]{:S(2)}, u32[]{:S(2)}) collective-permute-start(f32[32,344]{1,0:T(8,128)} %get-tuple-element.220), channel_id=1, source_target_pairs={{3,0},{0,1},{1,2},{2,3},{7,4},{4,5},{5,6},{6,7},{11,8},{8,9},{9,10... | collective-permute-start | bytes 132104 | tf_op jit(solution)/shard_map/ppermute | solution.py:25
  138.2 4.3 %collective-permute-start.18 = (f32[32,344]{1,0:T(8,128)}, f32[32,344]{1,0:T(8,128)S(1)}, u32[]{:S(2)}, u32[]{:S(2)}) collective-permute-start(f32[32,344]{1,0:T(8,128)} %get-tuple-element.222), channel_id=1, source_target_pairs={{1,0},{2,1},{3,2},{0,3},{5,4},{6,5},{7,6},{4,7},{9,8},{10,9},{11,1... | collective-permute-start | bytes 132104 | tf_op jit(solution)/shard_map/ppermute | solution.py:25
  146.9 18.8 %copy-start.5 = (f32[8,2048]{1,0:T(8,128)S(1)}, f32[8,2048]{1,0:T(8,128)}, u32[]{:S(2)}) copy-start(f32[8,2048]{1,0:T(8,128)} %get-tuple-element.455.p_ref) | copy-start | bytes 196612
  146.9 18.7 %all-to-all-start.3 = ((f32[16,8,2048]{2,1,0:T(8,128)}), f32[16,8,2048]{2,1,0:T(8,128)S(1)}, u32[]{:S(2)}, u32[]{:S(2)}) async-start(f32[16,8,2048]{2,1,0:T(8,128)} %bitcast.68), calls=%async_computation.3 | async-start | bytes 2097152 | tf_op jit(solution)/shard_map/all_to_all | solution.py:308
  167.8 25.7 %all-to-all-start.4 = ((bf16[128,2,2048]{2,1,0:T(2,128)(2,1)}), bf16[128,2,2048]{2,1,0:T(2,128)(2,1)S(1)}, u32[]{:S(2)}, u32[]{:S(2)}) async-start(bf16[128,2,2048]{2,1,0:T(2,128)(2,1)} %emb.5), calls=%async_computation.4 | async-start | bytes 2097152 | tf_op jit(solution)/shard_map/all_to_all | solution.py:313
  204.2 14.6 %all-to-all-start.5 = ((f32[128,1,2]{2,1,0:T(1,128)}), f32[128,1,2]{2,1,0:T(1,128)S(1)}, u32[]{:S(2)}, u32[]{:S(2)}) async-start(f32[128,1,2]{2,1,0:T(1,128)} %bitcast.43), calls=%async_computation.5 | async-start | bytes 131072 | tf_op jit(solution)/shard_map/all_to_all | solution.py:315
  (26 other events, 126.0 us)

commit v3 on v2

v3 whole, which is shorter than its diff:
```python
import functools

import jax
import jax.numpy as jnp
from jax import lax
from jax.experimental import pallas as pl
from jax.experimental.pallas import tpu as pltpu
from jax.sharding import PartitionSpec as P

ALL = ("dp", "mp")
NX, NY, NZ, NC = 4, 4, 4, 2
ORDERS = 1 << 20
BF, F32, I32 = jnp.bfloat16, jnp.float32, jnp.int32
VMEM = pltpu.CompilerParams(vmem_limit_bytes=56 * 1024 * 1024)
NT = (((1,), (1,)), ((), ()))


def from_x(v, j):
    perm = [(((x + j) % NX) * NY + y, x * NY + y) for x in range(NX) for y in range(NY)]
    return lax.ppermute(v, "mp", perm)


def from_y(v, k):
    perm = [(x * NY + (y + k) % NY, x * NY + y) for x in range(NX) for y in range(NY)]
    return lax.ppermute(v, "mp", perm)


def from_core(v):
    return lax.ppermute(v, "dp", [(d ^ 1, d) for d in range(NZ * NC)])


def block_ones(files, file_len, dtype):
    row = lax.broadcasted_iota(I32, (files, files * file_len), 0)
    col = lax.broadcasted_iota(I32, (files, files * file_len), 1)
    return jnp.where(col // file_len == row, 1.0, 0.0).astype(dtype)


def prep_kernel(file_len, len_ref, h_ref, gain_ref, n_ref, p_ref):
    gain = gain_ref[...].astype(F32)
    ones = jnp.ones((p_ref.shape[0], file_len), BF)
    for f in range(p_ref.shape[0]):
        rows = slice(f * file_len, (f + 1) * file_len)
        raw = h_ref[rows, :]
        resid = raw.astype(F32)
        scale = lax.rsqrt(jnp.mean(resid * resid, axis=-1, keepdims=True) + 1e-05)
        keep = lax.broadcasted_iota(I32, (file_len, 1), 0) < len_ref[f]
        n_ref[rows, :] = jnp.where(keep, resid * scale * gain, 0.0).astype(BF)
        valid = jnp.where(keep, resid, 0.0).astype(BF)
        p_ref[f:f + 1, :] = jnp.dot(ones, valid, preferred_element_type=F32)[:1]


def prep(hidden, gain, lengths):
    tok, width = hidden.shape
    files = lengths.shape[0]
    vm = pl.BlockSpec(memory_space=pltpu.VMEM)
    return pl.pallas_call(
        functools.partial(prep_kernel, tok // files),
        in_specs=[pl.BlockSpec(memory_space=pltpu.SMEM), vm, vm],
        out_specs=(vm, vm),
        out_shape=(jax.ShapeDtypeStruct((tok, width), BF), jax.ShapeDtypeStruct((files, width), F32)),
        compiler_params=pltpu.CompilerParams(vmem_limit_bytes=16 * 1024 * 1024),
        name="prep",
    )(lengths, hidden, gain[None, :])


def ffn_kernel(slice_parts, n_tok, n_old, file_len, off_ref, *refs):
    toks, refs = refs[:n_tok], refs[n_tok:]
    n_parts = sum(slice_parts)
    parts, refs = refs[:n_parts], refs[n_parts:]
    olds, refs = refs[:n_old], refs[n_old:]
    outs, bufs = refs[:len(slice_parts)], refs[len(slice_parts):]
    at = 0
    for s, count in enumerate(slice_parts):
        mine = parts[at:at + count]
        cols = mine[0].shape[-1]
        offs = [pl.multiple_of(off_ref[at + p], 128) for p in range(count)]
        at += count
        hid = mine[0].shape[-2] // 2
        row = 0
        if n_old:
            row = olds[s].shape[0]
            outs[s][:row, :] = olds[s][...]
        if len(mine[0].shape) == 3:
            for part, off in zip(mine, offs):
                for q in range(part.shape[0]):
                    bufs[0][:, pl.ds(off + q * count * cols, cols)] = part[q]
            mine, offs, cols = [bufs[0]], [0], bufs[0].shape[1]
        for t in toks:
            both = None
            for w, off in zip(mine, offs):
                x = t[...] if len(mine) == 1 else t[:, pl.ds(off, cols)]
                term = lax.dot_general(w[...], x, NT, preferred_element_type=F32)
                both = term if both is None else both + term
            gate = both[:hid]
            units = (0.5 * gate * (1.0 + jnp.tanh(0.5 * gate)) * both[hid:]).astype(BF)
            n = t.shape[0] // file_len
            ones = block_ones(n, file_len, BF)
            outs[s][row:row + n, :] = lax.dot_general(ones, units, NT, preferred_element_type=F32)
            row += n


def ffn(toks, slices, offs, file_len, name, olds=()):
    width = toks[0].shape[1]
    n_files = sum(t.shape[0] for t in toks) // file_len + (olds[0].shape[0] if olds else 0)
    rows = slices[0][0].shape[-2]
    flat = [p for s in slices for p in s]
    vm = pl.BlockSpec(memory_space=pltpu.VMEM)
    return pl.pallas_call(
        functools.partial(ffn_kernel, tuple(len(s) for s in slices), len(toks), len(olds), file_len),
        in_specs=[pl.BlockSpec(memory_space=pltpu.SMEM)] + [vm] * (len(toks) + len(flat) + len(olds)),
        out_specs=tuple(vm for _ in slices),
        out_shape=tuple(jax.ShapeDtypeStruct((n_files, rows // 2), F32) for _ in slices),
        scratch_shapes=[pltpu.VMEM((rows, width), BF)] if max(p.ndim for p in flat) > 2 else [],
        compiler_params=pltpu.CompilerParams(vmem_limit_bytes=24 * 1024 * 1024),
        name=name,
    )(offs, *toks, *flat, *olds)


def down_kernel(files, pos_ref, u0, u1, u2, u3, w_ref, o_ref, buf):
    for k, u in enumerate((u0, u1, u2, u3)):
        for j in range(NX):
            dst = pl.multiple_of(pos_ref[k * NX + j], files)
            buf[pl.ds(dst, files), :] = u[j * files:(j + 1) * files, :]
    rows = buf[...]
    hi = rows.astype(BF)
    lo = (rows - hi.astype(F32)).astype(BF)
    w = w_ref[...]
    o_ref[...] = jnp.dot(hi, w, preferred_element_type=F32) + jnp.dot(lo, w, preferred_element_type=F32)


def down(us, w_down, pos, files):
    rows = NX * NY * files
    vm = pl.BlockSpec(memory_space=pltpu.VMEM)
    return pl.pallas_call(
        functools.partial(down_kernel, files),
        in_specs=[pl.BlockSpec(memory_space=pltpu.SMEM)] + [vm] * 5,
        out_specs=vm,
        out_shape=jax.ShapeDtypeStruct((rows, w_down.shape[1]), F32),
        scratch_shapes=[pltpu.VMEM((rows, us[0].shape[1]), F32)],
        compiler_params=VMEM,
        name="down",
    )(pos, *us, w_down)


def emb_kernel(files, copies, t_ref, p_ref, len_ref, sel_ref, meta_ref, o_ref):
    total = p_ref[...]
    for m in range(t_ref.shape[0] // files):
        total = total + t_ref[m * files:(m + 1) * files, :]
    pooled = total / len_ref[...]
    norm = lax.rsqrt(jnp.sum(pooled * pooled, axis=-1, keepdims=True) + 1e-06)
    emb = (pooled * norm).astype(BF)
    width = emb.shape[1]
    rows = jnp.dot(sel_ref[...], emb, preferred_element_type=F32)
    for d in range(sel_ref.shape[0] // 2):
        pair = rows[2 * d:2 * d + 2, :].astype(BF)
        about = meta_ref[2 * d:2 * d + 2, :].astype(BF)
        for m in range(copies):
            o_ref[d * copies + m, :, :width] = pair
            o_ref[d * copies + m, :, width:] = about


def emb_to_owners(terms, pooled, lens, sel, meta, files, copies):
    return pl.pallas_call(
        functools.partial(emb_kernel, files, copies),
        out_shape=jax.ShapeDtypeStruct((sel.shape[0] // 2 * copies, 2, pooled.shape[1] + meta.shape[1]), BF),
        compiler_params=pltpu.CompilerParams(vmem_limit_bytes=16 * 1024 * 1024),
        name="emb",
    )(terms, pooled, lens, sel, meta)


def match_kernel(mp_ref, rows_ref, bank_ref, key_ref, best_ref, sums_ref, about_ref):
    width = bank_ref.shape[1]
    rows = rows_ref[:, :width]
    pick = lax.broadcasted_iota(I32, (8, 128), 0) == lax.broadcasted_iota(I32, (8, 128), 1)
    digits = lax.dot_general(
        jnp.where(pick, 1.0, 0.0).astype(BF), rows_ref[:, width:], NT, preferred_element_type=F32
    )
    low = digits[0:1] * 65536.0 + digits[1:2] * 256.0 + digits[2:3]
    high = digits[3:4] * 65536.0 + digits[4:5] * 256.0 + digits[5:6]
    mine = digits[6:7] == (mp_ref[0] + 1).astype(F32)
    member = jnp.broadcast_to(jnp.where(mine, 1.0, 0.0), (8, rows.shape[0])).astype(BF)
    best = jnp.full((1, rows.shape[0]), -1.0, F32)
    block = 512
    for i in range(bank_ref.shape[0] // block):
        at = slice(i * block, (i + 1) * block)
        sims = lax.dot_general(bank_ref[at, :], rows, NT, preferred_element_type=F32)
        key = key_ref[at, :]
        valid = (key >= low) & (key < high)
        best = jnp.maximum(best, jnp.max(jnp.where(valid, sims, -1.0), axis=0, keepdims=True))
    best_ref[...] = best
    sums_ref[...] = jnp.dot(member, rows, preferred_element_type=F32)
    count = jnp.sum(jnp.where(mine, 1.0, 0.0), axis=1, keepdims=True)
    most = jnp.max(digits[7:8], axis=1, keepdims=True)
    lane = lax.broadcasted_iota(I32, (1, 128), 1)
    about_ref[...] = jnp.where(lane == 0, count, most)


def match(rows, mp, bank, key):
    n = rows.shape[0]
    vm = pl.BlockSpec(memory_space=pltpu.VMEM)
    return pl.pallas_call(
        match_kernel,
        in_specs=[pl.BlockSpec(memory_space=pltpu.SMEM)] + [vm] * 3,
        out_specs=(vm, vm, vm),
        out_shape=(
            jax.ShapeDtypeStruct((1, n), F32),
            jax.ShapeDtypeStruct((8, bank.shape[1]), F32),
            jax.ShapeDtypeStruct((1, 128), F32),
        ),
        compiler_params=pltpu.CompilerParams(vmem_limit_bytes=24 * 1024 * 1024),
        name="match",
    )(mp[None], rows, bank, key)


def on_device(
    hidden_in,
    mlp_gain,
    w_gate,
    w_up,
    w_down,
    lengths,
    file_cluster,
    file_order,
    cluster_slot,
    bank,
    bank_slot,
    bank_order,
    centroid_old,
    count_old,
):
    tok, width = hidden_in.shape
    files = lengths.shape[0]
    file_len = tok // files
    n_dp, n_mp = NZ * NC, NX * NY
    dp, mp = lax.axis_index("dp"), lax.axis_index("mp")
    z, c, x, y = dp // NC, dp % NC, mp // NY, mp % NY
    tie = lax.optimization_barrier

    k_total = cluster_slot.shape[0]
    owned = k_total // n_dp
    lookup = file_cluster[:, None] == jnp.arange(k_total, dtype=I32)[None, :]
    slot = jnp.sum(jnp.where(lookup, cluster_slot[None, :], 0), axis=1)
    owner = slot // owned
    ids = jnp.arange(files, dtype=I32)
    rank = jnp.sum(((owner[:, None] == owner[None, :]) & (ids[None, :] < ids[:, None])).astype(I32), axis=1)
    place = (owner[None, None, :] == jnp.arange(n_dp, dtype=I32)[:, None, None]) & (
        rank[None, None, :] == ids[None, :, None]
    )
    local = slot % owned
    first = local * ORDERS
    key = first + file_order
    bank_key = (bank_slot * ORDERS + bank_order).astype(F32)[:, None]
    low_key, high_key = [first >> 16, first * 0, first * 0], [key >> 16, (key >> 8) & 255, key & 255]
    digits = jnp.stack(low_key + high_key + [local + 1, jnp.broadcast_to(jnp.max(rank) + 1, slot.shape)], axis=1)

    def files_of(r):
        here = lax.dynamic_slice_in_dim(place, 2 * r, 2, 1)
        sel = here.reshape(-1, files)
        meta = jnp.sum(jnp.where(sel[:, :, None], digits[None], 0), axis=1).astype(F32)
        return here, sel.astype(BF), jnp.pad(meta, ((0, 0), (0, 120)))

    eighth, half = width // 8, width // 2
    w_t = [w_gate.T, w_up.T]
    cut = lambda start, n: jnp.concatenate([lax.dynamic_slice_in_dim(w, start, n, 1) for w in w_t], axis=0)
    w_own = jnp.concatenate(w_t, axis=0)
    w_e = cut(dp * eighth, eighth)
    w_e, hidden_in, w_t = tie((w_e, hidden_in, w_t))
    e0 = from_y(w_e, 2)
    w_h = cut(c * half, half)
    normed, pooled_in = prep(hidden_in, mlp_gain, lengths)
    w_h, normed, w_t = tie((w_h, normed, w_t))
    t1, t3 = from_x(normed, 1), from_x(normed, 3)
    h1, h3 = from_y(w_h, 1), from_y(w_h, 3)
    e0, normed = tie((e0, normed))
    column = [[z_ * NC + c_ for z_ in range(NZ)] for c_ in range(NC)]
    es = lax.all_to_all(jnp.broadcast_to(e0[None], (NZ,) + e0.shape), "dp", 0, 0, axis_index_groups=column, tiled=True)
    es, t1, t3 = tie((es, t1, t3))
    es = [es, from_core(es)]
    t2a, t2b = from_x(t1[:tok // 2], 1), from_x(t3[tok // 2:], 3)
    toks, last = [normed, t1, t3], [t2a, t2b]

    e_off = jnp.stack([c * eighth, (1 - c) * eighth]).astype(I32)
    h_off = jnp.stack([c * half, (1 - c) * half] * 2).astype(I32)
    pos = jnp.stack(
        [(((x + j) % NX) * NY + (y - k) % NY) * files for k in range(NY) for j in (0, 1, 3, 2)]
    ).astype(I32)
    lens = lengths.astype(F32)[:, None]
    ready = files_of(0)
    normed, e_off, h_off, pos, lens, bank_key, ready = tie((normed, e_off, h_off, pos, lens, bank_key, ready))
    toks[0] = normed

    zero = jnp.zeros((1,), I32)
    (u0,) = ffn(toks, [[w_own]], zero, file_len, "ffn_own")
    u0, es = tie((u0, es))
    (u2,) = ffn(toks + last, [es], e_off, file_len, "ffn_far")
    h1, h3, u2, last = tie((h1, h3, u2, last))
    (u0,) = ffn(last, [[w_own]], zero, file_len, "ffn_last", (u0,))
    g1, g3 = from_core(h1), from_core(h3)
    r2 = from_y(u2, NY - 2)
    u1, u3 = ffn(toks + last, [[h1, g1], [h3, g3]], h_off, file_len, "ffn_near")
    r1, r3 = from_y(u1, NY - 1), from_y(u3, NY - 3)
    terms = down([u0, r1, r2, r3], w_down, pos, files)
    terms = lax.all_to_all(terms, "mp", 0, 0, tiled=True)

    def one_round(ready, best, sums, counts):
        here, sel, meta = ready
        rows = emb_to_owners(terms, pooled_in, lens, sel, meta, files, n_mp)
        rows = lax.all_to_all(rows, ALL, 0, 0, tiled=True)
        top, new, about = match(rows.reshape(-1, rows.shape[2]), mp, bank, bank_key)
        back = lax.all_to_all(top.reshape(-1, 2), ALL, 0, 0, tiled=True)
        back = jnp.max(back.reshape(n_dp, n_mp, 2), axis=1)
        best = jnp.maximum(best, jnp.max(jnp.where(here, back[:, :, None], -1.0), axis=(0, 1)))
        return about[0, 1], (best, sums + new[:1], counts + about[0, 0])

    most, state = one_round(ready, jnp.full((files,), -1.0, F32), jnp.zeros((1, width), F32), jnp.float32(0))
    _, (best, sums, counts) = lax.while_loop(
        lambda s: 2 * s[0] < most.astype(I32),
        lambda s: (s[0] + 1, one_round(files_of(s[0]), *s[1])[1]),
        (jnp.int32(1), state),
    )
    centroid_new = (count_old[:, None] * centroid_old + sums) / (count_old + counts)[:, None]
    return best, centroid_new


def solution(mesh):
    both = P(ALL)
    rows = P(ALL, None)
    return jax.shard_map(
        on_device,
        mesh=mesh,
        in_specs=(
            rows, P(), P(None, "mp"), P(None, "mp"), P("mp", None), both, both, both, P(), rows, both, both, rows, both,
        ),
        out_specs=(both, rows),
        check_vma=False,
    )
```

time: 221 us -> 191 us (0.86)
  waiting for transfers between devices: 93.7 us -> 73.3 us
  starting transfers between devices: 53 us -> 43.5 us
  Pallas kernels: 41.2 us -> 49.3 us
  other arithmetic: 11.4 us -> 6.7 us
  local copies, waits for them, and re-layouts: 17.1 us -> 14.7 us
    ppermute x6, waiting for transfers between devices: 37 us -> 3.22 us  [from_y(): return lax.ppermute(v, 'mp', perm)]
    ppermute x4, waiting for transfers between devices: 0.01 us -> 26.7 us  [from_x(): return lax.ppermute(v, 'mp', perm)]
    all_to_all x2, waiting for transfers between devices: 26.3 us -> 17 us  [the longest x1 16.9 us: one_round(): rows = lax.all_to_all(rows, ALL, 0, 0, tiled=True)]
    pallas_call x5 -> x6, Pallas kernels: 35.9 us -> 44.8 us  [the longest x4 37.4 us: ffn(): pl.pallas_call(functools.partial(ffn_kernel, tuple((len(s) for s in slice...]
    ppermute x6 -> x3, starting transfers between devices: 10.7 us -> 4.55 us  [from_core(): return lax.ppermute(v, 'dp', [(d ^ 1, d) for d in range(NZ * NC)])]
    ppermute x3 -> x0, starting transfers between devices: 4.44 us -> none  [from_z(): return lax.ppermute(v, 'dp', perm)]
    ppermute x6, starting transfers between devices: 8.56 us -> 12.2 us  [from_y(): return lax.ppermute(v, 'mp', perm)]
    ppermute x3 -> x0, waiting for transfers between devices: 3.17 us -> none  [from_z(): return lax.ppermute(v, 'dp', perm)]
  transfers between devices with their start and end apart: 23 -> 17, of which waited for: 10 -> 9; matrix products, arithmetic and copies ran while one was open for 6% -> 6% of each run, Pallas kernels for 12% -> 20%
where the time goes in v3:
time: 191 us
  waiting for transfers between devices  73.3 us (38%)
  Pallas kernels  49.3 us (26%)
  starting transfers between devices  43.5 us (23%)
  local copies, waits for them, and re-layouts  14.7 us (8%)
  other arithmetic  6.7 us (4%)
  between operations  2.73 us (1%)
    pallas_call x4, Pallas kernels, ffn(): pl.pallas_call(functools.partial(ffn_kernel, tuple((len(s) for s in slice...  37.4 us
    ppermute x4, waiting for transfers between devices, from_x(): return lax.ppermute(v, 'mp', perm)  26.7 us
    all_to_all x1, waiting for transfers between devices, one_round(): rows = lax.all_to_all(rows, ALL, 0, 0, tiled=True)  16.9 us
    all_to_all x1, waiting for transfers between devices, on_device(): terms = lax.all_to_all(terms, 'mp', 0, 0, tiled=True)  15.5 us
    ppermute x6, starting transfers between devices, from_y(): return lax.ppermute(v, 'mp', perm)  12.2 us
    all_to_all x1, waiting for transfers between devices, one_round(): back = lax.all_to_all(top.reshape(-1, 2), ALL, 0, 0, tiled=True)  9.06 us
    all_to_all x1, starting transfers between devices, one_round(): rows = lax.all_to_all(rows, ALL, 0, 0, tiled=True)  9.03 us
    pallas_call x1, Pallas kernels, match(): pl.pallas_call(match_kernel, in_specs=[pl.BlockSpec(memory_space=pltpu.SM...  6.2 us
  transfers between devices with their start and end apart: 17, of which 9 were waited for; matrix products, arithmetic and copies ran while one was open for 6% of the time, Pallas kernels for 20%

profile of v3, /device:TPU:1, one launch (start us, length us, event | category | flops | bytes accessed | tf_op | source)
XLA Modules:
  0.0 190.8 jit_solution(7159103451315874993)
XLA Ops:
  2.6 3.7 %collective-permute-start = (bf16[688,256]{1,0:T(8,128)(2,1)}, bf16[688,256]{1,0:T(8,128)(2,1)S(1)}, u32[]{:S(2)}, u32[]{:S(2)}) collective-permute-start(bf16[688,256]{1,0:T(8,128)(2,1)} %pad_maximum_fusion.2), channel_id=1, source_target_pairs={{2,0},{3,1},{0,2},{1,3},{6,4},{7,5},{4,6},{5,7},{10,8},{11,9},{8,1... | collective-permute-start | bytes 1056776 | tf_op jit(solution)/shard_map/ppermute | solution.py:25
  11.0 3.2 %collective-permute-done = bf16[688,256]{1,0:T(8,128)(2,1)S(1)} collective-permute-done((bf16[688,256]{1,0:T(8,128)(2,1)}, bf16[688,256]{1,0:T(8,128)(2,1)S(1)}, u32[]{:S(2)}, u32[]{:S(2)}) %collective-permute-start) | collective-permute-done | bytes 352288 | tf_op jit(solution)/shard_map/ppermute | solution.py:25
  15.4 5.2 %all-to-all-start.2 = ((bf16[4,688,256]{2,1,0:T(8,128)(2,1)}), bf16[4,688,256]{2,1,0:T(8,128)(2,1)}, u32[]{:S(2)}, u32[]{:S(2)}) async-start(bf16[4,688,256]{2,1,0:T(8,128)(2,1)} %broadcast_in_dim.139), calls=%async_computation.2 | async-start | bytes 2818048 | tf_op jit(solution)/shard_map/all_to_all | solution.py:276
  20.6 2.5 %collective-permute-start.3 = (bf16[256,2048]{1,0:T(8,128)(2,1)S(1)}, bf16[256,2048]{1,0:T(8,128)(2,1)S(1)}, u32[]{:S(2)}, u32[]{:S(2)}) collective-permute-start(bf16[256,2048]{1,0:T(8,128)(2,1)S(1)} %get-tuple-element.212.refs_0_), channel_id=1, source_target_pairs={{4,0},{5,1},{6,2},{7,3},{8,4},{9,5},{10,6},{11,7},{12,8},{13,9},{1... | collective-permute-start | bytes 3145736 | tf_op jit(solution)/shard_map/ppermute | solution.py:20
  23.1 2.7 %collective-permute-start.1 = (bf16[688,1024]{1,0:T(8,128)(2,1)}, bf16[688,1024]{1,0:T(8,128)(2,1)}, u32[]{:S(2)}, u32[]{:S(2)}) collective-permute-start(bf16[688,1024]{1,0:T(8,128)(2,1)} %pad_maximum_fusion.1), channel_id=1, source_target_pairs={{1,0},{2,1},{3,2},{0,3},{5,4},{6,5},{7,6},{4,7},{9,8},{10,9},{11,1... | collective-permute-start | bytes 4227080 | tf_op jit(solution)/shard_map/ppermute | solution.py:25
  26.2 17.5 %collective-permute-done.3.refs_1_ = bf16[256,2048]{1,0:T(8,128)(2,1)S(1)} collective-permute-done((bf16[256,2048]{1,0:T(8,128)(2,1)S(1)}, bf16[256,2048]{1,0:T(8,128)(2,1)S(1)}, u32[]{:S(2)}, u32[]{:S(2)}) %collective-permute-start.3) | collective-permute-done | bytes 1048608 | tf_op jit(solution)/shard_map/ppermute | solution.py:20
  43.7 3.2 %collective-permute-done.4.refs_2_ = bf16[256,2048]{1,0:T(8,128)(2,1)S(1)} collective-permute-done((bf16[256,2048]{1,0:T(8,128)(2,1)S(1)}, bf16[256,2048]{1,0:T(8,128)(2,1)S(1)}, u32[]{:S(2)}, u32[]{:S(2)}) %collective-permute-start.4) | collective-permute-done | bytes 1048608 | tf_op jit(solution)/shard_map/ppermute | solution.py:20
  46.9 2.9 %collective-permute-start.7 = (bf16[4,688,256]{2,1,0:T(8,128)(2,1)}, bf16[4,688,256]{2,1,0:T(8,128)(2,1)}, u32[]{:S(2)}, u32[]{:S(2)}) collective-permute-start(bf16[4,688,256]{2,1,0:T(8,128)(2,1)} %all-to-all-done.2.refs_5_), channel_id=1, source_target_pairs={{16,0},{0,16},{48,32},{32,48},{80,64},{64,80},{112,96},{96,112},{1... | collective-permute-start | bytes 4227080 | tf_op jit(solution)/shard_map/ppermute | solution.py:29
  56.1 2.0 %pad_maximum_fusion.refs_3_.refs_2_ = bf16[688,2048]{1,0:T(8,128)(2,1)S(1)} fusion(bf16[344,2048]{1,0:T(8,128)(2,1)} %bitcast.77, bf16[344,2048]{1,0:T(8,128)(2,1)} %bitcast.79), kind=kLoop, calls=%fused_computation.5 | loop fusion | flops 5636096 | bytes 5636096 | tf_op jit(solution)/shard_map/concatenate | solution.py:265
  58.1 4.4 %ffn_own.1.refs_3_ = f32[24,344]{1,0:T(8,128)S(1)} custom-call(s32[1]{0:T(128)} %constant.220.clone.1.off_ref, bf16[256,2048]{1,0:T(8,128)(2,1)S(1)} %get-tuple-element.212.refs_0_, bf16[256,2048]{1,0:T(8,128)(2,1)S(1)} %collective-permute-done.3.refs_1_, bf16[256,2048]{1,0:T(8,128)(2,1)S(1)} %collective-permute-done.4.refs_2_, ...), custom_call_target="tpu_custom_call" | custom-call | tf_op jit(solution)/shard_map/ffn_own/pallas_call | solution.py:108
  62.5 4.2 %collective-permute-done.5.refs_3_.refs_0_ = bf16[128,2048]{1,0:T(8,128)(2,1)} collective-permute-done((bf16[128,2048]{1,0:T(8,128)(2,1)}, bf16[128,2048]{1,0:T(8,128)(2,1)}, u32[]{:S(2)}, u32[]{:S(2)}) %collective-permute-start.5) | collective-permute-done | bytes 524320 | tf_op jit(solution)/shard_map/ppermute | solution.py:20
  68.4 10.0 %ffn_far.1 = f32[32,344]{1,0:T(8,128)S(1)} custom-call(s32[2]{0:T(128)S(1)} %pad_add_fusion.off_ref, bf16[256,2048]{1,0:T(8,128)(2,1)S(1)} %get-tuple-element.212.refs_0_, bf16[256,2048]{1,0:T(8,128)(2,1)S(1)} %collective-permute-done.3.refs_1_, bf16[256,2048]{1,0:T(8,128)(2,1)S(1)} %collective-permute-done.4.refs_2_, ...), custom_call_target="tpu_custom_call" | custom-call | tf_op jit(solution)/shard_map/ffn_far/pallas_call | solution.py:108
  80.1 2.9 %collective-permute-start.11 = (f32[32,344]{1,0:T(8,128)S(1)}, f32[32,344]{1,0:T(8,128)S(1)}, u32[]{:S(2)}, u32[]{:S(2)}) collective-permute-start(f32[32,344]{1,0:T(8,128)S(1)} %ffn_far.1), channel_id=1, source_target_pairs={{2,0},{3,1},{0,2},{1,3},{6,4},{7,5},{4,6},{5,7},{10,8},{11,9},{8,1... | collective-permute-start | bytes 132104 | tf_op jit(solution)/shard_map/ppermute | solution.py:25
  83.0 1.8 collective-permute-done.9.refs_8_
  84.9 18.5 %ffn_near.1 = (f32[32,344]{1,0:T(8,128)S(1)}, f32[32,344]{1,0:T(8,128)S(1)}) custom-call(s32[4]{0:T(128)S(1)} %pad_add_fusion.1.off_ref, bf16[256,2048]{1,0:T(8,128)(2,1)S(1)} %get-tuple-element.212.refs_0_, bf16[256,2048]{1,0:T(8,128)(2,1)S(1)} %collective-permute-done.3.refs_1_, bf16[256,2048]{1,0:T(8,128)(2,1)S(1)} %collective-permute-done.4.refs_2_, ...), custom_call_target="tpu_custom_call" | custom-call | tf_op jit(solution)/shard_map/ffn_near/pallas_call | solution.py:108
  106.2 4.5 %ffn_last.1.u0 = f32[32,344]{1,0:T(8,128)S(1)} custom-call(s32[1]{0:T(128)} %constant.220.clone.1.off_ref, bf16[128,2048]{1,0:T(8,128)(2,1)} %collective-permute-done.5.refs_3_.refs_0_, bf16[128,2048]{1,0:T(8,128)(2,1)} %collective-permute-done.6.refs_4_.refs_1_, bf16[688,2048]{1,0:T(8,128)(2,1)S(1)} %pad_maximum_fusion.refs_3_.refs_2_, ...), custom_call_target="tpu_custom_call" | custom-call | tf_op jit(solution)/shard_map/ffn_last/pallas_call | solution.py:108
  112.6 3.2 %down.1 = f32[128,2048]{1,0:T(8,128)} custom-call(s32[16]{0:T(128)} %stack.107.pos_ref, f32[32,344]{1,0:T(8,128)} %copy-done.1, f32[32,344]{1,0:T(8,128)} %copy-done.6, f32[32,344]{1,0:T(8,128)} %copy-done.5, f32[32,344]{1,0:T(8,128)} %copy-done.7, bf16[344,2048]{1,0:T(8,128)(2,1)} %w_ref.1), custom_call_target="tpu_custom_call" | custom-call | tf_op jit(solution)/shard_map/down/pallas_call | solution.py:134
  115.7 3.7 %all-to-all-start.3 = ((f32[16,8,2048]{2,1,0:T(8,128)}), f32[16,8,2048]{2,1,0:T(8,128)S(1)}, u32[]{:S(2)}, u32[]{:S(2)}) async-start(f32[16,8,2048]{2,1,0:T(8,128)} %bitcast.75), calls=%async_computation.3 | async-start | bytes 2097152 | tf_op jit(solution)/shard_map/all_to_all | solution.py:303
  119.5 15.5 %all-to-all-done.3 = f32[16,8,2048]{2,1,0:T(8,128)S(1)} async-done(((f32[16,8,2048]{2,1,0:T(8,128)}), f32[16,8,2048]{2,1,0:T(8,128)S(1)}, u32[]{:S(2)}, u32[]{:S(2)}) %all-to-all-start.3) | async-done | bytes 1048608 | tf_op jit(solution)/shard_map/all_to_all | solution.py:303
  136.4 9.0 %all-to-all-start.4 = ((bf16[128,2,2176]{2,1,0:T(2,128)(2,1)}), bf16[128,2,2176]{2,1,0:T(2,128)(2,1)}, u32[]{:S(2)}, u32[]{:S(2)}) async-start(bf16[128,2,2176]{2,1,0:T(2,128)(2,1)} %emb.5), calls=%async_computation.4 | async-start | bytes 2228224 | tf_op jit(solution)/shard_map/all_to_all | solution.py:308
  147.4 16.9 %all-to-all-done.4 = bf16[128,2,2176]{2,1,0:T(2,128)(2,1)} async-done(((bf16[128,2,2176]{2,1,0:T(2,128)(2,1)}), bf16[128,2,2176]{2,1,0:T(2,128)(2,1)}, u32[]{:S(2)}, u32[]{:S(2)}) %all-to-all-start.4) | async-done | bytes 1114144 | tf_op jit(solution)/shard_map/all_to_all | solution.py:308
  165.9 6.2 %match.5 = (f32[1,256]{1,0:T(1,128)S(1)}, f32[8,2048]{1,0:T(8,128)S(1)}, f32[1,128]{1,0:T(1,128)S(1)}) custom-call(s32[1]{0:T(128)} %bitcast.34.mp_ref, bf16[256,2176]{1,0:T(8,128)(2,1)S(1)} %reshape.208.rows_ref, bf16[2048,2048]{1,0:T(8,128)(2,1)} %bank_ref.1, f32[2048,1]{1,0:T(8,128)} %copy.69.key_ref), custom_call_target="tpu_custom_call" | custom-call | tf_op jit(solution)/shard_map/match/pallas_call | solution.py:201
  174.2 4.9 %all-to-all-start.5 = ((f32[128,1,2]{2,1,0:T(1,128)}), f32[128,1,2]{2,1,0:T(1,128)S(1)}, u32[]{:S(2)}, u32[]{:S(2)}) async-start(f32[128,1,2]{2,1,0:T(1,128)} %bitcast.37), calls=%async_computation.5 | async-start | bytes 131072 | tf_op jit(solution)/shard_map/all_to_all | solution.py:310
  179.8 9.1 %all-to-all-done.5 = f32[128,1,2]{2,1,0:T(1,128)S(1)} async-done(((f32[128,1,2]{2,1,0:T(1,128)}), f32[128,1,2]{2,1,0:T(1,128)S(1)}, u32[]{:S(2)}, u32[]{:S(2)}) %all-to-all-start.5) | async-done | bytes 1056 | tf_op jit(solution)/shard_map/all_to_all | solution.py:310
  (98 shorter events, 30.3 us)
Async XLA Ops:
  0.6 5.7 %copy-start = (bf16[256,2048]{1,0:T(8,128)(2,1)S(1)}, bf16[256,2048]{1,0:T(8,128)(2,1)}, u32[]{:S(2)}) copy-start(bf16[256,2048]{1,0:T(8,128)(2,1)} %h_ref) | copy-start | bytes 3145732
  0.6 5.7 %copy-start.2 = (s32[8]{0:T(128)S(1)}, s32[8]{0:T(128)}, u32[]{:S(2)}) copy-start(s32[8]{0:T(128)} %len_ref.1) | copy-start | bytes 100
  2.6 11.6 %collective-permute-start = (bf16[688,256]{1,0:T(8,128)(2,1)}, bf16[688,256]{1,0:T(8,128)(2,1)S(1)}, u32[]{:S(2)}, u32[]{:S(2)}) collective-permute-start(bf16[688,256]{1,0:T(8,128)(2,1)} %pad_maximum_fusion.2), channel_id=1, source_target_pairs={{2,0},{3,1},{0,2},{1,3},{6,4},{7,5},{4,6},{5,7},{10,8},{11,9},{8,1... | collective-permute-start | bytes 1056776 | tf_op jit(solution)/shard_map/ppermute | solution.py:25
  15.4 10.4 %copy-start.13 = (s32[128]{0:T(128)S(1)}, s32[128]{0:T(128)}, u32[]{:S(2)}) copy-start(s32[128]{0:T(128)} %param.24) | copy-start | bytes 1540
  15.4 10.4 %copy-start.14 = (s32[8]{0:T(128)S(1)}, s32[8]{0:T(128)}, u32[]{:S(2)}) copy-start(s32[8]{0:T(128)} %param.22) | copy-start | bytes 100
  15.4 10.6 %copy-start.12 = (s32[8]{0:T(128)S(1)}, s32[8]{0:T(128)}, u32[]{:S(2)}) copy-start(s32[8]{0:T(128)} %param.23) | copy-start | bytes 100
  15.4 31.5 %all-to-all-start.2 = ((bf16[4,688,256]{2,1,0:T(8,128)(2,1)}), bf16[4,688,256]{2,1,0:T(8,128)(2,1)}, u32[]{:S(2)}, u32[]{:S(2)}) async-start(bf16[4,688,256]{2,1,0:T(8,128)(2,1)} %broadcast_in_dim.139), calls=%async_computation.2 | async-start | bytes 2818048 | tf_op jit(solution)/shard_map/all_to_all | solution.py:276
  20.6 35.5 %copy-start.8 = (s32[2048]{0:T(1024)S(1)}, s32[2048]{0:T(1024)}, u32[]{:S(2)}) copy-start(s32[2048]{0:T(1024)} %param.27) | copy-start | bytes 24580
  20.6 35.5 %copy-start.9 = (s32[2048]{0:T(1024)S(1)}, s32[2048]{0:T(1024)}, u32[]{:S(2)}) copy-start(s32[2048]{0:T(1024)} %param.26) | copy-start | bytes 24580
  20.6 23.1 %collective-permute-start.3 = (bf16[256,2048]{1,0:T(8,128)(2,1)S(1)}, bf16[256,2048]{1,0:T(8,128)(2,1)S(1)}, u32[]{:S(2)}, u32[]{:S(2)}) collective-permute-start(bf16[256,2048]{1,0:T(8,128)(2,1)S(1)} %get-tuple-element.212.refs_0_), channel_id=1, source_target_pairs={{4,0},{5,1},{6,2},{7,3},{8,4},{9,5},{10,6},{11,7},{12,8},{13,9},{1... | collective-permute-start | bytes 3145736 | tf_op jit(solution)/shard_map/ppermute | solution.py:20
  23.1 23.9 %collective-permute-start.4 = (bf16[256,2048]{1,0:T(8,128)(2,1)S(1)}, bf16[256,2048]{1,0:T(8,128)(2,1)S(1)}, u32[]{:S(2)}, u32[]{:S(2)}) collective-permute-start(bf16[256,2048]{1,0:T(8,128)(2,1)S(1)} %get-tuple-element.212.refs_0_), channel_id=1, source_target_pairs={{12,0},{13,1},{14,2},{15,3},{0,4},{1,5},{2,6},{3,7},{4,8},{5,9},{6... | collective-permute-start | bytes 3145736 | tf_op jit(solution)/shard_map/ppermute | solution.py:20
  23.1 55.4 %collective-permute-start.1 = (bf16[688,1024]{1,0:T(8,128)(2,1)}, bf16[688,1024]{1,0:T(8,128)(2,1)}, u32[]{:S(2)}, u32[]{:S(2)}) collective-permute-start(bf16[688,1024]{1,0:T(8,128)(2,1)} %pad_maximum_fusion.1), channel_id=1, source_target_pairs={{1,0},{2,1},{3,2},{0,3},{5,4},{6,5},{7,6},{4,7},{9,8},{10,9},{11,1... | collective-permute-start | bytes 4227080 | tf_op jit(solution)/shard_map/ppermute | solution.py:25
  25.8 52.7 %collective-permute-start.2 = (bf16[688,1024]{1,0:T(8,128)(2,1)}, bf16[688,1024]{1,0:T(8,128)(2,1)}, u32[]{:S(2)}, u32[]{:S(2)}) collective-permute-start(bf16[688,1024]{1,0:T(8,128)(2,1)} %pad_maximum_fusion.1), channel_id=1, source_target_pairs={{3,0},{0,1},{1,2},{2,3},{7,4},{4,5},{5,6},{6,7},{11,8},{8,9},{9,10... | collective-permute-start | bytes 4227080 | tf_op jit(solution)/shard_map/ppermute | solution.py:25
  46.9 15.5 %collective-permute-start.7 = (bf16[4,688,256]{2,1,0:T(8,128)(2,1)}, bf16[4,688,256]{2,1,0:T(8,128)(2,1)}, u32[]{:S(2)}, u32[]{:S(2)}) collective-permute-start(bf16[4,688,256]{2,1,0:T(8,128)(2,1)} %all-to-all-done.2.refs_5_), channel_id=1, source_target_pairs={{16,0},{0,16},{48,32},{32,48},{80,64},{64,80},{112,96},{96,112},{1... | collective-permute-start | bytes 4227080 | tf_op jit(solution)/shard_map/ppermute | solution.py:29
  52.9 13.7 %collective-permute-start.5 = (bf16[128,2048]{1,0:T(8,128)(2,1)}, bf16[128,2048]{1,0:T(8,128)(2,1)}, u32[]{:S(2)}, u32[]{:S(2)}) collective-permute-start(bf16[128,2048]{1,0:T(8,128)(2,1)} %slice.27), channel_id=1, source_target_pairs={{4,0},{5,1},{6,2},{7,3},{8,4},{9,5},{10,6},{11,7},{12,8},{13,9},{1... | collective-permute-start | bytes 1572872 | tf_op jit(solution)/shard_map/ppermute | solution.py:20
  53.8 14.6 %collective-permute-start.6 = (bf16[128,2048]{1,0:T(8,128)(2,1)}, bf16[128,2048]{1,0:T(8,128)(2,1)}, u32[]{:S(2)}, u32[]{:S(2)}) collective-permute-start(bf16[128,2048]{1,0:T(8,128)(2,1)} %slice.28), channel_id=1, source_target_pairs={{12,0},{13,1},{14,2},{15,3},{0,4},{1,5},{2,6},{3,7},{4,8},{5,9},{6... | collective-permute-start | bytes 1572872 | tf_op jit(solution)/shard_map/ppermute | solution.py:20
  78.5 4.6 %collective-permute-start.8 = (bf16[688,1024]{1,0:T(8,128)(2,1)}, bf16[688,1024]{1,0:T(8,128)(2,1)S(1)}, u32[]{:S(2)}, u32[]{:S(2)}) collective-permute-start(bf16[688,1024]{1,0:T(8,128)(2,1)} %collective-permute-done.1.refs_5_), channel_id=1, source_target_pairs={{16,0},{0,16},{48,32},{32,48},{80,64},{64,80},{112,96},{96,112},{1... | collective-permute-start | bytes 4227080 | tf_op jit(solution)/shard_map/ppermute | solution.py:29
  79.8 5.0 %collective-permute-start.9 = (bf16[688,1024]{1,0:T(8,128)(2,1)}, bf16[688,1024]{1,0:T(8,128)(2,1)S(1)}, u32[]{:S(2)}, u32[]{:S(2)}) collective-permute-start(bf16[688,1024]{1,0:T(8,128)(2,1)} %collective-permute-done.2.refs_7_), channel_id=1, source_target_pairs={{16,0},{0,16},{48,32},{32,48},{80,64},{64,80},{112,96},{96,112},{1... | collective-permute-start | bytes 4227080 | tf_op jit(solution)/shard_map/ppermute | solution.py:29
  80.1 31.2 %collective-permute-start.11 = (f32[32,344]{1,0:T(8,128)S(1)}, f32[32,344]{1,0:T(8,128)S(1)}, u32[]{:S(2)}, u32[]{:S(2)}) collective-permute-start(f32[32,344]{1,0:T(8,128)S(1)} %ffn_far.1), channel_id=1, source_target_pairs={{2,0},{3,1},{0,2},{1,3},{6,4},{7,5},{4,6},{5,7},{10,8},{11,9},{8,1... | collective-permute-start | bytes 132104 | tf_op jit(solution)/shard_map/ppermute | solution.py:25
  103.4 8.0 %collective-permute-start.10 = (f32[32,344]{1,0:T(8,128)S(1)}, f32[32,344]{1,0:T(8,128)S(1)}, u32[]{:S(2)}, u32[]{:S(2)}) collective-permute-start(f32[32,344]{1,0:T(8,128)S(1)} %get-tuple-element.225), channel_id=1, source_target_pairs={{3,0},{0,1},{1,2},{2,3},{7,4},{4,5},{5,6},{6,7},{11,8},{8,9},{9,10... | collective-permute-start | bytes 132104 | tf_op jit(solution)/shard_map/ppermute | solution.py:25
  104.7 6.7 %collective-permute-start.12 = (f32[32,344]{1,0:T(8,128)S(1)}, f32[32,344]{1,0:T(8,128)S(1)}, u32[]{:S(2)}, u32[]{:S(2)}) collective-permute-start(f32[32,344]{1,0:T(8,128)S(1)} %get-tuple-element.227), channel_id=1, source_target_pairs={{1,0},{2,1},{3,2},{0,3},{5,4},{6,5},{7,6},{4,7},{9,8},{10,9},{11,1... | collective-permute-start | bytes 132104 | tf_op jit(solution)/shard_map/ppermute | solution.py:25
  115.7 19.3 %all-to-all-start.3 = ((f32[16,8,2048]{2,1,0:T(8,128)}), f32[16,8,2048]{2,1,0:T(8,128)S(1)}, u32[]{:S(2)}, u32[]{:S(2)}) async-start(f32[16,8,2048]{2,1,0:T(8,128)} %bitcast.75), calls=%async_computation.3 | async-start | bytes 2097152 | tf_op jit(solution)/shard_map/all_to_all | solution.py:303
  136.4 28.0 %all-to-all-start.4 = ((bf16[128,2,2176]{2,1,0:T(2,128)(2,1)}), bf16[128,2,2176]{2,1,0:T(2,128)(2,1)}, u32[]{:S(2)}, u32[]{:S(2)}) async-start(bf16[128,2,2176]{2,1,0:T(2,128)(2,1)} %emb.5), calls=%async_computation.4 | async-start | bytes 2228224 | tf_op jit(solution)/shard_map/all_to_all | solution.py:308
  174.2 14.7 %all-to-all-start.5 = ((f32[128,1,2]{2,1,0:T(1,128)}), f32[128,1,2]{2,1,0:T(1,128)S(1)}, u32[]{:S(2)}, u32[]{:S(2)}) async-start(f32[128,1,2]{2,1,0:T(1,128)} %bitcast.37), calls=%async_computation.5 | async-start | bytes 131072 | tf_op jit(solution)/shard_map/all_to_all | solution.py:310
  (7 other events, 10.6 us)

commit v4 on v3

--- a/solution.py
+++ b/solution.py
@@ -11,7 +11,6 @@
 NX, NY, NZ, NC = 4, 4, 4, 2
 ORDERS = 1 << 20
 BF, F32, I32 = jnp.bfloat16, jnp.float32, jnp.int32
-VMEM = pltpu.CompilerParams(vmem_limit_bytes=56 * 1024 * 1024)
 NT = (((1,), (1,)), ((), ()))
 
 
@@ -23,6 +22,10 @@
 def from_y(v, k):
     perm = [(x * NY + (y + k) % NY, x * NY + y) for x in range(NX) for y in range(NY)]
     return lax.ppermute(v, "mp", perm)
+
+
+def from_z(v, other):
+    return lax.ppermute(v, "dp", [(other[z] * NC + c, z * NC + c) for z in range(NZ) for c in range(NC)])
 
 
 def from_core(v):
@@ -63,55 +66,76 @@
     )(lengths, hidden, gain[None, :])
 
 
-def ffn_kernel(slice_parts, n_tok, n_old, file_len, off_ref, *refs):
+def ffn_kernel(plan, n_tok, file_len, off_ref, *refs):
+    n_parts = sum(len(p) for p, _ in plan)
+    n_old = sum(1 for _, first in plan if first)
     toks, refs = refs[:n_tok], refs[n_tok:]
-    n_parts = sum(slice_parts)
     parts, refs = refs[:n_parts], refs[n_parts:]
-    olds, refs = refs[:n_old], refs[n_old:]
-    outs, bufs = refs[:len(slice_parts)], refs[len(slice_parts):]
-    at = 0
-    for s, count in enumerate(slice_parts):
-        mine = parts[at:at + count]
-        cols = mine[0].shape[-1]
-        offs = [pl.multiple_of(off_ref[at + p], 128) for p in range(count)]
-        at += count
-        hid = mine[0].shape[-2] // 2
-        row = 0
-        if n_old:
-            row = olds[s].shape[0]
-            outs[s][:row, :] = olds[s][...]
-        if len(mine[0].shape) == 3:
-            for part, off in zip(mine, offs):
-                for q in range(part.shape[0]):
-                    bufs[0][:, pl.ds(off + q * count * cols, cols)] = part[q]
-            mine, offs, cols = [bufs[0]], [0], bufs[0].shape[1]
-        for t in toks:
-            both = None
-            for w, off in zip(mine, offs):
-                x = t[...] if len(mine) == 1 else t[:, pl.ds(off, cols)]
-                term = lax.dot_general(w[...], x, NT, preferred_element_type=F32)
-                both = term if both is None else both + term
-            gate = both[:hid]
-            units = (0.5 * gate * (1.0 + jnp.tanh(0.5 * gate)) * both[hid:]).astype(BF)
-            n = t.shape[0] // file_len
-            ones = block_ones(n, file_len, BF)
-            outs[s][row:row + n, :] = lax.dot_general(ones, units, NT, preferred_element_type=F32)
-            row += n
-
-
-def ffn(toks, slices, offs, file_len, name, olds=()):
+    olds, refs = list(refs[:n_old]), refs[n_old:]
+    outs, refs = refs[:len(plan)], refs[len(plan):]
+    t_buf, w_buf, t_sem, w_sem = refs
+    hid = w_buf.shape[1] // 2
+
+    def load_tokens():
+        row, done = 0, []
+        for t in range(n_tok):
+            rows = toks[t].shape[0]
+            done.append(pltpu.make_async_copy(toks[t], t_buf.at[pl.ds(row, rows)], t_sem.at[t]))
+            done[-1].start()
+            row += rows
+        return done
+
+    at, sem, waits = 0, 0, []
+    for s, (pieces, _) in enumerate(plan):
+        mine = []
+        for p, n in enumerate(pieces):
+            ref = parts[at + p]
+            cols = ref.shape[-1]
+            for q in range(n):
+                start = pl.multiple_of(off_ref[sem], 128)
+                src = ref.at[q] if len(ref.shape) == 3 else ref
+                mine.append(pltpu.make_async_copy(src, w_buf.at[s, :, pl.ds(start, cols)], w_sem.at[sem]))
+                mine[-1].start()
+                sem += 1
+        at += len(pieces)
+        waits.append(mine)
+        if s == 0:
+            t_waits = load_tokens()
+    for cp in t_waits:
+        cp.wait()
+    for s, (_, first) in enumerate(plan):
+        for cp in waits[s]:
+            cp.wait()
+        rows = t_buf.shape[0] - first
+        both = lax.dot_general(w_buf[s], t_buf[first:, :], NT, preferred_element_type=F32)
+        gate = both[:hid]
+        units = (0.5 * gate * (1.0 + jnp.tanh(0.5 * gate)) * both[hid:]).astype(BF)
+        ones = block_ones(rows // file_len, file_len, BF)
+        new = lax.dot_general(ones, units, NT, preferred_element_type=F32)
+        if first:
+            outs[s][:first // file_len, :] = olds.pop(0)[...]
+        outs[s][first // file_len:, :] = new
+
+
+def ffn(toks, slices, firsts, offs, file_len, name, olds=()):
     width = toks[0].shape[1]
-    n_files = sum(t.shape[0] for t in toks) // file_len + (olds[0].shape[0] if olds else 0)
+    n_rows = sum(t.shape[0] for t in toks)
     rows = slices[0][0].shape[-2]
+    plan = tuple((tuple(p.shape[0] if p.ndim == 3 else 1 for p in s), f) for s, f in zip(slices, firsts))
     flat = [p for s in slices for p in s]
-    vm = pl.BlockSpec(memory_space=pltpu.VMEM)
-    return pl.pallas_call(
-        functools.partial(ffn_kernel, tuple(len(s) for s in slices), len(toks), len(olds), file_len),
-        in_specs=[pl.BlockSpec(memory_space=pltpu.SMEM)] + [vm] * (len(toks) + len(flat) + len(olds)),
+    vm, hbm = pl.BlockSpec(memory_space=pltpu.VMEM), pl.BlockSpec(memory_space=pl.ANY)
+    return pl.pallas_call(
+        functools.partial(ffn_kernel, plan, len(toks), file_len),
+        in_specs=[pl.BlockSpec(memory_space=pltpu.SMEM)] + [hbm] * (len(toks) + len(flat)) + [vm] * len(olds),
         out_specs=tuple(vm for _ in slices),
-        out_shape=tuple(jax.ShapeDtypeStruct((n_files, rows // 2), F32) for _ in slices),
-        scratch_shapes=[pltpu.VMEM((rows, width), BF)] if max(p.ndim for p in flat) > 2 else [],
-        compiler_params=pltpu.CompilerParams(vmem_limit_bytes=24 * 1024 * 1024),
+        out_shape=tuple(jax.ShapeDtypeStruct((n_rows // file_len, rows // 2), F32) for _ in slices),
+        scratch_shapes=[
+            pltpu.VMEM((n_rows, width), BF),
+            pltpu.VMEM((len(slices), rows, width), BF),
+            pltpu.SemaphoreType.DMA((len(toks),)),
+            pltpu.SemaphoreType.DMA((sum(sum(p) for p, _ in plan),)),
+        ],
+        compiler_params=pltpu.CompilerParams(vmem_limit_bytes=(16 + 4 * len(slices)) * 1024 * 1024),
         name=name,
     )(offs, *toks, *flat, *olds)
 
@@ -137,7 +161,7 @@
         out_specs=vm,
         out_shape=jax.ShapeDtypeStruct((rows, w_down.shape[1]), F32),
         scratch_shapes=[pltpu.VMEM((rows, us[0].shape[1]), F32)],
-        compiler_params=VMEM,
+        compiler_params=pltpu.CompilerParams(vmem_limit_bytes=16 * 1024 * 1024),
         name="down",
     )(pos, *us, w_down)
 
@@ -168,9 +192,17 @@
     )(terms, pooled, lens, sel, meta)
 
 
-def match_kernel(mp_ref, rows_ref, bank_ref, key_ref, best_ref, sums_ref, about_ref):
+def match_kernel(mp_ref, rows_ref, bank_ref, key_ref, best_ref, sums_ref, about_ref, buf, sem):
     width = bank_ref.shape[1]
+    n_blocks = sem.shape[0]
+    block = bank_ref.shape[0] // n_blocks
+    copies = []
+    for i in range(n_blocks):
+        at = pl.ds(i * block, block)
+        copies.append(pltpu.make_async_copy(bank_ref.at[at], buf.at[at], sem.at[i]))
+        copies[-1].start()
     rows = rows_ref[:, :width]
+    n = rows.shape[0]
     pick = lax.broadcasted_iota(I32, (8, 128), 0) == lax.broadcasted_iota(I32, (8, 128), 1)
     digits = lax.dot_general(
         jnp.where(pick, 1.0, 0.0).astype(BF), rows_ref[:, width:], NT, preferred_element_type=F32
@@ -178,21 +210,25 @@
     low = digits[0:1] * 65536.0 + digits[1:2] * 256.0 + digits[2:3]
     high = digits[3:4] * 65536.0 + digits[4:5] * 256.0 + digits[5:6]
     mine = digits[6:7] == (mp_ref[0] + 1).astype(F32)
-    member = jnp.broadcast_to(jnp.where(mine, 1.0, 0.0), (8, rows.shape[0])).astype(BF)
-    best = jnp.full((1, rows.shape[0]), -1.0, F32)
-    block = 512
-    for i in range(bank_ref.shape[0] // block):
+    member = jnp.broadcast_to(jnp.where(mine, 1.0, 0.0), (8, n)).astype(BF)
+    sums_ref[...] = jnp.dot(member, rows, preferred_element_type=F32)
+    count = jnp.sum(jnp.where(mine, 1.0, 0.0), axis=1, keepdims=True)
+    most = jnp.max(digits[7:8], axis=1, keepdims=True)
+    about_ref[...] = jnp.where(lax.broadcasted_iota(I32, (1, 128), 1) == 0, count, most)
+    best = jnp.full((1, n), -1.0, F32)
+    for i in range(n_blocks):
+        copies[i].wait()
         at = slice(i * block, (i + 1) * block)
-        sims = lax.dot_general(bank_ref[at, :], rows, NT, preferred_element_type=F32)
+        sims = lax.dot_general(buf[at, :], rows, NT, preferred_element_type=F32)
         key = key_ref[at, :]
         valid = (key >= low) & (key < high)
         best = jnp.maximum(best, jnp.max(jnp.where(valid, sims, -1.0), axis=0, keepdims=True))
-    best_ref[...] = best
-    sums_ref[...] = jnp.dot(member, rows, preferred_element_type=F32)
-    count = jnp.sum(jnp.where(mine, 1.0, 0.0), axis=1, keepdims=True)
-    most = jnp.max(digits[7:8], axis=1, keepdims=True)
-    lane = lax.broadcasted_iota(I32, (1, 128), 1)
-    about_ref[...] = jnp.where(lane == 0, count, most)
+    row = lax.broadcasted_iota(I32, (n // 2, n), 0)
+    lane = lax.broadcasted_iota(I32, (n // 2, n), 1)
+    best = jnp.broadcast_to(best, (n // 2, n))
+    pair = [jnp.max(jnp.where(lane == 2 * row + i, best, -1.0), axis=1, keepdims=True) for i in (0, 1)]
+    out_lane = lax.broadcasted_iota(I32, (n // 2, 128), 1)
+    best_ref[:, 0, :] = jnp.where(out_lane == 0, pair[0], pair[1])
 
 
 def match(rows, mp, bank, key):
@@ -200,13 +236,14 @@
     vm = pl.BlockSpec(memory_space=pltpu.VMEM)
     return pl.pallas_call(
         match_kernel,
-        in_specs=[pl.BlockSpec(memory_space=pltpu.SMEM)] + [vm] * 3,
+        in_specs=[pl.BlockSpec(memory_space=pltpu.SMEM), vm, pl.BlockSpec(memory_space=pl.ANY), vm],
         out_specs=(vm, vm, vm),
         out_shape=(
-            jax.ShapeDtypeStruct((1, n), F32),
+            jax.ShapeDtypeStruct((n // 2, 1, 128), F32),
             jax.ShapeDtypeStruct((8, bank.shape[1]), F32),
             jax.ShapeDtypeStruct((1, 128), F32),
         ),
+        scratch_shapes=[pltpu.VMEM(bank.shape, BF), pltpu.SemaphoreType.DMA((8,))],
         compiler_params=pltpu.CompilerParams(vmem_limit_bytes=24 * 1024 * 1024),
         name="match",
     )(mp[None], rows, bank, key)
@@ -272,14 +309,16 @@
     t1, t3 = from_x(normed, 1), from_x(normed, 3)
     h1, h3 = from_y(w_h, 1), from_y(w_h, 3)
     e0, normed = tie((e0, normed))
-    column = [[z_ * NC + c_ for z_ in range(NZ)] for c_ in range(NC)]
-    es = lax.all_to_all(jnp.broadcast_to(e0[None], (NZ,) + e0.shape), "dp", 0, 0, axis_index_groups=column, tiled=True)
-    es, t1, t3 = tie((es, t1, t3))
+    e1 = from_z(e0, (1, 0, 3, 2))
+    e01 = jnp.stack([e0, e1])
+    es = jnp.concatenate([e01, from_z(e01, (3, 2, 1, 0))])
+    t1, t3 = tie((t1, t3))
     es = [es, from_core(es)]
     t2a, t2b = from_x(t1[:tok // 2], 1), from_x(t3[tok // 2:], 3)
     toks, last = [normed, t1, t3], [t2a, t2b]
 
-    e_off = jnp.stack([c * eighth, (1 - c) * eighth]).astype(I32)
+    held = [z, z ^ 1, 3 - z, (3 - z) ^ 1]
+    e_off = jnp.stack([(q * NC + k) * eighth for k in (c, 1 - c) for q in held]).astype(I32)
     h_off = jnp.stack([c * half, (1 - c) * half] * 2).astype(I32)
     pos = jnp.stack(
         [(((x + j) % NX) * NY + (y - k) % NY) * files for k in range(NY) for j in (0, 1, 3, 2)]
@@ -290,14 +329,22 @@
     toks[0] = normed
 
     zero = jnp.zeros((1,), I32)
-    (u0,) = ffn(toks, [[w_own]], zero, file_len, "ffn_own")
+    (u0,) = ffn(toks, [[w_own]], (0,), zero, file_len, "ffn_own")
     u0, es = tie((u0, es))
-    (u2,) = ffn(toks + last, [es], e_off, file_len, "ffn_far")
+    (u2,) = ffn(toks, [es], (0,), e_off, file_len, "ffn_far")
     h1, h3, u2, last = tie((h1, h3, u2, last))
-    (u0,) = ffn(last, [[w_own]], zero, file_len, "ffn_last", (u0,))
     g1, g3 = from_core(h1), from_core(h3)
+    first = sum(t.shape[0] for t in toks)
+    u2, u0, u1, u3 = ffn(
+        toks + last,
+        [es, [w_own], [h1, g1], [h3, g3]],
+        (first, first, 0, 0),
+        jnp.concatenate([e_off, zero, h_off]),
+        file_len,
+        "ffn_last",
+        (u2, u0),
+    )
     r2 = from_y(u2, NY - 2)
-    u1, u3 = ffn(toks + last, [[h1, g1], [h3, g3]], h_off, file_len, "ffn_near")
     r1, r3 = from_y(u1, NY - 1), from_y(u3, NY - 3)
     terms = down([u0, r1, r2, r3], w_down, pos, files)
     terms = lax.all_to_all(terms, "mp", 0, 0, tiled=True)
@@ -307,8 +354,8 @@
         rows = emb_to_owners(terms, pooled_in, lens, sel, meta, files, n_mp)
         rows = lax.all_to_all(rows, ALL, 0, 0, tiled=True)
         top, new, about = match(rows.reshape(-1, rows.shape[2]), mp, bank, bank_key)
-        back = lax.all_to_all(top.reshape(-1, 2), ALL, 0, 0, tiled=True)
-        back = jnp.max(back.reshape(n_dp, n_mp, 2), axis=1)
+        back = lax.all_to_all(top, ALL, 0, 0, tiled=True)
+        back = jnp.max(back.reshape(n_dp, n_mp, -1), axis=1)[:, :2]
         best = jnp.maximum(best, jnp.max(jnp.where(here, back[:, :, None], -1.0), axis=(0, 1)))
         return about[0, 1], (best, sums + new[:1], counts + about[0, 0])
 

time: 191 us -> 173 us (0.906)
  Pallas kernels: 49.3 us -> 37.7 us
  waiting for transfers between devices: 73.3 us -> 67.4 us
  local copies, waits for them, and re-layouts: 14.7 us -> 9.42 us
  other arithmetic: 6.7 us -> 9.93 us
    ppermute x4, waiting for transfers between devices: 26.7 us -> 1.98 us  [from_x(): return lax.ppermute(v, 'mp', perm)]
    pallas_call x4 -> x3, Pallas kernels: 37.4 us -> 22.7 us  [ffn(): pl.pallas_call(functools.partial(ffn_kernel, plan, len(toks), file_len),...]
    ppermute x0 -> x2, waiting for transfers between devices: none -> 13.3 us  [from_z(): lax.ppermute(v, 'dp', [(other[z] * NC + c, z * NC + c) for z in range(NZ)...]
    ppermute x0 -> x2, starting transfers between devices: none -> 5.2 us  [from_z(): lax.ppermute(v, 'dp', [(other[z] * NC + c, z * NC + c) for z in range(NZ)...]
    all_to_all x2 -> x1, starting transfers between devices: 10.1 us -> 4.96 us  [one_round(): back = lax.all_to_all(top, ALL, 0, 0, tiled=True)]
    ppermute x6, waiting for transfers between devices: 3.22 us -> 6.41 us  [from_y(): return lax.ppermute(v, 'mp', perm)]
    ppermute x3, waiting for transfers between devices: 1.83 us -> 4.95 us  [from_core(): return lax.ppermute(v, 'dp', [(d ^ 1, d) for d in range(NZ * NC)])]
    pallas_call x1, Pallas kernels: 6.2 us -> 9.17 us  [match(): pl.pallas_call(match_kernel, in_specs=[pl.BlockSpec(memory_space=pltpu.SM...]
  transfers between devices with their start and end apart: 17 -> 18, of which waited for: 9 -> 11; matrix products, arithmetic and copies ran while one was open for 6% -> 9% of each run, Pallas kernels for 20% -> 7%
where the time goes in v4:
time: 173 us; the launch traced here: 172 us
  waiting for transfers between devices  67.4 us (39%)
  starting transfers between devices  43.7 us (25%)
  Pallas kernels  37.7 us (22%)
  other arithmetic  9.93 us (6%)
  local copies, waits for them, and re-layouts  9.42 us (5%)
  between operations  2.98 us (2%)
    pallas_call x3, Pallas kernels, ffn(): pl.pallas_call(functools.partial(ffn_kernel, plan, len(toks), file_len),...  22.7 us
    all_to_all x1, waiting for transfers between devices, one_round(): rows = lax.all_to_all(rows, ALL, 0, 0, tiled=True)  16.9 us
    all_to_all x1, waiting for transfers between devices, on_device(): terms = lax.all_to_all(terms, 'mp', 0, 0, tiled=True)  14.7 us
    ppermute x2, waiting for transfers between devices, from_z(): lax.ppermute(v, 'dp', [(other[z] * NC + c, z * NC + c) for z in range(NZ)...  13.3 us
    ppermute x6, starting transfers between devices, from_y(): return lax.ppermute(v, 'mp', perm)  11.6 us
    pallas_call x1, Pallas kernels, match(): pl.pallas_call(match_kernel, in_specs=[pl.BlockSpec(memory_space=pltpu.SM...  9.17 us
    all_to_all x1, starting transfers between devices, one_round(): rows = lax.all_to_all(rows, ALL, 0, 0, tiled=True)  9.14 us
    all_to_all x1, waiting for transfers between devices, one_round(): back = lax.all_to_all(top, ALL, 0, 0, tiled=True)  9.12 us
  transfers between devices with their start and end apart: 18, of which 11 were waited for; matrix products, arithmetic and copies ran while one was open for 9% of the time, Pallas kernels for 7%

profile of v4, /device:TPU:1, one launch (start us, length us, event | category | flops | bytes accessed | tf_op | source)
XLA Modules:
  0.0 171.8 jit_solution(14638270616648044539)
XLA Ops:
  1.9 3.8 %collective-permute-start = (bf16[688,256]{1,0:T(8,128)(2,1)S(1)}, bf16[688,256]{1,0:T(8,128)(2,1)}, u32[]{:S(2)}, u32[]{:S(2)}) collective-permute-start(bf16[688,256]{1,0:T(8,128)(2,1)S(1)} %pad_maximum_fusion.4), channel_id=1, source_target_pairs={{2,0},{3,1},{0,2},{1,3},{6,4},{7,5},{4,6},{5,7},{10,8},{11,9},{8,1... | collective-permute-start | bytes 1056776 | tf_op jit(solution)/shard_map/ppermute | solution.py:24
  5.8 2.1 %prep.1 = (bf16[256,2048]{1,0:T(8,128)(2,1)}, f32[8,2048]{1,0:T(8,128)}) custom-call(s32[8]{0:T(128)S(1)} %copy-done.2, bf16[256,2048]{1,0:T(8,128)(2,1)S(1)} %copy-done.1, bf16[1,2048]{1,0:T(2,128)(2,1)S(1)} %broadcast_in_dim.124.gain_ref), custom_call_target="tpu_custom_call" | custom-call | tf_op jit(solution)/shard_map/prep/pallas_call | solution.py:59
  9.3 4.2 %collective-permute-done = bf16[688,256]{1,0:T(8,128)(2,1)} collective-permute-done((bf16[688,256]{1,0:T(8,128)(2,1)S(1)}, bf16[688,256]{1,0:T(8,128)(2,1)}, u32[]{:S(2)}, u32[]{:S(2)}) %collective-permute-start) | collective-permute-done | bytes 352288 | tf_op jit(solution)/shard_map/ppermute | solution.py:24
  15.2 2.5 %collective-permute-start.1 = (bf16[256,2048]{1,0:T(8,128)(2,1)}, bf16[256,2048]{1,0:T(8,128)(2,1)S(1)}, u32[]{:S(2)}, u32[]{:S(2)}) collective-permute-start(bf16[256,2048]{1,0:T(8,128)(2,1)} %get-tuple-element.213.refs_0_), channel_id=1, source_target_pairs={{4,0},{5,1},{6,2},{7,3},{8,4},{9,5},{10,6},{11,7},{12,8},{13,9},{1... | collective-permute-start | bytes 3145736 | tf_op jit(solution)/shard_map/ppermute | solution.py:19
  17.6 2.7 %collective-permute-start.3 = (bf16[688,1024]{1,0:T(8,128)(2,1)}, bf16[688,1024]{1,0:T(8,128)(2,1)}, u32[]{:S(2)}, u32[]{:S(2)}) collective-permute-start(bf16[688,1024]{1,0:T(8,128)(2,1)} %pad_maximum_fusion.1), channel_id=1, source_target_pairs={{1,0},{2,1},{3,2},{0,3},{5,4},{6,5},{7,6},{4,7},{9,8},{10,9},{11,1... | collective-permute-start | bytes 4227080 | tf_op jit(solution)/shard_map/ppermute | solution.py:24
  23.5 3.5 %collective-permute-start.6 = (bf16[2,688,256]{2,1,0:T(8,128)(2,1)S(1)}, bf16[2,688,256]{2,1,0:T(8,128)(2,1)}, u32[]{:S(2)}, u32[]{:S(2)}) collective-permute-start(bf16[2,688,256]{2,1,0:T(8,128)(2,1)S(1)} %pad_maximum_fusion.3), channel_id=1, source_target_pairs={{96,0},{112,16},{64,32},{80,48},{32,64},{48,80},{0,96},{16,112},{9... | collective-permute-start | bytes 2113544 | tf_op jit(solution)/shard_map/ppermute | solution.py:28
  29.3 11.6 %collective-permute-done.6 = bf16[2,688,256]{2,1,0:T(8,128)(2,1)} collective-permute-done((bf16[2,688,256]{2,1,0:T(8,128)(2,1)S(1)}, bf16[2,688,256]{2,1,0:T(8,128)(2,1)}, u32[]{:S(2)}, u32[]{:S(2)}) %collective-permute-start.6) | collective-permute-done | bytes 704544 | tf_op jit(solution)/shard_map/ppermute | solution.py:28
  42.3 3.1 %collective-permute-start.7 = (bf16[4,688,256]{2,1,0:T(8,128)(2,1)S(1)}, bf16[4,688,256]{2,1,0:T(8,128)(2,1)}, u32[]{:S(2)}, u32[]{:S(2)}) collective-permute-start(bf16[4,688,256]{2,1,0:T(8,128)(2,1)S(1)} %pad_maximum_fusion.2.refs_3_.refs_5_), channel_id=1, source_target_pairs={{16,0},{0,16},{48,32},{32,48},{80,64},{64,80},{112,96},{96,112},{1... | collective-permute-start | bytes 4227080 | tf_op jit(solution)/shard_map/ppermute | solution.py:32
  49.5 2.4 %collective-permute-start.8 = (bf16[128,2048]{1,0:T(8,128)(2,1)}, bf16[128,2048]{1,0:T(8,128)(2,1)}, u32[]{:S(2)}, u32[]{:S(2)}) collective-permute-start(bf16[128,2048]{1,0:T(8,128)(2,1)} %slice.36), channel_id=1, source_target_pairs={{4,0},{5,1},{6,2},{7,3},{8,4},{9,5},{10,6},{11,7},{12,8},{13,9},{1... | collective-permute-start | bytes 1572872 | tf_op jit(solution)/shard_map/ppermute | solution.py:19
  53.8 2.1 %pad_maximum_fusion.refs_3_.refs_7_ = bf16[688,2048]{1,0:T(8,128)(2,1)S(1)} fusion(bf16[344,2048]{1,0:T(8,128)(2,1)} %bitcast.83, bf16[344,2048]{1,0:T(8,128)(2,1)} %bitcast.85), kind=kLoop, calls=%fused_computation.5 | loop fusion | flops 5636096 | bytes 5636096 | tf_op jit(solution)/shard_map/concatenate | solution.py:302
  55.9 4.4 %ffn_own.1.refs_13_ = f32[24,344]{1,0:T(8,128)S(1)} custom-call(s32[1]{0:T(128)} %constant.228.clone.1.off_ref, bf16[256,2048]{1,0:T(8,128)(2,1)} %get-tuple-element.213.refs_0_, bf16[256,2048]{1,0:T(8,128)(2,1)S(1)} %collective-permute-done.1.refs_1_, bf16[256,2048]{1,0:T(8,128)(2,1)S(1)} %collective-permute-done.2.refs_2_, ...), custom_call_target="tpu_custom_call" | custom-call | tf_op jit(solution)/shard_map/ffn_own/pallas_call | solution.py:127
  60.3 5.2 %ffn_far.1.refs_12_ = f32[24,344]{1,0:T(8,128)S(1)} custom-call(s32[8]{0:T(128)S(1)} %stack.120.off_ref, bf16[256,2048]{1,0:T(8,128)(2,1)} %get-tuple-element.213.refs_0_, bf16[256,2048]{1,0:T(8,128)(2,1)S(1)} %collective-permute-done.1.refs_1_, bf16[256,2048]{1,0:T(8,128)(2,1)S(1)} %collective-permute-done.2.refs_2_, ...), custom_call_target="tpu_custom_call" | custom-call | tf_op jit(solution)/shard_map/ffn_far/pallas_call | solution.py:127
  68.7 2.9 %collective-permute-done.10.refs_9_ = bf16[688,1024]{1,0:T(8,128)(2,1)S(1)} collective-permute-done((bf16[688,1024]{1,0:T(8,128)(2,1)}, bf16[688,1024]{1,0:T(8,128)(2,1)S(1)}, u32[]{:S(2)}, u32[]{:S(2)}) %collective-permute-start.10) | collective-permute-done | bytes 1409056 | tf_op jit(solution)/shard_map/ppermute | solution.py:32
  71.7 2.0 %collective-permute-done.11.refs_11_ = bf16[688,1024]{1,0:T(8,128)(2,1)S(1)} collective-permute-done((bf16[688,1024]{1,0:T(8,128)(2,1)}, bf16[688,1024]{1,0:T(8,128)(2,1)S(1)}, u32[]{:S(2)}, u32[]{:S(2)}) %collective-permute-start.11) | collective-permute-done | bytes 1409056 | tf_op jit(solution)/shard_map/ppermute | solution.py:32
  73.7 13.2 %ffn_last.1 = (f32[32,344]{1,0:T(8,128)S(1)}, f32[32,344]{1,0:T(8,128)S(1)}, f32[32,344]{1,0:T(8,128)S(1)}, f32[32,344]{1,0:T(8,128)S(1)}) custom-call(s32[13]{0:T(128)S(1)} %pad_add_fusion.1.off_ref, bf16[256,2048]{1,0:T(8,128)(2,1)} %get-tuple-element.213.refs_0_, bf16[256,2048]{1,0:T(8,128)(2,1)S(1)} %collective-permute-done.1.refs_1_, ...), custom_call_target="tpu_custom_call" | custom-call | tf_op jit(solution)/shard_map/ffn_last/pallas_call | solution.py:127
  88.2 2.6 %collective-permute-start.13 = (f32[32,344]{1,0:T(8,128)S(1)}, f32[32,344]{1,0:T(8,128)S(1)}, u32[]{:S(2)}, u32[]{:S(2)}) collective-permute-start(f32[32,344]{1,0:T(8,128)S(1)} %get-tuple-element.228), channel_id=1, source_target_pairs={{2,0},{3,1},{0,2},{1,3},{6,4},{7,5},{4,6},{5,7},{10,8},{11,9},{8,1... | collective-permute-start | bytes 132104 | tf_op jit(solution)/shard_map/ppermute | solution.py:24
  94.1 2.3 %down.1 = f32[128,2048]{1,0:T(8,128)} custom-call(s32[16]{0:T(128)S(1)} %stack.140.pos_ref, f32[32,344]{1,0:T(8,128)S(1)} %get-tuple-element.226.u0, f32[32,344]{1,0:T(8,128)S(1)} %collective-permute-done.12.u1, f32[32,344]{1,0:T(8,128)S(1)} %collective-permute-done.13.u2, f32[32,344]{1,0:T(8,128)S(1)} %collective-permute-done.14.u3, ...), custom_call_target="tpu_custom_call" | custom-call | tf_op jit(solution)/shard_map/down/pallas_call | solution.py:158
  96.3 3.8 %all-to-all-start.2 = ((f32[16,8,2048]{2,1,0:T(8,128)}), f32[16,8,2048]{2,1,0:T(8,128)S(1)}, u32[]{:S(2)}, u32[]{:S(2)}) async-start(f32[16,8,2048]{2,1,0:T(8,128)} %bitcast.42), calls=%async_computation.2 | async-start | bytes 2097152 | tf_op jit(solution)/shard_map/all_to_all | solution.py:350
  100.2 14.7 %all-to-all-done.2 = f32[16,8,2048]{2,1,0:T(8,128)S(1)} async-done(((f32[16,8,2048]{2,1,0:T(8,128)}), f32[16,8,2048]{2,1,0:T(8,128)S(1)}, u32[]{:S(2)}, u32[]{:S(2)}) %all-to-all-start.2) | async-done | bytes 1048608 | tf_op jit(solution)/shard_map/all_to_all | solution.py:350
  116.3 9.1 %all-to-all-start.3 = ((bf16[128,2,2176]{2,1,0:T(2,128)(2,1)}), bf16[128,2,2176]{2,1,0:T(2,128)(2,1)}, u32[]{:S(2)}, u32[]{:S(2)}) async-start(bf16[128,2,2176]{2,1,0:T(2,128)(2,1)} %emb.5), calls=%async_computation.3 | async-start | bytes 2228224 | tf_op jit(solution)/shard_map/all_to_all | solution.py:355
  127.4 16.9 %all-to-all-done.3 = bf16[128,2,2176]{2,1,0:T(2,128)(2,1)} async-done(((bf16[128,2,2176]{2,1,0:T(2,128)(2,1)}), bf16[128,2,2176]{2,1,0:T(2,128)(2,1)}, u32[]{:S(2)}, u32[]{:S(2)}) %all-to-all-start.3) | async-done | bytes 1114144 | tf_op jit(solution)/shard_map/all_to_all | solution.py:355
  145.9 9.2 %match.5 = (f32[128,1,128]{2,1,0:T(1,128)}, f32[8,2048]{1,0:T(8,128)S(1)}, f32[1,128]{1,0:T(1,128)S(1)}) custom-call(s32[1]{0:T(128)} %bitcast.39.mp_ref, bf16[256,2176]{1,0:T(8,128)(2,1)S(1)} %reshape.194.rows_ref, bf16[2048,2048]{1,0:T(8,128)(2,1)} %bank_ref.1, f32[2048,1]{1,0:T(8,128)} %copy.55.key_ref), custom_call_target="tpu_custom_call" | custom-call | tf_op jit(solution)/shard_map/match/pallas_call | solution.py:237
  155.1 5.0 %all-to-all-start.4 = ((f32[128,1,128]{2,1,0:T(1,128)}), f32[128,1,128]{2,1,0:T(1,128)S(1)}, u32[]{:S(2)}, u32[]{:S(2)}) async-start(f32[128,1,128]{2,1,0:T(1,128)} %get-tuple-element.235), calls=%async_computation.4 | async-start | bytes 131072 | tf_op jit(solution)/shard_map/all_to_all | solution.py:357
  160.6 9.1 %all-to-all-done.4 = f32[128,1,128]{2,1,0:T(1,128)S(1)} async-done(((f32[128,1,128]{2,1,0:T(1,128)}), f32[128,1,128]{2,1,0:T(1,128)S(1)}, u32[]{:S(2)}, u32[]{:S(2)}) %all-to-all-start.4) | async-done | bytes 65568 | tf_op jit(solution)/shard_map/all_to_all | solution.py:357
  (98 shorter events, 30.3 us)
Async XLA Ops:
  1.9 11.6 %collective-permute-start = (bf16[688,256]{1,0:T(8,128)(2,1)S(1)}, bf16[688,256]{1,0:T(8,128)(2,1)}, u32[]{:S(2)}, u32[]{:S(2)}) collective-permute-start(bf16[688,256]{1,0:T(8,128)(2,1)S(1)} %pad_maximum_fusion.4), channel_id=1, source_target_pairs={{2,0},{3,1},{0,2},{1,3},{6,4},{7,5},{4,6},{5,7},{10,8},{11,9},{8,1... | collective-permute-start | bytes 1056776 | tf_op jit(solution)/shard_map/ppermute | solution.py:24
  8.1 12.3 %copy-start.13 = (s32[128]{0:T(128)S(1)}, s32[128]{0:T(128)}, u32[]{:S(2)}) copy-start(s32[128]{0:T(128)} %param.24) | copy-start | bytes 1540
  8.1 12.3 %copy-start.14 = (s32[8]{0:T(128)S(1)}, s32[8]{0:T(128)}, u32[]{:S(2)}) copy-start(s32[8]{0:T(128)} %param.22) | copy-start | bytes 100
  9.3 17.8 %copy-start.11 = (s32[8]{0:T(128)S(1)}, s32[8]{0:T(128)}, u32[]{:S(2)}) copy-start(s32[8]{0:T(128)} %param.23) | copy-start | bytes 100
  13.5 8.8 %collective-permute-start.5 = (bf16[688,256]{1,0:T(8,128)(2,1)}, bf16[688,256]{1,0:T(8,128)(2,1)S(1)}, u32[]{:S(2)}, u32[]{:S(2)}) collective-permute-start(bf16[688,256]{1,0:T(8,128)(2,1)} %collective-permute-done), channel_id=1, source_target_pairs={{32,0},{48,16},{0,32},{16,48},{96,64},{112,80},{64,96},{80,112},{3... | collective-permute-start | bytes 1056776 | tf_op jit(solution)/shard_map/ppermute | solution.py:28
  15.2 33.4 %collective-permute-start.1 = (bf16[256,2048]{1,0:T(8,128)(2,1)}, bf16[256,2048]{1,0:T(8,128)(2,1)S(1)}, u32[]{:S(2)}, u32[]{:S(2)}) collective-permute-start(bf16[256,2048]{1,0:T(8,128)(2,1)} %get-tuple-element.213.refs_0_), channel_id=1, source_target_pairs={{4,0},{5,1},{6,2},{7,3},{8,4},{9,5},{10,6},{11,7},{12,8},{13,9},{1... | collective-permute-start | bytes 3145736 | tf_op jit(solution)/shard_map/ppermute | solution.py:19
  17.6 31.0 %collective-permute-start.2 = (bf16[256,2048]{1,0:T(8,128)(2,1)}, bf16[256,2048]{1,0:T(8,128)(2,1)S(1)}, u32[]{:S(2)}, u32[]{:S(2)}) collective-permute-start(bf16[256,2048]{1,0:T(8,128)(2,1)} %get-tuple-element.213.refs_0_), channel_id=1, source_target_pairs={{12,0},{13,1},{14,2},{15,3},{0,4},{1,5},{2,6},{3,7},{4,8},{5,9},{6... | collective-permute-start | bytes 3145736 | tf_op jit(solution)/shard_map/ppermute | solution.py:19
  17.6 47.9 %collective-permute-start.3 = (bf16[688,1024]{1,0:T(8,128)(2,1)}, bf16[688,1024]{1,0:T(8,128)(2,1)}, u32[]{:S(2)}, u32[]{:S(2)}) collective-permute-start(bf16[688,1024]{1,0:T(8,128)(2,1)} %pad_maximum_fusion.1), channel_id=1, source_target_pairs={{1,0},{2,1},{3,2},{0,3},{5,4},{6,5},{7,6},{4,7},{9,8},{10,9},{11,1... | collective-permute-start | bytes 4227080 | tf_op jit(solution)/shard_map/ppermute | solution.py:24
  20.4 45.2 %collective-permute-start.4 = (bf16[688,1024]{1,0:T(8,128)(2,1)}, bf16[688,1024]{1,0:T(8,128)(2,1)}, u32[]{:S(2)}, u32[]{:S(2)}) collective-permute-start(bf16[688,1024]{1,0:T(8,128)(2,1)} %pad_maximum_fusion.1), channel_id=1, source_target_pairs={{3,0},{0,1},{1,2},{2,3},{7,4},{4,5},{5,6},{6,7},{11,8},{8,9},{9,10... | collective-permute-start | bytes 4227080 | tf_op jit(solution)/shard_map/ppermute | solution.py:24
  23.5 17.4 %collective-permute-start.6 = (bf16[2,688,256]{2,1,0:T(8,128)(2,1)S(1)}, bf16[2,688,256]{2,1,0:T(8,128)(2,1)}, u32[]{:S(2)}, u32[]{:S(2)}) collective-permute-start(bf16[2,688,256]{2,1,0:T(8,128)(2,1)S(1)} %pad_maximum_fusion.3), channel_id=1, source_target_pairs={{96,0},{112,16},{64,32},{80,48},{32,64},{48,80},{0,96},{16,112},{9... | collective-permute-start | bytes 2113544 | tf_op jit(solution)/shard_map/ppermute | solution.py:28
  42.3 18.0 %collective-permute-start.7 = (bf16[4,688,256]{2,1,0:T(8,128)(2,1)S(1)}, bf16[4,688,256]{2,1,0:T(8,128)(2,1)}, u32[]{:S(2)}, u32[]{:S(2)}) collective-permute-start(bf16[4,688,256]{2,1,0:T(8,128)(2,1)S(1)} %pad_maximum_fusion.2.refs_3_.refs_5_), channel_id=1, source_target_pairs={{16,0},{0,16},{48,32},{32,48},{80,64},{64,80},{112,96},{96,112},{1... | collective-permute-start | bytes 4227080 | tf_op jit(solution)/shard_map/ppermute | solution.py:32
  49.5 16.0 %collective-permute-start.8 = (bf16[128,2048]{1,0:T(8,128)(2,1)}, bf16[128,2048]{1,0:T(8,128)(2,1)}, u32[]{:S(2)}, u32[]{:S(2)}) collective-permute-start(bf16[128,2048]{1,0:T(8,128)(2,1)} %slice.36), channel_id=1, source_target_pairs={{4,0},{5,1},{6,2},{7,3},{8,4},{9,5},{10,6},{11,7},{12,8},{13,9},{1... | collective-permute-start | bytes 1572872 | tf_op jit(solution)/shard_map/ppermute | solution.py:19
  52.8 14.7 %collective-permute-start.9 = (bf16[128,2048]{1,0:T(8,128)(2,1)}, bf16[128,2048]{1,0:T(8,128)(2,1)}, u32[]{:S(2)}, u32[]{:S(2)}) collective-permute-start(bf16[128,2048]{1,0:T(8,128)(2,1)} %slice.37), channel_id=1, source_target_pairs={{12,0},{13,1},{14,2},{15,3},{0,4},{1,5},{2,6},{3,7},{4,8},{5,9},{6... | collective-permute-start | bytes 1572872 | tf_op jit(solution)/shard_map/ppermute | solution.py:19
  60.3 8.4 %copy-start.12 = (s32[4]{0:T(128)S(1)}, s32[4]{0:T(128)}, u32[]{:S(2)}) copy-start(s32[4]{0:T(128)} %pad_add_fusion) | copy-start | bytes 52
  67.5 4.1 %collective-permute-start.10 = (bf16[688,1024]{1,0:T(8,128)(2,1)}, bf16[688,1024]{1,0:T(8,128)(2,1)S(1)}, u32[]{:S(2)}, u32[]{:S(2)}) collective-permute-start(bf16[688,1024]{1,0:T(8,128)(2,1)} %collective-permute-done.3.refs_8_), channel_id=1, source_target_pairs={{16,0},{0,16},{48,32},{32,48},{80,64},{64,80},{112,96},{96,112},{1... | collective-permute-start | bytes 4227080 | tf_op jit(solution)/shard_map/ppermute | solution.py:32
  68.6 5.0 %collective-permute-start.11 = (bf16[688,1024]{1,0:T(8,128)(2,1)}, bf16[688,1024]{1,0:T(8,128)(2,1)S(1)}, u32[]{:S(2)}, u32[]{:S(2)}) collective-permute-start(bf16[688,1024]{1,0:T(8,128)(2,1)} %collective-permute-done.4.refs_10_), channel_id=1, source_target_pairs={{16,0},{0,16},{48,32},{32,48},{80,64},{64,80},{112,96},{96,112},{1... | collective-permute-start | bytes 4227080 | tf_op jit(solution)/shard_map/ppermute | solution.py:32
  68.7 25.3 %copy-start = (bf16[344,2048]{1,0:T(8,128)(2,1)S(1)}, bf16[344,2048]{1,0:T(8,128)(2,1)}, u32[]{:S(2)}) copy-start(bf16[344,2048]{1,0:T(8,128)(2,1)} %w_ref.1) | copy-start | bytes 4227076
  86.8 5.1 %collective-permute-start.12 = (f32[32,344]{1,0:T(8,128)S(1)}, f32[32,344]{1,0:T(8,128)S(1)}, u32[]{:S(2)}, u32[]{:S(2)}) collective-permute-start(f32[32,344]{1,0:T(8,128)S(1)} %get-tuple-element.227), channel_id=1, source_target_pairs={{3,0},{0,1},{1,2},{2,3},{7,4},{4,5},{5,6},{6,7},{11,8},{8,9},{9,10... | collective-permute-start | bytes 132104 | tf_op jit(solution)/shard_map/ppermute | solution.py:24
  88.2 4.9 %collective-permute-start.13 = (f32[32,344]{1,0:T(8,128)S(1)}, f32[32,344]{1,0:T(8,128)S(1)}, u32[]{:S(2)}, u32[]{:S(2)}) collective-permute-start(f32[32,344]{1,0:T(8,128)S(1)} %get-tuple-element.228), channel_id=1, source_target_pairs={{2,0},{3,1},{0,2},{1,3},{6,4},{7,5},{4,6},{5,7},{10,8},{11,9},{8,1... | collective-permute-start | bytes 132104 | tf_op jit(solution)/shard_map/ppermute | solution.py:24
  90.8 3.2 %collective-permute-start.14 = (f32[32,344]{1,0:T(8,128)S(1)}, f32[32,344]{1,0:T(8,128)S(1)}, u32[]{:S(2)}, u32[]{:S(2)}) collective-permute-start(f32[32,344]{1,0:T(8,128)S(1)} %get-tuple-element.229), channel_id=1, source_target_pairs={{1,0},{2,1},{3,2},{0,3},{5,4},{6,5},{7,6},{4,7},{9,8},{10,9},{11,1... | collective-permute-start | bytes 132104 | tf_op jit(solution)/shard_map/ppermute | solution.py:24
  96.3 18.6 %copy-start.7 = (f32[8,2048]{1,0:T(8,128)S(1)}, f32[8,2048]{1,0:T(8,128)}, u32[]{:S(2)}) copy-start(f32[8,2048]{1,0:T(8,128)} %get-tuple-element.427.p_ref) | copy-start | bytes 196612
  96.3 18.6 %all-to-all-start.2 = ((f32[16,8,2048]{2,1,0:T(8,128)}), f32[16,8,2048]{2,1,0:T(8,128)S(1)}, u32[]{:S(2)}, u32[]{:S(2)}) async-start(f32[16,8,2048]{2,1,0:T(8,128)} %bitcast.42), calls=%async_computation.2 | async-start | bytes 2097152 | tf_op jit(solution)/shard_map/all_to_all | solution.py:350
  116.3 28.1 %all-to-all-start.3 = ((bf16[128,2,2176]{2,1,0:T(2,128)(2,1)}), bf16[128,2,2176]{2,1,0:T(2,128)(2,1)}, u32[]{:S(2)}, u32[]{:S(2)}) async-start(bf16[128,2,2176]{2,1,0:T(2,128)(2,1)} %emb.5), calls=%async_computation.3 | async-start | bytes 2228224 | tf_op jit(solution)/shard_map/all_to_all | solution.py:355
  155.1 14.7 %all-to-all-start.4 = ((f32[128,1,128]{2,1,0:T(1,128)}), f32[128,1,128]{2,1,0:T(1,128)S(1)}, u32[]{:S(2)}, u32[]{:S(2)}) async-start(f32[128,1,128]{2,1,0:T(1,128)} %get-tuple-element.235), calls=%async_computation.4 | async-start | bytes 131072 | tf_op jit(solution)/shard_map/all_to_all | solution.py:357
  (8 other events, 34.4 us)

commit v5 on v4

--- a/solution.py
+++ b/solution.py
@@ -22,10 +22,6 @@
 def from_y(v, k):
     perm = [(x * NY + (y + k) % NY, x * NY + y) for x in range(NX) for y in range(NY)]
     return lax.ppermute(v, "mp", perm)
-
-
-def from_z(v, other):
-    return lax.ppermute(v, "dp", [(other[z] * NC + c, z * NC + c) for z in range(NZ) for c in range(NC)])
 
 
 def from_core(v):
@@ -103,14 +99,13 @@
             t_waits = load_tokens()
     for cp in t_waits:
         cp.wait()
+    ones = block_ones(t_buf.shape[0] // file_len, file_len, BF)
     for s, (_, first) in enumerate(plan):
         for cp in waits[s]:
             cp.wait()
-        rows = t_buf.shape[0] - first
-        both = lax.dot_general(w_buf[s], t_buf[first:, :], NT, preferred_element_type=F32)
+        both = lax.dot_general(w_buf[s], t_buf[...], NT, preferred_element_type=F32)
         gate = both[:hid]
         units = (0.5 * gate * (1.0 + jnp.tanh(0.5 * gate)) * both[hid:]).astype(BF)
-        ones = block_ones(rows // file_len, file_len, BF)
         new = lax.dot_general(ones, units, NT, preferred_element_type=F32)
         if first:
             outs[s][:first // file_len, :] = olds.pop(0)[...]
@@ -128,7 +123,7 @@
         functools.partial(ffn_kernel, plan, len(toks), file_len),
         in_specs=[pl.BlockSpec(memory_space=pltpu.SMEM)] + [hbm] * (len(toks) + len(flat)) + [vm] * len(olds),
         out_specs=tuple(vm for _ in slices),
-        out_shape=tuple(jax.ShapeDtypeStruct((n_rows // file_len, rows // 2), F32) for _ in slices),
+        out_shape=tuple(jax.ShapeDtypeStruct(((n_rows + f) // file_len, rows // 2), F32) for f in firsts),
         scratch_shapes=[
             pltpu.VMEM((n_rows, width), BF),
             pltpu.VMEM((len(slices), rows, width), BF),
@@ -201,12 +196,11 @@
         at = pl.ds(i * block, block)
         copies.append(pltpu.make_async_copy(bank_ref.at[at], buf.at[at], sem.at[i]))
         copies[-1].start()
-    rows = rows_ref[:, :width]
+    rows = jnp.concatenate([rows_ref[:, 0, :width], rows_ref[:, 1, :width]], axis=0)
+    about = jnp.concatenate([rows_ref[:, 0, width:], rows_ref[:, 1, width:]], axis=0)
     n = rows.shape[0]
     pick = lax.broadcasted_iota(I32, (8, 128), 0) == lax.broadcasted_iota(I32, (8, 128), 1)
-    digits = lax.dot_general(
-        jnp.where(pick, 1.0, 0.0).astype(BF), rows_ref[:, width:], NT, preferred_element_type=F32
-    )
+    digits = lax.dot_general(jnp.where(pick, 1.0, 0.0).astype(BF), about, NT, preferred_element_type=F32)
     low = digits[0:1] * 65536.0 + digits[1:2] * 256.0 + digits[2:3]
     high = digits[3:4] * 65536.0 + digits[4:5] * 256.0 + digits[5:6]
     mine = digits[6:7] == (mp_ref[0] + 1).astype(F32)
@@ -216,30 +210,33 @@
     most = jnp.max(digits[7:8], axis=1, keepdims=True)
     about_ref[...] = jnp.where(lax.broadcasted_iota(I32, (1, 128), 1) == 0, count, most)
     best = jnp.full((1, n), -1.0, F32)
-    for i in range(n_blocks):
-        copies[i].wait()
+    block *= n_blocks // 2
+    for i in range(2):
+        for cp in copies[i * n_blocks // 2:(i + 1) * n_blocks // 2]:
+            cp.wait()
         at = slice(i * block, (i + 1) * block)
         sims = lax.dot_general(buf[at, :], rows, NT, preferred_element_type=F32)
         key = key_ref[at, :]
         valid = (key >= low) & (key < high)
         best = jnp.maximum(best, jnp.max(jnp.where(valid, sims, -1.0), axis=0, keepdims=True))
-    row = lax.broadcasted_iota(I32, (n // 2, n), 0)
-    lane = lax.broadcasted_iota(I32, (n // 2, n), 1)
-    best = jnp.broadcast_to(best, (n // 2, n))
-    pair = [jnp.max(jnp.where(lane == 2 * row + i, best, -1.0), axis=1, keepdims=True) for i in (0, 1)]
-    out_lane = lax.broadcasted_iota(I32, (n // 2, 128), 1)
+    n //= 2
+    eye = lax.broadcasted_iota(I32, (n, n), 0) == lax.broadcasted_iota(I32, (n, n), 1)
+    pair = [
+        jnp.max(jnp.where(eye, jnp.broadcast_to(best[:, i * n:(i + 1) * n], (n, n)), -1.0), axis=1, keepdims=True)
+        for i in (0, 1)
+    ]
+    out_lane = lax.broadcasted_iota(I32, (n, 128), 1)
     best_ref[:, 0, :] = jnp.where(out_lane == 0, pair[0], pair[1])
 
 
 def match(rows, mp, bank, key):
-    n = rows.shape[0]
     vm = pl.BlockSpec(memory_space=pltpu.VMEM)
     return pl.pallas_call(
         match_kernel,
         in_specs=[pl.BlockSpec(memory_space=pltpu.SMEM), vm, pl.BlockSpec(memory_space=pl.ANY), vm],
         out_specs=(vm, vm, vm),
         out_shape=(
-            jax.ShapeDtypeStruct((n // 2, 1, 128), F32),
+            jax.ShapeDtypeStruct((rows.shape[0], 1, 128), F32),
             jax.ShapeDtypeStruct((8, bank.shape[1]), F32),
             jax.ShapeDtypeStruct((1, 128), F32),
         ),
@@ -296,30 +293,20 @@
         meta = jnp.sum(jnp.where(sel[:, :, None], digits[None], 0), axis=1).astype(F32)
         return here, sel.astype(BF), jnp.pad(meta, ((0, 0), (0, 120)))
 
-    eighth, half = width // 8, width // 2
+    half, quarter = width // 2, width // 4
     w_t = [w_gate.T, w_up.T]
-    cut = lambda start, n: jnp.concatenate([lax.dynamic_slice_in_dim(w, start, n, 1) for w in w_t], axis=0)
-    w_own = jnp.concatenate(w_t, axis=0)
-    w_e = cut(dp * eighth, eighth)
-    w_e, hidden_in, w_t = tie((w_e, hidden_in, w_t))
-    e0 = from_y(w_e, 2)
-    w_h = cut(c * half, half)
+    w_h = jnp.concatenate([lax.dynamic_slice_in_dim(w, c * half, half, 1) for w in w_t], axis=0)
     normed, pooled_in = prep(hidden_in, mlp_gain, lengths)
     w_h, normed, w_t = tie((w_h, normed, w_t))
     t1, t3 = from_x(normed, 1), from_x(normed, 3)
     h1, h3 = from_y(w_h, 1), from_y(w_h, 3)
-    e0, normed = tie((e0, normed))
-    e1 = from_z(e0, (1, 0, 3, 2))
-    e01 = jnp.stack([e0, e1])
-    es = jnp.concatenate([e01, from_z(e01, (3, 2, 1, 0))])
+    w_own = jnp.concatenate(w_t, axis=0)
     t1, t3 = tie((t1, t3))
-    es = [es, from_core(es)]
     t2a, t2b = from_x(t1[:tok // 2], 1), from_x(t3[tok // 2:], 3)
     toks, last = [normed, t1, t3], [t2a, t2b]
 
-    held = [z, z ^ 1, 3 - z, (3 - z) ^ 1]
-    e_off = jnp.stack([(q * NC + k) * eighth for k in (c, 1 - c) for q in held]).astype(I32)
-    h_off = jnp.stack([c * half, (1 - c) * half] * 2).astype(I32)
+    h_off = jnp.stack([c * half, (1 - c) * half]).astype(I32)
+    e_off = jnp.stack([k * half + q * quarter for k in (c, 1 - c) for q in (0, 1)]).astype(I32)
     pos = jnp.stack(
         [(((x + j) % NX) * NY + (y - k) % NY) * files for k in range(NY) for j in (0, 1, 3, 2)]
     ).astype(I32)
@@ -330,22 +317,20 @@
 
     zero = jnp.zeros((1,), I32)
     (u0,) = ffn(toks, [[w_own]], (0,), zero, file_len, "ffn_own")
-    u0, es = tie((u0, es))
-    (u2,) = ffn(toks, [es], (0,), e_off, file_len, "ffn_far")
-    h1, h3, u2, last = tie((h1, h3, u2, last))
-    g1, g3 = from_core(h1), from_core(h3)
+    h1, h3, u0 = tie((h1, h3, u0))
+    k2a, k2b = from_y(h1[:, :quarter], 1), from_y(h3[:, quarter:], 3)
+    near = [[h1, from_core(h1)], [h3, from_core(h3)]]
+    near_off = jnp.concatenate([h_off, h_off])
+    u1, u3 = ffn(toks, near, (0, 0), near_off, file_len, "ffn_near")
     first = sum(t.shape[0] for t in toks)
-    u2, u0, u1, u3 = ffn(
-        toks + last,
-        [es, [w_own], [h1, g1], [h3, g3]],
-        (first, first, 0, 0),
-        jnp.concatenate([e_off, zero, h_off]),
-        file_len,
-        "ffn_last",
-        (u2, u0),
-    )
+    u1, u3, last = tie((u1, u3, last))
+    rest = jnp.concatenate([near_off, zero])
+    u1, u3, u0 = ffn(last, near + [[w_own]], (first,) * 3, rest, file_len, "ffn_rest", (u1, u3, u0))
+    r1, r3 = from_y(u1, NY - 1), from_y(u3, NY - 3)
+    k2a, k2b, u0 = tie((k2a, k2b, u0))
+    far = [k2a, k2b, from_core(k2a), from_core(k2b)]
+    (u2,) = ffn(toks + last, [far], (0,), e_off, file_len, "ffn_far")
     r2 = from_y(u2, NY - 2)
-    r1, r3 = from_y(u1, NY - 1), from_y(u3, NY - 3)
     terms = down([u0, r1, r2, r3], w_down, pos, files)
     terms = lax.all_to_all(terms, "mp", 0, 0, tiled=True)
 
@@ -353,7 +338,7 @@
         here, sel, meta = ready
         rows = emb_to_owners(terms, pooled_in, lens, sel, meta, files, n_mp)
         rows = lax.all_to_all(rows, ALL, 0, 0, tiled=True)
-        top, new, about = match(rows.reshape(-1, rows.shape[2]), mp, bank, bank_key)
+        top, new, about = match(rows, mp, bank, bank_key)
         back = lax.all_to_all(top, ALL, 0, 0, tiled=True)
         back = jnp.max(back.reshape(n_dp, n_mp, -1), axis=1)[:, :2]
         best = jnp.maximum(best, jnp.max(jnp.where(here, back[:, :, None], -1.0), axis=(0, 1)))

time: 173 us -> 167 us (0.965)
  starting transfers between devices: 43.7 us -> 36.3 us
  waiting for transfers between devices: 67.4 us -> 74.5 us
  other arithmetic: 9.93 us -> 3.45 us
    ppermute x4, waiting for transfers between devices: 1.98 us -> 21.9 us  [from_x(): return lax.ppermute(v, 'mp', perm)]
    ppermute x2 -> x0, waiting for transfers between devices: 13.3 us -> none  [from_z(): lax.ppermute(v, 'dp', [(other[z] * NC + c, z * NC + c) for z in range(NZ)...]
    ppermute x2 -> x0, starting transfers between devices: 5.2 us -> none  [from_z(): lax.ppermute(v, 'dp', [(other[z] * NC + c, z * NC + c) for z in range(NZ)...]
    ppermute x6 -> x7, waiting for transfers between devices: 6.41 us -> 11.4 us  [from_y(): return lax.ppermute(v, 'mp', perm)]
    ppermute x3 -> x4, waiting for transfers between devices: 4.95 us -> 0.03 us  [from_core(): return lax.ppermute(v, 'dp', [(d ^ 1, d) for d in range(NZ * NC)])]
    ppermute x6 -> x7, starting transfers between devices: 11.6 us -> 7.03 us  [from_y(): return lax.ppermute(v, 'mp', perm)]
    concatenate x5 -> x3, other arithmetic: 4.86 us -> 1.35 us  [the longest x1 1.2 us: on_device(): jnp.concatenate([lax.dynamic_slice_in_dim(w, c * half, half, 1) for w in...]
    slice x0 -> x2, local copies, waits for them, and re-layouts: none -> 2.3 us  [on_device(): k2a, k2b = (from_y(h1[:, :quarter], 1), from_y(h3[:, quarter:], 3))]
  transfers between devices with their start and end apart: 18 -> 18, of which waited for: 11 -> 10; matrix products, arithmetic and copies ran while one was open for 9% -> 5% of each run, Pallas kernels for 7% -> 14%
where the time goes in v5:
time: 167 us; the launch traced here: 166 us
  waiting for transfers between devices  74.5 us (45%)
  Pallas kernels  38.4 us (23%)
  starting transfers between devices  36.3 us (22%)
  local copies, waits for them, and re-layouts  9.51 us (6%)
  other arithmetic  3.45 us (2%)
  between operations  3.06 us (2%)
    pallas_call x4, Pallas kernels, ffn(): pl.pallas_call(functools.partial(ffn_kernel, plan, len(toks), file_len),...  23.2 us
    ppermute x4, waiting for transfers between devices, from_x(): return lax.ppermute(v, 'mp', perm)  21.9 us
    all_to_all x1, waiting for transfers between devices, one_round(): rows = lax.all_to_all(rows, ALL, 0, 0, tiled=True)  17.3 us
    all_to_all x1, waiting for transfers between devices, on_device(): terms = lax.all_to_all(terms, 'mp', 0, 0, tiled=True)  14.7 us
    ppermute x7, waiting for transfers between devices, from_y(): return lax.ppermute(v, 'mp', perm)  11.4 us
    pallas_call x1, Pallas kernels, match(): pl.pallas_call(match_kernel, in_specs=[pl.BlockSpec(memory_space=pltpu.SM...  10.4 us
    all_to_all x1, starting transfers between devices, one_round(): rows = lax.all_to_all(rows, ALL, 0, 0, tiled=True)  9.78 us
    all_to_all x1, waiting for transfers between devices, one_round(): back = lax.all_to_all(top, ALL, 0, 0, tiled=True)  9.1 us
  transfers between devices with their start and end apart: 18, of which 10 were waited for; matrix products, arithmetic and copies ran while one was open for 5% of the time, Pallas kernels for 14%

profile of v5, /device:TPU:1, one launch (start us, length us, event | category | flops | bytes accessed | tf_op | source)
XLA Modules:
  0.0 166.1 jit_solution(8081272405130325545)
XLA Ops:
  5.5 3.4 %collective-permute-start.2 = (bf16[256,2048]{1,0:T(8,128)(2,1)S(1)}, bf16[256,2048]{1,0:T(8,128)(2,1)S(1)}, u32[]{:S(2)}, u32[]{:S(2)}) collective-permute-start(bf16[256,2048]{1,0:T(8,128)(2,1)S(1)} %get-tuple-element.206.refs_0_), channel_id=1, source_target_pairs={{4,0},{5,1},{6,2},{7,3},{8,4},{9,5},{10,6},{11,7},{12,8},{13,9},{1... | collective-permute-start | bytes 3145736 | tf_op jit(solution)/shard_map/ppermute | solution.py:19
  8.9 2.7 %collective-permute-start = (bf16[688,1024]{1,0:T(8,128)(2,1)}, bf16[688,1024]{1,0:T(8,128)(2,1)}, u32[]{:S(2)}, u32[]{:S(2)}) collective-permute-start(bf16[688,1024]{1,0:T(8,128)(2,1)} %pad_maximum_fusion), channel_id=1, source_target_pairs={{1,0},{2,1},{3,2},{0,3},{5,4},{6,5},{7,6},{4,7},{9,8},{10,9},{11,1... | collective-permute-start | bytes 4227080 | tf_op jit(solution)/shard_map/ppermute | solution.py:24
  16.5 14.2 %collective-permute-done.2.refs_1_ = bf16[256,2048]{1,0:T(8,128)(2,1)S(1)} collective-permute-done((bf16[256,2048]{1,0:T(8,128)(2,1)S(1)}, bf16[256,2048]{1,0:T(8,128)(2,1)S(1)}, u32[]{:S(2)}, u32[]{:S(2)}) %collective-permute-start.2) | collective-permute-done | bytes 1048608 | tf_op jit(solution)/shard_map/ppermute | solution.py:19
  30.7 3.2 %collective-permute-done.3.refs_2_ = bf16[256,2048]{1,0:T(8,128)(2,1)S(1)} collective-permute-done((bf16[256,2048]{1,0:T(8,128)(2,1)S(1)}, bf16[256,2048]{1,0:T(8,128)(2,1)S(1)}, u32[]{:S(2)}, u32[]{:S(2)}) %collective-permute-start.3) | collective-permute-done | bytes 1048608 | tf_op jit(solution)/shard_map/ppermute | solution.py:19
  33.9 3.4 %ffn_own.1.refs_9_ = f32[24,344]{1,0:T(8,128)S(1)} custom-call(s32[1]{0:T(128)} %constant.220.clone.1.off_ref, bf16[256,2048]{1,0:T(8,128)(2,1)S(1)} %get-tuple-element.206.refs_0_, bf16[256,2048]{1,0:T(8,128)(2,1)S(1)} %collective-permute-done.2.refs_1_, bf16[256,2048]{1,0:T(8,128)(2,1)S(1)} %collective-permute-done.3.refs_2_, ...), custom_call_target="tpu_custom_call" | custom-call | tf_op jit(solution)/shard_map/ffn_own/pallas_call | solution.py:122
  37.3 3.9 %collective-permute-done.refs_3_.refs_2_ = bf16[688,1024]{1,0:T(8,128)(2,1)} collective-permute-done((bf16[688,1024]{1,0:T(8,128)(2,1)}, bf16[688,1024]{1,0:T(8,128)(2,1)}, u32[]{:S(2)}, u32[]{:S(2)}) %collective-permute-start) | collective-permute-done | bytes 1409056 | tf_op jit(solution)/shard_map/ppermute | solution.py:24
  41.1 3.1 %collective-permute-done.1.refs_5_.refs_4_ = bf16[688,1024]{1,0:T(8,128)(2,1)} collective-permute-done((bf16[688,1024]{1,0:T(8,128)(2,1)}, bf16[688,1024]{1,0:T(8,128)(2,1)}, u32[]{:S(2)}, u32[]{:S(2)}) %collective-permute-start.1) | collective-permute-done | bytes 1409056 | tf_op jit(solution)/shard_map/ppermute | solution.py:24
  44.3 2.2 %collective-permute-start.6 = (bf16[688,1024]{1,0:T(8,128)(2,1)}, bf16[688,1024]{1,0:T(8,128)(2,1)S(1)}, u32[]{:S(2)}, u32[]{:S(2)}) collective-permute-start(bf16[688,1024]{1,0:T(8,128)(2,1)} %collective-permute-done.refs_3_.refs_2_), channel_id=1, source_target_pairs={{16,0},{0,16},{48,32},{32,48},{80,64},{64,80},{112,96},{96,112},{1... | collective-permute-start | bytes 4227080 | tf_op jit(solution)/shard_map/ppermute | solution.py:28
  50.4 2.7 %collective-permute-start.8 = (bf16[128,2048]{1,0:T(8,128)(2,1)S(1)}, bf16[128,2048]{1,0:T(8,128)(2,1)S(1)}, u32[]{:S(2)}, u32[]{:S(2)}) collective-permute-start(bf16[128,2048]{1,0:T(8,128)(2,1)S(1)} %slice.44), channel_id=1, source_target_pairs={{4,0},{5,1},{6,2},{7,3},{8,4},{9,5},{10,6},{11,7},{12,8},{13,9},{1... | collective-permute-start | bytes 1572872 | tf_op jit(solution)/shard_map/ppermute | solution.py:19
  53.3 8.6 %ffn_near.1 = (f32[24,344]{1,0:T(8,128)S(1)}, f32[24,344]{1,0:T(8,128)S(1)}) custom-call(s32[4]{0:T(128)S(1)} %pad_add_fusion.3.off_ref, bf16[256,2048]{1,0:T(8,128)(2,1)S(1)} %get-tuple-element.206.refs_0_, bf16[256,2048]{1,0:T(8,128)(2,1)S(1)} %collective-permute-done.2.refs_1_, bf16[256,2048]{1,0:T(8,128)(2,1)S(1)} %collective-permute-done.3.refs_2_, ...), custom_call_target="tpu_custom_call" | custom-call | tf_op jit(solution)/shard_map/ffn_near/pallas_call | solution.py:122
  63.3 3.1 %collective-permute-done.9.refs_1_.refs_4_ = bf16[128,2048]{1,0:T(8,128)(2,1)S(1)} collective-permute-done((bf16[128,2048]{1,0:T(8,128)(2,1)S(1)}, bf16[128,2048]{1,0:T(8,128)(2,1)S(1)}, u32[]{:S(2)}, u32[]{:S(2)}) %collective-permute-start.9) | collective-permute-done | bytes 524320 | tf_op jit(solution)/shard_map/ppermute | solution.py:19
  66.4 6.6 %ffn_rest.1 = (f32[32,344]{1,0:T(8,128)S(1)}, f32[32,344]{1,0:T(8,128)S(1)}, f32[32,344]{1,0:T(8,128)S(1)}) custom-call(s32[5]{0:T(128)S(1)} %pad_add_fusion.2.off_ref, bf16[128,2048]{1,0:T(8,128)(2,1)S(1)} %collective-permute-done.8.refs_0_.refs_3_, bf16[128,2048]{1,0:T(8,128)(2,1)S(1)} %collective-permute-done.9.refs_1_.refs_4_, ...), custom_call_target="tpu_custom_call" | custom-call | tf_op jit(solution)/shard_map/ffn_rest/pallas_call | solution.py:122
  73.1 2.4 %collective-permute-start.11 = (bf16[688,512]{1,0:T(8,128)(2,1)S(1)}, bf16[688,512]{1,0:T(8,128)(2,1)S(1)}, u32[]{:S(2)}, u32[]{:S(2)}) collective-permute-start(bf16[688,512]{1,0:T(8,128)(2,1)S(1)} %collective-permute-done.4.refs_5_), channel_id=1, source_target_pairs={{16,0},{0,16},{48,32},{32,48},{80,64},{64,80},{112,96},{96,112},{1... | collective-permute-start | bytes 2113544 | tf_op jit(solution)/shard_map/ppermute | solution.py:28
  75.5 2.7 %collective-permute-start.14 = (f32[32,344]{1,0:T(8,128)S(1)}, f32[32,344]{1,0:T(8,128)S(1)}, u32[]{:S(2)}, u32[]{:S(2)}) collective-permute-start(f32[32,344]{1,0:T(8,128)S(1)} %get-tuple-element.227), channel_id=1, source_target_pairs={{1,0},{2,1},{3,2},{0,3},{5,4},{6,5},{7,6},{4,7},{9,8},{10,9},{11,1... | collective-permute-start | bytes 132104 | tf_op jit(solution)/shard_map/ppermute | solution.py:24
  78.2 4.6 %ffn_far.1 = f32[32,344]{1,0:T(8,128)S(1)} custom-call(s32[4]{0:T(128)S(1)} %pad_add_fusion.off_ref, bf16[256,2048]{1,0:T(8,128)(2,1)S(1)} %get-tuple-element.206.refs_0_, bf16[256,2048]{1,0:T(8,128)(2,1)S(1)} %collective-permute-done.2.refs_1_, bf16[256,2048]{1,0:T(8,128)(2,1)S(1)} %collective-permute-done.3.refs_2_, ...), custom_call_target="tpu_custom_call" | custom-call | tf_op jit(solution)/shard_map/ffn_far/pallas_call | solution.py:122
  83.0 4.4 %collective-permute-done.13.u2 = f32[32,344]{1,0:T(8,128)S(1)} collective-permute-done((f32[32,344]{1,0:T(8,128)S(1)}, f32[32,344]{1,0:T(8,128)S(1)}, u32[]{:S(2)}, u32[]{:S(2)}) %collective-permute-start.13) | collective-permute-done | bytes 44064 | tf_op jit(solution)/shard_map/ppermute | solution.py:24
  87.4 2.2 %down.1 = f32[128,2048]{1,0:T(8,128)} custom-call(s32[16]{0:T(128)S(1)} %stack.107.pos_ref, f32[32,344]{1,0:T(8,128)S(1)} %get-tuple-element.222.u0, f32[32,344]{1,0:T(8,128)S(1)} %collective-permute-done.10.u1, f32[32,344]{1,0:T(8,128)S(1)} %collective-permute-done.13.u2, f32[32,344]{1,0:T(8,128)S(1)} %collective-permute-done.14.u3, ...), custom_call_target="tpu_custom_call" | custom-call | tf_op jit(solution)/shard_map/down/pallas_call | solution.py:153
  89.6 3.9 %all-to-all-start.2 = ((f32[16,8,2048]{2,1,0:T(8,128)}), f32[16,8,2048]{2,1,0:T(8,128)S(1)}, u32[]{:S(2)}, u32[]{:S(2)}) async-start(f32[16,8,2048]{2,1,0:T(8,128)} %bitcast.34), calls=%async_computation.2 | async-start | bytes 2097152 | tf_op jit(solution)/shard_map/all_to_all | solution.py:335
  93.6 14.7 %all-to-all-done.2 = f32[16,8,2048]{2,1,0:T(8,128)S(1)} async-done(((f32[16,8,2048]{2,1,0:T(8,128)}), f32[16,8,2048]{2,1,0:T(8,128)S(1)}, u32[]{:S(2)}, u32[]{:S(2)}) %all-to-all-start.2) | async-done | bytes 1048608 | tf_op jit(solution)/shard_map/all_to_all | solution.py:335
  109.7 9.8 %all-to-all-start.3 = ((bf16[128,2,2176]{2,1,0:T(2,128)(2,1)}), bf16[128,2,2176]{2,1,0:T(2,128)(2,1)S(1)}, u32[]{:S(2)}, u32[]{:S(2)}) async-start(bf16[128,2,2176]{2,1,0:T(2,128)(2,1)} %emb.5), calls=%async_computation.3 | async-start | bytes 2228224 | tf_op jit(solution)/shard_map/all_to_all | solution.py:340
  121.5 17.3 %all-to-all-done.3.rows_ref = bf16[128,2,2176]{2,1,0:T(2,128)(2,1)S(1)} async-done(((bf16[128,2,2176]{2,1,0:T(2,128)(2,1)}), bf16[128,2,2176]{2,1,0:T(2,128)(2,1)S(1)}, u32[]{:S(2)}, u32[]{:S(2)}) %all-to-all-start.3) | async-done | bytes 1114144 | tf_op jit(solution)/shard_map/all_to_all | solution.py:340
  138.7 10.4 %match.5 = (f32[128,1,128]{2,1,0:T(1,128)}, f32[8,2048]{1,0:T(8,128)S(1)}, f32[1,128]{1,0:T(1,128)S(1)}) custom-call(s32[1]{0:T(128)} %bitcast.33.mp_ref, bf16[128,2,2176]{2,1,0:T(2,128)(2,1)S(1)} %all-to-all-done.3.rows_ref, bf16[2048,2048]{1,0:T(8,128)(2,1)} %bank_ref.1, f32[2048,1]{1,0:T(8,128)} %copy.55.key_ref), custom_call_target="tpu_custom_call" | custom-call | tf_op jit(solution)/shard_map/match/pallas_call | solution.py:234
  149.2 4.9 %all-to-all-start.4 = ((f32[128,1,128]{2,1,0:T(1,128)}), f32[128,1,128]{2,1,0:T(1,128)S(1)}, u32[]{:S(2)}, u32[]{:S(2)}) async-start(f32[128,1,128]{2,1,0:T(1,128)} %get-tuple-element.233), calls=%async_computation.4 | async-start | bytes 131072 | tf_op jit(solution)/shard_map/all_to_all | solution.py:342
  154.7 9.1 %all-to-all-done.4 = f32[128,1,128]{2,1,0:T(1,128)S(1)} async-done(((f32[128,1,128]{2,1,0:T(1,128)}), f32[128,1,128]{2,1,0:T(1,128)S(1)}, u32[]{:S(2)}, u32[]{:S(2)}) %all-to-all-start.4) | async-done | bytes 65568 | tf_op jit(solution)/shard_map/all_to_all | solution.py:342
  (91 shorter events, 19.6 us)
Async XLA Ops:
  2.8 8.8 %copy-start.8 = (s32[128]{0:T(128)S(1)}, s32[128]{0:T(128)}, u32[]{:S(2)}) copy-start(s32[128]{0:T(128)} %param.24) | copy-start | bytes 1540
  2.8 8.8 %copy-start.9 = (s32[8]{0:T(128)S(1)}, s32[8]{0:T(128)}, u32[]{:S(2)}) copy-start(s32[8]{0:T(128)} %param.22) | copy-start | bytes 100
  2.8 9.0 %copy-start.7 = (s32[8]{0:T(128)S(1)}, s32[8]{0:T(128)}, u32[]{:S(2)}) copy-start(s32[8]{0:T(128)} %param.23) | copy-start | bytes 100
  4.3 10.3 %copy-start.4 = (s32[2048]{0:T(1024)S(1)}, s32[2048]{0:T(1024)}, u32[]{:S(2)}) copy-start(s32[2048]{0:T(1024)} %param.27) | copy-start | bytes 24580
  4.3 10.3 %copy-start.5 = (s32[2048]{0:T(1024)S(1)}, s32[2048]{0:T(1024)}, u32[]{:S(2)}) copy-start(s32[2048]{0:T(1024)} %param.26) | copy-start | bytes 24580
  5.5 25.2 %collective-permute-start.2 = (bf16[256,2048]{1,0:T(8,128)(2,1)S(1)}, bf16[256,2048]{1,0:T(8,128)(2,1)S(1)}, u32[]{:S(2)}, u32[]{:S(2)}) collective-permute-start(bf16[256,2048]{1,0:T(8,128)(2,1)S(1)} %get-tuple-element.206.refs_0_), channel_id=1, source_target_pairs={{4,0},{5,1},{6,2},{7,3},{8,4},{9,5},{10,6},{11,7},{12,8},{13,9},{1... | collective-permute-start | bytes 3145736 | tf_op jit(solution)/shard_map/ppermute | solution.py:19
  8.9 25.0 %collective-permute-start.3 = (bf16[256,2048]{1,0:T(8,128)(2,1)S(1)}, bf16[256,2048]{1,0:T(8,128)(2,1)S(1)}, u32[]{:S(2)}, u32[]{:S(2)}) collective-permute-start(bf16[256,2048]{1,0:T(8,128)(2,1)S(1)} %get-tuple-element.206.refs_0_), channel_id=1, source_target_pairs={{12,0},{13,1},{14,2},{15,3},{0,4},{1,5},{2,6},{3,7},{4,8},{5,9},{6... | collective-permute-start | bytes 3145736 | tf_op jit(solution)/shard_map/ppermute | solution.py:19
  8.9 32.3 %collective-permute-start = (bf16[688,1024]{1,0:T(8,128)(2,1)}, bf16[688,1024]{1,0:T(8,128)(2,1)}, u32[]{:S(2)}, u32[]{:S(2)}) collective-permute-start(bf16[688,1024]{1,0:T(8,128)(2,1)} %pad_maximum_fusion), channel_id=1, source_target_pairs={{1,0},{2,1},{3,2},{0,3},{5,4},{6,5},{7,6},{4,7},{9,8},{10,9},{11,1... | collective-permute-start | bytes 4227080 | tf_op jit(solution)/shard_map/ppermute | solution.py:24
  11.6 32.7 %collective-permute-start.1 = (bf16[688,1024]{1,0:T(8,128)(2,1)}, bf16[688,1024]{1,0:T(8,128)(2,1)}, u32[]{:S(2)}, u32[]{:S(2)}) collective-permute-start(bf16[688,1024]{1,0:T(8,128)(2,1)} %pad_maximum_fusion), channel_id=1, source_target_pairs={{3,0},{0,1},{1,2},{2,3},{7,4},{4,5},{5,6},{6,7},{11,8},{8,9},{9,10... | collective-permute-start | bytes 4227080 | tf_op jit(solution)/shard_map/ppermute | solution.py:24
  44.3 8.8 %collective-permute-start.6 = (bf16[688,1024]{1,0:T(8,128)(2,1)}, bf16[688,1024]{1,0:T(8,128)(2,1)S(1)}, u32[]{:S(2)}, u32[]{:S(2)}) collective-permute-start(bf16[688,1024]{1,0:T(8,128)(2,1)} %collective-permute-done.refs_3_.refs_2_), channel_id=1, source_target_pairs={{16,0},{0,16},{48,32},{32,48},{80,64},{64,80},{112,96},{96,112},{1... | collective-permute-start | bytes 4227080 | tf_op jit(solution)/shard_map/ppermute | solution.py:28
  46.4 6.8 %collective-permute-start.7 = (bf16[688,1024]{1,0:T(8,128)(2,1)}, bf16[688,1024]{1,0:T(8,128)(2,1)S(1)}, u32[]{:S(2)}, u32[]{:S(2)}) collective-permute-start(bf16[688,1024]{1,0:T(8,128)(2,1)} %collective-permute-done.1.refs_5_.refs_4_), channel_id=1, source_target_pairs={{16,0},{0,16},{48,32},{32,48},{80,64},{64,80},{112,96},{96,112},{1... | collective-permute-start | bytes 4227080 | tf_op jit(solution)/shard_map/ppermute | solution.py:28
  48.7 24.3 %collective-permute-start.4 = (bf16[688,512]{1,0:T(8,128)(2,1)S(1)}, bf16[688,512]{1,0:T(8,128)(2,1)S(1)}, u32[]{:S(2)}, u32[]{:S(2)}) collective-permute-start(bf16[688,512]{1,0:T(8,128)(2,1)S(1)} %slice.42), channel_id=1, source_target_pairs={{1,0},{2,1},{3,2},{0,3},{5,4},{6,5},{7,6},{4,7},{9,8},{10,9},{11,1... | collective-permute-start | bytes 2113544 | tf_op jit(solution)/shard_map/ppermute | solution.py:24
  48.8 24.2 %collective-permute-start.5 = (bf16[688,512]{1,0:T(8,128)(2,1)S(1)}, bf16[688,512]{1,0:T(8,128)(2,1)S(1)}, u32[]{:S(2)}, u32[]{:S(2)}) collective-permute-start(bf16[688,512]{1,0:T(8,128)(2,1)S(1)} %slice.43), channel_id=1, source_target_pairs={{3,0},{0,1},{1,2},{2,3},{7,4},{4,5},{5,6},{6,7},{11,8},{8,9},{9,10... | collective-permute-start | bytes 2113544 | tf_op jit(solution)/shard_map/ppermute | solution.py:24
  50.4 12.9 %collective-permute-start.8 = (bf16[128,2048]{1,0:T(8,128)(2,1)S(1)}, bf16[128,2048]{1,0:T(8,128)(2,1)S(1)}, u32[]{:S(2)}, u32[]{:S(2)}) collective-permute-start(bf16[128,2048]{1,0:T(8,128)(2,1)S(1)} %slice.44), channel_id=1, source_target_pairs={{4,0},{5,1},{6,2},{7,3},{8,4},{9,5},{10,6},{11,7},{12,8},{13,9},{1... | collective-permute-start | bytes 1572872 | tf_op jit(solution)/shard_map/ppermute | solution.py:19
  53.1 13.3 %collective-permute-start.9 = (bf16[128,2048]{1,0:T(8,128)(2,1)S(1)}, bf16[128,2048]{1,0:T(8,128)(2,1)S(1)}, u32[]{:S(2)}, u32[]{:S(2)}) collective-permute-start(bf16[128,2048]{1,0:T(8,128)(2,1)S(1)} %slice.45), channel_id=1, source_target_pairs={{12,0},{13,1},{14,2},{15,3},{0,4},{1,5},{2,6},{3,7},{4,8},{5,9},{6... | collective-permute-start | bytes 1572872 | tf_op jit(solution)/shard_map/ppermute | solution.py:19
  73.1 5.1 %collective-permute-start.11 = (bf16[688,512]{1,0:T(8,128)(2,1)S(1)}, bf16[688,512]{1,0:T(8,128)(2,1)S(1)}, u32[]{:S(2)}, u32[]{:S(2)}) collective-permute-start(bf16[688,512]{1,0:T(8,128)(2,1)S(1)} %collective-permute-done.4.refs_5_), channel_id=1, source_target_pairs={{16,0},{0,16},{48,32},{32,48},{80,64},{64,80},{112,96},{96,112},{1... | collective-permute-start | bytes 2113544 | tf_op jit(solution)/shard_map/ppermute | solution.py:28
  75.4 2.8 %collective-permute-start.12 = (bf16[688,512]{1,0:T(8,128)(2,1)S(1)}, bf16[688,512]{1,0:T(8,128)(2,1)S(1)}, u32[]{:S(2)}, u32[]{:S(2)}) collective-permute-start(bf16[688,512]{1,0:T(8,128)(2,1)S(1)} %collective-permute-done.5.refs_6_), channel_id=1, source_target_pairs={{16,0},{0,16},{48,32},{32,48},{80,64},{64,80},{112,96},{96,112},{1... | collective-permute-start | bytes 2113544 | tf_op jit(solution)/shard_map/ppermute | solution.py:28
  75.5 7.4 %collective-permute-start.10 = (f32[32,344]{1,0:T(8,128)S(1)}, f32[32,344]{1,0:T(8,128)S(1)}, u32[]{:S(2)}, u32[]{:S(2)}) collective-permute-start(f32[32,344]{1,0:T(8,128)S(1)} %get-tuple-element.223), channel_id=1, source_target_pairs={{3,0},{0,1},{1,2},{2,3},{7,4},{4,5},{5,6},{6,7},{11,8},{8,9},{9,10... | collective-permute-start | bytes 132104 | tf_op jit(solution)/shard_map/ppermute | solution.py:24
  75.5 11.9 %copy-start = (bf16[344,2048]{1,0:T(8,128)(2,1)S(1)}, bf16[344,2048]{1,0:T(8,128)(2,1)}, u32[]{:S(2)}) copy-start(bf16[344,2048]{1,0:T(8,128)(2,1)} %w_ref.1) | copy-start | bytes 4227076
  75.5 7.4 %collective-permute-start.14 = (f32[32,344]{1,0:T(8,128)S(1)}, f32[32,344]{1,0:T(8,128)S(1)}, u32[]{:S(2)}, u32[]{:S(2)}) collective-permute-start(f32[32,344]{1,0:T(8,128)S(1)} %get-tuple-element.227), channel_id=1, source_target_pairs={{1,0},{2,1},{3,2},{0,3},{5,4},{6,5},{7,6},{4,7},{9,8},{10,9},{11,1... | collective-permute-start | bytes 132104 | tf_op jit(solution)/shard_map/ppermute | solution.py:24
  82.8 4.5 %collective-permute-start.13 = (f32[32,344]{1,0:T(8,128)S(1)}, f32[32,344]{1,0:T(8,128)S(1)}, u32[]{:S(2)}, u32[]{:S(2)}) collective-permute-start(f32[32,344]{1,0:T(8,128)S(1)} %ffn_far.1), channel_id=1, source_target_pairs={{2,0},{3,1},{0,2},{1,3},{6,4},{7,5},{4,6},{5,7},{10,8},{11,9},{8,1... | collective-permute-start | bytes 132104 | tf_op jit(solution)/shard_map/ppermute | solution.py:24
  89.6 18.7 %all-to-all-start.2 = ((f32[16,8,2048]{2,1,0:T(8,128)}), f32[16,8,2048]{2,1,0:T(8,128)S(1)}, u32[]{:S(2)}, u32[]{:S(2)}) async-start(f32[16,8,2048]{2,1,0:T(8,128)} %bitcast.34), calls=%async_computation.2 | async-start | bytes 2097152 | tf_op jit(solution)/shard_map/all_to_all | solution.py:335
  109.7 29.0 %all-to-all-start.3 = ((bf16[128,2,2176]{2,1,0:T(2,128)(2,1)}), bf16[128,2,2176]{2,1,0:T(2,128)(2,1)S(1)}, u32[]{:S(2)}, u32[]{:S(2)}) async-start(bf16[128,2,2176]{2,1,0:T(2,128)(2,1)} %emb.5), calls=%async_computation.3 | async-start | bytes 2228224 | tf_op jit(solution)/shard_map/all_to_all | solution.py:340
  149.2 14.6 %all-to-all-start.4 = ((f32[128,1,128]{2,1,0:T(1,128)}), f32[128,1,128]{2,1,0:T(1,128)S(1)}, u32[]{:S(2)}, u32[]{:S(2)}) async-start(f32[128,1,128]{2,1,0:T(1,128)} %get-tuple-element.233), calls=%async_computation.4 | async-start | bytes 131072 | tf_op jit(solution)/shard_map/all_to_all | solution.py:342
  (5 other events, 7.7 us)

commit v6 on v5

--- a/solution.py
+++ b/solution.py
@@ -144,7 +144,8 @@
     hi = rows.astype(BF)
     lo = (rows - hi.astype(F32)).astype(BF)
     w = w_ref[...]
-    o_ref[...] = jnp.dot(hi, w, preferred_element_type=F32) + jnp.dot(lo, w, preferred_element_type=F32)
+    term = jnp.dot(hi, w, preferred_element_type=F32) + jnp.dot(lo, w, preferred_element_type=F32)
+    o_ref[...] = term.astype(BF).reshape(o_ref.shape)
 
 
 def down(us, w_down, pos, files):
@@ -154,17 +155,17 @@
         functools.partial(down_kernel, files),
         in_specs=[pl.BlockSpec(memory_space=pltpu.SMEM)] + [vm] * 5,
         out_specs=vm,
-        out_shape=jax.ShapeDtypeStruct((rows, w_down.shape[1]), F32),
+        out_shape=jax.ShapeDtypeStruct((NX * NY, files, w_down.shape[1]), BF),
         scratch_shapes=[pltpu.VMEM((rows, us[0].shape[1]), F32)],
         compiler_params=pltpu.CompilerParams(vmem_limit_bytes=16 * 1024 * 1024),
         name="down",
     )(pos, *us, w_down)
 
 
-def emb_kernel(files, copies, t_ref, p_ref, len_ref, sel_ref, meta_ref, o_ref):
+def emb_kernel(copies, t_ref, p_ref, len_ref, sel_ref, meta_ref, o_ref):
     total = p_ref[...]
-    for m in range(t_ref.shape[0] // files):
-        total = total + t_ref[m * files:(m + 1) * files, :]
+    for m in range(t_ref.shape[0]):
+        total = total + t_ref[m].astype(F32)
     pooled = total / len_ref[...]
     norm = lax.rsqrt(jnp.sum(pooled * pooled, axis=-1, keepdims=True) + 1e-06)
     emb = (pooled * norm).astype(BF)
@@ -178,9 +179,9 @@
             o_ref[d * copies + m, :, width:] = about
 
 
-def emb_to_owners(terms, pooled, lens, sel, meta, files, copies):
-    return pl.pallas_call(
-        functools.partial(emb_kernel, files, copies),
+def emb_to_owners(terms, pooled, lens, sel, meta, copies):
+    return pl.pallas_call(
+        functools.partial(emb_kernel, copies),
         out_shape=jax.ShapeDtypeStruct((sel.shape[0] // 2 * copies, 2, pooled.shape[1] + meta.shape[1]), BF),
         compiler_params=pltpu.CompilerParams(vmem_limit_bytes=16 * 1024 * 1024),
         name="emb",
@@ -196,8 +197,7 @@
         at = pl.ds(i * block, block)
         copies.append(pltpu.make_async_copy(bank_ref.at[at], buf.at[at], sem.at[i]))
         copies[-1].start()
-    rows = jnp.concatenate([rows_ref[:, 0, :width], rows_ref[:, 1, :width]], axis=0)
-    about = jnp.concatenate([rows_ref[:, 0, width:], rows_ref[:, 1, width:]], axis=0)
+    rows, about = rows_ref[:, :width], rows_ref[:, width:]
     n = rows.shape[0]
     pick = lax.broadcasted_iota(I32, (8, 128), 0) == lax.broadcasted_iota(I32, (8, 128), 1)
     digits = lax.dot_general(jnp.where(pick, 1.0, 0.0).astype(BF), about, NT, preferred_element_type=F32)
@@ -209,22 +209,15 @@
     count = jnp.sum(jnp.where(mine, 1.0, 0.0), axis=1, keepdims=True)
     most = jnp.max(digits[7:8], axis=1, keepdims=True)
     about_ref[...] = jnp.where(lax.broadcasted_iota(I32, (1, 128), 1) == 0, count, most)
-    best = jnp.full((1, n), -1.0, F32)
-    block *= n_blocks // 2
-    for i in range(2):
-        for cp in copies[i * n_blocks // 2:(i + 1) * n_blocks // 2]:
-            cp.wait()
-        at = slice(i * block, (i + 1) * block)
-        sims = lax.dot_general(buf[at, :], rows, NT, preferred_element_type=F32)
-        key = key_ref[at, :]
-        valid = (key >= low) & (key < high)
-        best = jnp.maximum(best, jnp.max(jnp.where(valid, sims, -1.0), axis=0, keepdims=True))
+    for cp in copies:
+        cp.wait()
+    sims = lax.dot_general(buf[...], rows, NT, preferred_element_type=F32)
+    key = key_ref[...]
+    best = jnp.max(jnp.where((key >= low) & (key < high), sims, -1.0), axis=0, keepdims=True)
     n //= 2
-    eye = lax.broadcasted_iota(I32, (n, n), 0) == lax.broadcasted_iota(I32, (n, n), 1)
-    pair = [
-        jnp.max(jnp.where(eye, jnp.broadcast_to(best[:, i * n:(i + 1) * n], (n, n)), -1.0), axis=1, keepdims=True)
-        for i in (0, 1)
-    ]
+    row, lane = (lax.broadcasted_iota(I32, (n, 2 * n), d) for d in (0, 1))
+    best = jnp.broadcast_to(best, (n, 2 * n))
+    pair = [jnp.max(jnp.where(lane == 2 * row + i, best, -1.0), axis=1, keepdims=True) for i in (0, 1)]
     out_lane = lax.broadcasted_iota(I32, (n, 128), 1)
     best_ref[:, 0, :] = jnp.where(out_lane == 0, pair[0], pair[1])
 
@@ -236,7 +229,7 @@
         in_specs=[pl.BlockSpec(memory_space=pltpu.SMEM), vm, pl.BlockSpec(memory_space=pl.ANY), vm],
         out_specs=(vm, vm, vm),
         out_shape=(
-            jax.ShapeDtypeStruct((rows.shape[0], 1, 128), F32),
+            jax.ShapeDtypeStruct((rows.shape[0] // 2, 1, 128), F32),
             jax.ShapeDtypeStruct((8, bank.shape[1]), F32),
             jax.ShapeDtypeStruct((1, 128), F32),
         ),
@@ -298,47 +291,39 @@
     w_h = jnp.concatenate([lax.dynamic_slice_in_dim(w, c * half, half, 1) for w in w_t], axis=0)
     normed, pooled_in = prep(hidden_in, mlp_gain, lengths)
     w_h, normed, w_t = tie((w_h, normed, w_t))
-    t1, t3 = from_x(normed, 1), from_x(normed, 3)
+    t1, t2, t3 = from_x(normed, 1), from_x(normed, 2), from_x(normed, 3)
     h1, h3 = from_y(w_h, 1), from_y(w_h, 3)
     w_own = jnp.concatenate(w_t, axis=0)
-    t1, t3 = tie((t1, t3))
-    t2a, t2b = from_x(t1[:tok // 2], 1), from_x(t3[tok // 2:], 3)
-    toks, last = [normed, t1, t3], [t2a, t2b]
+    toks = [normed, t1, t2, t3]
 
     h_off = jnp.stack([c * half, (1 - c) * half]).astype(I32)
     e_off = jnp.stack([k * half + q * quarter for k in (c, 1 - c) for q in (0, 1)]).astype(I32)
     pos = jnp.stack(
-        [(((x + j) % NX) * NY + (y - k) % NY) * files for k in range(NY) for j in (0, 1, 3, 2)]
+        [(((x + j) % NX) * NY + (y - k) % NY) * files for k in range(NY) for j in range(NX)]
     ).astype(I32)
     lens = lengths.astype(F32)[:, None]
     ready = files_of(0)
-    normed, e_off, h_off, pos, lens, bank_key, ready = tie((normed, e_off, h_off, pos, lens, bank_key, ready))
-    toks[0] = normed
-
-    zero = jnp.zeros((1,), I32)
-    (u0,) = ffn(toks, [[w_own]], (0,), zero, file_len, "ffn_own")
-    h1, h3, u0 = tie((h1, h3, u0))
-    k2a, k2b = from_y(h1[:, :quarter], 1), from_y(h3[:, quarter:], 3)
+    offs = jnp.concatenate([jnp.zeros((1,), I32), h_off, h_off])
+    h1, h3, t2, pos, lens, ready = tie((h1, h3, t2, pos, lens, ready))
+    toks = [normed, t1, t2, t3]
+    s1, s3 = h1[:, :quarter], h3[:, quarter:]
+    k2a, k2b = from_y(s1, 1), from_y(s3, 3)
+    h1, h3 = tie((h1, h3, s1, s3, t1, t3))[:2]
     near = [[h1, from_core(h1)], [h3, from_core(h3)]]
-    near_off = jnp.concatenate([h_off, h_off])
-    u1, u3 = ffn(toks, near, (0, 0), near_off, file_len, "ffn_near")
-    first = sum(t.shape[0] for t in toks)
-    u1, u3, last = tie((u1, u3, last))
-    rest = jnp.concatenate([near_off, zero])
-    u1, u3, u0 = ffn(last, near + [[w_own]], (first,) * 3, rest, file_len, "ffn_rest", (u1, u3, u0))
+    u0, u1, u3 = ffn(toks, [[w_own]] + near, (0,) * 3, offs, file_len, "ffn_main")
     r1, r3 = from_y(u1, NY - 1), from_y(u3, NY - 3)
     k2a, k2b, u0 = tie((k2a, k2b, u0))
     far = [k2a, k2b, from_core(k2a), from_core(k2b)]
-    (u2,) = ffn(toks + last, [far], (0,), e_off, file_len, "ffn_far")
+    (u2,) = ffn(toks, [far], (0,), e_off, file_len, "ffn_far")
     r2 = from_y(u2, NY - 2)
     terms = down([u0, r1, r2, r3], w_down, pos, files)
     terms = lax.all_to_all(terms, "mp", 0, 0, tiled=True)
 
     def one_round(ready, best, sums, counts):
         here, sel, meta = ready
-        rows = emb_to_owners(terms, pooled_in, lens, sel, meta, files, n_mp)
+        rows = emb_to_owners(terms, pooled_in, lens, sel, meta, n_mp)
         rows = lax.all_to_all(rows, ALL, 0, 0, tiled=True)
-        top, new, about = match(rows, mp, bank, bank_key)
+        top, new, about = match(rows.reshape(-1, rows.shape[2]), mp, bank, bank_key)
         back = lax.all_to_all(top, ALL, 0, 0, tiled=True)
         back = jnp.max(back.reshape(n_dp, n_mp, -1), axis=1)[:, :2]
         best = jnp.maximum(best, jnp.max(jnp.where(here, back[:, :, None], -1.0), axis=(0, 1)))

time: 167 us -> 167 us (level)
  waiting for transfers between devices: 74.5 us -> 82.2 us
  Pallas kernels: 38.4 us -> 31.3 us
  starting transfers between devices: 36.3 us -> 33.5 us
  other arithmetic: 3.45 us -> 5.14 us
    ppermute x4 -> x3, waiting for transfers between devices: 21.9 us -> 30.4 us  [from_x(): return lax.ppermute(v, 'mp', perm)]
    all_to_all x1, waiting for transfers between devices: 14.7 us -> 9.14 us  [on_device(): terms = lax.all_to_all(terms, 'mp', 0, 0, tiled=True)]
    pallas_call x1, Pallas kernels: 10.4 us -> 6.75 us  [match(): pl.pallas_call(match_kernel, in_specs=[pl.BlockSpec(memory_space=pltpu.SM...]
    pallas_call x4 -> x2, Pallas kernels: 23.2 us -> 20 us  [ffn(): pl.pallas_call(functools.partial(ffn_kernel, plan, len(toks), file_len),...]
    ppermute x4, starting transfers between devices: 4.61 us -> 2.21 us  [from_core(): return lax.ppermute(v, 'dp', [(d ^ 1, d) for d in range(NZ * NC)])]
    ppermute x7, waiting for transfers between devices: 11.4 us -> 13.8 us  [from_y(): return lax.ppermute(v, 'mp', perm)]
    ppermute x4, waiting for transfers between devices: 0.03 us -> 2 us  [from_core(): return lax.ppermute(v, 'dp', [(d ^ 1, d) for d in range(NZ * NC)])]
    ppermute x4 -> x3, starting transfers between devices: 6.13 us -> 4.21 us  [from_x(): return lax.ppermute(v, 'mp', perm)]
  transfers between devices with their start and end apart: 18 -> 17, of which waited for: 10 -> 13; matrix products, arithmetic and copies ran while one was open for 5% -> 6% of each run, Pallas kernels for 14% -> 12%
where the time goes in v6:
time: 167 us; the launch traced here: 166 us
  waiting for transfers between devices  82.2 us (49%)
  starting transfers between devices  33.5 us (20%)
  Pallas kernels  31.3 us (19%)
  local copies, waits for them, and re-layouts  10 us (6%)
  other arithmetic  5.14 us (3%)
  between operations  3.02 us (2%)
    ppermute x3, waiting for transfers between devices, from_x(): return lax.ppermute(v, 'mp', perm)  30.4 us
    pallas_call x2, Pallas kernels, ffn(): pl.pallas_call(functools.partial(ffn_kernel, plan, len(toks), file_len),...  20 us
    all_to_all x1, waiting for transfers between devices, one_round(): rows = lax.all_to_all(rows, ALL, 0, 0, tiled=True)  17.9 us
    ppermute x7, waiting for transfers between devices, from_y(): return lax.ppermute(v, 'mp', perm)  13.8 us
    all_to_all x1, starting transfers between devices, one_round(): rows = lax.all_to_all(rows, ALL, 0, 0, tiled=True)  10 us
    all_to_all x1, waiting for transfers between devices, on_device(): terms = lax.all_to_all(terms, 'mp', 0, 0, tiled=True)  9.14 us
    all_to_all x1, waiting for transfers between devices, one_round(): back = lax.all_to_all(top, ALL, 0, 0, tiled=True)  9.04 us
    ppermute x7, starting transfers between devices, from_y(): return lax.ppermute(v, 'mp', perm)  8.09 us
  transfers between devices with their start and end apart: 17, of which 13 were waited for; matrix products, arithmetic and copies ran while one was open for 6% of the time, Pallas kernels for 12%

profile of v6, /device:TPU:1, one launch (start us, length us, event | category | flops | bytes accessed | tf_op | source)
XLA Modules:
  0.0 165.9 jit_solution(16712335928011870709)
XLA Ops:
  5.5 3.6 %collective-permute-start = (bf16[688,1024]{1,0:T(8,128)(2,1)}, bf16[688,1024]{1,0:T(8,128)(2,1)}, u32[]{:S(2)}, u32[]{:S(2)}) collective-permute-start(bf16[688,1024]{1,0:T(8,128)(2,1)} %pad_maximum_fusion.1), channel_id=1, source_target_pairs={{1,0},{2,1},{3,2},{0,3},{5,4},{6,5},{7,6},{4,7},{9,8},{10,9},{11,1... | collective-permute-start | bytes 4227080 | tf_op jit(solution)/shard_map/ppermute | solution.py:24
  9.1 2.7 %collective-permute-start.2 = (bf16[256,2048]{1,0:T(8,128)(2,1)S(1)}, bf16[256,2048]{1,0:T(8,128)(2,1)S(1)}, u32[]{:S(2)}, u32[]{:S(2)}) collective-permute-start(bf16[256,2048]{1,0:T(8,128)(2,1)S(1)} %get-tuple-element.193.refs_0_), channel_id=1, source_target_pairs={{8,0},{9,1},{10,2},{11,3},{12,4},{13,5},{14,6},{15,7},{0,8},{1,9},... | collective-permute-start | bytes 3145736 | tf_op jit(solution)/shard_map/ppermute | solution.py:19
  16.1 18.3 %collective-permute-done.2.refs_2_ = bf16[256,2048]{1,0:T(8,128)(2,1)S(1)} collective-permute-done((bf16[256,2048]{1,0:T(8,128)(2,1)S(1)}, bf16[256,2048]{1,0:T(8,128)(2,1)S(1)}, u32[]{:S(2)}, u32[]{:S(2)}) %collective-permute-start.2) | collective-permute-done | bytes 1048608 | tf_op jit(solution)/shard_map/ppermute | solution.py:19
  34.4 4.6 %collective-permute-done.refs_5_ = bf16[688,1024]{1,0:T(8,128)(2,1)} collective-permute-done((bf16[688,1024]{1,0:T(8,128)(2,1)}, bf16[688,1024]{1,0:T(8,128)(2,1)}, u32[]{:S(2)}, u32[]{:S(2)}) %collective-permute-start) | collective-permute-done | bytes 1409056 | tf_op jit(solution)/shard_map/ppermute | solution.py:24
  39.0 3.1 %collective-permute-done.1.refs_7_ = bf16[688,1024]{1,0:T(8,128)(2,1)} collective-permute-done((bf16[688,1024]{1,0:T(8,128)(2,1)}, bf16[688,1024]{1,0:T(8,128)(2,1)}, u32[]{:S(2)}, u32[]{:S(2)}) %collective-permute-start.1) | collective-permute-done | bytes 1409056 | tf_op jit(solution)/shard_map/ppermute | solution.py:24
  42.1 2.1 %slice.36 = bf16[688,512]{1,0:T(8,128)(2,1)} slice(bf16[688,1024]{1,0:T(8,128)(2,1)} %collective-permute-done.refs_5_), slice={[0:688], [0:512]} | slice | bytes 1409024 | tf_op jit(solution)/shard_map/slice | solution.py:309
  44.1 2.0 %slice.37 = bf16[688,512]{1,0:T(8,128)(2,1)} slice(bf16[688,1024]{1,0:T(8,128)(2,1)} %collective-permute-done.1.refs_7_), slice={[0:688], [512:1024]} | slice | bytes 1409024 | tf_op jit(solution)/shard_map/slice | solution.py:309
  46.1 11.1 %collective-permute-done.5.refs_1_ = bf16[256,2048]{1,0:T(8,128)(2,1)S(1)} collective-permute-done((bf16[256,2048]{1,0:T(8,128)(2,1)S(1)}, bf16[256,2048]{1,0:T(8,128)(2,1)S(1)}, u32[]{:S(2)}, u32[]{:S(2)}) %collective-permute-start.5) | collective-permute-done | bytes 1048608 | tf_op jit(solution)/shard_map/ppermute | solution.py:19
  58.8 2.7 %collective-permute-start.3 = (bf16[688,512]{1,0:T(8,128)(2,1)}, bf16[688,512]{1,0:T(8,128)(2,1)}, u32[]{:S(2)}, u32[]{:S(2)}) collective-permute-start(bf16[688,512]{1,0:T(8,128)(2,1)} %slice.36), channel_id=1, source_target_pairs={{1,0},{2,1},{3,2},{0,3},{5,4},{6,5},{7,6},{4,7},{9,8},{10,9},{11,1... | collective-permute-start | bytes 2113544 | tf_op jit(solution)/shard_map/ppermute | solution.py:24
  61.6 2.0 %pad_maximum_fusion.refs_4_ = bf16[688,2048]{1,0:T(8,128)(2,1)S(1)} fusion(bf16[344,2048]{1,0:T(8,128)(2,1)} %bitcast.71, bf16[344,2048]{1,0:T(8,128)(2,1)} %bitcast.72), kind=kLoop, calls=%fused_computation.5 | loop fusion | flops 5636096 | bytes 5636096 | tf_op jit(solution)/shard_map/concatenate | solution.py:296
  64.0 13.9 %ffn_main.1 = (f32[32,344]{1,0:T(8,128)S(1)}, f32[32,344]{1,0:T(8,128)S(1)}, f32[32,344]{1,0:T(8,128)S(1)}) custom-call(s32[5]{0:T(128)S(1)} %concatenate.11.off_ref, bf16[256,2048]{1,0:T(8,128)(2,1)S(1)} %get-tuple-element.193.refs_0_, bf16[256,2048]{1,0:T(8,128)(2,1)S(1)} %collective-permute-done.5.refs_1_, ...), custom_call_target="tpu_custom_call" | custom-call | tf_op jit(solution)/shard_map/ffn_main/pallas_call | solution.py:122
  77.9 1.7 %collective-permute-done.4.refs_5_ = bf16[688,512]{1,0:T(8,128)(2,1)} collective-permute-done((bf16[688,512]{1,0:T(8,128)(2,1)}, bf16[688,512]{1,0:T(8,128)(2,1)}, u32[]{:S(2)}, u32[]{:S(2)}) %collective-permute-start.4) | collective-permute-done | bytes 704544 | tf_op jit(solution)/shard_map/ppermute | solution.py:24
  79.5 1.7 %collective-permute-start.10 = (bf16[688,512]{1,0:T(8,128)(2,1)}, bf16[688,512]{1,0:T(8,128)(2,1)}, u32[]{:S(2)}, u32[]{:S(2)}) collective-permute-start(bf16[688,512]{1,0:T(8,128)(2,1)} %collective-permute-done.3.refs_4_), channel_id=1, source_target_pairs={{16,0},{0,16},{48,32},{32,48},{80,64},{64,80},{112,96},{96,112},{1... | collective-permute-start | bytes 2113544 | tf_op jit(solution)/shard_map/ppermute | solution.py:28
  84.3 6.1 %ffn_far.1 = f32[32,344]{1,0:T(8,128)S(1)} custom-call(s32[4]{0:T(128)S(1)} %pad_add_fusion.off_ref, bf16[256,2048]{1,0:T(8,128)(2,1)S(1)} %get-tuple-element.193.refs_0_, bf16[256,2048]{1,0:T(8,128)(2,1)S(1)} %collective-permute-done.5.refs_1_, bf16[256,2048]{1,0:T(8,128)(2,1)S(1)} %collective-permute-done.2.refs_2_, ...), custom_call_target="tpu_custom_call" | custom-call | tf_op jit(solution)/shard_map/ffn_far/pallas_call | solution.py:122
  90.8 4.4 %collective-permute-done.12.u2 = f32[32,344]{1,0:T(8,128)S(1)} collective-permute-done((f32[32,344]{1,0:T(8,128)S(1)}, f32[32,344]{1,0:T(8,128)S(1)}, u32[]{:S(2)}, u32[]{:S(2)}) %collective-permute-start.12) | collective-permute-done | bytes 44064 | tf_op jit(solution)/shard_map/ppermute | solution.py:24
  95.2 2.0 %down.1 = bf16[16,8,2048]{2,1,0:T(8,128)(2,1)} custom-call(s32[16]{0:T(128)S(1)} %stack.99.pos_ref, f32[32,344]{1,0:T(8,128)S(1)} %get-tuple-element.204.u0, f32[32,344]{1,0:T(8,128)S(1)} %collective-permute-done.9.u1, f32[32,344]{1,0:T(8,128)S(1)} %collective-permute-done.12.u2, f32[32,344]{1,0:T(8,128)S(1)} %collective-permute-done.13.u3, ...), custom_call_target="tpu_custom_call" | custom-call | tf_op jit(solution)/shard_map/down/pallas_call | solution.py:154
  97.2 4.1 %all-to-all-start.2 = ((bf16[16,8,2048]{2,1,0:T(8,128)(2,1)}), bf16[16,8,2048]{2,1,0:T(8,128)(2,1)S(1)}, u32[]{:S(2)}, u32[]{:S(2)}) async-start(bf16[16,8,2048]{2,1,0:T(8,128)(2,1)} %down.1), calls=%async_computation.2 | async-start | bytes 1048576 | tf_op jit(solution)/shard_map/all_to_all | solution.py:320
  101.4 9.1 %all-to-all-done.2.t_ref = bf16[16,8,2048]{2,1,0:T(8,128)(2,1)S(1)} async-done(((bf16[16,8,2048]{2,1,0:T(8,128)(2,1)}), bf16[16,8,2048]{2,1,0:T(8,128)(2,1)S(1)}, u32[]{:S(2)}, u32[]{:S(2)}) %all-to-all-start.2) | async-done | bytes 524320 | tf_op jit(solution)/shard_map/all_to_all | solution.py:320
  111.9 10.0 %all-to-all-start.3 = ((bf16[128,2,2176]{2,1,0:T(2,128)(2,1)}), bf16[128,2,2176]{2,1,0:T(2,128)(2,1)}, u32[]{:S(2)}, u32[]{:S(2)}) async-start(bf16[128,2,2176]{2,1,0:T(2,128)(2,1)} %emb.5), calls=%async_computation.3 | async-start | bytes 2228224 | tf_op jit(solution)/shard_map/all_to_all | solution.py:325
  123.1 17.9 %all-to-all-done.3 = bf16[128,2,2176]{2,1,0:T(2,128)(2,1)} async-done(((bf16[128,2,2176]{2,1,0:T(2,128)(2,1)}), bf16[128,2,2176]{2,1,0:T(2,128)(2,1)}, u32[]{:S(2)}, u32[]{:S(2)}) %all-to-all-start.3) | async-done | bytes 1114144 | tf_op jit(solution)/shard_map/all_to_all | solution.py:325
  141.0 1.5 reshape.192.rows_ref
  142.5 6.7 %match.5 = (f32[128,1,128]{2,1,0:T(1,128)}, f32[8,2048]{1,0:T(8,128)S(1)}, f32[1,128]{1,0:T(1,128)S(1)}) custom-call(s32[1]{0:T(128)} %bitcast.28.mp_ref, bf16[256,2176]{1,0:T(8,128)(2,1)S(1)} %reshape.192.rows_ref, bf16[2048,2048]{1,0:T(8,128)(2,1)} %bank_ref.1, f32[2048,1]{1,0:T(8,128)S(1)} %copy.55.key_ref), custom_call_target="tpu_custom_call" | custom-call | tf_op jit(solution)/shard_map/match/pallas_call | solution.py:227
  149.2 4.9 %all-to-all-start.4 = ((f32[128,1,128]{2,1,0:T(1,128)}), f32[128,1,128]{2,1,0:T(1,128)S(1)}, u32[]{:S(2)}, u32[]{:S(2)}) async-start(f32[128,1,128]{2,1,0:T(1,128)} %get-tuple-element.213), calls=%async_computation.4 | async-start | bytes 131072 | tf_op jit(solution)/shard_map/all_to_all | solution.py:327
  154.8 9.0 %all-to-all-done.4 = f32[128,1,128]{2,1,0:T(1,128)S(1)} async-done(((f32[128,1,128]{2,1,0:T(1,128)}), f32[128,1,128]{2,1,0:T(1,128)S(1)}, u32[]{:S(2)}, u32[]{:S(2)}) %all-to-all-start.4) | async-done | bytes 65568 | tf_op jit(solution)/shard_map/all_to_all | solution.py:327
  (81 shorter events, 17.7 us)
Async XLA Ops:
  2.8 1.6 copy-start.1
  2.8 10.5 %copy-start.9 = (s32[128]{0:T(128)S(1)}, s32[128]{0:T(128)}, u32[]{:S(2)}) copy-start(s32[128]{0:T(128)} %param.24) | copy-start | bytes 1540
  2.8 10.5 %copy-start.10 = (s32[8]{0:T(128)S(1)}, s32[8]{0:T(128)}, u32[]{:S(2)}) copy-start(s32[8]{0:T(128)} %param.22) | copy-start | bytes 100
  2.8 10.7 %copy-start.8 = (s32[8]{0:T(128)S(1)}, s32[8]{0:T(128)}, u32[]{:S(2)}) copy-start(s32[8]{0:T(128)} %param.23) | copy-start | bytes 100
  5.5 33.5 %collective-permute-start = (bf16[688,1024]{1,0:T(8,128)(2,1)}, bf16[688,1024]{1,0:T(8,128)(2,1)}, u32[]{:S(2)}, u32[]{:S(2)}) collective-permute-start(bf16[688,1024]{1,0:T(8,128)(2,1)} %pad_maximum_fusion.1), channel_id=1, source_target_pairs={{1,0},{2,1},{3,2},{0,3},{5,4},{6,5},{7,6},{4,7},{9,8},{10,9},{11,1... | collective-permute-start | bytes 4227080 | tf_op jit(solution)/shard_map/ppermute | solution.py:24
  9.1 33.0 %collective-permute-start.1 = (bf16[688,1024]{1,0:T(8,128)(2,1)}, bf16[688,1024]{1,0:T(8,128)(2,1)}, u32[]{:S(2)}, u32[]{:S(2)}) collective-permute-start(bf16[688,1024]{1,0:T(8,128)(2,1)} %pad_maximum_fusion.1), channel_id=1, source_target_pairs={{3,0},{0,1},{1,2},{2,3},{7,4},{4,5},{5,6},{6,7},{11,8},{8,9},{9,10... | collective-permute-start | bytes 4227080 | tf_op jit(solution)/shard_map/ppermute | solution.py:24
  9.1 25.3 %collective-permute-start.2 = (bf16[256,2048]{1,0:T(8,128)(2,1)S(1)}, bf16[256,2048]{1,0:T(8,128)(2,1)S(1)}, u32[]{:S(2)}, u32[]{:S(2)}) collective-permute-start(bf16[256,2048]{1,0:T(8,128)(2,1)S(1)} %get-tuple-element.193.refs_0_), channel_id=1, source_target_pairs={{8,0},{9,1},{10,2},{11,3},{12,4},{13,5},{14,6},{15,7},{0,8},{1,9},... | collective-permute-start | bytes 3145736 | tf_op jit(solution)/shard_map/ppermute | solution.py:19
  11.9 45.4 %collective-permute-start.5 = (bf16[256,2048]{1,0:T(8,128)(2,1)S(1)}, bf16[256,2048]{1,0:T(8,128)(2,1)S(1)}, u32[]{:S(2)}, u32[]{:S(2)}) collective-permute-start(bf16[256,2048]{1,0:T(8,128)(2,1)S(1)} %get-tuple-element.193.refs_0_), channel_id=1, source_target_pairs={{4,0},{5,1},{6,2},{7,3},{8,4},{9,5},{10,6},{11,7},{12,8},{13,9},{1... | collective-permute-start | bytes 3145736 | tf_op jit(solution)/shard_map/ppermute | solution.py:19
  12.7 45.6 %collective-permute-start.6 = (bf16[256,2048]{1,0:T(8,128)(2,1)S(1)}, bf16[256,2048]{1,0:T(8,128)(2,1)}, u32[]{:S(2)}, u32[]{:S(2)}) collective-permute-start(bf16[256,2048]{1,0:T(8,128)(2,1)S(1)} %get-tuple-element.193.refs_0_), channel_id=1, source_target_pairs={{12,0},{13,1},{14,2},{15,3},{0,4},{1,5},{2,6},{3,7},{4,8},{5,9},{6... | collective-permute-start | bytes 3145736 | tf_op jit(solution)/shard_map/ppermute | solution.py:19
  58.3 5.3 %collective-permute-start.7 = (bf16[688,1024]{1,0:T(8,128)(2,1)}, bf16[688,1024]{1,0:T(8,128)(2,1)}, u32[]{:S(2)}, u32[]{:S(2)}) collective-permute-start(bf16[688,1024]{1,0:T(8,128)(2,1)} %collective-permute-done.refs_5_), channel_id=1, source_target_pairs={{16,0},{0,16},{48,32},{32,48},{80,64},{64,80},{112,96},{96,112},{1... | collective-permute-start | bytes 4227080 | tf_op jit(solution)/shard_map/ppermute | solution.py:28
  58.8 5.2 %collective-permute-start.8 = (bf16[688,1024]{1,0:T(8,128)(2,1)}, bf16[688,1024]{1,0:T(8,128)(2,1)}, u32[]{:S(2)}, u32[]{:S(2)}) collective-permute-start(bf16[688,1024]{1,0:T(8,128)(2,1)} %collective-permute-done.1.refs_7_), channel_id=1, source_target_pairs={{16,0},{0,16},{48,32},{32,48},{80,64},{64,80},{112,96},{96,112},{1... | collective-permute-start | bytes 4227080 | tf_op jit(solution)/shard_map/ppermute | solution.py:28
  58.8 19.1 %collective-permute-start.3 = (bf16[688,512]{1,0:T(8,128)(2,1)}, bf16[688,512]{1,0:T(8,128)(2,1)}, u32[]{:S(2)}, u32[]{:S(2)}) collective-permute-start(bf16[688,512]{1,0:T(8,128)(2,1)} %slice.36), channel_id=1, source_target_pairs={{1,0},{2,1},{3,2},{0,3},{5,4},{6,5},{7,6},{4,7},{9,8},{10,9},{11,1... | collective-permute-start | bytes 2113544 | tf_op jit(solution)/shard_map/ppermute | solution.py:24
  61.5 18.0 %collective-permute-start.4 = (bf16[688,512]{1,0:T(8,128)(2,1)}, bf16[688,512]{1,0:T(8,128)(2,1)}, u32[]{:S(2)}, u32[]{:S(2)}) collective-permute-start(bf16[688,512]{1,0:T(8,128)(2,1)} %slice.37), channel_id=1, source_target_pairs={{3,0},{0,1},{1,2},{2,3},{7,4},{4,5},{5,6},{6,7},{11,8},{8,9},{9,10... | collective-permute-start | bytes 2113544 | tf_op jit(solution)/shard_map/ppermute | solution.py:24
  79.5 3.8 %collective-permute-start.10 = (bf16[688,512]{1,0:T(8,128)(2,1)}, bf16[688,512]{1,0:T(8,128)(2,1)}, u32[]{:S(2)}, u32[]{:S(2)}) collective-permute-start(bf16[688,512]{1,0:T(8,128)(2,1)} %collective-permute-done.3.refs_4_), channel_id=1, source_target_pairs={{16,0},{0,16},{48,32},{32,48},{80,64},{64,80},{112,96},{96,112},{1... | collective-permute-start | bytes 2113544 | tf_op jit(solution)/shard_map/ppermute | solution.py:28
  81.2 3.1 %collective-permute-start.11 = (bf16[688,512]{1,0:T(8,128)(2,1)}, bf16[688,512]{1,0:T(8,128)(2,1)}, u32[]{:S(2)}, u32[]{:S(2)}) collective-permute-start(bf16[688,512]{1,0:T(8,128)(2,1)} %collective-permute-done.4.refs_5_), channel_id=1, source_target_pairs={{16,0},{0,16},{48,32},{32,48},{80,64},{64,80},{112,96},{96,112},{1... | collective-permute-start | bytes 2113544 | tf_op jit(solution)/shard_map/ppermute | solution.py:28
  81.3 9.5 %collective-permute-start.13 = (f32[32,344]{1,0:T(8,128)S(1)}, f32[32,344]{1,0:T(8,128)S(1)}, u32[]{:S(2)}, u32[]{:S(2)}) collective-permute-start(f32[32,344]{1,0:T(8,128)S(1)} %get-tuple-element.208), channel_id=1, source_target_pairs={{1,0},{2,1},{3,2},{0,3},{5,4},{6,5},{7,6},{4,7},{9,8},{10,9},{11,1... | collective-permute-start | bytes 132104 | tf_op jit(solution)/shard_map/ppermute | solution.py:24
  81.5 13.7 %copy-start = (bf16[344,2048]{1,0:T(8,128)(2,1)S(1)}, bf16[344,2048]{1,0:T(8,128)(2,1)}, u32[]{:S(2)}) copy-start(bf16[344,2048]{1,0:T(8,128)(2,1)} %w_ref.1) | copy-start | bytes 4227076
  81.5 9.3 %collective-permute-start.9 = (f32[32,344]{1,0:T(8,128)S(1)}, f32[32,344]{1,0:T(8,128)S(1)}, u32[]{:S(2)}, u32[]{:S(2)}) collective-permute-start(f32[32,344]{1,0:T(8,128)S(1)} %get-tuple-element.205), channel_id=1, source_target_pairs={{3,0},{0,1},{1,2},{2,3},{7,4},{4,5},{5,6},{6,7},{11,8},{8,9},{9,10... | collective-permute-start | bytes 132104 | tf_op jit(solution)/shard_map/ppermute | solution.py:24
  90.4 4.7 %collective-permute-start.12 = (f32[32,344]{1,0:T(8,128)S(1)}, f32[32,344]{1,0:T(8,128)S(1)}, u32[]{:S(2)}, u32[]{:S(2)}) collective-permute-start(f32[32,344]{1,0:T(8,128)S(1)} %ffn_far.1), channel_id=1, source_target_pairs={{2,0},{3,1},{0,2},{1,3},{6,4},{7,5},{4,6},{5,7},{10,8},{11,9},{8,1... | collective-permute-start | bytes 132104 | tf_op jit(solution)/shard_map/ppermute | solution.py:24
  97.2 13.3 %all-to-all-start.2 = ((bf16[16,8,2048]{2,1,0:T(8,128)(2,1)}), bf16[16,8,2048]{2,1,0:T(8,128)(2,1)S(1)}, u32[]{:S(2)}, u32[]{:S(2)}) async-start(bf16[16,8,2048]{2,1,0:T(8,128)(2,1)} %down.1), calls=%async_computation.2 | async-start | bytes 1048576 | tf_op jit(solution)/shard_map/all_to_all | solution.py:320
  111.9 10.1 %copy-start.5 = (s32[2048]{0:T(1024)S(1)}, s32[2048]{0:T(1024)}, u32[]{:S(2)}) copy-start(s32[2048]{0:T(1024)} %param.27) | copy-start | bytes 24580
  111.9 10.1 %copy-start.6 = (s32[2048]{0:T(1024)S(1)}, s32[2048]{0:T(1024)}, u32[]{:S(2)}) copy-start(s32[2048]{0:T(1024)} %param.26) | copy-start | bytes 24580
  111.9 29.0 %all-to-all-start.3 = ((bf16[128,2,2176]{2,1,0:T(2,128)(2,1)}), bf16[128,2,2176]{2,1,0:T(2,128)(2,1)}, u32[]{:S(2)}, u32[]{:S(2)}) async-start(bf16[128,2,2176]{2,1,0:T(2,128)(2,1)} %emb.5), calls=%async_computation.3 | async-start | bytes 2228224 | tf_op jit(solution)/shard_map/all_to_all | solution.py:325
  149.2 14.6 %all-to-all-start.4 = ((f32[128,1,128]{2,1,0:T(1,128)}), f32[128,1,128]{2,1,0:T(1,128)S(1)}, u32[]{:S(2)}, u32[]{:S(2)}) async-start(f32[128,1,128]{2,1,0:T(1,128)} %get-tuple-element.213), calls=%async_computation.4 | async-start | bytes 131072 | tf_op jit(solution)/shard_map/all_to_all | solution.py:327
  (3 other events, 4.2 us)

commit v7 on v6

--- a/solution.py
+++ b/solution.py
@@ -289,32 +289,39 @@
     half, quarter = width // 2, width // 4
     w_t = [w_gate.T, w_up.T]
     w_h = jnp.concatenate([lax.dynamic_slice_in_dim(w, c * half, half, 1) for w in w_t], axis=0)
+    w_h, hidden_in, w_t = tie((w_h, hidden_in, w_t))
     normed, pooled_in = prep(hidden_in, mlp_gain, lengths)
-    w_h, normed, w_t = tie((w_h, normed, w_t))
-    t1, t2, t3 = from_x(normed, 1), from_x(normed, 2), from_x(normed, 3)
+    t1, t3 = from_x(normed, 1), from_x(normed, 3)
     h1, h3 = from_y(w_h, 1), from_y(w_h, 3)
     w_own = jnp.concatenate(w_t, axis=0)
-    toks = [normed, t1, t2, t3]
+    t1, t3 = tie((t1, t3))
+    t2a, t2b = from_x(t1[:tok // 2], 1), from_x(t3[tok // 2:], 3)
+    toks, last = [normed, t1, t3], [t2a, t2b]
 
     h_off = jnp.stack([c * half, (1 - c) * half]).astype(I32)
     e_off = jnp.stack([k * half + q * quarter for k in (c, 1 - c) for q in (0, 1)]).astype(I32)
     pos = jnp.stack(
-        [(((x + j) % NX) * NY + (y - k) % NY) * files for k in range(NY) for j in range(NX)]
+        [(((x + j) % NX) * NY + (y - k) % NY) * files for k in range(NY) for j in (0, 1, 3, 2)]
     ).astype(I32)
     lens = lengths.astype(F32)[:, None]
     ready = files_of(0)
-    offs = jnp.concatenate([jnp.zeros((1,), I32), h_off, h_off])
-    h1, h3, t2, pos, lens, ready = tie((h1, h3, t2, pos, lens, ready))
-    toks = [normed, t1, t2, t3]
-    s1, s3 = h1[:, :quarter], h3[:, quarter:]
-    k2a, k2b = from_y(s1, 1), from_y(s3, 3)
-    h1, h3 = tie((h1, h3, s1, s3, t1, t3))[:2]
+    normed, e_off, h_off, pos, lens, bank_key, ready = tie((normed, e_off, h_off, pos, lens, bank_key, ready))
+    toks[0] = normed
+
+    zero = jnp.zeros((1,), I32)
+    (u0,) = ffn(toks, [[w_own]], (0,), zero, file_len, "ffn_own")
+    h1, h3, u0 = tie((h1, h3, u0))
+    k2a, k2b = from_y(h1[:, :quarter], 1), from_y(h3[:, quarter:], 3)
     near = [[h1, from_core(h1)], [h3, from_core(h3)]]
-    u0, u1, u3 = ffn(toks, [[w_own]] + near, (0,) * 3, offs, file_len, "ffn_main")
+    near_off = jnp.concatenate([h_off, h_off])
+    u1, u3 = ffn(toks, near, (0, 0), near_off, file_len, "ffn_near")
+    first = sum(t.shape[0] for t in toks)
+    k2a, k2b, u1, u3, last = tie((k2a, k2b, u1, u3, last))
+    far = [k2a, k2b, from_core(k2a), from_core(k2b)]
+    rest = jnp.concatenate([near_off, zero])
+    u1, u3, u0 = ffn(last, near + [[w_own]], (first,) * 3, rest, file_len, "ffn_rest", (u1, u3, u0))
     r1, r3 = from_y(u1, NY - 1), from_y(u3, NY - 3)
-    k2a, k2b, u0 = tie((k2a, k2b, u0))
-    far = [k2a, k2b, from_core(k2a), from_core(k2b)]
-    (u2,) = ffn(toks, [far], (0,), e_off, file_len, "ffn_far")
+    (u2,) = ffn(toks + last, [far], (0,), e_off, file_len, "ffn_far")
     r2 = from_y(u2, NY - 2)
     terms = down([u0, r1, r2, r3], w_down, pos, files)
     terms = lax.all_to_all(terms, "mp", 0, 0, tiled=True)

time: 167 us -> 155 us (0.928)
  waiting for transfers between devices: 82.2 us -> 68.5 us
  Pallas kernels: 31.3 us -> 34.6 us
  other arithmetic: 5.14 us -> 3.44 us
    ppermute x3 -> x4, waiting for transfers between devices: 30.4 us -> 24.5 us  [from_x(): return lax.ppermute(v, 'mp', perm)]
    ppermute x7, waiting for transfers between devices: 13.8 us -> 7.9 us  [from_y(): return lax.ppermute(v, 'mp', perm)]
    pallas_call x2 -> x4, Pallas kernels: 20 us -> 23.3 us  [ffn(): pl.pallas_call(functools.partial(ffn_kernel, plan, len(toks), file_len),...]
    ppermute x4, waiting for transfers between devices: 2 us -> 0.01 us  [from_core(): return lax.ppermute(v, 'dp', [(d ^ 1, d) for d in range(NZ * NC)])]
    concatenate x1 -> x2, other arithmetic: 1.97 us -> 0.15 us  [the longest x1 0.08 us: on_device(): rest = jnp.concatenate([near_off, zero])]
    slice x2 -> x4, local copies, waits for them, and re-layouts: 4.08 us -> 2.38 us  [the longest x2 2.3 us: on_device(): k2a, k2b = (from_y(h1[:, :quarter], 1), from_y(h3[:, quarter:], 3))]
    ppermute x3 -> x4, starting transfers between devices: 4.21 us -> 4.64 us  [from_x(): return lax.ppermute(v, 'mp', perm)]
  transfers between devices with their start and end apart: 17 -> 18, of which waited for: 13 -> 10; matrix products, arithmetic and copies ran while one was open for 6% -> 5% of each run, Pallas kernels for 12% -> 16%
where the time goes in v7:
time: 155 us; the launch traced here: 154 us
  waiting for transfers between devices  68.5 us (44%)
  starting transfers between devices  35 us (23%)
  Pallas kernels  34.6 us (22%)
  local copies, waits for them, and re-layouts  9.04 us (6%)
  other arithmetic  3.44 us (2%)
  between operations  3.04 us (2%)
    ppermute x4, waiting for transfers between devices, from_x(): return lax.ppermute(v, 'mp', perm)  24.5 us
    pallas_call x4, Pallas kernels, ffn(): pl.pallas_call(functools.partial(ffn_kernel, plan, len(toks), file_len),...  23.3 us
    all_to_all x1, waiting for transfers between devices, one_round(): rows = lax.all_to_all(rows, ALL, 0, 0, tiled=True)  17.9 us
    all_to_all x1, starting transfers between devices, one_round(): rows = lax.all_to_all(rows, ALL, 0, 0, tiled=True)  10.1 us
    all_to_all x1, waiting for transfers between devices, one_round(): back = lax.all_to_all(top, ALL, 0, 0, tiled=True)  9.11 us
    all_to_all x1, waiting for transfers between devices, on_device(): terms = lax.all_to_all(terms, 'mp', 0, 0, tiled=True)  9.07 us
    ppermute x7, starting transfers between devices, from_y(): return lax.ppermute(v, 'mp', perm)  8.37 us
    ppermute x7, waiting for transfers between devices, from_y(): return lax.ppermute(v, 'mp', perm)  7.9 us
  transfers between devices with their start and end apart: 18, of which 10 were waited for; matrix products, arithmetic and copies ran while one was open for 5% of the time, Pallas kernels for 16%

profile of v7, /device:TPU:1, one launch (start us, length us, event | category | flops | bytes accessed | tf_op | source)
XLA Modules:
  0.0 154.5 jit_solution(11174157592947808125)
XLA Ops:
  3.4 3.6 %collective-permute-start = (bf16[688,1024]{1,0:T(8,128)(2,1)}, bf16[688,1024]{1,0:T(8,128)(2,1)}, u32[]{:S(2)}, u32[]{:S(2)}) collective-permute-start(bf16[688,1024]{1,0:T(8,128)(2,1)} %pad_maximum_fusion), channel_id=1, source_target_pairs={{1,0},{2,1},{3,2},{0,3},{5,4},{6,5},{7,6},{4,7},{9,8},{10,9},{11,1... | collective-permute-start | bytes 4227080 | tf_op jit(solution)/shard_map/ppermute | solution.py:24
  8.1 2.5 %collective-permute-start.2 = (bf16[256,2048]{1,0:T(8,128)(2,1)S(1)}, bf16[256,2048]{1,0:T(8,128)(2,1)S(1)}, u32[]{:S(2)}, u32[]{:S(2)}) collective-permute-start(bf16[256,2048]{1,0:T(8,128)(2,1)S(1)} %get-tuple-element.206.refs_0_), channel_id=1, source_target_pairs={{4,0},{5,1},{6,2},{7,3},{8,4},{9,5},{10,6},{11,7},{12,8},{13,9},{1... | collective-permute-start | bytes 3145736 | tf_op jit(solution)/shard_map/ppermute | solution.py:19
  15.5 16.7 %collective-permute-done.2.refs_1_ = bf16[256,2048]{1,0:T(8,128)(2,1)S(1)} collective-permute-done((bf16[256,2048]{1,0:T(8,128)(2,1)S(1)}, bf16[256,2048]{1,0:T(8,128)(2,1)S(1)}, u32[]{:S(2)}, u32[]{:S(2)}) %collective-permute-start.2) | collective-permute-done | bytes 1048608 | tf_op jit(solution)/shard_map/ppermute | solution.py:19
  32.2 3.2 %collective-permute-done.3.refs_2_ = bf16[256,2048]{1,0:T(8,128)(2,1)S(1)} collective-permute-done((bf16[256,2048]{1,0:T(8,128)(2,1)S(1)}, bf16[256,2048]{1,0:T(8,128)(2,1)S(1)}, u32[]{:S(2)}, u32[]{:S(2)}) %collective-permute-start.3) | collective-permute-done | bytes 1048608 | tf_op jit(solution)/shard_map/ppermute | solution.py:19
  35.4 3.4 %ffn_own.1.refs_9_ = f32[24,344]{1,0:T(8,128)S(1)} custom-call(s32[1]{0:T(128)} %constant.220.clone.1.off_ref, bf16[256,2048]{1,0:T(8,128)(2,1)S(1)} %get-tuple-element.206.refs_0_, bf16[256,2048]{1,0:T(8,128)(2,1)S(1)} %collective-permute-done.2.refs_1_, bf16[256,2048]{1,0:T(8,128)(2,1)S(1)} %collective-permute-done.3.refs_2_, ...), custom_call_target="tpu_custom_call" | custom-call | tf_op jit(solution)/shard_map/ffn_own/pallas_call | solution.py:122
  39.9 1.9 %collective-permute-start.6 = (bf16[688,1024]{1,0:T(8,128)(2,1)}, bf16[688,1024]{1,0:T(8,128)(2,1)S(1)}, u32[]{:S(2)}, u32[]{:S(2)}) collective-permute-start(bf16[688,1024]{1,0:T(8,128)(2,1)} %collective-permute-done.refs_3_.refs_2_), channel_id=1, source_target_pairs={{16,0},{0,16},{48,32},{32,48},{80,64},{64,80},{112,96},{96,112},{1... | collective-permute-start | bytes 4227080 | tf_op jit(solution)/shard_map/ppermute | solution.py:28
  44.1 2.0 %collective-permute-start.4 = (bf16[688,512]{1,0:T(8,128)(2,1)S(1)}, bf16[688,512]{1,0:T(8,128)(2,1)S(1)}, u32[]{:S(2)}, u32[]{:S(2)}) collective-permute-start(bf16[688,512]{1,0:T(8,128)(2,1)S(1)} %slice.42), channel_id=1, source_target_pairs={{1,0},{2,1},{3,2},{0,3},{5,4},{6,5},{7,6},{4,7},{9,8},{10,9},{11,1... | collective-permute-start | bytes 2113544 | tf_op jit(solution)/shard_map/ppermute | solution.py:24
  46.2 2.1 %collective-permute-start.8 = (bf16[128,2048]{1,0:T(8,128)(2,1)S(1)}, bf16[128,2048]{1,0:T(8,128)(2,1)S(1)}, u32[]{:S(2)}, u32[]{:S(2)}) collective-permute-start(bf16[128,2048]{1,0:T(8,128)(2,1)S(1)} %slice.44), channel_id=1, source_target_pairs={{4,0},{5,1},{6,2},{7,3},{8,4},{9,5},{10,6},{11,7},{12,8},{13,9},{1... | collective-permute-start | bytes 1572872 | tf_op jit(solution)/shard_map/ppermute | solution.py:19
  48.3 8.6 %ffn_near.1 = (f32[24,344]{1,0:T(8,128)S(1)}, f32[24,344]{1,0:T(8,128)S(1)}) custom-call(s32[4]{0:T(128)S(1)} %pad_add_fusion.3.off_ref, bf16[256,2048]{1,0:T(8,128)(2,1)S(1)} %get-tuple-element.206.refs_0_, bf16[256,2048]{1,0:T(8,128)(2,1)S(1)} %collective-permute-done.2.refs_1_, bf16[256,2048]{1,0:T(8,128)(2,1)S(1)} %collective-permute-done.3.refs_2_, ...), custom_call_target="tpu_custom_call" | custom-call | tf_op jit(solution)/shard_map/ffn_near/pallas_call | solution.py:122
  56.9 2.1 %collective-permute-done.8.refs_0_.refs_3_ = bf16[128,2048]{1,0:T(8,128)(2,1)S(1)} collective-permute-done((bf16[128,2048]{1,0:T(8,128)(2,1)S(1)}, bf16[128,2048]{1,0:T(8,128)(2,1)S(1)}, u32[]{:S(2)}, u32[]{:S(2)}) %collective-permute-start.8) | collective-permute-done | bytes 524320 | tf_op jit(solution)/shard_map/ppermute | solution.py:19
  59.0 2.5 %collective-permute-done.9.refs_1_.refs_4_ = bf16[128,2048]{1,0:T(8,128)(2,1)S(1)} collective-permute-done((bf16[128,2048]{1,0:T(8,128)(2,1)S(1)}, bf16[128,2048]{1,0:T(8,128)(2,1)S(1)}, u32[]{:S(2)}, u32[]{:S(2)}) %collective-permute-start.9) | collective-permute-done | bytes 524320 | tf_op jit(solution)/shard_map/ppermute | solution.py:19
  61.5 2.4 %collective-permute-done.5.refs_6_ = bf16[688,512]{1,0:T(8,128)(2,1)S(1)} collective-permute-done((bf16[688,512]{1,0:T(8,128)(2,1)S(1)}, bf16[688,512]{1,0:T(8,128)(2,1)S(1)}, u32[]{:S(2)}, u32[]{:S(2)}) %collective-permute-start.5) | collective-permute-done | bytes 704544 | tf_op jit(solution)/shard_map/ppermute | solution.py:24
  65.6 6.6 %ffn_rest.1 = (f32[32,344]{1,0:T(8,128)S(1)}, f32[32,344]{1,0:T(8,128)S(1)}, f32[32,344]{1,0:T(8,128)S(1)}) custom-call(s32[5]{0:T(128)S(1)} %pad_add_fusion.2.off_ref, bf16[128,2048]{1,0:T(8,128)(2,1)S(1)} %collective-permute-done.8.refs_0_.refs_3_, bf16[128,2048]{1,0:T(8,128)(2,1)S(1)} %collective-permute-done.9.refs_1_.refs_4_, ...), custom_call_target="tpu_custom_call" | custom-call | tf_op jit(solution)/shard_map/ffn_rest/pallas_call | solution.py:122
  72.3 2.7 %collective-permute-start.14 = (f32[32,344]{1,0:T(8,128)S(1)}, f32[32,344]{1,0:T(8,128)S(1)}, u32[]{:S(2)}, u32[]{:S(2)}) collective-permute-start(f32[32,344]{1,0:T(8,128)S(1)} %get-tuple-element.225), channel_id=1, source_target_pairs={{1,0},{2,1},{3,2},{0,3},{5,4},{6,5},{7,6},{4,7},{9,8},{10,9},{11,1... | collective-permute-start | bytes 132104 | tf_op jit(solution)/shard_map/ppermute | solution.py:24
  75.0 4.7 %ffn_far.1 = f32[32,344]{1,0:T(8,128)S(1)} custom-call(s32[4]{0:T(128)S(1)} %pad_add_fusion.off_ref, bf16[256,2048]{1,0:T(8,128)(2,1)S(1)} %get-tuple-element.206.refs_0_, bf16[256,2048]{1,0:T(8,128)(2,1)S(1)} %collective-permute-done.2.refs_1_, bf16[256,2048]{1,0:T(8,128)(2,1)S(1)} %collective-permute-done.3.refs_2_, ...), custom_call_target="tpu_custom_call" | custom-call | tf_op jit(solution)/shard_map/ffn_far/pallas_call | solution.py:122
  79.8 4.4 %collective-permute-done.13.u2 = f32[32,344]{1,0:T(8,128)S(1)} collective-permute-done((f32[32,344]{1,0:T(8,128)S(1)}, f32[32,344]{1,0:T(8,128)S(1)}, u32[]{:S(2)}, u32[]{:S(2)}) %collective-permute-start.13) | collective-permute-done | bytes 44064 | tf_op jit(solution)/shard_map/ppermute | solution.py:24
  84.2 2.1 %down.1 = bf16[16,8,2048]{2,1,0:T(8,128)(2,1)} custom-call(s32[16]{0:T(128)S(1)} %stack.107.pos_ref, f32[32,344]{1,0:T(8,128)S(1)} %get-tuple-element.220.u0, f32[32,344]{1,0:T(8,128)S(1)} %collective-permute-done.10.u1, f32[32,344]{1,0:T(8,128)S(1)} %collective-permute-done.13.u2, f32[32,344]{1,0:T(8,128)S(1)} %collective-permute-done.14.u3, ...), custom_call_target="tpu_custom_call" | custom-call | tf_op jit(solution)/shard_map/down/pallas_call | solution.py:154
  86.2 3.6 %all-to-all-start.2 = ((bf16[16,8,2048]{2,1,0:T(8,128)(2,1)}), bf16[16,8,2048]{2,1,0:T(8,128)(2,1)S(1)}, u32[]{:S(2)}, u32[]{:S(2)}) async-start(bf16[16,8,2048]{2,1,0:T(8,128)(2,1)} %down.1), calls=%async_computation.2 | async-start | bytes 1048576 | tf_op jit(solution)/shard_map/all_to_all | solution.py:327
  89.9 9.1 %all-to-all-done.2.t_ref = bf16[16,8,2048]{2,1,0:T(8,128)(2,1)S(1)} async-done(((bf16[16,8,2048]{2,1,0:T(8,128)(2,1)}), bf16[16,8,2048]{2,1,0:T(8,128)(2,1)S(1)}, u32[]{:S(2)}, u32[]{:S(2)}) %all-to-all-start.2) | async-done | bytes 524320 | tf_op jit(solution)/shard_map/all_to_all | solution.py:327
  100.4 10.1 %all-to-all-start.3 = ((bf16[128,2,2176]{2,1,0:T(2,128)(2,1)}), bf16[128,2,2176]{2,1,0:T(2,128)(2,1)}, u32[]{:S(2)}, u32[]{:S(2)}) async-start(bf16[128,2,2176]{2,1,0:T(2,128)(2,1)} %emb.5), calls=%async_computation.3 | async-start | bytes 2228224 | tf_op jit(solution)/shard_map/all_to_all | solution.py:332
  111.5 17.9 %all-to-all-done.3 = bf16[128,2,2176]{2,1,0:T(2,128)(2,1)} async-done(((bf16[128,2,2176]{2,1,0:T(2,128)(2,1)}), bf16[128,2,2176]{2,1,0:T(2,128)(2,1)}, u32[]{:S(2)}, u32[]{:S(2)}) %all-to-all-start.3) | async-done | bytes 1114144 | tf_op jit(solution)/shard_map/all_to_all | solution.py:332
  130.9 6.8 %match.5 = (f32[128,1,128]{2,1,0:T(1,128)}, f32[8,2048]{1,0:T(8,128)S(1)}, f32[1,128]{1,0:T(1,128)S(1)}) custom-call(s32[1]{0:T(128)} %bitcast.33.mp_ref, bf16[256,2176]{1,0:T(8,128)(2,1)S(1)} %reshape.192.rows_ref, bf16[2048,2048]{1,0:T(8,128)(2,1)} %bank_ref.1, f32[2048,1]{1,0:T(8,128)S(1)} %copy.55.key_ref), custom_call_target="tpu_custom_call" | custom-call | tf_op jit(solution)/shard_map/match/pallas_call | solution.py:227
  137.7 4.9 %all-to-all-start.4 = ((f32[128,1,128]{2,1,0:T(1,128)}), f32[128,1,128]{2,1,0:T(1,128)S(1)}, u32[]{:S(2)}, u32[]{:S(2)}) async-start(f32[128,1,128]{2,1,0:T(1,128)} %get-tuple-element.231), calls=%async_computation.4 | async-start | bytes 131072 | tf_op jit(solution)/shard_map/all_to_all | solution.py:334
  143.2 9.1 %all-to-all-done.4 = f32[128,1,128]{2,1,0:T(1,128)S(1)} async-done(((f32[128,1,128]{2,1,0:T(1,128)}), f32[128,1,128]{2,1,0:T(1,128)S(1)}, u32[]{:S(2)}, u32[]{:S(2)}) %all-to-all-start.4) | async-done | bytes 65568 | tf_op jit(solution)/shard_map/all_to_all | solution.py:334
  (94 shorter events, 18.7 us)
Async XLA Ops:
  2.1 8.6 %copy-start.11 = (s32[128]{0:T(128)S(1)}, s32[128]{0:T(128)}, u32[]{:S(2)}) copy-start(s32[128]{0:T(128)} %param.24) | copy-start | bytes 1540
  2.1 8.6 %copy-start.12 = (s32[8]{0:T(128)S(1)}, s32[8]{0:T(128)}, u32[]{:S(2)}) copy-start(s32[8]{0:T(128)} %param.22) | copy-start | bytes 100
  2.1 8.7 %copy-start.10 = (s32[8]{0:T(128)S(1)}, s32[8]{0:T(128)}, u32[]{:S(2)}) copy-start(s32[8]{0:T(128)} %param.23) | copy-start | bytes 100
  3.4 10.2 %copy-start.6 = (s32[2048]{0:T(1024)S(1)}, s32[2048]{0:T(1024)}, u32[]{:S(2)}) copy-start(s32[2048]{0:T(1024)} %param.27) | copy-start | bytes 24580
  3.4 10.2 %copy-start.7 = (s32[2048]{0:T(1024)S(1)}, s32[2048]{0:T(1024)}, u32[]{:S(2)}) copy-start(s32[2048]{0:T(1024)} %param.26) | copy-start | bytes 24580
  3.4 35.4 %collective-permute-start = (bf16[688,1024]{1,0:T(8,128)(2,1)}, bf16[688,1024]{1,0:T(8,128)(2,1)}, u32[]{:S(2)}, u32[]{:S(2)}) collective-permute-start(bf16[688,1024]{1,0:T(8,128)(2,1)} %pad_maximum_fusion), channel_id=1, source_target_pairs={{1,0},{2,1},{3,2},{0,3},{5,4},{6,5},{7,6},{4,7},{9,8},{10,9},{11,1... | collective-permute-start | bytes 4227080 | tf_op jit(solution)/shard_map/ppermute | solution.py:24
  6.9 33.0 %collective-permute-start.1 = (bf16[688,1024]{1,0:T(8,128)(2,1)}, bf16[688,1024]{1,0:T(8,128)(2,1)}, u32[]{:S(2)}, u32[]{:S(2)}) collective-permute-start(bf16[688,1024]{1,0:T(8,128)(2,1)} %pad_maximum_fusion), channel_id=1, source_target_pairs={{3,0},{0,1},{1,2},{2,3},{7,4},{4,5},{5,6},{6,7},{11,8},{8,9},{9,10... | collective-permute-start | bytes 4227080 | tf_op jit(solution)/shard_map/ppermute | solution.py:24
  8.1 24.1 %collective-permute-start.2 = (bf16[256,2048]{1,0:T(8,128)(2,1)S(1)}, bf16[256,2048]{1,0:T(8,128)(2,1)S(1)}, u32[]{:S(2)}, u32[]{:S(2)}) collective-permute-start(bf16[256,2048]{1,0:T(8,128)(2,1)S(1)} %get-tuple-element.206.refs_0_), channel_id=1, source_target_pairs={{4,0},{5,1},{6,2},{7,3},{8,4},{9,5},{10,6},{11,7},{12,8},{13,9},{1... | collective-permute-start | bytes 3145736 | tf_op jit(solution)/shard_map/ppermute | solution.py:19
  10.7 24.7 %collective-permute-start.3 = (bf16[256,2048]{1,0:T(8,128)(2,1)S(1)}, bf16[256,2048]{1,0:T(8,128)(2,1)S(1)}, u32[]{:S(2)}, u32[]{:S(2)}) collective-permute-start(bf16[256,2048]{1,0:T(8,128)(2,1)S(1)} %get-tuple-element.206.refs_0_), channel_id=1, source_target_pairs={{12,0},{13,1},{14,2},{15,3},{0,4},{1,5},{2,6},{3,7},{4,8},{5,9},{6... | collective-permute-start | bytes 3145736 | tf_op jit(solution)/shard_map/ppermute | solution.py:19
  39.9 8.4 %collective-permute-start.6 = (bf16[688,1024]{1,0:T(8,128)(2,1)}, bf16[688,1024]{1,0:T(8,128)(2,1)S(1)}, u32[]{:S(2)}, u32[]{:S(2)}) collective-permute-start(bf16[688,1024]{1,0:T(8,128)(2,1)} %collective-permute-done.refs_3_.refs_2_), channel_id=1, source_target_pairs={{16,0},{0,16},{48,32},{32,48},{80,64},{64,80},{112,96},{96,112},{1... | collective-permute-start | bytes 4227080 | tf_op jit(solution)/shard_map/ppermute | solution.py:28
  41.8 6.6 %collective-permute-start.7 = (bf16[688,1024]{1,0:T(8,128)(2,1)}, bf16[688,1024]{1,0:T(8,128)(2,1)S(1)}, u32[]{:S(2)}, u32[]{:S(2)}) collective-permute-start(bf16[688,1024]{1,0:T(8,128)(2,1)} %collective-permute-done.1.refs_5_.refs_4_), channel_id=1, source_target_pairs={{16,0},{0,16},{48,32},{32,48},{80,64},{64,80},{112,96},{96,112},{1... | collective-permute-start | bytes 4227080 | tf_op jit(solution)/shard_map/ppermute | solution.py:28
  44.1 17.5 %collective-permute-start.4 = (bf16[688,512]{1,0:T(8,128)(2,1)S(1)}, bf16[688,512]{1,0:T(8,128)(2,1)S(1)}, u32[]{:S(2)}, u32[]{:S(2)}) collective-permute-start(bf16[688,512]{1,0:T(8,128)(2,1)S(1)} %slice.42), channel_id=1, source_target_pairs={{1,0},{2,1},{3,2},{0,3},{5,4},{6,5},{7,6},{4,7},{9,8},{10,9},{11,1... | collective-permute-start | bytes 2113544 | tf_op jit(solution)/shard_map/ppermute | solution.py:24
  46.1 17.8 %collective-permute-start.5 = (bf16[688,512]{1,0:T(8,128)(2,1)S(1)}, bf16[688,512]{1,0:T(8,128)(2,1)S(1)}, u32[]{:S(2)}, u32[]{:S(2)}) collective-permute-start(bf16[688,512]{1,0:T(8,128)(2,1)S(1)} %slice.43), channel_id=1, source_target_pairs={{3,0},{0,1},{1,2},{2,3},{7,4},{4,5},{5,6},{6,7},{11,8},{8,9},{9,10... | collective-permute-start | bytes 2113544 | tf_op jit(solution)/shard_map/ppermute | solution.py:24
  46.2 12.8 %collective-permute-start.8 = (bf16[128,2048]{1,0:T(8,128)(2,1)S(1)}, bf16[128,2048]{1,0:T(8,128)(2,1)S(1)}, u32[]{:S(2)}, u32[]{:S(2)}) collective-permute-start(bf16[128,2048]{1,0:T(8,128)(2,1)S(1)} %slice.44), channel_id=1, source_target_pairs={{4,0},{5,1},{6,2},{7,3},{8,4},{9,5},{10,6},{11,7},{12,8},{13,9},{1... | collective-permute-start | bytes 1572872 | tf_op jit(solution)/shard_map/ppermute | solution.py:19
  48.3 13.3 %collective-permute-start.9 = (bf16[128,2048]{1,0:T(8,128)(2,1)S(1)}, bf16[128,2048]{1,0:T(8,128)(2,1)S(1)}, u32[]{:S(2)}, u32[]{:S(2)}) collective-permute-start(bf16[128,2048]{1,0:T(8,128)(2,1)S(1)} %slice.45), channel_id=1, source_target_pairs={{12,0},{13,1},{14,2},{15,3},{0,4},{1,5},{2,6},{3,7},{4,8},{5,9},{6... | collective-permute-start | bytes 1572872 | tf_op jit(solution)/shard_map/ppermute | solution.py:19
  63.9 11.1 %collective-permute-start.11 = (bf16[688,512]{1,0:T(8,128)(2,1)S(1)}, bf16[688,512]{1,0:T(8,128)(2,1)S(1)}, u32[]{:S(2)}, u32[]{:S(2)}) collective-permute-start(bf16[688,512]{1,0:T(8,128)(2,1)S(1)} %collective-permute-done.4.refs_5_), channel_id=1, source_target_pairs={{16,0},{0,16},{48,32},{32,48},{80,64},{64,80},{112,96},{96,112},{1... | collective-permute-start | bytes 2113544 | tf_op jit(solution)/shard_map/ppermute | solution.py:28
  65.5 9.5 %collective-permute-start.12 = (bf16[688,512]{1,0:T(8,128)(2,1)S(1)}, bf16[688,512]{1,0:T(8,128)(2,1)S(1)}, u32[]{:S(2)}, u32[]{:S(2)}) collective-permute-start(bf16[688,512]{1,0:T(8,128)(2,1)S(1)} %collective-permute-done.5.refs_6_), channel_id=1, source_target_pairs={{16,0},{0,16},{48,32},{32,48},{80,64},{64,80},{112,96},{96,112},{1... | collective-permute-start | bytes 2113544 | tf_op jit(solution)/shard_map/ppermute | solution.py:28
  72.2 7.5 %collective-permute-start.10 = (f32[32,344]{1,0:T(8,128)S(1)}, f32[32,344]{1,0:T(8,128)S(1)}, u32[]{:S(2)}, u32[]{:S(2)}) collective-permute-start(f32[32,344]{1,0:T(8,128)S(1)} %get-tuple-element.221), channel_id=1, source_target_pairs={{3,0},{0,1},{1,2},{2,3},{7,4},{4,5},{5,6},{6,7},{11,8},{8,9},{9,10... | collective-permute-start | bytes 132104 | tf_op jit(solution)/shard_map/ppermute | solution.py:24
  72.3 11.9 %copy-start = (bf16[344,2048]{1,0:T(8,128)(2,1)S(1)}, bf16[344,2048]{1,0:T(8,128)(2,1)}, u32[]{:S(2)}) copy-start(bf16[344,2048]{1,0:T(8,128)(2,1)} %w_ref.1) | copy-start | bytes 4227076
  72.3 7.4 %collective-permute-start.14 = (f32[32,344]{1,0:T(8,128)S(1)}, f32[32,344]{1,0:T(8,128)S(1)}, u32[]{:S(2)}, u32[]{:S(2)}) collective-permute-start(f32[32,344]{1,0:T(8,128)S(1)} %get-tuple-element.225), channel_id=1, source_target_pairs={{1,0},{2,1},{3,2},{0,3},{5,4},{6,5},{7,6},{4,7},{9,8},{10,9},{11,1... | collective-permute-start | bytes 132104 | tf_op jit(solution)/shard_map/ppermute | solution.py:24
  79.6 4.5 %collective-permute-start.13 = (f32[32,344]{1,0:T(8,128)S(1)}, f32[32,344]{1,0:T(8,128)S(1)}, u32[]{:S(2)}, u32[]{:S(2)}) collective-permute-start(f32[32,344]{1,0:T(8,128)S(1)} %ffn_far.1), channel_id=1, source_target_pairs={{2,0},{3,1},{0,2},{1,3},{6,4},{7,5},{4,6},{5,7},{10,8},{11,9},{8,1... | collective-permute-start | bytes 132104 | tf_op jit(solution)/shard_map/ppermute | solution.py:24
  86.2 12.7 %all-to-all-start.2 = ((bf16[16,8,2048]{2,1,0:T(8,128)(2,1)}), bf16[16,8,2048]{2,1,0:T(8,128)(2,1)S(1)}, u32[]{:S(2)}, u32[]{:S(2)}) async-start(bf16[16,8,2048]{2,1,0:T(8,128)(2,1)} %down.1), calls=%async_computation.2 | async-start | bytes 1048576 | tf_op jit(solution)/shard_map/all_to_all | solution.py:327
  100.4 29.1 %all-to-all-start.3 = ((bf16[128,2,2176]{2,1,0:T(2,128)(2,1)}), bf16[128,2,2176]{2,1,0:T(2,128)(2,1)}, u32[]{:S(2)}, u32[]{:S(2)}) async-start(bf16[128,2,2176]{2,1,0:T(2,128)(2,1)} %emb.5), calls=%async_computation.3 | async-start | bytes 2228224 | tf_op jit(solution)/shard_map/all_to_all | solution.py:332
  137.7 14.6 %all-to-all-start.4 = ((f32[128,1,128]{2,1,0:T(1,128)}), f32[128,1,128]{2,1,0:T(1,128)S(1)}, u32[]{:S(2)}, u32[]{:S(2)}) async-start(f32[128,1,128]{2,1,0:T(1,128)} %get-tuple-element.231), calls=%async_computation.4 | async-start | bytes 131072 | tf_op jit(solution)/shard_map/all_to_all | solution.py:334
  (6 other events, 19.1 us)

commit v8 on v7

--- a/solution.py
+++ b/solution.py
@@ -60,6 +60,31 @@
         compiler_params=pltpu.CompilerParams(vmem_limit_bytes=16 * 1024 * 1024),
         name="prep",
     )(lengths, hidden, gain[None, :])
+
+
+def cut_kernel(a_ref, b_ref, left_ref, right_ref, sem):
+    cols = left_ref.shape[1]
+    copies = [
+        pltpu.make_async_copy(a_ref.at[:, pl.ds(0, cols)], left_ref, sem.at[0]),
+        pltpu.make_async_copy(b_ref.at[:, pl.ds(cols, cols)], right_ref, sem.at[1]),
+    ]
+    for cp in copies:
+        cp.start()
+    for cp in copies:
+        cp.wait()
+
+
+def cut_halves(a, b):
+    hbm = pl.BlockSpec(memory_space=pl.ANY)
+    out = jax.ShapeDtypeStruct((a.shape[0], a.shape[1] // 2), a.dtype)
+    return pl.pallas_call(
+        cut_kernel,
+        in_specs=[hbm, hbm],
+        out_specs=(hbm, hbm),
+        out_shape=(out, out),
+        scratch_shapes=[pltpu.SemaphoreType.DMA((2,))],
+        name="cut",
+    )(a, b)
 
 
 def ffn_kernel(plan, n_tok, file_len, off_ref, *refs):
@@ -197,29 +222,27 @@
         at = pl.ds(i * block, block)
         copies.append(pltpu.make_async_copy(bank_ref.at[at], buf.at[at], sem.at[i]))
         copies[-1].start()
-    rows, about = rows_ref[:, :width], rows_ref[:, width:]
+    rows = rows_ref[:, :width]
     n = rows.shape[0]
-    pick = lax.broadcasted_iota(I32, (8, 128), 0) == lax.broadcasted_iota(I32, (8, 128), 1)
-    digits = lax.dot_general(jnp.where(pick, 1.0, 0.0).astype(BF), about, NT, preferred_element_type=F32)
-    low = digits[0:1] * 65536.0 + digits[1:2] * 256.0 + digits[2:3]
-    high = digits[3:4] * 65536.0 + digits[4:5] * 256.0 + digits[5:6]
-    mine = digits[6:7] == (mp_ref[0] + 1).astype(F32)
-    member = jnp.broadcast_to(jnp.where(mine, 1.0, 0.0), (8, n)).astype(BF)
-    sums_ref[...] = jnp.dot(member, rows, preferred_element_type=F32)
-    count = jnp.sum(jnp.where(mine, 1.0, 0.0), axis=1, keepdims=True)
-    most = jnp.max(digits[7:8], axis=1, keepdims=True)
+    digits = rows_ref[:, width:].astype(F32)
+    low = digits[:, 0:1] * 65536.0 + digits[:, 1:2] * 256.0 + digits[:, 2:3]
+    high = digits[:, 3:4] * 65536.0 + digits[:, 4:5] * 256.0 + digits[:, 5:6]
+    mine = jnp.where(digits[:, 6:7] == (mp_ref[0] + 1).astype(F32), 1.0, 0.0)
+    member = jnp.broadcast_to(mine, (n, 8)).astype(BF)
+    sums_ref[...] = lax.dot_general(member, rows, (((0,), (0,)), ((), ())), preferred_element_type=F32)
+    count = jnp.sum(mine, axis=0, keepdims=True)
+    most = jnp.max(digits[:, 7:8], axis=0, keepdims=True)
     about_ref[...] = jnp.where(lax.broadcasted_iota(I32, (1, 128), 1) == 0, count, most)
-    for cp in copies:
-        cp.wait()
-    sims = lax.dot_general(buf[...], rows, NT, preferred_element_type=F32)
-    key = key_ref[...]
-    best = jnp.max(jnp.where((key >= low) & (key < high), sims, -1.0), axis=0, keepdims=True)
-    n //= 2
-    row, lane = (lax.broadcasted_iota(I32, (n, 2 * n), d) for d in (0, 1))
-    best = jnp.broadcast_to(best, (n, 2 * n))
-    pair = [jnp.max(jnp.where(lane == 2 * row + i, best, -1.0), axis=1, keepdims=True) for i in (0, 1)]
-    out_lane = lax.broadcasted_iota(I32, (n, 128), 1)
-    best_ref[:, 0, :] = jnp.where(out_lane == 0, pair[0], pair[1])
+    best = jnp.full((n, 1), -1.0, F32)
+    block *= n_blocks // 2
+    for i in range(2):
+        for cp in copies[i * n_blocks // 2:(i + 1) * n_blocks // 2]:
+            cp.wait()
+        at = slice(i * block, (i + 1) * block)
+        sims = lax.dot_general(rows, buf[at, :], NT, preferred_element_type=F32)
+        key = key_ref[:, at]
+        best = jnp.maximum(best, jnp.max(jnp.where((key >= low) & (key < high), sims, -1.0), axis=1, keepdims=True))
+    best_ref[:, 0, :] = jnp.broadcast_to(best, (n, 128))
 
 
 def match(rows, mp, bank, key):
@@ -229,7 +252,7 @@
         in_specs=[pl.BlockSpec(memory_space=pltpu.SMEM), vm, pl.BlockSpec(memory_space=pl.ANY), vm],
         out_specs=(vm, vm, vm),
         out_shape=(
-            jax.ShapeDtypeStruct((rows.shape[0] // 2, 1, 128), F32),
+            jax.ShapeDtypeStruct((rows.shape[0], 1, 128), F32),
             jax.ShapeDtypeStruct((8, bank.shape[1]), F32),
             jax.ShapeDtypeStruct((1, 128), F32),
         ),
@@ -276,7 +299,7 @@
     local = slot % owned
     first = local * ORDERS
     key = first + file_order
-    bank_key = (bank_slot * ORDERS + bank_order).astype(F32)[:, None]
+    bank_key = (bank_slot * ORDERS + bank_order).astype(F32)[None, :]
     low_key, high_key = [first >> 16, first * 0, first * 0], [key >> 16, (key >> 8) & 255, key & 255]
     digits = jnp.stack(low_key + high_key + [local + 1, jnp.broadcast_to(jnp.max(rank) + 1, slot.shape)], axis=1)
 
@@ -311,7 +334,8 @@
     zero = jnp.zeros((1,), I32)
     (u0,) = ffn(toks, [[w_own]], (0,), zero, file_len, "ffn_own")
     h1, h3, u0 = tie((h1, h3, u0))
-    k2a, k2b = from_y(h1[:, :quarter], 1), from_y(h3[:, quarter:], 3)
+    left, right = cut_halves(h1, h3)
+    k2a, k2b = from_y(left, 1), from_y(right, 3)
     near = [[h1, from_core(h1)], [h3, from_core(h3)]]
     near_off = jnp.concatenate([h_off, h_off])
     u1, u3 = ffn(toks, near, (0, 0), near_off, file_len, "ffn_near")
@@ -326,23 +350,25 @@
     terms = down([u0, r1, r2, r3], w_down, pos, files)
     terms = lax.all_to_all(terms, "mp", 0, 0, tiled=True)
 
-    def one_round(ready, best, sums, counts):
+    def one_round(ready, best, sums, counts, _):
         here, sel, meta = ready
         rows = emb_to_owners(terms, pooled_in, lens, sel, meta, n_mp)
         rows = lax.all_to_all(rows, ALL, 0, 0, tiled=True)
         top, new, about = match(rows.reshape(-1, rows.shape[2]), mp, bank, bank_key)
+        sums, counts = sums + new[:1], counts + about[0, 0]
+        centroid = (count_old[:, None] * centroid_old + sums) / (count_old + counts)[:, None]
         back = lax.all_to_all(top, ALL, 0, 0, tiled=True)
-        back = jnp.max(back.reshape(n_dp, n_mp, -1), axis=1)[:, :2]
+        back = jnp.max(back.reshape(n_dp, n_mp, 2, -1), axis=1)[:, :, 0]
         best = jnp.maximum(best, jnp.max(jnp.where(here, back[:, :, None], -1.0), axis=(0, 1)))
-        return about[0, 1], (best, sums + new[:1], counts + about[0, 0])
-
-    most, state = one_round(ready, jnp.full((files,), -1.0, F32), jnp.zeros((1, width), F32), jnp.float32(0))
-    _, (best, sums, counts) = lax.while_loop(
+        return about[0, 1], (best, sums, counts, centroid)
+
+    blank = jnp.zeros((1, width), F32)
+    most, state = one_round(ready, jnp.full((files,), -1.0, F32), blank, jnp.float32(0), blank)
+    _, (best, _, _, centroid_new) = lax.while_loop(
         lambda s: 2 * s[0] < most.astype(I32),
         lambda s: (s[0] + 1, one_round(files_of(s[0]), *s[1])[1]),
         (jnp.int32(1), state),
     )
-    centroid_new = (count_old[:, None] * centroid_old + sums) / (count_old + counts)[:, None]
     return best, centroid_new
 
 

time: 155 us -> 202 us (1.30)
  Pallas kernels: 34.6 us -> 84 us
  waiting for transfers between devices: 68.5 us -> 64.5 us
    pallas_call x0 -> x1, Pallas kernels: none -> 43.8 us  [cut_halves(): pl.pallas_call(cut_kernel, in_specs=[hbm, hbm], out_specs=(hbm, hbm), out...]
    ppermute x4, waiting for transfers between devices: 24.5 us -> 15.6 us  [from_x(): return lax.ppermute(v, 'mp', perm)]
    pallas_call x4, Pallas kernels: 23.3 us -> 28.7 us  [ffn(): pl.pallas_call(functools.partial(ffn_kernel, plan, len(toks), file_len),...]
    ppermute x7, waiting for transfers between devices: 7.9 us -> 11.5 us  [from_y(): return lax.ppermute(v, 'mp', perm)]
    slice x4 -> x2, local copies, waits for them, and re-layouts: 2.9 us -> 0.71 us  [the longest x1 0.61 us: one_round(): return (about[0, 1], (best, sums, counts, centroid))]
    slice x2, local copies, waits for them, and re-layouts: 0.08 us -> 2.16 us  [on_device(): t2a, t2b = (from_x(t1[:tok // 2], 1), from_x(t3[tok // 2:], 3))]
  transfers between devices with their start and end apart: 18 -> 18, of which waited for: 10 -> 8; matrix products, arithmetic and copies ran while one was open for 5% -> 3% of each run, Pallas kernels for 16% -> 36%
where the time goes in v8:
time: 202 us; the launch traced here: 201 us
  Pallas kernels  84 us (42%)
  waiting for transfers between devices  64.5 us (32%)
  starting transfers between devices  36.5 us (18%)
  local copies, waits for them, and re-layouts  9.12 us (5%)
  other arithmetic  3.5 us (2%)
  between operations  3.03 us (2%)
    pallas_call x1, Pallas kernels, cut_halves(): pl.pallas_call(cut_kernel, in_specs=[hbm, hbm], out_specs=(hbm, hbm), out...  43.8 us
    pallas_call x4, Pallas kernels, ffn(): pl.pallas_call(functools.partial(ffn_kernel, plan, len(toks), file_len),...  28.7 us
    all_to_all x1, waiting for transfers between devices, one_round(): rows = lax.all_to_all(rows, ALL, 0, 0, tiled=True)  18.6 us
    ppermute x4, waiting for transfers between devices, from_x(): return lax.ppermute(v, 'mp', perm)  15.6 us
    ppermute x7, waiting for transfers between devices, from_y(): return lax.ppermute(v, 'mp', perm)  11.5 us
    all_to_all x1, starting transfers between devices, one_round(): rows = lax.all_to_all(rows, ALL, 0, 0, tiled=True)  9.65 us
    all_to_all x1, waiting for transfers between devices, one_round(): back = lax.all_to_all(top, ALL, 0, 0, tiled=True)  9.57 us
    all_to_all x1, waiting for transfers between devices, on_device(): terms = lax.all_to_all(terms, 'mp', 0, 0, tiled=True)  9.13 us
  transfers between devices with their start and end apart: 18, of which 8 were waited for; matrix products, arithmetic and copies ran while one was open for 3% of the time, Pallas kernels for 36%

profile of v8, /device:TPU:1, one launch (start us, length us, event | category | flops | bytes accessed | tf_op | source)
XLA Modules:
  0.0 201.4 jit_solution(9100486007921767182)
XLA Ops:
  4.3 2.1 %prep.1 = (bf16[256,2048]{1,0:T(8,128)(2,1)}, f32[8,2048]{1,0:T(8,128)S(1)}) custom-call(s32[8]{0:T(128)S(1)} %copy-done.2, bf16[256,2048]{1,0:T(8,128)(2,1)S(1)} %copy-done.1, bf16[1,2048]{1,0:T(2,128)(2,1)S(1)} %broadcast_in_dim.131.gain_ref), custom_call_target="tpu_custom_call" | custom-call | tf_op jit(solution)/shard_map/prep/pallas_call | solution.py:55
  6.4 2.0 %collective-permute-start.3 = (bf16[256,2048]{1,0:T(8,128)(2,1)}, bf16[256,2048]{1,0:T(8,128)(2,1)}, u32[]{:S(2)}, u32[]{:S(2)}) collective-permute-start(bf16[256,2048]{1,0:T(8,128)(2,1)} %get-tuple-element.239.refs_0_), channel_id=1, source_target_pairs={{12,0},{13,1},{14,2},{15,3},{0,4},{1,5},{2,6},{3,7},{4,8},{5,9},{6... | collective-permute-start | bytes 3145736 | tf_op jit(solution)/shard_map/ppermute | solution.py:19
  17.7 14.8 %collective-permute-done.3.refs_2_ = bf16[256,2048]{1,0:T(8,128)(2,1)} collective-permute-done((bf16[256,2048]{1,0:T(8,128)(2,1)}, bf16[256,2048]{1,0:T(8,128)(2,1)}, u32[]{:S(2)}, u32[]{:S(2)}) %collective-permute-start.3) | collective-permute-done | bytes 1048608 | tf_op jit(solution)/shard_map/ppermute | solution.py:19
  32.5 5.0 %ffn_own.1.refs_9_ = f32[24,344]{1,0:T(8,128)S(1)} custom-call(s32[1]{0:T(128)} %constant.220.clone.1.off_ref, bf16[256,2048]{1,0:T(8,128)(2,1)} %get-tuple-element.239.refs_0_, bf16[256,2048]{1,0:T(8,128)(2,1)} %collective-permute-done.2.refs_1_, bf16[256,2048]{1,0:T(8,128)(2,1)} %collective-permute-done.3.refs_2_, ...), custom_call_target="tpu_custom_call" | custom-call | tf_op jit(solution)/shard_map/ffn_own/pallas_call | solution.py:147
  37.5 5.3 %collective-permute-done.1.b_ref.refs_5_.refs_4_ = bf16[688,1024]{1,0:T(8,128)(2,1)} collective-permute-done((bf16[688,1024]{1,0:T(8,128)(2,1)}, bf16[688,1024]{1,0:T(8,128)(2,1)}, u32[]{:S(2)}, u32[]{:S(2)}) %collective-permute-start.1) | collective-permute-done | bytes 1409056 | tf_op jit(solution)/shard_map/ppermute | solution.py:24
  42.8 2.0 %collective-permute-start.6 = (bf16[688,1024]{1,0:T(8,128)(2,1)}, bf16[688,1024]{1,0:T(8,128)(2,1)}, u32[]{:S(2)}, u32[]{:S(2)}) collective-permute-start(bf16[688,1024]{1,0:T(8,128)(2,1)} %collective-permute-done.a_ref.refs_3_.refs_2_), channel_id=1, source_target_pairs={{16,0},{0,16},{48,32},{32,48},{80,64},{64,80},{112,96},{96,112},{1... | collective-permute-start | bytes 4227080 | tf_op jit(solution)/shard_map/ppermute | solution.py:28
  44.9 43.8 %cut.1 = (bf16[688,512]{1,0:T(8,128)(2,1)}, bf16[688,512]{1,0:T(8,128)(2,1)}) custom-call(bf16[688,1024]{1,0:T(8,128)(2,1)} %collective-permute-done.a_ref.refs_3_.refs_2_, bf16[688,1024]{1,0:T(8,128)(2,1)} %collective-permute-done.1.b_ref.refs_5_.refs_4_), custom_call_target="tpu_custom_call" | custom-call | tf_op jit(solution)/shard_map/cut/pallas_call | solution.py:80
  88.7 2.7 %collective-permute-start.4 = (bf16[688,512]{1,0:T(8,128)(2,1)}, bf16[688,512]{1,0:T(8,128)(2,1)S(1)}, u32[]{:S(2)}, u32[]{:S(2)}) collective-permute-start(bf16[688,512]{1,0:T(8,128)(2,1)} %get-tuple-element.246), channel_id=1, source_target_pairs={{1,0},{2,1},{3,2},{0,3},{5,4},{6,5},{7,6},{4,7},{9,8},{10,9},{11,1... | collective-permute-start | bytes 2113544 | tf_op jit(solution)/shard_map/ppermute | solution.py:24
  93.7 2.7 %collective-permute-start.8 = (bf16[128,2048]{1,0:T(8,128)(2,1)S(1)}, bf16[128,2048]{1,0:T(8,128)(2,1)S(1)}, u32[]{:S(2)}, u32[]{:S(2)}) collective-permute-start(bf16[128,2048]{1,0:T(8,128)(2,1)S(1)} %slice.36), channel_id=1, source_target_pairs={{4,0},{5,1},{6,2},{7,3},{8,4},{9,5},{10,6},{11,7},{12,8},{13,9},{1... | collective-permute-start | bytes 1572872 | tf_op jit(solution)/shard_map/ppermute | solution.py:19
  96.4 10.3 %ffn_near.1 = (f32[24,344]{1,0:T(8,128)S(1)}, f32[24,344]{1,0:T(8,128)S(1)}) custom-call(s32[4]{0:T(128)S(1)} %pad_add_fusion.3.off_ref, bf16[256,2048]{1,0:T(8,128)(2,1)} %get-tuple-element.239.refs_0_, bf16[256,2048]{1,0:T(8,128)(2,1)} %collective-permute-done.2.refs_1_, bf16[256,2048]{1,0:T(8,128)(2,1)} %collective-permute-done.3.refs_2_, ...), custom_call_target="tpu_custom_call" | custom-call | tf_op jit(solution)/shard_map/ffn_near/pallas_call | solution.py:147
  107.5 1.8 collective-permute-done.5.refs_6_
  109.3 1.7 collective-permute-start.11
  111.1 7.1 %ffn_rest.1 = (f32[32,344]{1,0:T(8,128)S(1)}, f32[32,344]{1,0:T(8,128)S(1)}, f32[32,344]{1,0:T(8,128)S(1)}) custom-call(s32[5]{0:T(128)S(1)} %pad_add_fusion.2.off_ref, bf16[128,2048]{1,0:T(8,128)(2,1)S(1)} %collective-permute-done.8.refs_0_.refs_3_, bf16[128,2048]{1,0:T(8,128)(2,1)S(1)} %collective-permute-done.9.refs_1_.refs_4_, ...), custom_call_target="tpu_custom_call" | custom-call | tf_op jit(solution)/shard_map/ffn_rest/pallas_call | solution.py:147
  118.2 2.7 %collective-permute-start.14 = (f32[32,344]{1,0:T(8,128)S(1)}, f32[32,344]{1,0:T(8,128)S(1)}, u32[]{:S(2)}, u32[]{:S(2)}) collective-permute-start(f32[32,344]{1,0:T(8,128)S(1)} %get-tuple-element.260), channel_id=1, source_target_pairs={{1,0},{2,1},{3,2},{0,3},{5,4},{6,5},{7,6},{4,7},{9,8},{10,9},{11,1... | collective-permute-start | bytes 132104 | tf_op jit(solution)/shard_map/ppermute | solution.py:24
  120.9 6.3 %ffn_far.1 = f32[32,344]{1,0:T(8,128)S(1)} custom-call(s32[4]{0:T(128)S(1)} %pad_add_fusion.off_ref, bf16[256,2048]{1,0:T(8,128)(2,1)} %get-tuple-element.239.refs_0_, bf16[256,2048]{1,0:T(8,128)(2,1)} %collective-permute-done.2.refs_1_, bf16[256,2048]{1,0:T(8,128)(2,1)} %collective-permute-done.3.refs_2_, ...), custom_call_target="tpu_custom_call" | custom-call | tf_op jit(solution)/shard_map/ffn_far/pallas_call | solution.py:147
  127.3 4.4 %collective-permute-done.13.u2 = f32[32,344]{1,0:T(8,128)S(1)} collective-permute-done((f32[32,344]{1,0:T(8,128)S(1)}, f32[32,344]{1,0:T(8,128)S(1)}, u32[]{:S(2)}, u32[]{:S(2)}) %collective-permute-start.13) | collective-permute-done | bytes 44064 | tf_op jit(solution)/shard_map/ppermute | solution.py:24
  131.7 2.1 %down.1 = bf16[16,8,2048]{2,1,0:T(8,128)(2,1)} custom-call(s32[16]{0:T(128)S(1)} %stack.107.pos_ref, f32[32,344]{1,0:T(8,128)S(1)} %get-tuple-element.255.u0, f32[32,344]{1,0:T(8,128)S(1)} %collective-permute-done.10.u1, f32[32,344]{1,0:T(8,128)S(1)} %collective-permute-done.13.u2, f32[32,344]{1,0:T(8,128)S(1)} %collective-permute-done.14.u3, ...), custom_call_target="tpu_custom_call" | custom-call | tf_op jit(solution)/shard_map/down/pallas_call | solution.py:179
  133.8 3.7 %all-to-all-start.2 = ((bf16[16,8,2048]{2,1,0:T(8,128)(2,1)}), bf16[16,8,2048]{2,1,0:T(8,128)(2,1)S(1)}, u32[]{:S(2)}, u32[]{:S(2)}) async-start(bf16[16,8,2048]{2,1,0:T(8,128)(2,1)} %down.1), calls=%async_computation.2 | async-start | bytes 1048576 | tf_op jit(solution)/shard_map/all_to_all | solution.py:351
  137.6 9.1 %all-to-all-done.2.t_ref = bf16[16,8,2048]{2,1,0:T(8,128)(2,1)S(1)} async-done(((bf16[16,8,2048]{2,1,0:T(8,128)(2,1)}), bf16[16,8,2048]{2,1,0:T(8,128)(2,1)S(1)}, u32[]{:S(2)}, u32[]{:S(2)}) %all-to-all-start.2) | async-done | bytes 524320 | tf_op jit(solution)/shard_map/all_to_all | solution.py:351
  148.1 9.6 %all-to-all-start.3 = ((bf16[128,2,2176]{2,1,0:T(2,128)(2,1)}), bf16[128,2,2176]{2,1,0:T(2,128)(2,1)S(1)}, u32[]{:S(2)}, u32[]{:S(2)}) async-start(bf16[128,2,2176]{2,1,0:T(2,128)(2,1)} %emb.5), calls=%async_computation.3 | async-start | bytes 2228224 | tf_op jit(solution)/shard_map/all_to_all | solution.py:356
  158.4 18.6 %all-to-all-done.3 = bf16[128,2,2176]{2,1,0:T(2,128)(2,1)S(1)} async-done(((bf16[128,2,2176]{2,1,0:T(2,128)(2,1)}), bf16[128,2,2176]{2,1,0:T(2,128)(2,1)S(1)}, u32[]{:S(2)}, u32[]{:S(2)}) %all-to-all-start.3) | async-done | bytes 1114144 | tf_op jit(solution)/shard_map/all_to_all | solution.py:356
  177.5 5.9 %match.5 = (f32[256,1,128]{2,1,0:T(1,128)}, f32[8,2048]{1,0:T(8,128)S(1)}, f32[1,128]{1,0:T(1,128)S(1)}) custom-call(s32[1]{0:T(128)} %bitcast.37.mp_ref, bf16[256,2176]{1,0:T(8,128)(2,1)S(1)} %reshape.210.rows_ref, bf16[2048,2048]{1,0:T(8,128)(2,1)} %bank_ref.1, f32[1,2048]{1,0:T(1,128)S(1)} %bitcast.84), custom_call_target="tpu_custom_call" | custom-call | tf_op jit(solution)/shard_map/match/pallas_call | solution.py:250
  184.6 4.9 %all-to-all-start.4 = ((f32[256,1,128]{2,1,0:T(1,128)}), f32[256,1,128]{2,1,0:T(1,128)S(1)}, u32[]{:S(2)}, u32[]{:S(2)}) async-start(f32[256,1,128]{2,1,0:T(1,128)} %get-tuple-element.266), calls=%async_computation.4 | async-start | bytes 262144 | tf_op jit(solution)/shard_map/all_to_all | solution.py:360
  190.1 9.6 %all-to-all-done.4 = f32[256,1,128]{2,1,0:T(1,128)S(1)} async-done(((f32[256,1,128]{2,1,0:T(1,128)}), f32[256,1,128]{2,1,0:T(1,128)S(1)}, u32[]{:S(2)}, u32[]{:S(2)}) %all-to-all-start.4) | async-done | bytes 131104 | tf_op jit(solution)/shard_map/all_to_all | solution.py:360
  (91 shorter events, 20.1 us)
Async XLA Ops:
  2.8 9.9 %copy-start.8 = (s32[128]{0:T(128)S(1)}, s32[128]{0:T(128)}, u32[]{:S(2)}) copy-start(s32[128]{0:T(128)} %param.24) | copy-start | bytes 1540
  2.8 10.1 %copy-start.7 = (s32[8]{0:T(128)S(1)}, s32[8]{0:T(128)}, u32[]{:S(2)}) copy-start(s32[8]{0:T(128)} %param.23) | copy-start | bytes 100
  4.0 11.7 %copy-start.5 = (s32[2048]{0:T(1024)S(1)}, s32[2048]{0:T(1024)}, u32[]{:S(2)}) copy-start(s32[2048]{0:T(1024)} %param.27) | copy-start | bytes 24580
  4.0 11.7 %copy-start.6 = (s32[2048]{0:T(1024)S(1)}, s32[2048]{0:T(1024)}, u32[]{:S(2)}) copy-start(s32[2048]{0:T(1024)} %param.26) | copy-start | bytes 24580
  6.4 26.1 %collective-permute-start.3 = (bf16[256,2048]{1,0:T(8,128)(2,1)}, bf16[256,2048]{1,0:T(8,128)(2,1)}, u32[]{:S(2)}, u32[]{:S(2)}) collective-permute-start(bf16[256,2048]{1,0:T(8,128)(2,1)} %get-tuple-element.239.refs_0_), channel_id=1, source_target_pairs={{12,0},{13,1},{14,2},{15,3},{0,4},{1,5},{2,6},{3,7},{4,8},{5,9},{6... | collective-permute-start | bytes 3145736 | tf_op jit(solution)/shard_map/ppermute | solution.py:19
  8.5 24.0 %collective-permute-start.2 = (bf16[256,2048]{1,0:T(8,128)(2,1)}, bf16[256,2048]{1,0:T(8,128)(2,1)}, u32[]{:S(2)}, u32[]{:S(2)}) collective-permute-start(bf16[256,2048]{1,0:T(8,128)(2,1)} %get-tuple-element.239.refs_0_), channel_id=1, source_target_pairs={{4,0},{5,1},{6,2},{7,3},{8,4},{9,5},{10,6},{11,7},{12,8},{13,9},{1... | collective-permute-start | bytes 3145736 | tf_op jit(solution)/shard_map/ppermute | solution.py:19
  9.7 33.1 %collective-permute-start.1 = (bf16[688,1024]{1,0:T(8,128)(2,1)}, bf16[688,1024]{1,0:T(8,128)(2,1)}, u32[]{:S(2)}, u32[]{:S(2)}) collective-permute-start(bf16[688,1024]{1,0:T(8,128)(2,1)} %pad_maximum_fusion), channel_id=1, source_target_pairs={{3,0},{0,1},{1,2},{2,3},{7,4},{4,5},{5,6},{6,7},{11,8},{8,9},{9,10... | collective-permute-start | bytes 4227080 | tf_op jit(solution)/shard_map/ppermute | solution.py:24
  11.2 31.6 %collective-permute-start = (bf16[688,1024]{1,0:T(8,128)(2,1)}, bf16[688,1024]{1,0:T(8,128)(2,1)}, u32[]{:S(2)}, u32[]{:S(2)}) collective-permute-start(bf16[688,1024]{1,0:T(8,128)(2,1)} %pad_maximum_fusion), channel_id=1, source_target_pairs={{1,0},{2,1},{3,2},{0,3},{5,4},{6,5},{7,6},{4,7},{9,8},{10,9},{11,1... | collective-permute-start | bytes 4227080 | tf_op jit(solution)/shard_map/ppermute | solution.py:24
  42.8 50.8 %collective-permute-start.6 = (bf16[688,1024]{1,0:T(8,128)(2,1)}, bf16[688,1024]{1,0:T(8,128)(2,1)}, u32[]{:S(2)}, u32[]{:S(2)}) collective-permute-start(bf16[688,1024]{1,0:T(8,128)(2,1)} %collective-permute-done.a_ref.refs_3_.refs_2_), channel_id=1, source_target_pairs={{16,0},{0,16},{48,32},{32,48},{80,64},{64,80},{112,96},{96,112},{1... | collective-permute-start | bytes 4227080 | tf_op jit(solution)/shard_map/ppermute | solution.py:28
  44.8 51.5 %collective-permute-start.7 = (bf16[688,1024]{1,0:T(8,128)(2,1)}, bf16[688,1024]{1,0:T(8,128)(2,1)}, u32[]{:S(2)}, u32[]{:S(2)}) collective-permute-start(bf16[688,1024]{1,0:T(8,128)(2,1)} %collective-permute-done.1.b_ref.refs_5_.refs_4_), channel_id=1, source_target_pairs={{16,0},{0,16},{48,32},{32,48},{80,64},{64,80},{112,96},{96,112},{1... | collective-permute-start | bytes 4227080 | tf_op jit(solution)/shard_map/ppermute | solution.py:28
  88.7 18.8 %collective-permute-start.4 = (bf16[688,512]{1,0:T(8,128)(2,1)}, bf16[688,512]{1,0:T(8,128)(2,1)S(1)}, u32[]{:S(2)}, u32[]{:S(2)}) collective-permute-start(bf16[688,512]{1,0:T(8,128)(2,1)} %get-tuple-element.246), channel_id=1, source_target_pairs={{1,0},{2,1},{3,2},{0,3},{5,4},{6,5},{7,6},{4,7},{9,8},{10,9},{11,1... | collective-permute-start | bytes 2113544 | tf_op jit(solution)/shard_map/ppermute | solution.py:24
  91.4 17.9 %collective-permute-start.5 = (bf16[688,512]{1,0:T(8,128)(2,1)}, bf16[688,512]{1,0:T(8,128)(2,1)S(1)}, u32[]{:S(2)}, u32[]{:S(2)}) collective-permute-start(bf16[688,512]{1,0:T(8,128)(2,1)} %get-tuple-element.247), channel_id=1, source_target_pairs={{3,0},{0,1},{1,2},{2,3},{7,4},{4,5},{5,6},{6,7},{11,8},{8,9},{9,10... | collective-permute-start | bytes 2113544 | tf_op jit(solution)/shard_map/ppermute | solution.py:24
  93.6 13.9 %collective-permute-start.9 = (bf16[128,2048]{1,0:T(8,128)(2,1)S(1)}, bf16[128,2048]{1,0:T(8,128)(2,1)S(1)}, u32[]{:S(2)}, u32[]{:S(2)}) collective-permute-start(bf16[128,2048]{1,0:T(8,128)(2,1)S(1)} %slice.37), channel_id=1, source_target_pairs={{12,0},{13,1},{14,2},{15,3},{0,4},{1,5},{2,6},{3,7},{4,8},{5,9},{6... | collective-permute-start | bytes 1572872 | tf_op jit(solution)/shard_map/ppermute | solution.py:19
  93.7 13.8 %collective-permute-start.8 = (bf16[128,2048]{1,0:T(8,128)(2,1)S(1)}, bf16[128,2048]{1,0:T(8,128)(2,1)S(1)}, u32[]{:S(2)}, u32[]{:S(2)}) collective-permute-start(bf16[128,2048]{1,0:T(8,128)(2,1)S(1)} %slice.36), channel_id=1, source_target_pairs={{4,0},{5,1},{6,2},{7,3},{8,4},{9,5},{10,6},{11,7},{12,8},{13,9},{1... | collective-permute-start | bytes 1572872 | tf_op jit(solution)/shard_map/ppermute | solution.py:19
  109.3 11.6 %collective-permute-start.11 = (bf16[688,512]{1,0:T(8,128)(2,1)S(1)}, bf16[688,512]{1,0:T(8,128)(2,1)S(1)}, u32[]{:S(2)}, u32[]{:S(2)}) collective-permute-start(bf16[688,512]{1,0:T(8,128)(2,1)S(1)} %collective-permute-done.4.refs_5_), channel_id=1, source_target_pairs={{16,0},{0,16},{48,32},{32,48},{80,64},{64,80},{112,96},{96,112},{1... | collective-permute-start | bytes 2113544 | tf_op jit(solution)/shard_map/ppermute | solution.py:28
  111.0 9.9 %collective-permute-start.12 = (bf16[688,512]{1,0:T(8,128)(2,1)S(1)}, bf16[688,512]{1,0:T(8,128)(2,1)S(1)}, u32[]{:S(2)}, u32[]{:S(2)}) collective-permute-start(bf16[688,512]{1,0:T(8,128)(2,1)S(1)} %collective-permute-done.5.refs_6_), channel_id=1, source_target_pairs={{16,0},{0,16},{48,32},{32,48},{80,64},{64,80},{112,96},{96,112},{1... | collective-permute-start | bytes 2113544 | tf_op jit(solution)/shard_map/ppermute | solution.py:28
  118.2 9.1 %collective-permute-start.10 = (f32[32,344]{1,0:T(8,128)S(1)}, f32[32,344]{1,0:T(8,128)S(1)}, u32[]{:S(2)}, u32[]{:S(2)}) collective-permute-start(f32[32,344]{1,0:T(8,128)S(1)} %get-tuple-element.256), channel_id=1, source_target_pairs={{3,0},{0,1},{1,2},{2,3},{7,4},{4,5},{5,6},{6,7},{11,8},{8,9},{9,10... | collective-permute-start | bytes 132104 | tf_op jit(solution)/shard_map/ppermute | solution.py:24
  118.2 13.5 %copy-start = (bf16[344,2048]{1,0:T(8,128)(2,1)S(1)}, bf16[344,2048]{1,0:T(8,128)(2,1)}, u32[]{:S(2)}) copy-start(bf16[344,2048]{1,0:T(8,128)(2,1)} %w_ref.1) | copy-start | bytes 4227076
  118.2 9.0 %collective-permute-start.14 = (f32[32,344]{1,0:T(8,128)S(1)}, f32[32,344]{1,0:T(8,128)S(1)}, u32[]{:S(2)}, u32[]{:S(2)}) collective-permute-start(f32[32,344]{1,0:T(8,128)S(1)} %get-tuple-element.260), channel_id=1, source_target_pairs={{1,0},{2,1},{3,2},{0,3},{5,4},{6,5},{7,6},{4,7},{9,8},{10,9},{11,1... | collective-permute-start | bytes 132104 | tf_op jit(solution)/shard_map/ppermute | solution.py:24
  127.2 4.5 %collective-permute-start.13 = (f32[32,344]{1,0:T(8,128)S(1)}, f32[32,344]{1,0:T(8,128)S(1)}, u32[]{:S(2)}, u32[]{:S(2)}) collective-permute-start(f32[32,344]{1,0:T(8,128)S(1)} %ffn_far.1), channel_id=1, source_target_pairs={{2,0},{3,1},{0,2},{1,3},{6,4},{7,5},{4,6},{5,7},{10,8},{11,9},{8,1... | collective-permute-start | bytes 132104 | tf_op jit(solution)/shard_map/ppermute | solution.py:24
  133.8 12.9 %all-to-all-start.2 = ((bf16[16,8,2048]{2,1,0:T(8,128)(2,1)}), bf16[16,8,2048]{2,1,0:T(8,128)(2,1)S(1)}, u32[]{:S(2)}, u32[]{:S(2)}) async-start(bf16[16,8,2048]{2,1,0:T(8,128)(2,1)} %down.1), calls=%async_computation.2 | async-start | bytes 1048576 | tf_op jit(solution)/shard_map/all_to_all | solution.py:351
  148.1 28.9 %all-to-all-start.3 = ((bf16[128,2,2176]{2,1,0:T(2,128)(2,1)}), bf16[128,2,2176]{2,1,0:T(2,128)(2,1)S(1)}, u32[]{:S(2)}, u32[]{:S(2)}) async-start(bf16[128,2,2176]{2,1,0:T(2,128)(2,1)} %emb.5), calls=%async_computation.3 | async-start | bytes 2228224 | tf_op jit(solution)/shard_map/all_to_all | solution.py:356
  177.5 12.0 %copy-start.4 = (f32[1,2048]{1,0:T(1,128)S(1)}, f32[1,2048]{1,0:T(1,128)}, u32[]{:S(2)}) copy-start(f32[1,2048]{1,0:T(1,128)} %param.28) | copy-start | bytes 24580
  184.6 15.1 %all-to-all-start.4 = ((f32[256,1,128]{2,1,0:T(1,128)}), f32[256,1,128]{2,1,0:T(1,128)S(1)}, u32[]{:S(2)}, u32[]{:S(2)}) async-start(f32[256,1,128]{2,1,0:T(1,128)} %get-tuple-element.266), calls=%async_computation.4 | async-start | bytes 262144 | tf_op jit(solution)/shard_map/all_to_all | solution.py:360
  (5 other events, 15.3 us)

commit v9 on v8

--- a/solution.py
+++ b/solution.py
@@ -60,31 +60,6 @@
         compiler_params=pltpu.CompilerParams(vmem_limit_bytes=16 * 1024 * 1024),
         name="prep",
     )(lengths, hidden, gain[None, :])
-
-
-def cut_kernel(a_ref, b_ref, left_ref, right_ref, sem):
-    cols = left_ref.shape[1]
-    copies = [
-        pltpu.make_async_copy(a_ref.at[:, pl.ds(0, cols)], left_ref, sem.at[0]),
-        pltpu.make_async_copy(b_ref.at[:, pl.ds(cols, cols)], right_ref, sem.at[1]),
-    ]
-    for cp in copies:
-        cp.start()
-    for cp in copies:
-        cp.wait()
-
-
-def cut_halves(a, b):
-    hbm = pl.BlockSpec(memory_space=pl.ANY)
-    out = jax.ShapeDtypeStruct((a.shape[0], a.shape[1] // 2), a.dtype)
-    return pl.pallas_call(
-        cut_kernel,
-        in_specs=[hbm, hbm],
-        out_specs=(hbm, hbm),
-        out_shape=(out, out),
-        scratch_shapes=[pltpu.SemaphoreType.DMA((2,))],
-        name="cut",
-    )(a, b)
 
 
 def ffn_kernel(plan, n_tok, file_len, off_ref, *refs):
@@ -334,8 +309,7 @@
     zero = jnp.zeros((1,), I32)
     (u0,) = ffn(toks, [[w_own]], (0,), zero, file_len, "ffn_own")
     h1, h3, u0 = tie((h1, h3, u0))
-    left, right = cut_halves(h1, h3)
-    k2a, k2b = from_y(left, 1), from_y(right, 3)
+    k2a, k2b = from_y(h1[:, :quarter], 1), from_y(h3[:, quarter:], 3)
     near = [[h1, from_core(h1)], [h3, from_core(h3)]]
     near_off = jnp.concatenate([h_off, h_off])
     u1, u3 = ffn(toks, near, (0, 0), near_off, file_len, "ffn_near")

time: 202 us -> 155 us (0.77)
  Pallas kernels: 84 us -> 33.8 us
    pallas_call x1 -> x0, Pallas kernels: 43.8 us -> none  [cut_halves(): pl.pallas_call(cut_kernel, in_specs=[hbm, hbm], out_specs=(hbm, hbm), out...]
    pallas_call x4, Pallas kernels: 28.7 us -> 23.2 us  [ffn(): pl.pallas_call(functools.partial(ffn_kernel, plan, len(toks), file_len),...]
    slice x0 -> x2, local copies, waits for them, and re-layouts: none -> 2.3 us  [on_device(): k2a, k2b = (from_y(h1[:, :quarter], 1), from_y(h3[:, quarter:], 3))]
    slice x2, local copies, waits for them, and re-layouts: 2.16 us -> 0.08 us  [on_device(): t2a, t2b = (from_x(t1[:tok // 2], 1), from_x(t3[tok // 2:], 3))]
  transfers between devices with their start and end apart: 18 -> 18, of which waited for: 8 -> 8; matrix products, arithmetic and copies ran while one was open for 3% -> 5% of each run, Pallas kernels for 36% -> 15%
where the time goes in v9:
time: 155 us
  waiting for transfers between devices  66.2 us (43%)
  starting transfers between devices  38.1 us (25%)
  Pallas kernels  33.8 us (22%)
  local copies, waits for them, and re-layouts  9.3 us (6%)
  other arithmetic  3.52 us (2%)
  between operations  3.07 us (2%)
    pallas_call x4, Pallas kernels, ffn(): pl.pallas_call(functools.partial(ffn_kernel, plan, len(toks), file_len),...  23.2 us
    all_to_all x1, waiting for transfers between devices, one_round(): rows = lax.all_to_all(rows, ALL, 0, 0, tiled=True)  18.6 us
    ppermute x4, waiting for transfers between devices, from_x(): return lax.ppermute(v, 'mp', perm)  17 us
    ppermute x7, waiting for transfers between devices, from_y(): return lax.ppermute(v, 'mp', perm)  11.9 us
    ppermute x7, starting transfers between devices, from_y(): return lax.ppermute(v, 'mp', perm)  9.8 us
    all_to_all x1, starting transfers between devices, one_round(): rows = lax.all_to_all(rows, ALL, 0, 0, tiled=True)  9.69 us
    all_to_all x1, waiting for transfers between devices, one_round(): back = lax.all_to_all(top, ALL, 0, 0, tiled=True)  9.57 us
    all_to_all x1, waiting for transfers between devices, on_device(): terms = lax.all_to_all(terms, 'mp', 0, 0, tiled=True)  9.23 us
  transfers between devices with their start and end apart: 18, of which 8 were waited for; matrix products, arithmetic and copies ran while one was open for 5% of the time, Pallas kernels for 15%

profile of v9, /device:TPU:1, one launch (start us, length us, event | category | flops | bytes accessed | tf_op | source)
XLA Modules:
  0.0 154.7 jit_solution(2334913634874184809)
XLA Ops:
  5.5 2.1 %collective-permute-start.3 = (bf16[256,2048]{1,0:T(8,128)(2,1)S(1)}, bf16[256,2048]{1,0:T(8,128)(2,1)S(1)}, u32[]{:S(2)}, u32[]{:S(2)}) collective-permute-start(bf16[256,2048]{1,0:T(8,128)(2,1)S(1)} %get-tuple-element.237.refs_0_), channel_id=1, source_target_pairs={{12,0},{13,1},{14,2},{15,3},{0,4},{1,5},{2,6},{3,7},{4,8},{5,9},{6... | collective-permute-start | bytes 3145736 | tf_op jit(solution)/shard_map/ppermute | solution.py:19
  10.3 1.4 collective-permute-start
  14.9 1.6 %constant_dynamic-update-slice_fusion.1 = bf16[688,2048]{1,0:T(8,128)(2,1)S(1)} fusion(bf16[344,2048]{1,0:T(8,128)(2,1)} %bitcast.80), kind=kLoop, calls=%fused_computation.14 | loop fusion | bytes 2818048
  16.7 14.7 %collective-permute-done.3.refs_2_ = bf16[256,2048]{1,0:T(8,128)(2,1)S(1)} collective-permute-done((bf16[256,2048]{1,0:T(8,128)(2,1)S(1)}, bf16[256,2048]{1,0:T(8,128)(2,1)S(1)}, u32[]{:S(2)}, u32[]{:S(2)}) %collective-permute-start.3) | collective-permute-done | bytes 1048608 | tf_op jit(solution)/shard_map/ppermute | solution.py:19
  31.4 3.4 %ffn_own.1.refs_9_ = f32[24,344]{1,0:T(8,128)S(1)} custom-call(s32[1]{0:T(128)} %constant.220.clone.1.off_ref, bf16[256,2048]{1,0:T(8,128)(2,1)S(1)} %get-tuple-element.237.refs_0_, bf16[256,2048]{1,0:T(8,128)(2,1)S(1)} %collective-permute-done.2.refs_1_, bf16[256,2048]{1,0:T(8,128)(2,1)S(1)} %collective-permute-done.3.refs_2_, ...), custom_call_target="tpu_custom_call" | custom-call | tf_op jit(solution)/shard_map/ffn_own/pallas_call | solution.py:122
  34.8 7.1 %collective-permute-done.1.refs_5_.refs_4_ = bf16[688,1024]{1,0:T(8,128)(2,1)} collective-permute-done((bf16[688,1024]{1,0:T(8,128)(2,1)}, bf16[688,1024]{1,0:T(8,128)(2,1)}, u32[]{:S(2)}, u32[]{:S(2)}) %collective-permute-start.1) | collective-permute-done | bytes 1409056 | tf_op jit(solution)/shard_map/ppermute | solution.py:24
  41.9 2.0 %collective-permute-start.6 = (bf16[688,1024]{1,0:T(8,128)(2,1)}, bf16[688,1024]{1,0:T(8,128)(2,1)S(1)}, u32[]{:S(2)}, u32[]{:S(2)}) collective-permute-start(bf16[688,1024]{1,0:T(8,128)(2,1)} %collective-permute-done.refs_3_.refs_2_), channel_id=1, source_target_pairs={{16,0},{0,16},{48,32},{32,48},{80,64},{64,80},{112,96},{96,112},{1... | collective-permute-start | bytes 4227080 | tf_op jit(solution)/shard_map/ppermute | solution.py:28
  49.3 2.7 %collective-permute-start.8 = (bf16[128,2048]{1,0:T(8,128)(2,1)S(1)}, bf16[128,2048]{1,0:T(8,128)(2,1)S(1)}, u32[]{:S(2)}, u32[]{:S(2)}) collective-permute-start(bf16[128,2048]{1,0:T(8,128)(2,1)S(1)} %slice.44), channel_id=1, source_target_pairs={{4,0},{5,1},{6,2},{7,3},{8,4},{9,5},{10,6},{11,7},{12,8},{13,9},{1... | collective-permute-start | bytes 1572872 | tf_op jit(solution)/shard_map/ppermute | solution.py:19
  52.0 8.6 %ffn_near.1 = (f32[24,344]{1,0:T(8,128)S(1)}, f32[24,344]{1,0:T(8,128)S(1)}) custom-call(s32[4]{0:T(128)S(1)} %pad_add_fusion.3.off_ref, bf16[256,2048]{1,0:T(8,128)(2,1)S(1)} %get-tuple-element.237.refs_0_, bf16[256,2048]{1,0:T(8,128)(2,1)S(1)} %collective-permute-done.2.refs_1_, bf16[256,2048]{1,0:T(8,128)(2,1)S(1)} %collective-permute-done.3.refs_2_, ...), custom_call_target="tpu_custom_call" | custom-call | tf_op jit(solution)/shard_map/ffn_near/pallas_call | solution.py:122
  60.6 2.3 %collective-permute-done.9.refs_1_.refs_4_ = bf16[128,2048]{1,0:T(8,128)(2,1)S(1)} collective-permute-done((bf16[128,2048]{1,0:T(8,128)(2,1)S(1)}, bf16[128,2048]{1,0:T(8,128)(2,1)S(1)}, u32[]{:S(2)}, u32[]{:S(2)}) %collective-permute-start.9) | collective-permute-done | bytes 524320 | tf_op jit(solution)/shard_map/ppermute | solution.py:19
  62.8 1.5 collective-permute-done.5.refs_6_
  64.4 1.4 collective-permute-start.11
  65.9 6.6 %ffn_rest.1 = (f32[32,344]{1,0:T(8,128)S(1)}, f32[32,344]{1,0:T(8,128)S(1)}, f32[32,344]{1,0:T(8,128)S(1)}) custom-call(s32[5]{0:T(128)S(1)} %pad_add_fusion.2.off_ref, bf16[128,2048]{1,0:T(8,128)(2,1)S(1)} %collective-permute-done.8.refs_0_.refs_3_, bf16[128,2048]{1,0:T(8,128)(2,1)S(1)} %collective-permute-done.9.refs_1_.refs_4_, ...), custom_call_target="tpu_custom_call" | custom-call | tf_op jit(solution)/shard_map/ffn_rest/pallas_call | solution.py:122
  73.6 1.7 %collective-permute-start.14 = (f32[32,344]{1,0:T(8,128)S(1)}, f32[32,344]{1,0:T(8,128)S(1)}, u32[]{:S(2)}, u32[]{:S(2)}) collective-permute-start(f32[32,344]{1,0:T(8,128)S(1)} %get-tuple-element.256), channel_id=1, source_target_pairs={{1,0},{2,1},{3,2},{0,3},{5,4},{6,5},{7,6},{4,7},{9,8},{10,9},{11,1... | collective-permute-start | bytes 132104 | tf_op jit(solution)/shard_map/ppermute | solution.py:24
  75.4 4.7 %ffn_far.1 = f32[32,344]{1,0:T(8,128)S(1)} custom-call(s32[4]{0:T(128)S(1)} %pad_add_fusion.off_ref, bf16[256,2048]{1,0:T(8,128)(2,1)S(1)} %get-tuple-element.237.refs_0_, bf16[256,2048]{1,0:T(8,128)(2,1)S(1)} %collective-permute-done.2.refs_1_, bf16[256,2048]{1,0:T(8,128)(2,1)S(1)} %collective-permute-done.3.refs_2_, ...), custom_call_target="tpu_custom_call" | custom-call | tf_op jit(solution)/shard_map/ffn_far/pallas_call | solution.py:122
  81.4 3.2 %collective-permute-done.13.u2 = f32[32,344]{1,0:T(8,128)S(1)} collective-permute-done((f32[32,344]{1,0:T(8,128)S(1)}, f32[32,344]{1,0:T(8,128)S(1)}, u32[]{:S(2)}, u32[]{:S(2)}) %collective-permute-start.13) | collective-permute-done | bytes 44064 | tf_op jit(solution)/shard_map/ppermute | solution.py:24
  84.6 2.1 %down.1 = bf16[16,8,2048]{2,1,0:T(8,128)(2,1)} custom-call(s32[16]{0:T(128)S(1)} %stack.107.pos_ref, f32[32,344]{1,0:T(8,128)S(1)} %get-tuple-element.251.u0, f32[32,344]{1,0:T(8,128)S(1)} %collective-permute-done.10.u1, f32[32,344]{1,0:T(8,128)S(1)} %collective-permute-done.13.u2, f32[32,344]{1,0:T(8,128)S(1)} %collective-permute-done.14.u3, ...), custom_call_target="tpu_custom_call" | custom-call | tf_op jit(solution)/shard_map/down/pallas_call | solution.py:154
  86.6 4.0 %all-to-all-start.2 = ((bf16[16,8,2048]{2,1,0:T(8,128)(2,1)}), bf16[16,8,2048]{2,1,0:T(8,128)(2,1)S(1)}, u32[]{:S(2)}, u32[]{:S(2)}) async-start(bf16[16,8,2048]{2,1,0:T(8,128)(2,1)} %down.1), calls=%async_computation.2 | async-start | bytes 1048576 | tf_op jit(solution)/shard_map/all_to_all | solution.py:325
  90.8 9.2 %all-to-all-done.2.t_ref = bf16[16,8,2048]{2,1,0:T(8,128)(2,1)S(1)} async-done(((bf16[16,8,2048]{2,1,0:T(8,128)(2,1)}), bf16[16,8,2048]{2,1,0:T(8,128)(2,1)S(1)}, u32[]{:S(2)}, u32[]{:S(2)}) %all-to-all-start.2) | async-done | bytes 524320 | tf_op jit(solution)/shard_map/all_to_all | solution.py:325
  101.4 9.7 %all-to-all-start.3 = ((bf16[128,2,2176]{2,1,0:T(2,128)(2,1)}), bf16[128,2,2176]{2,1,0:T(2,128)(2,1)S(1)}, u32[]{:S(2)}, u32[]{:S(2)}) async-start(bf16[128,2,2176]{2,1,0:T(2,128)(2,1)} %emb.5), calls=%async_computation.3 | async-start | bytes 2228224 | tf_op jit(solution)/shard_map/all_to_all | solution.py:330
  111.7 18.6 %all-to-all-done.3 = bf16[128,2,2176]{2,1,0:T(2,128)(2,1)S(1)} async-done(((bf16[128,2,2176]{2,1,0:T(2,128)(2,1)}), bf16[128,2,2176]{2,1,0:T(2,128)(2,1)S(1)}, u32[]{:S(2)}, u32[]{:S(2)}) %all-to-all-start.3) | async-done | bytes 1114144 | tf_op jit(solution)/shard_map/all_to_all | solution.py:330
  130.8 5.9 %match.5 = (f32[256,1,128]{2,1,0:T(1,128)}, f32[8,2048]{1,0:T(8,128)S(1)}, f32[1,128]{1,0:T(1,128)S(1)}) custom-call(s32[1]{0:T(128)} %bitcast.37.mp_ref, bf16[256,2176]{1,0:T(8,128)(2,1)S(1)} %reshape.210.rows_ref, bf16[2048,2048]{1,0:T(8,128)(2,1)} %bank_ref.1, f32[1,2048]{1,0:T(1,128)S(1)} %bitcast.84), custom_call_target="tpu_custom_call" | custom-call | tf_op jit(solution)/shard_map/match/pallas_call | solution.py:225
  138.0 5.0 %all-to-all-start.4 = ((f32[256,1,128]{2,1,0:T(1,128)}), f32[256,1,128]{2,1,0:T(1,128)S(1)}, u32[]{:S(2)}, u32[]{:S(2)}) async-start(f32[256,1,128]{2,1,0:T(1,128)} %get-tuple-element.262), calls=%async_computation.4 | async-start | bytes 262144 | tf_op jit(solution)/shard_map/all_to_all | solution.py:334
  143.6 9.6 %all-to-all-done.4 = f32[256,1,128]{2,1,0:T(1,128)S(1)} async-done(((f32[256,1,128]{2,1,0:T(1,128)}), f32[256,1,128]{2,1,0:T(1,128)S(1)}, u32[]{:S(2)}, u32[]{:S(2)}) %all-to-all-start.4) | async-done | bytes 131104 | tf_op jit(solution)/shard_map/all_to_all | solution.py:334
  (92 shorter events, 22.5 us)
Async XLA Ops:
  2.8 9.0 %copy-start.8 = (s32[128]{0:T(128)S(1)}, s32[128]{0:T(128)}, u32[]{:S(2)}) copy-start(s32[128]{0:T(128)} %param.24) | copy-start | bytes 1540
  2.8 9.2 %copy-start.7 = (s32[8]{0:T(128)S(1)}, s32[8]{0:T(128)}, u32[]{:S(2)}) copy-start(s32[8]{0:T(128)} %param.23) | copy-start | bytes 100
  4.0 10.8 %copy-start.5 = (s32[2048]{0:T(1024)S(1)}, s32[2048]{0:T(1024)}, u32[]{:S(2)}) copy-start(s32[2048]{0:T(1024)} %param.27) | copy-start | bytes 24580
  4.0 10.8 %copy-start.6 = (s32[2048]{0:T(1024)S(1)}, s32[2048]{0:T(1024)}, u32[]{:S(2)}) copy-start(s32[2048]{0:T(1024)} %param.26) | copy-start | bytes 24580
  5.5 25.9 %collective-permute-start.3 = (bf16[256,2048]{1,0:T(8,128)(2,1)S(1)}, bf16[256,2048]{1,0:T(8,128)(2,1)S(1)}, u32[]{:S(2)}, u32[]{:S(2)}) collective-permute-start(bf16[256,2048]{1,0:T(8,128)(2,1)S(1)} %get-tuple-element.237.refs_0_), channel_id=1, source_target_pairs={{12,0},{13,1},{14,2},{15,3},{0,4},{1,5},{2,6},{3,7},{4,8},{5,9},{6... | collective-permute-start | bytes 3145736 | tf_op jit(solution)/shard_map/ppermute | solution.py:19
  7.6 23.8 %collective-permute-start.2 = (bf16[256,2048]{1,0:T(8,128)(2,1)S(1)}, bf16[256,2048]{1,0:T(8,128)(2,1)S(1)}, u32[]{:S(2)}, u32[]{:S(2)}) collective-permute-start(bf16[256,2048]{1,0:T(8,128)(2,1)S(1)} %get-tuple-element.237.refs_0_), channel_id=1, source_target_pairs={{4,0},{5,1},{6,2},{7,3},{8,4},{9,5},{10,6},{11,7},{12,8},{13,9},{1... | collective-permute-start | bytes 3145736 | tf_op jit(solution)/shard_map/ppermute | solution.py:19
  8.9 33.0 %collective-permute-start.1 = (bf16[688,1024]{1,0:T(8,128)(2,1)}, bf16[688,1024]{1,0:T(8,128)(2,1)}, u32[]{:S(2)}, u32[]{:S(2)}) collective-permute-start(bf16[688,1024]{1,0:T(8,128)(2,1)} %pad_maximum_fusion), channel_id=1, source_target_pairs={{3,0},{0,1},{1,2},{2,3},{7,4},{4,5},{5,6},{6,7},{11,8},{8,9},{9,10... | collective-permute-start | bytes 4227080 | tf_op jit(solution)/shard_map/ppermute | solution.py:24
  10.3 31.6 %collective-permute-start = (bf16[688,1024]{1,0:T(8,128)(2,1)}, bf16[688,1024]{1,0:T(8,128)(2,1)}, u32[]{:S(2)}, u32[]{:S(2)}) collective-permute-start(bf16[688,1024]{1,0:T(8,128)(2,1)} %pad_maximum_fusion), channel_id=1, source_target_pairs={{1,0},{2,1},{3,2},{0,3},{5,4},{6,5},{7,6},{4,7},{9,8},{10,9},{11,1... | collective-permute-start | bytes 4227080 | tf_op jit(solution)/shard_map/ppermute | solution.py:24
  41.9 7.3 %collective-permute-start.6 = (bf16[688,1024]{1,0:T(8,128)(2,1)}, bf16[688,1024]{1,0:T(8,128)(2,1)S(1)}, u32[]{:S(2)}, u32[]{:S(2)}) collective-permute-start(bf16[688,1024]{1,0:T(8,128)(2,1)} %collective-permute-done.refs_3_.refs_2_), channel_id=1, source_target_pairs={{16,0},{0,16},{48,32},{32,48},{80,64},{64,80},{112,96},{96,112},{1... | collective-permute-start | bytes 4227080 | tf_op jit(solution)/shard_map/ppermute | solution.py:28
  44.0 8.0 %collective-permute-start.7 = (bf16[688,1024]{1,0:T(8,128)(2,1)}, bf16[688,1024]{1,0:T(8,128)(2,1)S(1)}, u32[]{:S(2)}, u32[]{:S(2)}) collective-permute-start(bf16[688,1024]{1,0:T(8,128)(2,1)} %collective-permute-done.1.refs_5_.refs_4_), channel_id=1, source_target_pairs={{16,0},{0,16},{48,32},{32,48},{80,64},{64,80},{112,96},{96,112},{1... | collective-permute-start | bytes 4227080 | tf_op jit(solution)/shard_map/ppermute | solution.py:28
  46.3 18.1 %collective-permute-start.5 = (bf16[688,512]{1,0:T(8,128)(2,1)S(1)}, bf16[688,512]{1,0:T(8,128)(2,1)S(1)}, u32[]{:S(2)}, u32[]{:S(2)}) collective-permute-start(bf16[688,512]{1,0:T(8,128)(2,1)S(1)} %slice.43), channel_id=1, source_target_pairs={{3,0},{0,1},{1,2},{2,3},{7,4},{4,5},{5,6},{6,7},{11,8},{8,9},{9,10... | collective-permute-start | bytes 2113544 | tf_op jit(solution)/shard_map/ppermute | solution.py:24
  47.6 16.8 %collective-permute-start.4 = (bf16[688,512]{1,0:T(8,128)(2,1)S(1)}, bf16[688,512]{1,0:T(8,128)(2,1)S(1)}, u32[]{:S(2)}, u32[]{:S(2)}) collective-permute-start(bf16[688,512]{1,0:T(8,128)(2,1)S(1)} %slice.42), channel_id=1, source_target_pairs={{1,0},{2,1},{3,2},{0,3},{5,4},{6,5},{7,6},{4,7},{9,8},{10,9},{11,1... | collective-permute-start | bytes 2113544 | tf_op jit(solution)/shard_map/ppermute | solution.py:24
  49.2 13.7 %collective-permute-start.9 = (bf16[128,2048]{1,0:T(8,128)(2,1)S(1)}, bf16[128,2048]{1,0:T(8,128)(2,1)S(1)}, u32[]{:S(2)}, u32[]{:S(2)}) collective-permute-start(bf16[128,2048]{1,0:T(8,128)(2,1)S(1)} %slice.45), channel_id=1, source_target_pairs={{12,0},{13,1},{14,2},{15,3},{0,4},{1,5},{2,6},{3,7},{4,8},{5,9},{6... | collective-permute-start | bytes 1572872 | tf_op jit(solution)/shard_map/ppermute | solution.py:19
  49.3 13.6 %collective-permute-start.8 = (bf16[128,2048]{1,0:T(8,128)(2,1)S(1)}, bf16[128,2048]{1,0:T(8,128)(2,1)S(1)}, u32[]{:S(2)}, u32[]{:S(2)}) collective-permute-start(bf16[128,2048]{1,0:T(8,128)(2,1)S(1)} %slice.44), channel_id=1, source_target_pairs={{4,0},{5,1},{6,2},{7,3},{8,4},{9,5},{10,6},{11,7},{12,8},{13,9},{1... | collective-permute-start | bytes 1572872 | tf_op jit(solution)/shard_map/ppermute | solution.py:19
  64.4 11.0 %collective-permute-start.11 = (bf16[688,512]{1,0:T(8,128)(2,1)S(1)}, bf16[688,512]{1,0:T(8,128)(2,1)S(1)}, u32[]{:S(2)}, u32[]{:S(2)}) collective-permute-start(bf16[688,512]{1,0:T(8,128)(2,1)S(1)} %collective-permute-done.4.refs_5_), channel_id=1, source_target_pairs={{16,0},{0,16},{48,32},{32,48},{80,64},{64,80},{112,96},{96,112},{1... | collective-permute-start | bytes 2113544 | tf_op jit(solution)/shard_map/ppermute | solution.py:28
  65.8 9.5 %collective-permute-start.12 = (bf16[688,512]{1,0:T(8,128)(2,1)S(1)}, bf16[688,512]{1,0:T(8,128)(2,1)S(1)}, u32[]{:S(2)}, u32[]{:S(2)}) collective-permute-start(bf16[688,512]{1,0:T(8,128)(2,1)S(1)} %collective-permute-done.5.refs_6_), channel_id=1, source_target_pairs={{16,0},{0,16},{48,32},{32,48},{80,64},{64,80},{112,96},{96,112},{1... | collective-permute-start | bytes 2113544 | tf_op jit(solution)/shard_map/ppermute | solution.py:28
  72.6 8.8 %collective-permute-start.10 = (f32[32,344]{1,0:T(8,128)S(1)}, f32[32,344]{1,0:T(8,128)S(1)}, u32[]{:S(2)}, u32[]{:S(2)}) collective-permute-start(f32[32,344]{1,0:T(8,128)S(1)} %get-tuple-element.252), channel_id=1, source_target_pairs={{3,0},{0,1},{1,2},{2,3},{7,4},{4,5},{5,6},{6,7},{11,8},{8,9},{9,10... | collective-permute-start | bytes 132104 | tf_op jit(solution)/shard_map/ppermute | solution.py:24
  73.6 10.9 %copy-start = (bf16[344,2048]{1,0:T(8,128)(2,1)S(1)}, bf16[344,2048]{1,0:T(8,128)(2,1)}, u32[]{:S(2)}) copy-start(bf16[344,2048]{1,0:T(8,128)(2,1)} %w_ref.1) | copy-start | bytes 4227076
  73.6 7.8 %collective-permute-start.14 = (f32[32,344]{1,0:T(8,128)S(1)}, f32[32,344]{1,0:T(8,128)S(1)}, u32[]{:S(2)}, u32[]{:S(2)}) collective-permute-start(f32[32,344]{1,0:T(8,128)S(1)} %get-tuple-element.256), channel_id=1, source_target_pairs={{1,0},{2,1},{3,2},{0,3},{5,4},{6,5},{7,6},{4,7},{9,8},{10,9},{11,1... | collective-permute-start | bytes 132104 | tf_op jit(solution)/shard_map/ppermute | solution.py:24
  80.1 4.5 %collective-permute-start.13 = (f32[32,344]{1,0:T(8,128)S(1)}, f32[32,344]{1,0:T(8,128)S(1)}, u32[]{:S(2)}, u32[]{:S(2)}) collective-permute-start(f32[32,344]{1,0:T(8,128)S(1)} %ffn_far.1), channel_id=1, source_target_pairs={{2,0},{3,1},{0,2},{1,3},{6,4},{7,5},{4,6},{5,7},{10,8},{11,9},{8,1... | collective-permute-start | bytes 132104 | tf_op jit(solution)/shard_map/ppermute | solution.py:24
  86.6 13.3 %all-to-all-start.2 = ((bf16[16,8,2048]{2,1,0:T(8,128)(2,1)}), bf16[16,8,2048]{2,1,0:T(8,128)(2,1)S(1)}, u32[]{:S(2)}, u32[]{:S(2)}) async-start(bf16[16,8,2048]{2,1,0:T(8,128)(2,1)} %down.1), calls=%async_computation.2 | async-start | bytes 1048576 | tf_op jit(solution)/shard_map/all_to_all | solution.py:325
  101.4 29.0 %all-to-all-start.3 = ((bf16[128,2,2176]{2,1,0:T(2,128)(2,1)}), bf16[128,2,2176]{2,1,0:T(2,128)(2,1)S(1)}, u32[]{:S(2)}, u32[]{:S(2)}) async-start(bf16[128,2,2176]{2,1,0:T(2,128)(2,1)} %emb.5), calls=%async_computation.3 | async-start | bytes 2228224 | tf_op jit(solution)/shard_map/all_to_all | solution.py:330
  130.8 12.2 %copy-start.4 = (f32[1,2048]{1,0:T(1,128)S(1)}, f32[1,2048]{1,0:T(1,128)}, u32[]{:S(2)}) copy-start(f32[1,2048]{1,0:T(1,128)} %param.28) | copy-start | bytes 24580
  138.0 15.2 %all-to-all-start.4 = ((f32[256,1,128]{2,1,0:T(1,128)}), f32[256,1,128]{2,1,0:T(1,128)S(1)}, u32[]{:S(2)}, u32[]{:S(2)}) async-start(f32[256,1,128]{2,1,0:T(1,128)} %get-tuple-element.262), calls=%async_computation.4 | async-start | bytes 262144 | tf_op jit(solution)/shard_map/all_to_all | solution.py:334
  (5 other events, 14.4 us)

commit v10 on v9

--- a/solution.py
+++ b/solution.py
@@ -324,25 +324,23 @@
     terms = down([u0, r1, r2, r3], w_down, pos, files)
     terms = lax.all_to_all(terms, "mp", 0, 0, tiled=True)
 
-    def one_round(ready, best, sums, counts, _):
+    def one_round(ready, best, sums, counts):
         here, sel, meta = ready
         rows = emb_to_owners(terms, pooled_in, lens, sel, meta, n_mp)
         rows = lax.all_to_all(rows, ALL, 0, 0, tiled=True)
         top, new, about = match(rows.reshape(-1, rows.shape[2]), mp, bank, bank_key)
-        sums, counts = sums + new[:1], counts + about[0, 0]
-        centroid = (count_old[:, None] * centroid_old + sums) / (count_old + counts)[:, None]
         back = lax.all_to_all(top, ALL, 0, 0, tiled=True)
         back = jnp.max(back.reshape(n_dp, n_mp, 2, -1), axis=1)[:, :, 0]
         best = jnp.maximum(best, jnp.max(jnp.where(here, back[:, :, None], -1.0), axis=(0, 1)))
-        return about[0, 1], (best, sums, counts, centroid)
-
-    blank = jnp.zeros((1, width), F32)
-    most, state = one_round(ready, jnp.full((files,), -1.0, F32), blank, jnp.float32(0), blank)
-    _, (best, _, _, centroid_new) = lax.while_loop(
+        return about[0, 1], (best, sums + new[:1], counts + about[0, 0])
+
+    most, state = one_round(ready, jnp.full((files,), -1.0, F32), jnp.zeros((1, width), F32), jnp.float32(0))
+    _, (best, sums, counts) = lax.while_loop(
         lambda s: 2 * s[0] < most.astype(I32),
         lambda s: (s[0] + 1, one_round(files_of(s[0]), *s[1])[1]),
         (jnp.int32(1), state),
     )
+    centroid_new = (count_old[:, None] * centroid_old + sums) / (count_old + counts)[:, None]
     return best, centroid_new
 
 

time: 155 us -> 154 us (level)
  blocking collectives: 0 us -> 28.8 us
  waiting for transfers between devices: 66.2 us -> 47 us
  starting transfers between devices: 38.1 us -> 28.4 us
    all_to_all x0 -> x1, blocking collectives: none -> 28.8 us  [one_round(): rows = lax.all_to_all(rows, ALL, 0, 0, tiled=True)]
    all_to_all x1 -> x0, waiting for transfers between devices: 18.6 us -> none  [one_round(): rows = lax.all_to_all(rows, ALL, 0, 0, tiled=True)]
    all_to_all x1 -> x0, starting transfers between devices: 9.69 us -> none  [one_round(): rows = lax.all_to_all(rows, ALL, 0, 0, tiled=True)]
  transfers between devices with their start and end apart: 18 -> 17, of which waited for: 8 -> 7; matrix products, arithmetic and copies ran while one was open for 5% -> 5% of each run, Pallas kernels for 15% -> 15%
where the time goes in v10:
time: 154 us; the launch traced here: 153 us
  waiting for transfers between devices  47 us (31%)
  Pallas kernels  32.7 us (21%)
  blocking collectives  28.8 us (19%)
  starting transfers between devices  28.4 us (18%)
  local copies, waits for them, and re-layouts  8.82 us (6%)
  other arithmetic  3.5 us (2%)
  between operations  3.05 us (2%)
    all_to_all x1, blocking collectives, one_round(): rows = lax.all_to_all(rows, ALL, 0, 0, tiled=True)  28.8 us
    pallas_call x4, Pallas kernels, ffn(): pl.pallas_call(functools.partial(ffn_kernel, plan, len(toks), file_len),...  23.2 us
    ppermute x4, waiting for transfers between devices, from_x(): return lax.ppermute(v, 'mp', perm)  17 us
    ppermute x7, waiting for transfers between devices, from_y(): return lax.ppermute(v, 'mp', perm)  11.9 us
    ppermute x7, starting transfers between devices, from_y(): return lax.ppermute(v, 'mp', perm)  9.8 us
    all_to_all x1, waiting for transfers between devices, on_device(): terms = lax.all_to_all(terms, 'mp', 0, 0, tiled=True)  9.23 us
    all_to_all x1, waiting for transfers between devices, one_round(): back = lax.all_to_all(top, ALL, 0, 0, tiled=True)  8.89 us
    ppermute x4, starting transfers between devices, from_x(): return lax.ppermute(v, 'mp', perm)  6.19 us
  transfers between devices with their start and end apart: 17, of which 7 were waited for; matrix products, arithmetic and copies ran while one was open for 5% of the time, Pallas kernels for 15%

profile of v10, /device:TPU:1, one launch (start us, length us, event | category | flops | bytes accessed | tf_op | source)
XLA Modules:
  0.0 152.9 jit_solution(8356663148986221110)
XLA Ops:
  5.5 2.1 %collective-permute-start.3 = (bf16[256,2048]{1,0:T(8,128)(2,1)S(1)}, bf16[256,2048]{1,0:T(8,128)(2,1)S(1)}, u32[]{:S(2)}, u32[]{:S(2)}) collective-permute-start(bf16[256,2048]{1,0:T(8,128)(2,1)S(1)} %get-tuple-element.206.refs_0_), channel_id=1, source_target_pairs={{12,0},{13,1},{14,2},{15,3},{0,4},{1,5},{2,6},{3,7},{4,8},{5,9},{6... | collective-permute-start | bytes 3145736 | tf_op jit(solution)/shard_map/ppermute | solution.py:19
  10.3 1.4 collective-permute-start
  14.9 1.6 %constant_dynamic-update-slice_fusion.1 = bf16[688,2048]{1,0:T(8,128)(2,1)S(1)} fusion(bf16[344,2048]{1,0:T(8,128)(2,1)} %bitcast.71), kind=kLoop, calls=%fused_computation.13 | loop fusion | bytes 2818048
  16.7 14.7 %collective-permute-done.3.refs_2_ = bf16[256,2048]{1,0:T(8,128)(2,1)S(1)} collective-permute-done((bf16[256,2048]{1,0:T(8,128)(2,1)S(1)}, bf16[256,2048]{1,0:T(8,128)(2,1)S(1)}, u32[]{:S(2)}, u32[]{:S(2)}) %collective-permute-start.3) | collective-permute-done | bytes 1048608 | tf_op jit(solution)/shard_map/ppermute | solution.py:19
  31.4 3.4 %ffn_own.1.refs_9_ = f32[24,344]{1,0:T(8,128)S(1)} custom-call(s32[1]{0:T(128)} %constant.220.clone.1.off_ref, bf16[256,2048]{1,0:T(8,128)(2,1)S(1)} %get-tuple-element.206.refs_0_, bf16[256,2048]{1,0:T(8,128)(2,1)S(1)} %collective-permute-done.2.refs_1_, bf16[256,2048]{1,0:T(8,128)(2,1)S(1)} %collective-permute-done.3.refs_2_, ...), custom_call_target="tpu_custom_call" | custom-call | tf_op jit(solution)/shard_map/ffn_own/pallas_call | solution.py:122
  34.8 7.1 %collective-permute-done.1.refs_5_.refs_4_ = bf16[688,1024]{1,0:T(8,128)(2,1)} collective-permute-done((bf16[688,1024]{1,0:T(8,128)(2,1)}, bf16[688,1024]{1,0:T(8,128)(2,1)}, u32[]{:S(2)}, u32[]{:S(2)}) %collective-permute-start.1) | collective-permute-done | bytes 1409056 | tf_op jit(solution)/shard_map/ppermute | solution.py:24
  41.9 2.0 %collective-permute-start.6 = (bf16[688,1024]{1,0:T(8,128)(2,1)}, bf16[688,1024]{1,0:T(8,128)(2,1)S(1)}, u32[]{:S(2)}, u32[]{:S(2)}) collective-permute-start(bf16[688,1024]{1,0:T(8,128)(2,1)} %collective-permute-done.refs_3_.refs_2_), channel_id=1, source_target_pairs={{16,0},{0,16},{48,32},{32,48},{80,64},{64,80},{112,96},{96,112},{1... | collective-permute-start | bytes 4227080 | tf_op jit(solution)/shard_map/ppermute | solution.py:28
  47.6 1.4 collective-permute-start.4
  49.3 2.7 %collective-permute-start.8 = (bf16[128,2048]{1,0:T(8,128)(2,1)S(1)}, bf16[128,2048]{1,0:T(8,128)(2,1)S(1)}, u32[]{:S(2)}, u32[]{:S(2)}) collective-permute-start(bf16[128,2048]{1,0:T(8,128)(2,1)S(1)} %slice.44), channel_id=1, source_target_pairs={{4,0},{5,1},{6,2},{7,3},{8,4},{9,5},{10,6},{11,7},{12,8},{13,9},{1... | collective-permute-start | bytes 1572872 | tf_op jit(solution)/shard_map/ppermute | solution.py:19
  52.0 8.6 %ffn_near.1 = (f32[24,344]{1,0:T(8,128)S(1)}, f32[24,344]{1,0:T(8,128)S(1)}) custom-call(s32[4]{0:T(128)S(1)} %pad_add_fusion.3.off_ref, bf16[256,2048]{1,0:T(8,128)(2,1)S(1)} %get-tuple-element.206.refs_0_, bf16[256,2048]{1,0:T(8,128)(2,1)S(1)} %collective-permute-done.2.refs_1_, bf16[256,2048]{1,0:T(8,128)(2,1)S(1)} %collective-permute-done.3.refs_2_, ...), custom_call_target="tpu_custom_call" | custom-call | tf_op jit(solution)/shard_map/ffn_near/pallas_call | solution.py:122
  60.6 2.3 %collective-permute-done.9.refs_1_.refs_4_ = bf16[128,2048]{1,0:T(8,128)(2,1)S(1)} collective-permute-done((bf16[128,2048]{1,0:T(8,128)(2,1)S(1)}, bf16[128,2048]{1,0:T(8,128)(2,1)S(1)}, u32[]{:S(2)}, u32[]{:S(2)}) %collective-permute-start.9) | collective-permute-done | bytes 524320 | tf_op jit(solution)/shard_map/ppermute | solution.py:19
  62.8 1.5 %collective-permute-done.5.refs_6_ = bf16[688,512]{1,0:T(8,128)(2,1)S(1)} collective-permute-done((bf16[688,512]{1,0:T(8,128)(2,1)S(1)}, bf16[688,512]{1,0:T(8,128)(2,1)S(1)}, u32[]{:S(2)}, u32[]{:S(2)}) %collective-permute-start.5) | collective-permute-done | bytes 704544 | tf_op jit(solution)/shard_map/ppermute | solution.py:24
  64.4 1.4 collective-permute-start.11
  65.9 6.7 %ffn_rest.1 = (f32[32,344]{1,0:T(8,128)S(1)}, f32[32,344]{1,0:T(8,128)S(1)}, f32[32,344]{1,0:T(8,128)S(1)}) custom-call(s32[5]{0:T(128)S(1)} %pad_add_fusion.2.off_ref, bf16[128,2048]{1,0:T(8,128)(2,1)S(1)} %collective-permute-done.8.refs_0_.refs_3_, bf16[128,2048]{1,0:T(8,128)(2,1)S(1)} %collective-permute-done.9.refs_1_.refs_4_, ...), custom_call_target="tpu_custom_call" | custom-call | tf_op jit(solution)/shard_map/ffn_rest/pallas_call | solution.py:122
  73.6 1.7 %collective-permute-start.14 = (f32[32,344]{1,0:T(8,128)S(1)}, f32[32,344]{1,0:T(8,128)S(1)}, u32[]{:S(2)}, u32[]{:S(2)}) collective-permute-start(f32[32,344]{1,0:T(8,128)S(1)} %get-tuple-element.225), channel_id=1, source_target_pairs={{1,0},{2,1},{3,2},{0,3},{5,4},{6,5},{7,6},{4,7},{9,8},{10,9},{11,1... | collective-permute-start | bytes 132104 | tf_op jit(solution)/shard_map/ppermute | solution.py:24
  75.4 4.7 %ffn_far.1 = f32[32,344]{1,0:T(8,128)S(1)} custom-call(s32[4]{0:T(128)S(1)} %pad_add_fusion.off_ref, bf16[256,2048]{1,0:T(8,128)(2,1)S(1)} %get-tuple-element.206.refs_0_, bf16[256,2048]{1,0:T(8,128)(2,1)S(1)} %collective-permute-done.2.refs_1_, bf16[256,2048]{1,0:T(8,128)(2,1)S(1)} %collective-permute-done.3.refs_2_, ...), custom_call_target="tpu_custom_call" | custom-call | tf_op jit(solution)/shard_map/ffn_far/pallas_call | solution.py:122
  81.4 3.2 %collective-permute-done.13.u2 = f32[32,344]{1,0:T(8,128)S(1)} collective-permute-done((f32[32,344]{1,0:T(8,128)S(1)}, f32[32,344]{1,0:T(8,128)S(1)}, u32[]{:S(2)}, u32[]{:S(2)}) %collective-permute-start.13) | collective-permute-done | bytes 44064 | tf_op jit(solution)/shard_map/ppermute | solution.py:24
  84.6 2.1 %down.1 = bf16[16,8,2048]{2,1,0:T(8,128)(2,1)} custom-call(s32[16]{0:T(128)S(1)} %stack.107.pos_ref, f32[32,344]{1,0:T(8,128)S(1)} %get-tuple-element.220.u0, f32[32,344]{1,0:T(8,128)S(1)} %collective-permute-done.10.u1, f32[32,344]{1,0:T(8,128)S(1)} %collective-permute-done.13.u2, f32[32,344]{1,0:T(8,128)S(1)} %collective-permute-done.14.u3, ...), custom_call_target="tpu_custom_call" | custom-call | tf_op jit(solution)/shard_map/down/pallas_call | solution.py:154
  86.7 4.0 %all-to-all-start.2 = ((bf16[16,8,2048]{2,1,0:T(8,128)(2,1)}), bf16[16,8,2048]{2,1,0:T(8,128)(2,1)S(1)}, u32[]{:S(2)}, u32[]{:S(2)}) async-start(bf16[16,8,2048]{2,1,0:T(8,128)(2,1)} %down.1), calls=%async_computation.2 | async-start | bytes 1048576 | tf_op jit(solution)/shard_map/all_to_all | solution.py:325
  90.7 9.2 %all-to-all-done.2.t_ref = bf16[16,8,2048]{2,1,0:T(8,128)(2,1)S(1)} async-done(((bf16[16,8,2048]{2,1,0:T(8,128)(2,1)}), bf16[16,8,2048]{2,1,0:T(8,128)(2,1)S(1)}, u32[]{:S(2)}, u32[]{:S(2)}) %all-to-all-start.2) | async-done | bytes 524320 | tf_op jit(solution)/shard_map/all_to_all | solution.py:325
  100.4 28.8 %all_to_all.33 = bf16[128,2,2176]{2,1,0:T(2,128)(2,1)S(1)} all-to-all(bf16[128,2,2176]{2,1,0:T(2,128)(2,1)S(1)} %emb.5), channel_id=1, replica_groups=mesh['dp'=8,'mp'=16] {'dp','mp'}, dimensions={0} | all-to-all | bytes 2228224 | tf_op jit(solution)/shard_map/all_to_all | solution.py:330
  129.6 5.9 %match.5 = (f32[256,1,128]{2,1,0:T(1,128)}, f32[8,2048]{1,0:T(8,128)S(1)}, f32[1,128]{1,0:T(1,128)S(1)}) custom-call(s32[1]{0:T(128)} %bitcast.34.mp_ref, bf16[256,2176]{1,0:T(8,128)(2,1)S(1)} %reshape.190.rows_ref, bf16[2048,2048]{1,0:T(8,128)(2,1)} %bank_ref.1, f32[1,2048]{1,0:T(1,128)S(1)} %bitcast.75), custom_call_target="tpu_custom_call" | custom-call | tf_op jit(solution)/shard_map/match/pallas_call | solution.py:225
  135.5 5.0 %all-to-all-start.4 = ((f32[256,1,128]{2,1,0:T(1,128)}), f32[256,1,128]{2,1,0:T(1,128)S(1)}, u32[]{:S(2)}, u32[]{:S(2)}) async-start(f32[256,1,128]{2,1,0:T(1,128)} %get-tuple-element.231), calls=%async_computation.4 | async-start | bytes 262144 | tf_op jit(solution)/shard_map/all_to_all | solution.py:332
  141.8 8.9 %all-to-all-done.4 = f32[256,1,128]{2,1,0:T(1,128)S(1)} async-done(((f32[256,1,128]{2,1,0:T(1,128)}), f32[256,1,128]{2,1,0:T(1,128)S(1)}, u32[]{:S(2)}, u32[]{:S(2)}) %all-to-all-start.4) | async-done | bytes 131104 | tf_op jit(solution)/shard_map/all_to_all | solution.py:332
  (92 shorter events, 19.5 us)
Async XLA Ops:
  2.8 9.0 %copy-start.8 = (s32[128]{0:T(128)S(1)}, s32[128]{0:T(128)}, u32[]{:S(2)}) copy-start(s32[128]{0:T(128)} %param.24) | copy-start | bytes 1540
  2.8 9.0 %copy-start.9 = (s32[8]{0:T(128)S(1)}, s32[8]{0:T(128)}, u32[]{:S(2)}) copy-start(s32[8]{0:T(128)} %param.22) | copy-start | bytes 100
  2.8 9.2 %copy-start.7 = (s32[8]{0:T(128)S(1)}, s32[8]{0:T(128)}, u32[]{:S(2)}) copy-start(s32[8]{0:T(128)} %param.23) | copy-start | bytes 100
  4.0 10.8 %copy-start.4 = (s32[2048]{0:T(1024)S(1)}, s32[2048]{0:T(1024)}, u32[]{:S(2)}) copy-start(s32[2048]{0:T(1024)} %param.27) | copy-start | bytes 24580
  4.0 10.8 %copy-start.5 = (s32[2048]{0:T(1024)S(1)}, s32[2048]{0:T(1024)}, u32[]{:S(2)}) copy-start(s32[2048]{0:T(1024)} %param.26) | copy-start | bytes 24580
  5.5 25.9 %collective-permute-start.3 = (bf16[256,2048]{1,0:T(8,128)(2,1)S(1)}, bf16[256,2048]{1,0:T(8,128)(2,1)S(1)}, u32[]{:S(2)}, u32[]{:S(2)}) collective-permute-start(bf16[256,2048]{1,0:T(8,128)(2,1)S(1)} %get-tuple-element.206.refs_0_), channel_id=1, source_target_pairs={{12,0},{13,1},{14,2},{15,3},{0,4},{1,5},{2,6},{3,7},{4,8},{5,9},{6... | collective-permute-start | bytes 3145736 | tf_op jit(solution)/shard_map/ppermute | solution.py:19
  7.6 23.8 %collective-permute-start.2 = (bf16[256,2048]{1,0:T(8,128)(2,1)S(1)}, bf16[256,2048]{1,0:T(8,128)(2,1)S(1)}, u32[]{:S(2)}, u32[]{:S(2)}) collective-permute-start(bf16[256,2048]{1,0:T(8,128)(2,1)S(1)} %get-tuple-element.206.refs_0_), channel_id=1, source_target_pairs={{4,0},{5,1},{6,2},{7,3},{8,4},{9,5},{10,6},{11,7},{12,8},{13,9},{1... | collective-permute-start | bytes 3145736 | tf_op jit(solution)/shard_map/ppermute | solution.py:19
  8.9 33.0 %collective-permute-start.1 = (bf16[688,1024]{1,0:T(8,128)(2,1)}, bf16[688,1024]{1,0:T(8,128)(2,1)}, u32[]{:S(2)}, u32[]{:S(2)}) collective-permute-start(bf16[688,1024]{1,0:T(8,128)(2,1)} %pad_maximum_fusion), channel_id=1, source_target_pairs={{3,0},{0,1},{1,2},{2,3},{7,4},{4,5},{5,6},{6,7},{11,8},{8,9},{9,10... | collective-permute-start | bytes 4227080 | tf_op jit(solution)/shard_map/ppermute | solution.py:24
  10.3 31.6 %collective-permute-start = (bf16[688,1024]{1,0:T(8,128)(2,1)}, bf16[688,1024]{1,0:T(8,128)(2,1)}, u32[]{:S(2)}, u32[]{:S(2)}) collective-permute-start(bf16[688,1024]{1,0:T(8,128)(2,1)} %pad_maximum_fusion), channel_id=1, source_target_pairs={{1,0},{2,1},{3,2},{0,3},{5,4},{6,5},{7,6},{4,7},{9,8},{10,9},{11,1... | collective-permute-start | bytes 4227080 | tf_op jit(solution)/shard_map/ppermute | solution.py:24
  14.9 1.8 %copy-start.3 = (bf16[2048,344]{0,1:T(8,128)(2,1)S(1)}, bf16[2048,344]{0,1:T(8,128)(2,1)}, u32[]{:S(2)}) copy-start(bf16[2048,344]{0,1:T(8,128)(2,1)} %param.19) | copy-start | bytes 4227076
  41.9 7.3 %collective-permute-start.6 = (bf16[688,1024]{1,0:T(8,128)(2,1)}, bf16[688,1024]{1,0:T(8,128)(2,1)S(1)}, u32[]{:S(2)}, u32[]{:S(2)}) collective-permute-start(bf16[688,1024]{1,0:T(8,128)(2,1)} %collective-permute-done.refs_3_.refs_2_), channel_id=1, source_target_pairs={{16,0},{0,16},{48,32},{32,48},{80,64},{64,80},{112,96},{96,112},{1... | collective-permute-start | bytes 4227080 | tf_op jit(solution)/shard_map/ppermute | solution.py:28
  44.0 8.0 %collective-permute-start.7 = (bf16[688,1024]{1,0:T(8,128)(2,1)}, bf16[688,1024]{1,0:T(8,128)(2,1)S(1)}, u32[]{:S(2)}, u32[]{:S(2)}) collective-permute-start(bf16[688,1024]{1,0:T(8,128)(2,1)} %collective-permute-done.1.refs_5_.refs_4_), channel_id=1, source_target_pairs={{16,0},{0,16},{48,32},{32,48},{80,64},{64,80},{112,96},{96,112},{1... | collective-permute-start | bytes 4227080 | tf_op jit(solution)/shard_map/ppermute | solution.py:28
  46.3 18.1 %collective-permute-start.5 = (bf16[688,512]{1,0:T(8,128)(2,1)S(1)}, bf16[688,512]{1,0:T(8,128)(2,1)S(1)}, u32[]{:S(2)}, u32[]{:S(2)}) collective-permute-start(bf16[688,512]{1,0:T(8,128)(2,1)S(1)} %slice.43), channel_id=1, source_target_pairs={{3,0},{0,1},{1,2},{2,3},{7,4},{4,5},{5,6},{6,7},{11,8},{8,9},{9,10... | collective-permute-start | bytes 2113544 | tf_op jit(solution)/shard_map/ppermute | solution.py:24
  47.6 16.8 %collective-permute-start.4 = (bf16[688,512]{1,0:T(8,128)(2,1)S(1)}, bf16[688,512]{1,0:T(8,128)(2,1)S(1)}, u32[]{:S(2)}, u32[]{:S(2)}) collective-permute-start(bf16[688,512]{1,0:T(8,128)(2,1)S(1)} %slice.42), channel_id=1, source_target_pairs={{1,0},{2,1},{3,2},{0,3},{5,4},{6,5},{7,6},{4,7},{9,8},{10,9},{11,1... | collective-permute-start | bytes 2113544 | tf_op jit(solution)/shard_map/ppermute | solution.py:24
  49.2 13.7 %collective-permute-start.9 = (bf16[128,2048]{1,0:T(8,128)(2,1)S(1)}, bf16[128,2048]{1,0:T(8,128)(2,1)S(1)}, u32[]{:S(2)}, u32[]{:S(2)}) collective-permute-start(bf16[128,2048]{1,0:T(8,128)(2,1)S(1)} %slice.45), channel_id=1, source_target_pairs={{12,0},{13,1},{14,2},{15,3},{0,4},{1,5},{2,6},{3,7},{4,8},{5,9},{6... | collective-permute-start | bytes 1572872 | tf_op jit(solution)/shard_map/ppermute | solution.py:19
  49.3 13.6 %collective-permute-start.8 = (bf16[128,2048]{1,0:T(8,128)(2,1)S(1)}, bf16[128,2048]{1,0:T(8,128)(2,1)S(1)}, u32[]{:S(2)}, u32[]{:S(2)}) collective-permute-start(bf16[128,2048]{1,0:T(8,128)(2,1)S(1)} %slice.44), channel_id=1, source_target_pairs={{4,0},{5,1},{6,2},{7,3},{8,4},{9,5},{10,6},{11,7},{12,8},{13,9},{1... | collective-permute-start | bytes 1572872 | tf_op jit(solution)/shard_map/ppermute | solution.py:19
  64.4 11.0 %collective-permute-start.11 = (bf16[688,512]{1,0:T(8,128)(2,1)S(1)}, bf16[688,512]{1,0:T(8,128)(2,1)S(1)}, u32[]{:S(2)}, u32[]{:S(2)}) collective-permute-start(bf16[688,512]{1,0:T(8,128)(2,1)S(1)} %collective-permute-done.4.refs_5_), channel_id=1, source_target_pairs={{16,0},{0,16},{48,32},{32,48},{80,64},{64,80},{112,96},{96,112},{1... | collective-permute-start | bytes 2113544 | tf_op jit(solution)/shard_map/ppermute | solution.py:28
  65.8 9.6 %collective-permute-start.12 = (bf16[688,512]{1,0:T(8,128)(2,1)S(1)}, bf16[688,512]{1,0:T(8,128)(2,1)S(1)}, u32[]{:S(2)}, u32[]{:S(2)}) collective-permute-start(bf16[688,512]{1,0:T(8,128)(2,1)S(1)} %collective-permute-done.5.refs_6_), channel_id=1, source_target_pairs={{16,0},{0,16},{48,32},{32,48},{80,64},{64,80},{112,96},{96,112},{1... | collective-permute-start | bytes 2113544 | tf_op jit(solution)/shard_map/ppermute | solution.py:28
  72.6 8.8 %collective-permute-start.10 = (f32[32,344]{1,0:T(8,128)S(1)}, f32[32,344]{1,0:T(8,128)S(1)}, u32[]{:S(2)}, u32[]{:S(2)}) collective-permute-start(f32[32,344]{1,0:T(8,128)S(1)} %get-tuple-element.221), channel_id=1, source_target_pairs={{3,0},{0,1},{1,2},{2,3},{7,4},{4,5},{5,6},{6,7},{11,8},{8,9},{9,10... | collective-permute-start | bytes 132104 | tf_op jit(solution)/shard_map/ppermute | solution.py:24
  73.6 10.9 %copy-start = (bf16[344,2048]{1,0:T(8,128)(2,1)S(1)}, bf16[344,2048]{1,0:T(8,128)(2,1)}, u32[]{:S(2)}) copy-start(bf16[344,2048]{1,0:T(8,128)(2,1)} %w_ref.1) | copy-start | bytes 4227076
  73.6 7.8 %collective-permute-start.14 = (f32[32,344]{1,0:T(8,128)S(1)}, f32[32,344]{1,0:T(8,128)S(1)}, u32[]{:S(2)}, u32[]{:S(2)}) collective-permute-start(f32[32,344]{1,0:T(8,128)S(1)} %get-tuple-element.225), channel_id=1, source_target_pairs={{1,0},{2,1},{3,2},{0,3},{5,4},{6,5},{7,6},{4,7},{9,8},{10,9},{11,1... | collective-permute-start | bytes 132104 | tf_op jit(solution)/shard_map/ppermute | solution.py:24
  80.1 4.5 %collective-permute-start.13 = (f32[32,344]{1,0:T(8,128)S(1)}, f32[32,344]{1,0:T(8,128)S(1)}, u32[]{:S(2)}, u32[]{:S(2)}) collective-permute-start(f32[32,344]{1,0:T(8,128)S(1)} %ffn_far.1), channel_id=1, source_target_pairs={{2,0},{3,1},{0,2},{1,3},{6,4},{7,5},{4,6},{5,7},{10,8},{11,9},{8,1... | collective-permute-start | bytes 132104 | tf_op jit(solution)/shard_map/ppermute | solution.py:24
  86.7 13.3 %all-to-all-start.2 = ((bf16[16,8,2048]{2,1,0:T(8,128)(2,1)}), bf16[16,8,2048]{2,1,0:T(8,128)(2,1)S(1)}, u32[]{:S(2)}, u32[]{:S(2)}) async-start(bf16[16,8,2048]{2,1,0:T(8,128)(2,1)} %down.1), calls=%async_computation.2 | async-start | bytes 1048576 | tf_op jit(solution)/shard_map/all_to_all | solution.py:325
  135.5 15.2 %all-to-all-start.4 = ((f32[256,1,128]{2,1,0:T(1,128)}), f32[256,1,128]{2,1,0:T(1,128)S(1)}, u32[]{:S(2)}, u32[]{:S(2)}) async-start(f32[256,1,128]{2,1,0:T(1,128)} %get-tuple-element.231), calls=%async_computation.4 | async-start | bytes 262144 | tf_op jit(solution)/shard_map/all_to_all | solution.py:332
  (4 other events, 5.7 us)
